TPU v7x, 32 devices: a whole 2x2x4 slice. The times are simulated.
32 devices in a mesh: filter: 8 (over z, x), space: 4 (over y, core).
Axes of the slice: x: 2, y: 2, z: 4, core: 2. Of those that a mesh axis runs over, the one named last changes fastest.
Arguments:
- volume: bfloat16 [1024, 16, 1024], P('filter', 'space'), may hold values from -6 to 6
- mixing: bfloat16 [1024, 1024], P('filter'), may hold values from -0.1875 to 0.1875
- kernel_taps: float32 [1024, 27], P('filter'), may hold values from -1.25 to 1.25
- upstream: bfloat16 [1024, 16, 1024], P('filter', 'space'), may hold values from -6 to 6
Outputs:
- output: bfloat16 [1024, 16, 1024], P('filter', 'space')
- volume_grad: bfloat16 [1024, 16, 1024], P('filter', 'space')
- mixing_grad: float32 [1024, 1024], P('filter', 'space')
- taps_grad: float32 [1024, 27], P('filter')
All inputs are finite; a program needn't handle non-finite values.
Results may differ from a plain program's by a relative error of at most 0.0055.
Values may be sent and summed in bfloat16 or wider, within the bound.
No kernel may reach another device: no remote copies, remote signals or barrier semaphores. Data moves between devices by JAX's collectives and lax.ppermute only.
A program may use at most 64 MiB of HBM per device.

v0:
```python
import math

import jax
import jax.numpy as jnp
from jax import lax
from jax.sharding import PartitionSpec as P

WW = 64


def padded_2(array, sides, width):
    for axis, dim in sides:
        size, length = (lax.axis_size(axis), array.shape[dim])
        up = [(i, (i + 1) % size) for i in range(size - 1)]
        down = [(j, i) for i, j in up]
        last = lax.slice_in_dim(array, length - width, length, axis=dim)
        leading = lax.slice_in_dim(array, 0, width, axis=dim)
        before = lax.ppermute(last, axis, up)
        after = lax.ppermute(leading, axis, down)
        array = jnp.concatenate([before, array, after], axis=dim)
    return array


def pad_rows_cols(field):
    return jnp.pad(field, ((0, 0), (0, 0), (1, 1), (1, 1)))


def depth_conv(padded, kernel_taps, flip):
    depth = padded.shape[1] - 2
    height = padded.shape[2] - 2
    breadth = padded.shape[3] - 2
    summed = jnp.zeros((padded.shape[0], depth, height, breadth), jnp.float32)
    for plane_off in range(3):
        for row_off in range(3):
            for col_off in range(3):
                index_tap = plane_off * 9 + row_off * 3 + col_off
                if flip:
                    plane_at, row_at, col_at = (2 - plane_off, 2 - row_off, 2 - col_off)
                else:
                    plane_at, row_at, col_at = (plane_off, row_off, col_off)
                window = padded[
                    :,
                    plane_at : plane_at + depth,
                    row_at : row_at + height,
                    col_at : col_at + breadth,
                ]
                summed = summed + kernel_taps[:, index_tap][:, None, None, None] * window.astype(
                    jnp.float32
                )
    return summed


def tap_grads(grad_field, padded):
    depth = grad_field.shape[1]
    height = grad_field.shape[2]
    breadth = grad_field.shape[3]
    grad_wide = grad_field.astype(jnp.float32)
    columns_list = []
    for plane_off in range(3):
        for row_off in range(3):
            for col_off in range(3):
                window = padded[
                    :,
                    plane_off : plane_off + depth,
                    row_off : row_off + height,
                    col_off : col_off + breadth,
                ]
                columns_list.append(jnp.sum(grad_wide * window.astype(jnp.float32), axis=(1, 2, 3)))
    return jnp.stack(columns_list, axis=1)


def silu_slope(values):
    sig_val = jax.nn.sigmoid(values)
    return sig_val * (1.0 + values * (1.0 - sig_val))


def body(volume, mixing, kernel_taps, upstream):
    channels = volume.shape[0]
    planes = volume.shape[1]
    flat_cells = volume.shape[2]
    row_count = flat_cells // WW
    slab_cells = planes * flat_cells
    space_count = lax.axis_size("space")
    norm_factor = 1.0 / math.sqrt(planes * space_count * flat_cells)
    flat_vol = volume.reshape(channels, slab_cells)
    vol_all = lax.all_gather(flat_vol, "filter", axis=0, tiled=True)
    mixed = jnp.dot(mixing, vol_all, preferred_element_type=jnp.float32).astype(jnp.bfloat16)
    mixed_grid = mixed.reshape(channels, planes, row_count, WW)
    up_grid = upstream.reshape(channels, planes, row_count, WW)
    mixed_rim = padded_2(mixed_grid, (("space", 1),), 1)
    mixed_pad = pad_rows_cols(mixed_rim)
    spatial = depth_conv(mixed_pad, kernel_taps, False)
    grad_own = (up_grid.astype(jnp.float32) * silu_slope(spatial)).astype(jnp.bfloat16)
    grad_wide = padded_2(grad_own, (("space", 1),), 1)
    vol_grid = volume.reshape(channels, planes, row_count, WW).astype(jnp.float32)
    output = (
        (vol_grid + jax.nn.silu(spatial)).astype(jnp.bfloat16).reshape(channels, planes, flat_cells)
    )
    spatial_grad = grad_wide[:, 1:-1]
    mixed_grad = (
        depth_conv(pad_rows_cols(grad_wide), kernel_taps, True)
        .astype(jnp.bfloat16)
        .reshape(channels, slab_cells)
    )
    taps_part = tap_grads(spatial_grad, mixed_pad) * norm_factor
    taps_grad = lax.psum(taps_part, "space")
    weight_cols = lax.all_to_all(mixing, "filter", split_axis=1, concat_axis=0, tiled=True)
    back_sum = lax.dot_general(
        weight_cols,
        lax.all_gather(mixed_grad, "filter", axis=0, tiled=True),
        (((0,), (0,)), ((), ())),
        preferred_element_type=jnp.float32,
    )
    weight_term = (
        lax.dot_general(
            mixed_grad, vol_all, (((1,), (1,)), ((), ())), preferred_element_type=jnp.float32
        )
        * norm_factor
    )
    mixing_grad = lax.psum_scatter(weight_term, "space", scatter_dimension=1, tiled=True)
    volume_grad = (
        (upstream.reshape(channels, slab_cells).astype(jnp.float32) + back_sum)
        .astype(jnp.bfloat16)
        .reshape(channels, planes, flat_cells)
    )
    return (output, volume_grad, mixing_grad, taps_grad)


def solution(mesh):
    in_specs = (
        P("filter", "space", None),
        P("filter", None),
        P("filter", None),
        P("filter", "space", None),
    )
    out_specs = (
        P("filter", "space", None),
        P("filter", "space", None),
        P("filter", "space"),
        P("filter", None),
    )
    return jax.shard_map(body, mesh=mesh, in_specs=in_specs, out_specs=out_specs, check_vma=False)
```

profile of v0, /device:TPU:0, one launch (start us, length us, event | category | flops | bytes accessed | tf_op | source)
XLA Modules:
  0.0 345.5 jit_solution(3254620114481869023)
XLA Ops:
  7.2 2.6 copy.22
  9.9 128.5 %all-gather.3.cloned.1.call-done = bf16[1024,4096]{1,0:T(8,128)(2,1)} async-done(((bf16[128,4096]{1,0:T(8,128)(2,1)}), bf16[1024,4096]{1,0:T(8,128)(2,1)}) %all-gather.3.cloned.1.call-update) | async-done | bytes 8388624 | tf_op jit(solution)/shard_map/all_gather | solution.py:86
  138.4 4.6 %convolution_convert_fusion = bf16[128,4096]{1,0:T(8,128)(2,1)S(1)} fusion(bf16[128,1024]{1,0:T(8,128)(2,1)S(1)} %copy-done.6, bf16[1024,4096]{1,0:T(8,128)(2,1)} %all-gather.3.cloned.1.call-done), kind=kOutput, calls=%fused_computation.35 | convolution fusion | flops 1074266112 | bytes 9699328 | tf_op jit(solution)/shard_map/dot_general | solution.py:87
  143.0 0.7 copy.16
  143.8 1.3 collective-permute-start
  145.1 1.3 collective-permute-start.1
  146.4 1.9 copy.17
  148.4 0.1 convert_element_type.292
  148.6 1.8 collective-permute-done.1
  150.3 2.6 select_maximum_fusion.2
  152.9 14.7 %fusion.71 = (f32[128]{0:T(128)S(1)}, f32[128]{0:T(128)S(1)}, f32[128]{0:T(128)S(1)}, f32[128]{0:T(128)S(1)}, f32[128]{0:T(128)S(1)}, /*index=5*/f32[128]{0:T(12...) fusion(bf16[128,6,18,66]{0,3,2,1:T(8,128)(2,1)S(1)} %select_max, ...), kind=kLoop, calls=%fused_computation.132 | loop fusion | flops 67106560 | bytes 32004608 | tf_op jit(solution)/shard_map/reduce_sum | solution.py:68
  167.7 6.7 %collective-permute-start.2 = (bf16[128,1,16,64]{0,3,2,1:T(8,128)(2,1)S(1)}, bf16[128,1,16,64]{0,3,2,1:T(8,128)(2,1)S(1)}, u32[]{:S(2)}, u32[]{:S(2)}) collective-permute-start(bf16[128,1,16,64]{0,3,2,1:T(8,128)(2,1)S(1)} %get-tuple-element.47), channel_id=1, source_target_pairs={{0,1},{1,2},{2,3},{4,5},{5,6},{6,7},{8,9},{9,10},{10,11},{12,13},{... | collective-permute-start | bytes 786440 | tf_op jit(solution)/shard_map/ppermute | solution.py:18
  174.3 1.3 collective-permute-start.3
  175.6 2.1 collective-permute-done.3
  177.8 1.6 select_maximum_fusion
  179.4 8.7 %fusion.73 = bf16[128,4,16,64]{0,3,2,1:T(8,128)(2,1)} fusion(bf16[128,4,16,64]{0,3,2,1:T(8,128)(2,1)S(1)} %get-tuple-element.45, bf16[128,6,18,66]{0,3,2,1:T(8,128)(2,1)S(1)} %select_maximum_fusion, bf16[128,1,16,64]{0,3,2,1:T(8,128)(2,1)S(1)} %collective-permute-done.2, bf16[128,1,16,64]{0,3,2,1:T(8,128)(2,1)S(1)} %collective-permute-done.3, ...), kind=kLoop, calls=%fused_computation.137 | loop fusion | flops 43515904 | bytes 27801088 | tf_op jit(solution)/shard_map/convert_element_type | solution.py:102
  188.2 1.8 copy.18
  190.0 4.0 %all-to-all-start = ((bf16[128,8,128]{0,2,1:T(8,128)(2,1)}), bf16[128,8,128]{0,2,1:T(8,128)(2,1)}, u32[]{:S(2)}, u32[]{:S(2)}) async-start(bf16[128,8,128]{0,2,1:T(8,128)(2,1)} %bitcast.121), calls=%async_computation | async-start | bytes 524288 | tf_op jit(solution)/shard_map/all_to_all | solution.py:107
  194.0 0.2 reduce-scatter.2.cloned.1.call-start
  194.2 2.6 copy.15
  196.9 5.5 %all-to-all-done = bf16[128,8,128]{0,2,1:T(8,128)(2,1)} async-done(((bf16[128,8,128]{0,2,1:T(8,128)(2,1)}), bf16[128,8,128]{0,2,1:T(8,128)(2,1)}, u32[]{:S(2)}, u32[]{:S(2)}) %all-to-all-start) | async-done | bytes 262176 | tf_op jit(solution)/shard_map/all_to_all | solution.py:107
  202.4 1.8 copy.19
  204.2 4.0 %fusion.70 = (f32[128]{0:T(128)S(1)}, f32[128]{0:T(128)S(1)}, f32[128]{0:T(128)S(1)}, f32[128]{0:T(128)S(1)}, f32[128]{0:T(128)S(1)}, /*index=5*/f32[128]{0:T(12...) fusion(bf16[128,4,16,64]{0,3,2,1:T(8,128)(2,1)} %copy-done, bf16[128,6,18,66]{0,3,2,1:T(8,128)(2,1)S(1)} %select_maximum_fusion.2, ...), kind=kLoop, calls=%fused_computation.131 | loop fusion | flops 15727488 | bytes 9966080 | tf_op jit(solution)/shard_map/reduce_sum | solution.py:68
  208.2 7.3 %convolution_multiply_fusion = f32[128,1024]{1,0:T(8,128)} fusion(bf16[128,4096]{0,1:T(8,128)(2,1)S(1)} %bitcast.114, bf16[1024,4096]{1,0:T(8,128)(2,1)} %all-gather.3.cloned.1.call-done), kind=kOutput, calls=%fused_computation.143 | convolution fusion | flops 1073872896 | bytes 9961472 | tf_op jit(solution)/shard_map/dot_general | solution.py:115
  215.6 1.6 fusion.72
  217.1 2.8 copy.20
  219.9 0.1 stack.111
  220.0 21.5 %psum.7 = f32[128,27]{0,1:T(8,128)} all-reduce(f32[128,27]{0,1:T(8,128)S(1)} %broadcast_multiply_fusion), channel_id=1, replica_groups=mesh['filter'=8,'space'=4] {'space'}, use_global_device_ids=true, to_apply=%region_28.29 | all-reduce | flops 3456 | bytes 27648 | tf_op jit(solution)/shard_map/psum | solution.py:106
  241.5 74.5 %all-gather.5.cloned.1.call-done = bf16[1024,4096]{0,1:T(8,128)(2,1)} async-done(((bf16[128,4096]{0,1:T(8,128)(2,1)}), bf16[1024,4096]{0,1:T(8,128)(2,1)}) %all-gather.5.cloned.1.call-update) | async-done | bytes 8388624 | tf_op jit(solution)/shard_map/all_gather | solution.py:110
  316.0 5.7 %fusion.1 = bf16[128,4096]{0,1:T(8,128)(2,1)S(1)} fusion(f32[128,4096]{0,1:T(8,128)S(1)} %bitcast.112, bf16[1024,4096]{0,1:T(8,128)(2,1)} %all-gather.5.cloned.1.call-done, bf16[1024,128]{1,0:T(8,128)(2,1)S(1)} %bitcast.120), kind=kOutput, calls=%fused_computation.34 | convolution fusion | flops 1074790400 | bytes 11796480 | tf_op jit(solution)/shard_map/dot_general | solution.py:108
  321.7 1.7 copy.21
  323.4 15.5 %reduce-scatter.2.cloned.1.call-done = f32[128,256]{1,0:T(8,128)} async-done(((f32[128,1024]{1,0:T(8,128)}), f32[128,256]{1,0:T(8,128)}) %reduce-scatter.2.cloned.1.call-update) | async-done | bytes 131088 | tf_op jit(solution)/shard_map/reduce_scatter | solution.py:120
  (30 shorter events, 0.3 us)
Async XLA Ops:
  7.2 131.2 %copy-start.6 = (bf16[128,1024]{1,0:T(8,128)(2,1)S(1)}, bf16[128,1024]{1,0:T(8,128)(2,1)}, u32[]{:S(2)}) copy-start(bf16[128,1024]{1,0:T(8,128)(2,1)} %param.5) | copy-start | bytes 786436
  7.2 131.2 %all-gather.3.cloned.1.call-start = ((), (), s32[]{:S(2)}) async-start(), calls=%async_computation.2 | async-start | bytes 9437184 | tf_op jit(solution)/shard_map/all_gather | solution.py:86
  9.9 306.1 %all-gather.5.cloned.1.call-start = ((), (), s32[]{:S(2)}) async-start(), calls=%async_computation.3 | async-start | bytes 9437184 | tf_op jit(solution)/shard_map/all_gather | solution.py:110
  143.0 3.4 copy-start.8
  143.8 4.8 %collective-permute-start = (bf16[128,1,16,64]{0,3,2,1:T(8,128)(2,1)S(1)}, bf16[128,1,16,64]{0,3,2,1:T(8,128)(2,1)S(1)}, u32[]{:S(2)}, u32[]{:S(2)}) collective-permute-start(bf16[128,1,16,64]{0,3,2,1:T(8,128)(2,1)S(1)} %get-tuple-element.49), channel_id=1, source_target_pairs={{0,1},{1,2},{2,3},{4,5},{5,6},{6,7},{8,9},{9,10},{10,11},{12,13},{... | collective-permute-start | bytes 786440 | tf_op jit(solution)/shard_map/ppermute | solution.py:18
  145.1 5.2 %collective-permute-start.1 = (bf16[128,1,16,64]{0,3,2,1:T(8,128)(2,1)S(1)}, bf16[128,1,16,64]{0,3,2,1:T(8,128)(2,1)}, u32[]{:S(2)}, u32[]{:S(2)}) collective-permute-start(bf16[128,1,16,64]{0,3,2,1:T(8,128)(2,1)S(1)} %get-tuple-element.50), channel_id=1, source_target_pairs={{1,0},{2,1},{3,2},{5,4},{6,5},{7,6},{9,8},{10,9},{11,10},{13,12},{... | collective-permute-start | bytes 786440 | tf_op jit(solution)/shard_map/ppermute | solution.py:19
  148.5 19.1 %copy-start.1 = (f32[128,4,1024]{0,2,1:T(8,128)}, f32[128,4,1024]{0,2,1:T(8,128)S(1)}, u32[]{:S(2)}) copy-start(f32[128,4,1024]{0,2,1:T(8,128)S(1)} %convert_element_type.292) | copy-start | bytes 6291460
  167.6 11.8 %copy-start = (bf16[128,4,16,64]{0,3,2,1:T(8,128)(2,1)}, bf16[128,4,16,64]{0,3,2,1:T(8,128)(2,1)S(1)}, u32[]{:S(2)}) copy-start(bf16[128,4,16,64]{0,3,2,1:T(8,128)(2,1)S(1)} %get-tuple-element.45) | copy-start | bytes 3145732
  167.7 8.0 %collective-permute-start.2 = (bf16[128,1,16,64]{0,3,2,1:T(8,128)(2,1)S(1)}, bf16[128,1,16,64]{0,3,2,1:T(8,128)(2,1)S(1)}, u32[]{:S(2)}, u32[]{:S(2)}) collective-permute-start(bf16[128,1,16,64]{0,3,2,1:T(8,128)(2,1)S(1)} %get-tuple-element.47), channel_id=1, source_target_pairs={{0,1},{1,2},{2,3},{4,5},{5,6},{6,7},{8,9},{9,10},{10,11},{12,13},{... | collective-permute-start | bytes 786440 | tf_op jit(solution)/shard_map/ppermute | solution.py:18
  174.3 3.4 collective-permute-start.3
  190.0 12.4 %all-to-all-start = ((bf16[128,8,128]{0,2,1:T(8,128)(2,1)}), bf16[128,8,128]{0,2,1:T(8,128)(2,1)}, u32[]{:S(2)}, u32[]{:S(2)}) async-start(bf16[128,8,128]{0,2,1:T(8,128)(2,1)} %bitcast.121), calls=%async_computation | async-start | bytes 524288 | tf_op jit(solution)/shard_map/all_to_all | solution.py:107
  194.0 144.9 %reduce-scatter.2.cloned.1.call-start = ((), (), s32[]{:S(2)}) async-start(), calls=%async_computation.4 | async-start | bytes 655360 | tf_op jit(solution)/shard_map/reduce_scatter | solution.py:120
  204.2 4.0 %copy-start.3 = (bf16[128,4,16,64]{0,3,2,1:T(8,128)(2,1)S(1)}, bf16[128,4,16,64]{0,3,2,1:T(8,128)(2,1)}, u32[]{:S(2)}) copy-start(bf16[128,4,16,64]{0,3,2,1:T(8,128)(2,1)} %fusion.73) | copy-start | bytes 3145732
  208.2 7.3 %copy-start.4 = (f32[128,4,16,64]{0,3,2,1:T(8,128)S(1)}, f32[128,4,16,64]{0,3,2,1:T(8,128)}, u32[]{:S(2)}) copy-start(f32[128,4,16,64]{0,3,2,1:T(8,128)} %get-tuple-element.46) | copy-start | bytes 6291460
  208.2 7.3 %copy-start.5 = (bf16[128,4,1024]{0,2,1:T(8,128)(2,1)S(1)}, bf16[128,4,1024]{0,2,1:T(8,128)(2,1)}, u32[]{:S(2)}) copy-start(bf16[128,4,1024]{0,2,1:T(8,128)(2,1)} %copy.15) | copy-start | bytes 3145732
  215.5 100.5 %copy-start.7 = (bf16[8,128,128]{2,1,0:T(8,128)(2,1)S(1)}, bf16[8,128,128]{2,1,0:T(8,128)(2,1)}, u32[]{:S(2)}) copy-start(bf16[8,128,128]{2,1,0:T(8,128)(2,1)} %copy.19) | copy-start | bytes 786436
  217.1 98.9 %copy-start.2 = (f32[128,4,1024]{0,2,1:T(8,128)S(1)}, f32[128,4,1024]{0,2,1:T(8,128)}, u32[]{:S(2)}) copy-start(f32[128,4,1024]{0,2,1:T(8,128)} %copy-done.1) | copy-start | bytes 6291460
Sparse Core Ops, SparseCore 0:
  10.7 127.6 all-gather.2
  188.3 127.6 all-gather.4
  319.1 19.8 reduce-scatter.1
where the time goes:
time: 346 us; the launch traced here: 345 us
  waiting for transfers between devices  228 us (66%)
  other arithmetic  33.4 us (10%)
  blocking collectives  21.5 us (6%)
  matrix products  17.6 us (5%)
  local copies, waits for them, and re-layouts  16.2 us (5%)
  starting transfers between devices  14.9 us (4%)
  between operations  14 us (4%)
    all_gather x1, waiting for transfers between devices, body(): vol_all = lax.all_gather(flat_vol, 'filter', axis=0, tiled=True)  128 us
    all_gather x1, waiting for transfers between devices, body(): lax.all_gather(mixed_grad, 'filter', axis=0, tiled=True)  74.5 us
    psum x1, blocking collectives, body(): taps_grad = lax.psum(taps_part, 'space')  21.5 us
    reduce_sum x2, other arithmetic, tap_grads(): jnp.sum(grad_wide * window.astype(jnp.float32), axis=(1, 2, 3))  18.7 us
    reduce_scatter x1, waiting for transfers between devices, body(): lax.psum_scatter(weight_term, 'space', scatter_dimension=1, tiled=True)  15.5 us
    unnamed x24, local copies, waits for them, and re-layouts  13.5 us
    convert_element_type x1, other arithmetic, body(): mixed_grad = depth_conv(pad_rows_cols(grad_wide), kernel_taps, True).asty...  8.74 us
    ppermute x2, starting transfers between devices, padded_2(): before = lax.ppermute(last, axis, up)  8 us
  transfers between devices with their start and end apart: 8, of which 6 were waited for; matrix products, arithmetic and copies ran while one was open for 9% of the time, Pallas kernels for 0%

commit v1 on v0

v1 whole, which is shorter than its diff:
```python
import math

import jax
import jax.numpy as jnp
from jax import lax
from jax.sharding import PartitionSpec as P

WW = 64


def swap(block, axis, step):
    size = lax.axis_size(axis)
    return lax.ppermute(block, axis, [(i, i ^ step) for i in range(size)])


def exchange(pieces, axis):
    return [pieces[0]] + [swap(pieces[s], axis, s) for s in range(1, len(pieces))]


def place(pieces, me):
    out = jnp.zeros((len(pieces),) + pieces[0].shape, pieces[0].dtype)
    for s, piece in enumerate(pieces):
        out = lax.dynamic_update_index_in_dim(out, piece, me ^ s, 0)
    return out


def gather_weights(mixing, me_space):
    rows, cols = mixing.shape
    nf, ns = lax.axis_size("filter"), lax.axis_size("space")
    share = cols // ns
    own = lax.dynamic_slice_in_dim(mixing, me_space * share, share, axis=1)
    even = jnp.stack([own] + [swap(own, "filter", s) for s in range(2, nf, 2)])
    odd = swap(even, "filter", 1)
    part = jnp.stack([even, odd], axis=1).reshape(nf, rows, share)
    if ns == 1:
        return part
    held = jnp.stack([part] + [swap(part, "space", s) for s in range(2, ns, 2)])
    other = swap(held, "space", 1)
    both = jnp.stack([held, other], axis=1).reshape(ns, nf * rows, share)
    full = place([both[s] for s in range(ns)], me_space)
    return full.transpose(1, 0, 2).reshape(nf * rows, cols)


def scatter_weight_sum(part, rows, me, me_space):
    nf, ns = lax.axis_size("filter"), lax.axis_size("space")
    cols = part.shape[1]
    share = cols // ns
    bit = me_space & 1
    split = part.reshape(nf * rows, ns // 2, 2, share)
    mine = lax.dynamic_index_in_dim(split, bit, 2, keepdims=False)
    theirs = lax.dynamic_index_in_dim(split, bit ^ 1, 2, keepdims=False)
    half = mine + swap(theirs, "space", 1)
    total = lax.dynamic_index_in_dim(half, me_space >> 1, 1, keepdims=False)
    for s in range(2, ns, 2):
        out = lax.dynamic_index_in_dim(half, (me_space ^ s) >> 1, 1, keepdims=False)
        total = total + swap(out.astype(jnp.bfloat16), "space", s).astype(jnp.float32)
    total = total.reshape(nf // 2, 2, rows, share)
    near = total[:, 0] + swap(total[:, 1].astype(jnp.bfloat16), "filter", 1).astype(jnp.float32)
    result = near[0]
    for s in range(2, nf, 2):
        result = result + swap(near[s // 2].astype(jnp.bfloat16), "filter", s).astype(jnp.float32)
    return result


def with_planes(field):
    size = lax.axis_size("space")
    up = [(i, i + 1) for i in range(size - 1)]
    down = [(i + 1, i) for i in range(size - 1)]
    before = lax.ppermute(field[-1:], "space", up)
    after = lax.ppermute(field[:1], "space", down)
    return jnp.concatenate([before, field, after], axis=0)


def pad_rows_cols(field):
    return jnp.pad(field, ((0, 0), (1, 1), (1, 1), (0, 0)))


def depth_conv(padded, taps, flip):
    depth, height, width = padded.shape[0] - 2, padded.shape[1] - 2, padded.shape[2] - 2
    summed = jnp.zeros((depth, height, width, padded.shape[3]), jnp.float32)
    for a in range(3):
        for b in range(3):
            for e in range(3):
                i, j, k = (2 - a, 2 - b, 2 - e) if flip else (a, b, e)
                window = padded[i : i + depth, j : j + height, k : k + width]
                summed = summed + taps[a * 9 + b * 3 + e] * window.astype(jnp.float32)
    return summed


def tap_grads(grad, padded):
    depth, height, width = grad.shape[:3]
    wide = grad.astype(jnp.float32)
    columns = []
    for a in range(3):
        for b in range(3):
            for e in range(3):
                window = padded[a : a + depth, b : b + height, e : e + width]
                columns.append(jnp.sum(wide * window.astype(jnp.float32), axis=(0, 1, 2)))
    return jnp.stack(columns, axis=1)


def body(volume, mixing, kernel_taps, upstream):
    ch, planes, flat = volume.shape
    rows = flat // WW
    cells = planes * flat
    nf, ns = lax.axis_size("filter"), lax.axis_size("space")
    me, me_space = lax.axis_index("filter"), lax.axis_index("space")
    blk = cells // nf
    norm = 1.0 / math.sqrt(planes * ns * flat)

    vol_blocks = volume.reshape(ch, nf, blk)
    send = [lax.dynamic_index_in_dim(vol_blocks, me ^ s, 1, keepdims=False) for s in range(nf)]
    vol_all = place(exchange(send, "filter"), me).reshape(nf * ch, blk)
    weights = gather_weights(mixing, me_space)

    mixed_t = lax.dot_general(
        vol_all, weights, (((0,), (1,)), ((), ())), preferred_element_type=jnp.float32
    ).astype(jnp.bfloat16)
    send = [mixed_t[:, s * ch : (s + 1) * ch] for s in range(nf)]
    mixed = place(exchange(send, "filter"), me).reshape(planes, rows, WW, ch)

    taps = kernel_taps.T
    mixed_pad = pad_rows_cols(with_planes(mixed))
    spatial = depth_conv(mixed_pad, taps, False)
    sig = jax.nn.sigmoid(spatial)
    up_t = upstream.reshape(ch, cells).T.reshape(planes, rows, WW, ch)
    grad = (up_t.astype(jnp.float32) * (sig * (1.0 + spatial * (1.0 - sig)))).astype(jnp.bfloat16)
    silu_t = spatial * sig
    grad_wide = with_planes(grad)
    mixed_grad = depth_conv(pad_rows_cols(grad_wide), taps, True).astype(jnp.bfloat16)
    mixed_grad = mixed_grad.reshape(nf, blk, ch)

    send = [lax.dynamic_index_in_dim(mixed_grad, me ^ s, 0, keepdims=False) for s in range(nf)]
    mg_all = jnp.stack(exchange(send, "filter"))
    back = lax.dot_general(
        weights.reshape(nf, ch, nf * ch),
        mg_all,
        (((0, 1), (0, 2)), ((), ())),
        preferred_element_type=jnp.float32,
    ).astype(jnp.bfloat16)
    back = back.reshape(nf, ch, blk)
    send = [lax.dynamic_index_in_dim(back, me ^ s, 0, keepdims=False) for s in range(nf)]
    back_own = place(exchange(send, "filter"), me).transpose(1, 0, 2).reshape(ch, planes, flat)
    volume_grad = (upstream.astype(jnp.float32) + back_own.astype(jnp.float32)).astype(jnp.bfloat16)

    weight_part = lax.dot_general(
        mg_all, vol_all, (((1,), (1,)), ((), ())), preferred_element_type=jnp.float32
    )
    weight_part = weight_part.reshape(nf * ch, nf * ch) * norm
    mixing_grad = scatter_weight_sum(weight_part, ch, me, me_space)

    output = volume.astype(jnp.float32) + silu_t.reshape(cells, ch).T.reshape(ch, planes, flat)
    output = output.astype(jnp.bfloat16)
    taps_sum = tap_grads(grad, mixed_pad) * norm
    step = 1
    while step < ns:
        taps_sum = taps_sum + swap(taps_sum, "space", step)
        step *= 2
    return (output, volume_grad, mixing_grad, taps_sum)


def solution(mesh):
    in_specs = (
        P("filter", "space", None),
        P("filter", None),
        P("filter", None),
        P("filter", "space", None),
    )
    out_specs = (
        P("filter", "space", None),
        P("filter", "space", None),
        P("filter", "space"),
        P("filter", None),
    )
    return jax.shard_map(body, mesh=mesh, in_specs=in_specs, out_specs=out_specs, check_vma=False)
```

time: 346 us -> 241 us (0.70)
  waiting for transfers between devices: 228 us -> 68.8 us
  starting transfers between devices: 14.9 us -> 74.2 us
  local copies, waits for them, and re-layouts: 16.2 us -> 42.6 us
  blocking collectives: 21.5 us -> 0 us
  other arithmetic: 33.4 us -> 47.6 us
  between operations: 14 us -> 1.5 us
  matrix products: 17.6 us -> 5.41 us
    all_gather x2 -> x0, waiting for transfers between devices: 203 us -> none  [the longest x1 128 us: body(): vol_all = lax.all_gather(flat_vol, 'filter', axis=0, tiled=True)]
    ppermute x4 -> x46, waiting for transfers between devices: 3.89 us -> 68.8 us  [the longest x42 68.8 us: swap(): return lax.ppermute(block, axis, [(i, i ^ step) for i in range(size)])]
    ppermute x4 -> x46, starting transfers between devices: 10.6 us -> 74.2 us  [the longest x42 66.4 us: swap(): return lax.ppermute(block, axis, [(i, i ^ step) for i in range(size)])]
    psum x1 -> x0, blocking collectives: 21.5 us -> none  [body(): taps_grad = lax.psum(taps_part, 'space')]
    reduce_scatter x1 -> x0, waiting for transfers between devices: 15.5 us -> none  [body(): lax.psum_scatter(weight_term, 'space', scatter_dimension=1, tiled=True)]
    dot_general x3, matrix products: 17.6 us -> 5.41 us  [the longest x1 2.87 us: body(): lax.dot_general(weights.reshape(nf, ch, nf * ch), mg_all, (((0, 1), (0, 2...]
    dynamic_slice x0 -> x13, local copies, waits for them, and re-layouts: none -> 9.84 us  [the longest x2 4.44 us: scatter_weight_sum(): mine = lax.dynamic_index_in_dim(split, bit, 2, keepdims=False)]
    reshape x0 -> x2, local copies, waits for them, and re-layouts: none -> 5.54 us  [body(): silu_t.reshape(cells, ch).T.reshape(ch, planes, flat)]
  transfers between devices with their start and end apart: 8 -> 46, of which waited for: 6 -> 19; matrix products, arithmetic and copies ran while one was open for 9% -> 22% of each run, Pallas kernels for 0% -> 0%
where the time goes in v1:
time: 241 us; the launch traced here: 240 us
  starting transfers between devices  74.2 us (31%)
  waiting for transfers between devices  68.8 us (29%)
  other arithmetic  47.6 us (20%)
  local copies, waits for them, and re-layouts  42.6 us (18%)
  matrix products  5.41 us (2%)
    ppermute x42, waiting for transfers between devices, swap(): return lax.ppermute(block, axis, [(i, i ^ step) for i in range(size)])  68.8 us
    ppermute x42, starting transfers between devices, swap(): return lax.ppermute(block, axis, [(i, i ^ step) for i in range(size)])  66.4 us
    reduce_sum x2, other arithmetic, tap_grads(): columns.append(jnp.sum(wide * window.astype(jnp.float32), axis=(0, 1, 2)))  19.7 us
    unnamed x36, local copies, waits for them, and re-layouts  10.6 us
    convert_element_type x1, other arithmetic, body(): depth_conv(pad_rows_cols(grad_wide), taps, True).astype(jnp.bfloat16)  7.96 us
    reshape x2, local copies, waits for them, and re-layouts, body(): silu_t.reshape(cells, ch).T.reshape(ch, planes, flat)  5.54 us
    ppermute x2, starting transfers between devices, with_planes(): before = lax.ppermute(field[-1:], 'space', up)  5.02 us
  transfers between devices with their start and end apart: 46, of which 19 were waited for; matrix products, arithmetic and copies ran while one was open for 22% of the time, Pallas kernels for 0%

profile of v1, /device:TPU:0, one launch (start us, length us, event | category | flops | bytes accessed | tf_op | source)
XLA Modules:
  0.0 240.0 jit_solution(10034453726976669940)
XLA Ops:
  1.6 3.1 %collective-permute-start.7 = (bf16[128,256]{1,0:T(8,128)(2,1)S(1)}, bf16[128,256]{1,0:T(8,128)(2,1)S(1)}, u32[]{:S(2)}, u32[]{:S(2)}) collective-permute-start(bf16[128,256]{1,0:T(8,128)(2,1)S(1)} %constant_dynamic-slice_fusion.2), channel_id=1, source_target_pairs={{0,8},{4,12},{8,0},{12,4},{16,24},{20,28},{24,16},{28,20},{1,9},{5... | collective-permute-start | bytes 196616 | tf_op jit(solution)/shard_map/ppermute | solution.py:13
  4.7 2.6 %collective-permute-start.8 = (bf16[128,256]{1,0:T(8,128)(2,1)S(1)}, bf16[128,256]{1,0:T(8,128)(2,1)S(1)}, u32[]{:S(2)}, u32[]{:S(2)}) collective-permute-start(bf16[128,256]{1,0:T(8,128)(2,1)S(1)} %constant_dynamic-slice_fusion.2), channel_id=1, source_target_pairs={{0,16},{4,20},{8,24},{12,28},{16,0},{20,4},{24,8},{28,12},{1,17},{... | collective-permute-start | bytes 196616 | tf_op jit(solution)/shard_map/ppermute | solution.py:13
  7.3 4.6 %collective-permute-done.8 = bf16[128,256]{1,0:T(8,128)(2,1)S(1)} collective-permute-done((bf16[128,256]{1,0:T(8,128)(2,1)S(1)}, bf16[128,256]{1,0:T(8,128)(2,1)S(1)}, u32[]{:S(2)}, u32[]{:S(2)}) %collective-permute-start.8) | collective-permute-done | bytes 65568 | tf_op jit(solution)/shard_map/ppermute | solution.py:13
  19.2 3.0 %collective-permute-start.2 = (bf16[128,512]{1,0:T(8,128)(2,1)S(1)}, bf16[128,512]{1,0:T(8,128)(2,1)S(1)}, u32[]{:S(2)}, u32[]{:S(2)}) collective-permute-start(bf16[128,512]{1,0:T(8,128)(2,1)S(1)} %bitcast.294), channel_id=1, source_target_pairs={{0,12},{4,8},{8,4},{12,0},{16,28},{20,24},{24,20},{28,16},{1,13},{... | collective-permute-start | bytes 393224 | tf_op jit(solution)/shard_map/ppermute | solution.py:13
  30.5 4.9 %collective-permute-done.11 = bf16[8,128,256]{2,1,0:T(8,128)(2,1)S(1)} collective-permute-done((bf16[8,128,256]{2,1,0:T(8,128)(2,1)S(1)}, bf16[8,128,256]{2,1,0:T(8,128)(2,1)S(1)}, u32[]{:S(2)}, u32[]{:S(2)}) %collective-permute-start.11) | collective-permute-done | bytes 524320 | tf_op jit(solution)/shard_map/ppermute | solution.py:13
  38.0 2.8 %collective-permute-done.4 = bf16[128,512]{1,0:T(8,128)(2,1)S(1)} collective-permute-done((bf16[128,512]{1,0:T(8,128)(2,1)S(1)}, bf16[128,512]{1,0:T(8,128)(2,1)S(1)}, u32[]{:S(2)}, u32[]{:S(2)}) %collective-permute-start.4) | collective-permute-done | bytes 131104 | tf_op jit(solution)/shard_map/ppermute | solution.py:13
  51.5 4.7 %collective-permute-start.14 = (bf16[512,128]{1,0:T(8,128)(2,1)S(1)}, bf16[512,128]{1,0:T(8,128)(2,1)S(1)}, u32[]{:S(2)}, u32[]{:S(2)}) collective-permute-start(bf16[512,128]{1,0:T(8,128)(2,1)S(1)} %get-tuple-element.77), channel_id=1, source_target_pairs={{0,8},{4,12},{8,0},{12,4},{16,24},{20,28},{24,16},{28,20},{1,9},{5... | collective-permute-start | bytes 393224 | tf_op jit(solution)/shard_map/ppermute | solution.py:13
  65.8 8.8 %collective-permute-done.16 = bf16[512,128]{1,0:T(8,128)(2,1)S(1)} collective-permute-done((bf16[512,128]{1,0:T(8,128)(2,1)S(1)}, bf16[512,128]{1,0:T(8,128)(2,1)S(1)}, u32[]{:S(2)}, u32[]{:S(2)}) %collective-permute-start.16) | collective-permute-done | bytes 131104 | tf_op jit(solution)/shard_map/ppermute | solution.py:13
  74.6 3.2 %collective-permute-done.17 = bf16[512,128]{1,0:T(8,128)(2,1)S(1)} collective-permute-done((bf16[512,128]{1,0:T(8,128)(2,1)S(1)}, bf16[512,128]{1,0:T(8,128)(2,1)S(1)}, u32[]{:S(2)}, u32[]{:S(2)}) %collective-permute-start.17) | collective-permute-done | bytes 131104 | tf_op jit(solution)/shard_map/ppermute | solution.py:13
  81.4 2.6 %copy.59 = bf16[128,4,1024]{0,2,1:T(8,128)(2,1)} copy(bf16[128,4,1024]{2,1,0:T(4,128)(2,1)} %param.7) | data formatting | bytes 2097152 | tf_op args[3]
  84.0 2.7 %convert_element_type.305 = f32[128,4,1024]{0,2,1:T(8,128)} convert(bf16[128,4,1024]{0,2,1:T(8,128)(2,1)} %copy.59) | non-fusion elementwise | flops 524288 | bytes 3145728 | tf_op jit(solution)/shard_map/convert_element_type | solution.py:144
  88.7 2.7 %select_maximum_fusion.2 = bf16[6,18,66,128]{3,2,1,0:T(8,128)(2,1)S(1)} fusion(bf16[1,16,64,128]{3,2,1,0:T(8,128)(2,1)} %collective-permute-done.21, bf16[4,16,64,128]{3,2,1,0:T(8,128)(2,1)S(1)} %bitcast.267, bf16[1,16,64,128]{3,2,1,0:T(8,128)(2,1)S(1)} %collective-permute-done.20), kind=kLoop, calls=%fused_computation.145 | loop fusion | flops 17335296 | bytes 3397632 | tf_op jit(solution)/shard_map/concatenate | solution.py:71
  91.4 15.3 %fusion.69 = (f32[128]{0:T(128)S(1)}, f32[128]{0:T(128)S(1)}, f32[128]{0:T(128)S(1)}, f32[128]{0:T(128)S(1)}, f32[128]{0:T(128)S(1)}, /*index=5*/f32[128]{0:T(12...) fusion(bf16[6,18,66,128]{3,2,1,0:T(8,128)(2,1)S(1)} %select_max, ...), kind=kLoop, calls=%fused_computation.129 | loop fusion | flops 67106560 | bytes 32004608 | tf_op jit(solution)/shard_map/reduce_sum | solution.py:98
  106.7 3.7 %collective-permute-start.22 = (bf16[1,16,64,128]{3,2,1,0:T(8,128)(2,1)S(1)}, bf16[1,16,64,128]{3,2,1,0:T(8,128)(2,1)S(1)}, u32[]{:S(2)}, u32[]{:S(2)}) collective-permute-start(bf16[1,16,64,128]{3,2,1,0:T(8,128)(2,1)S(1)} %get-tuple-element.68), channel_id=1, source_target_pairs={{0,1},{1,2},{2,3},{4,5},{5,6},{6,7},{8,9},{9,10},{10,11},{12,13},{... | collective-permute-start | bytes 786440 | tf_op jit(solution)/shard_map/ppermute | solution.py:69
  112.0 4.4 %fusion.68 = (f32[128]{0:T(128)}, f32[128]{0:T(128)}, f32[128]{0:T(128)}, f32[128]{0:T(128)}, f32[128]{0:T(128)}, /*index=5*/f32[128]{0:T(128)}, f32[128]{0:T(128)}, f32[128]{0:T(128)}, f32[128]{0:T(128)}) fusion(bf16[4,16,64,128]{3,2,1,0:T(8,128)(2,1)S(1)} %get-tuple-element.42, bf16[6,18,66,128]{3,2,1,0:T(8,128)(2,1)S(1)} %select_maximum_fusion.2, ...), kind=kLoop, calls=%fused_computation.128 | loop fusion | flops 15727488 | bytes 8917504 | tf_op jit(solution)/shard_map/reduce_sum | solution.py:98
  116.3 2.8 %stack.196 = f32[128,27]{0,1:T(8,128)S(1)} concatenate(f32[128,1]{0,1:T(1,128)} %bitcast.326, f32[128,1]{0,1:T(1,128)} %bitcast.325, f32[128,1]{0,1:T(1,128)S(1)} %bitcast.304, f32[128,1]{0,1:T(1,128)S(1)} %bitcast.305, f32[128,1]{0,1:T(1,128)} %bitcast.328, f32[128,1]{0,1:T(1,128)S(1)} %bitcast.306, f32[128,1]{0,1:T(1,128)S(1)} %bitcast.307, f32[128,1]{0,1:T(1,128)S(1)} %bitcast.308, ...), dimensions={1} | concatenate | bytes 27648 | tf_op jit(solution)/shard_map/stack | solution.py:99
  120.8 8.0 %fusion.74 = bf16[4,16,64,128]{3,2,1,0:T(8,128)(2,1)S(1)} fusion(bf16[4,16,64,128]{3,2,1,0:T(8,128)(2,1)S(1)} %get-tuple-element.42, bf16[6,18,66,128]{3,2,1,0:T(8,128)(2,1)S(1)} %select_maximum_fusion, bf16[1,16,64,128]{3,2,1,0:T(8,128)(2,1)S(1)} %collective-permute-done.22, bf16[1,16,64,128]{3,2,1,0:T(8,128)(2,1)S(1)} %collective-permute-done.23, ...), kind=kLoop, calls=%fused_computation.142 | loop fusion | flops 43515904 | bytes 27801088 | tf_op jit(solution)/shard_map/convert_element_type | solution.py:130
  132.8 3.9 %collective-permute-start.25 = (bf16[512,128]{1,0:T(8,128)(2,1)S(1)}, bf16[512,128]{1,0:T(8,128)(2,1)S(1)}, u32[]{:S(2)}, u32[]{:S(2)}) collective-permute-start(bf16[512,128]{1,0:T(8,128)(2,1)S(1)} %get-tuple-element.65), channel_id=1, source_target_pairs={{0,8},{4,12},{8,0},{12,4},{16,24},{20,28},{24,16},{28,20},{1,9},{5... | collective-permute-start | bytes 393224 | tf_op jit(solution)/shard_map/ppermute | solution.py:13
  136.7 3.4 %collective-permute-start.27 = (bf16[512,128]{1,0:T(8,128)(2,1)S(1)}, bf16[512,128]{1,0:T(8,128)(2,1)S(1)}, u32[]{:S(2)}, u32[]{:S(2)}) collective-permute-start(bf16[512,128]{1,0:T(8,128)(2,1)S(1)} %get-tuple-element.63), channel_id=1, source_target_pairs={{0,16},{4,20},{8,24},{12,28},{16,0},{20,4},{24,8},{28,12},{1,17},{... | collective-permute-start | bytes 393224 | tf_op jit(solution)/shard_map/ppermute | solution.py:13
  140.5 4.4 %collective-permute-done.25 = bf16[512,128]{1,0:T(8,128)(2,1)S(1)} collective-permute-done((bf16[512,128]{1,0:T(8,128)(2,1)S(1)}, bf16[512,128]{1,0:T(8,128)(2,1)S(1)}, u32[]{:S(2)}, u32[]{:S(2)}) %collective-permute-start.25) | collective-permute-done | bytes 131104 | tf_op jit(solution)/shard_map/ppermute | solution.py:13
  145.0 2.7 %collective-permute-done.26 = bf16[512,128]{1,0:T(8,128)(2,1)S(1)} collective-permute-done((bf16[512,128]{1,0:T(8,128)(2,1)S(1)}, bf16[512,128]{1,0:T(8,128)(2,1)S(1)}, u32[]{:S(2)}, u32[]{:S(2)}) %collective-permute-start.26) | collective-permute-done | bytes 131104 | tf_op jit(solution)/shard_map/ppermute | solution.py:13
  149.9 9.3 %collective-permute-done.28 = bf16[512,128]{1,0:T(8,128)(2,1)S(1)} collective-permute-done((bf16[512,128]{1,0:T(8,128)(2,1)S(1)}, bf16[512,128]{1,0:T(8,128)(2,1)S(1)}, u32[]{:S(2)}, u32[]{:S(2)}) %collective-permute-start.28) | collective-permute-done | bytes 131104 | tf_op jit(solution)/shard_map/ppermute | solution.py:13
  163.4 3.1 %copy.64 = f32[1024,2,1,256]{3,0,1,2:T(8,128)} copy(f32[1024,2,1,256]{0,3,2,1:T(8,128)} %get-tuple-element.47) | data formatting | bytes 4194304 | tf_op jit(solution)/shard_map/jit(dynamic_index_in_dim)/dynamic_slice | solution.py:51
  168.4 2.9 %copy.58 = f32[4096,128]{0,1:T(8,128)} copy(f32[4096,128]{1,0:T(8,128)} %bitcast.277) | data formatting | bytes 4194304 | tf_op jit(solution)/shard_map/reshape | solution.py:152
  171.2 2.7 %reshape.97 = f32[128,4,1024]{2,1,0:T(4,128)S(1)} reshape(f32[128,4096]{1,0:T(8,128)} %bitcast.278) | data formatting | bytes 4194304 | tf_op jit(solution)/shard_map/reshape | solution.py:152
  176.2 2.9 %bitcast_convert_fusion = bf16[1024,512]{1,0:T(8,128)(2,1)S(1)} fusion(bf16[8,512,128]{2,1,0:T(8,128)(2,1)S(1)} %bitcast_dynamic-update-slice_fusion.7, bf16[8,128,1024]{1,0,2:T(8,128)(2,1)} %bitcast.284), kind=kOutput, calls=%fused_computation.134 | convolution fusion | flops 1074266112 | bytes 4194304 | tf_op jit(solution)/shard_map/dot_general | solution.py:135
  184.9 5.4 %collective-permute-start.32 = (bf16[128,512]{1,0:T(8,128)(2,1)}, bf16[128,512]{1,0:T(8,128)(2,1)S(1)}, u32[]{:S(2)}, u32[]{:S(2)}) collective-permute-start(bf16[128,512]{1,0:T(8,128)(2,1)} %get-tuple-element.57), channel_id=1, source_target_pairs={{0,8},{4,12},{8,0},{12,4},{16,24},{20,28},{24,16},{28,20},{1,9},{5... | collective-permute-start | bytes 393224 | tf_op jit(solution)/shard_map/ppermute | solution.py:13
  195.2 4.0 %collective-permute-done.32 = bf16[128,512]{1,0:T(8,128)(2,1)S(1)} collective-permute-done((bf16[128,512]{1,0:T(8,128)(2,1)}, bf16[128,512]{1,0:T(8,128)(2,1)S(1)}, u32[]{:S(2)}, u32[]{:S(2)}) %collective-permute-start.32) | collective-permute-done | bytes 131104 | tf_op jit(solution)/shard_map/ppermute | solution.py:13
  206.8 5.8 %collective-permute-done.35 = bf16[128,512]{1,0:T(8,128)(2,1)S(1)} collective-permute-done((bf16[128,512]{1,0:T(8,128)(2,1)S(1)}, bf16[128,512]{1,0:T(8,128)(2,1)S(1)}, u32[]{:S(2)}, u32[]{:S(2)}) %collective-permute-start.35) | collective-permute-done | bytes 131104 | tf_op jit(solution)/shard_map/ppermute | solution.py:13
  212.7 6.8 %collective-permute-done.39 = bf16[1024,256]{1,0:T(8,128)(2,1)S(1)} collective-permute-done((bf16[1024,256]{1,0:T(8,128)(2,1)S(1)}, bf16[1024,256]{1,0:T(8,128)(2,1)S(1)}, u32[]{:S(2)}, u32[]{:S(2)}) %collective-permute-start.39) | collective-permute-done | bytes 524320 | tf_op jit(solution)/shard_map/ppermute | solution.py:13
  228.9 3.1 %collective-permute-start.42 = (bf16[128,256]{1,0:T(8,128)(2,1)}, bf16[128,256]{1,0:T(8,128)(2,1)S(1)}, u32[]{:S(2)}, u32[]{:S(2)}) collective-permute-start(bf16[128,256]{1,0:T(8,128)(2,1)} %get-tuple-element.91), channel_id=1, source_target_pairs={{0,16},{4,20},{8,24},{12,28},{16,0},{20,4},{24,8},{28,12},{1,17},{... | collective-permute-start | bytes 196616 | tf_op jit(solution)/shard_map/ppermute | solution.py:13
  234.5 2.6 %copy.66 = bf16[128,4,1024]{2,1,0:T(4,128)(2,1)} copy(bf16[128,4,1024]{0,2,1:T(8,128)(2,1)} %fusion.70) | data formatting | bytes 2097152
  (187 shorter events, 95.6 us)
Async XLA Ops:
  13.4 10.7 %collective-permute-start.10 = (bf16[4,128,256]{2,1,0:T(8,128)(2,1)S(1)}, bf16[4,128,256]{2,1,0:T(8,128)(2,1)S(1)}, u32[]{:S(2)}, u32[]{:S(2)}) collective-permute-start(bf16[4,128,256]{2,1,0:T(8,128)(2,1)S(1)} %get-tuple-element.93), channel_id=1, source_target_pairs={{0,4},{4,0},{8,12},{12,8},{16,20},{20,16},{24,28},{28,24},{1,5},{5... | collective-permute-start | bytes 786440 | tf_op jit(solution)/shard_map/ppermute | solution.py:13
  19.1 9.7 %collective-permute-start.1 = (bf16[128,512]{1,0:T(8,128)(2,1)}, bf16[128,512]{1,0:T(8,128)(2,1)S(1)}, u32[]{:S(2)}, u32[]{:S(2)}) collective-permute-start(bf16[128,512]{1,0:T(8,128)(2,1)} %bitcast.6), channel_id=1, source_target_pairs={{0,8},{4,12},{8,0},{12,4},{16,24},{20,28},{24,16},{28,20},{1,9},{5... | collective-permute-start | bytes 393224 | tf_op jit(solution)/shard_map/ppermute | solution.py:13
  19.2 17.2 %collective-permute-start.2 = (bf16[128,512]{1,0:T(8,128)(2,1)S(1)}, bf16[128,512]{1,0:T(8,128)(2,1)S(1)}, u32[]{:S(2)}, u32[]{:S(2)}) collective-permute-start(bf16[128,512]{1,0:T(8,128)(2,1)S(1)} %bitcast.294), channel_id=1, source_target_pairs={{0,12},{4,8},{8,4},{12,0},{16,28},{20,24},{24,20},{28,16},{1,13},{... | collective-permute-start | bytes 393224 | tf_op jit(solution)/shard_map/ppermute | solution.py:13
  22.4 15.6 %collective-permute-start.3 = (bf16[128,512]{1,0:T(8,128)(2,1)S(1)}, bf16[128,512]{1,0:T(8,128)(2,1)S(1)}, u32[]{:S(2)}, u32[]{:S(2)}) collective-permute-start(bf16[128,512]{1,0:T(8,128)(2,1)S(1)} %bitcast.293), channel_id=1, source_target_pairs={{0,16},{4,20},{8,24},{12,28},{16,0},{20,4},{24,8},{28,12},{1,17},{... | collective-permute-start | bytes 393224 | tf_op jit(solution)/shard_map/ppermute | solution.py:13
  24.2 11.1 %collective-permute-start.11 = (bf16[8,128,256]{2,1,0:T(8,128)(2,1)S(1)}, bf16[8,128,256]{2,1,0:T(8,128)(2,1)S(1)}, u32[]{:S(2)}, u32[]{:S(2)}) collective-permute-start(bf16[8,128,256]{2,1,0:T(8,128)(2,1)S(1)} %bitcast.286), channel_id=1, source_target_pairs={{0,2},{1,3},{2,0},{3,1},{4,6},{5,7},{6,4},{7,5},{8,10},{9,11},{10,... | collective-permute-start | bytes 1572872 | tf_op jit(solution)/shard_map/ppermute | solution.py:13
  26.3 14.5 %collective-permute-start.4 = (bf16[128,512]{1,0:T(8,128)(2,1)S(1)}, bf16[128,512]{1,0:T(8,128)(2,1)S(1)}, u32[]{:S(2)}, u32[]{:S(2)}) collective-permute-start(bf16[128,512]{1,0:T(8,128)(2,1)S(1)} %bitcast.297), channel_id=1, source_target_pairs={{0,20},{4,16},{8,28},{12,24},{16,4},{20,0},{24,12},{28,8},{1,21},{... | collective-permute-start | bytes 393224 | tf_op jit(solution)/shard_map/ppermute | solution.py:13
  28.8 12.0 %collective-permute-start.5 = (bf16[128,512]{1,0:T(8,128)(2,1)S(1)}, bf16[128,512]{1,0:T(8,128)(2,1)S(1)}, u32[]{:S(2)}, u32[]{:S(2)}) collective-permute-start(bf16[128,512]{1,0:T(8,128)(2,1)S(1)} %bitcast.296), channel_id=1, source_target_pairs={{0,24},{4,28},{8,16},{12,20},{16,8},{20,12},{24,0},{28,4},{1,25},{... | collective-permute-start | bytes 393224 | tf_op jit(solution)/shard_map/ppermute | solution.py:13
  51.5 11.6 %collective-permute-start.14 = (bf16[512,128]{1,0:T(8,128)(2,1)S(1)}, bf16[512,128]{1,0:T(8,128)(2,1)S(1)}, u32[]{:S(2)}, u32[]{:S(2)}) collective-permute-start(bf16[512,128]{1,0:T(8,128)(2,1)S(1)} %get-tuple-element.77), channel_id=1, source_target_pairs={{0,8},{4,12},{8,0},{12,4},{16,24},{20,28},{24,16},{28,20},{1,9},{5... | collective-permute-start | bytes 393224 | tf_op jit(solution)/shard_map/ppermute | solution.py:13
  56.2 9.6 %collective-permute-start.15 = (bf16[512,128]{1,0:T(8,128)(2,1)S(1)}, bf16[512,128]{1,0:T(8,128)(2,1)S(1)}, u32[]{:S(2)}, u32[]{:S(2)}) collective-permute-start(bf16[512,128]{1,0:T(8,128)(2,1)S(1)} %get-tuple-element.76), channel_id=1, source_target_pairs={{0,12},{4,8},{8,4},{12,0},{16,28},{20,24},{24,20},{28,16},{1,13},{... | collective-permute-start | bytes 393224 | tf_op jit(solution)/shard_map/ppermute | solution.py:13
  56.7 17.9 %collective-permute-start.16 = (bf16[512,128]{1,0:T(8,128)(2,1)S(1)}, bf16[512,128]{1,0:T(8,128)(2,1)S(1)}, u32[]{:S(2)}, u32[]{:S(2)}) collective-permute-start(bf16[512,128]{1,0:T(8,128)(2,1)S(1)} %get-tuple-element.75), channel_id=1, source_target_pairs={{0,16},{4,20},{8,24},{12,28},{16,0},{20,4},{24,8},{28,12},{1,17},{... | collective-permute-start | bytes 393224 | tf_op jit(solution)/shard_map/ppermute | solution.py:13
  58.7 19.0 %collective-permute-start.17 = (bf16[512,128]{1,0:T(8,128)(2,1)S(1)}, bf16[512,128]{1,0:T(8,128)(2,1)S(1)}, u32[]{:S(2)}, u32[]{:S(2)}) collective-permute-start(bf16[512,128]{1,0:T(8,128)(2,1)S(1)} %get-tuple-element.74), channel_id=1, source_target_pairs={{0,20},{4,16},{8,28},{12,24},{16,4},{20,0},{24,12},{28,8},{1,21},{... | collective-permute-start | bytes 393224 | tf_op jit(solution)/shard_map/ppermute | solution.py:13
  60.2 17.6 %collective-permute-start.18 = (bf16[512,128]{1,0:T(8,128)(2,1)S(1)}, bf16[512,128]{1,0:T(8,128)(2,1)S(1)}, u32[]{:S(2)}, u32[]{:S(2)}) collective-permute-start(bf16[512,128]{1,0:T(8,128)(2,1)S(1)} %get-tuple-element.73), channel_id=1, source_target_pairs={{0,24},{4,28},{8,16},{12,20},{16,8},{20,12},{24,0},{28,4},{1,25},{... | collective-permute-start | bytes 393224 | tf_op jit(solution)/shard_map/ppermute | solution.py:13
  63.2 14.7 %collective-permute-start.19 = (bf16[512,128]{1,0:T(8,128)(2,1)S(1)}, bf16[512,128]{1,0:T(8,128)(2,1)S(1)}, u32[]{:S(2)}, u32[]{:S(2)}) collective-permute-start(bf16[512,128]{1,0:T(8,128)(2,1)S(1)} %get-tuple-element.72), channel_id=1, source_target_pairs={{0,28},{4,24},{8,20},{12,16},{16,12},{20,8},{24,4},{28,0},{1,29},{... | collective-permute-start | bytes 393224 | tf_op jit(solution)/shard_map/ppermute | solution.py:13
  78.7 9.9 %collective-permute-start.20 = (bf16[1,16,64,128]{3,2,1,0:T(8,128)(2,1)}, bf16[1,16,64,128]{3,2,1,0:T(8,128)(2,1)S(1)}, u32[]{:S(2)}, u32[]{:S(2)}) collective-permute-start(bf16[1,16,64,128]{3,2,1,0:T(8,128)(2,1)} %bitcast.42), channel_id=1, source_target_pairs={{0,1},{1,2},{2,3},{4,5},{5,6},{6,7},{8,9},{9,10},{10,11},{12,13},{... | collective-permute-start | bytes 786440 | tf_op jit(solution)/shard_map/ppermute | solution.py:69
  106.7 12.4 %collective-permute-start.22 = (bf16[1,16,64,128]{3,2,1,0:T(8,128)(2,1)S(1)}, bf16[1,16,64,128]{3,2,1,0:T(8,128)(2,1)S(1)}, u32[]{:S(2)}, u32[]{:S(2)}) collective-permute-start(bf16[1,16,64,128]{3,2,1,0:T(8,128)(2,1)S(1)} %get-tuple-element.68), channel_id=1, source_target_pairs={{0,1},{1,2},{2,3},{4,5},{5,6},{6,7},{8,9},{9,10},{10,11},{12,13},{... | collective-permute-start | bytes 786440 | tf_op jit(solution)/shard_map/ppermute | solution.py:69
  128.9 11.2 %collective-permute-start.24 = (bf16[512,128]{1,0:T(8,128)(2,1)S(1)}, bf16[512,128]{1,0:T(8,128)(2,1)S(1)}, u32[]{:S(2)}, u32[]{:S(2)}) collective-permute-start(bf16[512,128]{1,0:T(8,128)(2,1)S(1)} %get-tuple-element.66), channel_id=1, source_target_pairs={{0,4},{4,0},{8,12},{12,8},{16,20},{20,16},{24,28},{28,24},{1,5},{5... | collective-permute-start | bytes 393224 | tf_op jit(solution)/shard_map/ppermute | solution.py:13
  130.7 43.2 %collective-permute-start.44 = (f32[128,27]{0,1:T(8,128)S(1)}, f32[128,27]{0,1:T(8,128)S(1)}, u32[]{:S(2)}, u32[]{:S(2)}) collective-permute-start(f32[128,27]{0,1:T(8,128)S(1)} %broadcast_multiply_fusion), channel_id=1, source_target_pairs={{0,1},{1,0},{2,3},{3,2},{4,5},{5,4},{6,7},{7,6},{8,9},{9,8},{10,11... | collective-permute-start | bytes 41480 | tf_op jit(solution)/shard_map/ppermute | solution.py:13
  132.8 12.2 %collective-permute-start.25 = (bf16[512,128]{1,0:T(8,128)(2,1)S(1)}, bf16[512,128]{1,0:T(8,128)(2,1)S(1)}, u32[]{:S(2)}, u32[]{:S(2)}) collective-permute-start(bf16[512,128]{1,0:T(8,128)(2,1)S(1)} %get-tuple-element.65), channel_id=1, source_target_pairs={{0,8},{4,12},{8,0},{12,4},{16,24},{20,28},{24,16},{28,20},{1,9},{5... | collective-permute-start | bytes 393224 | tf_op jit(solution)/shard_map/ppermute | solution.py:13
  136.7 11.0 %collective-permute-start.26 = (bf16[512,128]{1,0:T(8,128)(2,1)S(1)}, bf16[512,128]{1,0:T(8,128)(2,1)S(1)}, u32[]{:S(2)}, u32[]{:S(2)}) collective-permute-start(bf16[512,128]{1,0:T(8,128)(2,1)S(1)} %get-tuple-element.64), channel_id=1, source_target_pairs={{0,12},{4,8},{8,4},{12,0},{16,28},{20,24},{24,20},{28,16},{1,13},{... | collective-permute-start | bytes 393224 | tf_op jit(solution)/shard_map/ppermute | solution.py:13
  136.7 13.2 %collective-permute-start.27 = (bf16[512,128]{1,0:T(8,128)(2,1)S(1)}, bf16[512,128]{1,0:T(8,128)(2,1)S(1)}, u32[]{:S(2)}, u32[]{:S(2)}) collective-permute-start(bf16[512,128]{1,0:T(8,128)(2,1)S(1)} %get-tuple-element.63), channel_id=1, source_target_pairs={{0,16},{4,20},{8,24},{12,28},{16,0},{20,4},{24,8},{28,12},{1,17},{... | collective-permute-start | bytes 393224 | tf_op jit(solution)/shard_map/ppermute | solution.py:13
  140.1 19.1 %collective-permute-start.28 = (bf16[512,128]{1,0:T(8,128)(2,1)S(1)}, bf16[512,128]{1,0:T(8,128)(2,1)S(1)}, u32[]{:S(2)}, u32[]{:S(2)}) collective-permute-start(bf16[512,128]{1,0:T(8,128)(2,1)S(1)} %get-tuple-element.62), channel_id=1, source_target_pairs={{0,20},{4,16},{8,28},{12,24},{16,4},{20,0},{24,12},{28,8},{1,21},{... | collective-permute-start | bytes 393224 | tf_op jit(solution)/shard_map/ppermute | solution.py:13
  145.0 14.3 %collective-permute-start.29 = (bf16[512,128]{1,0:T(8,128)(2,1)S(1)}, bf16[512,128]{1,0:T(8,128)(2,1)S(1)}, u32[]{:S(2)}, u32[]{:S(2)}) collective-permute-start(bf16[512,128]{1,0:T(8,128)(2,1)S(1)} %get-tuple-element.61), channel_id=1, source_target_pairs={{0,24},{4,28},{8,16},{12,20},{16,8},{20,12},{24,0},{28,4},{1,25},{... | collective-permute-start | bytes 393224 | tf_op jit(solution)/shard_map/ppermute | solution.py:13
  147.7 11.6 %collective-permute-start.30 = (bf16[512,128]{1,0:T(8,128)(2,1)S(1)}, bf16[512,128]{1,0:T(8,128)(2,1)S(1)}, u32[]{:S(2)}, u32[]{:S(2)}) collective-permute-start(bf16[512,128]{1,0:T(8,128)(2,1)S(1)} %get-tuple-element.60), channel_id=1, source_target_pairs={{0,28},{4,24},{8,20},{12,16},{16,12},{20,8},{24,4},{28,0},{1,29},{... | collective-permute-start | bytes 393224 | tf_op jit(solution)/shard_map/ppermute | solution.py:13
  166.5 38.0 %collective-permute-start.38 = (f32[1024,2,256]{2,0,1:T(8,128)}, f32[1024,2,256]{2,0,1:T(8,128)}, u32[]{:S(2)}, u32[]{:S(2)}) collective-permute-start(f32[1024,2,256]{2,0,1:T(8,128)} %bitcast.285), channel_id=1, source_target_pairs={{0,1},{1,0},{2,3},{3,2},{4,5},{5,4},{6,7},{7,6},{8,9},{9,8},{10,11... | collective-permute-start | bytes 6291464 | tf_op jit(solution)/shard_map/ppermute | solution.py:13
  180.1 13.2 %collective-permute-start.31 = (bf16[128,512]{1,0:T(8,128)(2,1)}, bf16[128,512]{1,0:T(8,128)(2,1)}, u32[]{:S(2)}, u32[]{:S(2)}) collective-permute-start(bf16[128,512]{1,0:T(8,128)(2,1)} %get-tuple-element.58), channel_id=1, source_target_pairs={{0,4},{4,0},{8,12},{12,8},{16,20},{20,16},{24,28},{28,24},{1,5},{5... | collective-permute-start | bytes 393224 | tf_op jit(solution)/shard_map/ppermute | solution.py:13
  184.9 14.3 %collective-permute-start.32 = (bf16[128,512]{1,0:T(8,128)(2,1)}, bf16[128,512]{1,0:T(8,128)(2,1)S(1)}, u32[]{:S(2)}, u32[]{:S(2)}) collective-permute-start(bf16[128,512]{1,0:T(8,128)(2,1)} %get-tuple-element.57), channel_id=1, source_target_pairs={{0,8},{4,12},{8,0},{12,4},{16,24},{20,28},{24,16},{28,20},{1,9},{5... | collective-permute-start | bytes 393224 | tf_op jit(solution)/shard_map/ppermute | solution.py:13
  190.3 11.6 %collective-permute-start.33 = (bf16[128,512]{1,0:T(8,128)(2,1)}, bf16[128,512]{1,0:T(8,128)(2,1)S(1)}, u32[]{:S(2)}, u32[]{:S(2)}) collective-permute-start(bf16[128,512]{1,0:T(8,128)(2,1)} %get-tuple-element.56), channel_id=1, source_target_pairs={{0,12},{4,8},{8,4},{12,0},{16,28},{20,24},{24,20},{28,16},{1,13},{... | collective-permute-start | bytes 393224 | tf_op jit(solution)/shard_map/ppermute | solution.py:13
  190.9 13.6 %collective-permute-start.34 = (bf16[128,512]{1,0:T(8,128)(2,1)}, bf16[128,512]{1,0:T(8,128)(2,1)S(1)}, u32[]{:S(2)}, u32[]{:S(2)}) collective-permute-start(bf16[128,512]{1,0:T(8,128)(2,1)} %get-tuple-element.55), channel_id=1, source_target_pairs={{0,16},{4,20},{8,24},{12,28},{16,0},{20,4},{24,8},{28,12},{1,17},{... | collective-permute-start | bytes 393224 | tf_op jit(solution)/shard_map/ppermute | solution.py:13
  193.3 19.3 %collective-permute-start.35 = (bf16[128,512]{1,0:T(8,128)(2,1)S(1)}, bf16[128,512]{1,0:T(8,128)(2,1)S(1)}, u32[]{:S(2)}, u32[]{:S(2)}) collective-permute-start(bf16[128,512]{1,0:T(8,128)(2,1)S(1)} %get-tuple-element.54), channel_id=1, source_target_pairs={{0,20},{4,16},{8,28},{12,24},{16,4},{20,0},{24,12},{28,8},{1,21},{... | collective-permute-start | bytes 393224 | tf_op jit(solution)/shard_map/ppermute | solution.py:13
  199.2 13.4 %collective-permute-start.36 = (bf16[128,512]{1,0:T(8,128)(2,1)S(1)}, bf16[128,512]{1,0:T(8,128)(2,1)S(1)}, u32[]{:S(2)}, u32[]{:S(2)}) collective-permute-start(bf16[128,512]{1,0:T(8,128)(2,1)S(1)} %get-tuple-element.53), channel_id=1, source_target_pairs={{0,24},{4,28},{8,16},{12,20},{16,8},{20,12},{24,0},{28,4},{1,25},{... | collective-permute-start | bytes 393224 | tf_op jit(solution)/shard_map/ppermute | solution.py:13
  202.0 10.7 %collective-permute-start.37 = (bf16[128,512]{1,0:T(8,128)(2,1)S(1)}, bf16[128,512]{1,0:T(8,128)(2,1)S(1)}, u32[]{:S(2)}, u32[]{:S(2)}) collective-permute-start(bf16[128,512]{1,0:T(8,128)(2,1)S(1)} %get-tuple-element.52), channel_id=1, source_target_pairs={{0,28},{4,24},{8,20},{12,16},{16,12},{20,8},{24,4},{28,0},{1,29},{... | collective-permute-start | bytes 393224 | tf_op jit(solution)/shard_map/ppermute | solution.py:13
  206.5 13.0 %collective-permute-start.39 = (bf16[1024,256]{1,0:T(8,128)(2,1)S(1)}, bf16[1024,256]{1,0:T(8,128)(2,1)S(1)}, u32[]{:S(2)}, u32[]{:S(2)}) collective-permute-start(bf16[1024,256]{1,0:T(8,128)(2,1)S(1)} %fusion.78), channel_id=1, source_target_pairs={{0,2},{1,3},{2,0},{3,1},{4,6},{5,7},{6,4},{7,5},{8,10},{9,11},{10,... | collective-permute-start | bytes 1572872 | tf_op jit(solution)/shard_map/ppermute | solution.py:13
  (27 other events, 197.3 us)

commit v2 on v1

v2 whole, which is shorter than its diff:
```python
import functools
import math

import jax
import jax.numpy as jnp
from jax import lax
from jax.experimental import pallas as pl
from jax.experimental.pallas import tpu as pltpu
from jax.sharding import PartitionSpec as P

WW = 64
BF = jnp.bfloat16
F32 = jnp.float32


def swap(block, axis, step):
    size = lax.axis_size(axis)
    return lax.ppermute(block, axis, [(i, i ^ step) for i in range(size)])


def exchange(pieces, axis):
    size = len(pieces)
    order = list(range(size // 2, size)) + list(range(1, size // 2))
    got = {0: pieces[0]}
    for s in order:
        got[s] = swap(pieces[s], axis, s)
    return [got[s] for s in range(size)]


def place(pieces, shift):
    out = jnp.zeros((len(pieces),) + pieces[0].shape, pieces[0].dtype)
    for s, piece in enumerate(pieces):
        out = lax.dynamic_update_index_in_dim(out, piece, shift ^ s, 0)
    return out


def restrip(part, count, strips):
    n, cells, ch = part.shape[0], part.shape[1] // count, part.shape[2]
    if n == strips:
        return part
    part = part.reshape(n, count, cells, ch).transpose(1, 0, 2, 3)
    part = part.reshape(count, strips, n * cells // strips, ch).transpose(1, 0, 2, 3)
    return part.reshape(strips, count * n * cells // strips, ch)


def pick(blocks, index):
    return lax.dynamic_index_in_dim(blocks, index, 0, keepdims=False)


def gather_weights(mixing, me_space):
    rows, cols = mixing.shape
    nf, ns = lax.axis_size("filter"), lax.axis_size("space")
    share = cols // ns
    own = lax.dynamic_slice_in_dim(mixing, me_space * share, share, axis=1)
    even = jnp.stack([own] + [swap(own, "filter", s) for s in range(2, nf, 2)])
    odd = swap(even, "filter", 1)
    part = jnp.stack([even, odd], axis=1).reshape(nf * rows, share)
    held = jnp.stack([part] + [swap(part, "space", s) for s in range(2, ns, 2)])
    other = swap(held, "space", 1)
    return jnp.stack([held, other], axis=1).reshape(ns, nf * rows, share)


def scatter_weight_sum(part, rows):
    nf, ns = lax.axis_size("filter"), lax.axis_size("space")
    share = part.shape[1] // ns
    split = [part[:, v * share : (v + 1) * share] for v in range(ns)]
    theirs = jnp.concatenate(split[1::2], axis=1)
    got = swap(theirs, "space", 1)
    half = [split[2 * k] + got[:, k * share : (k + 1) * share] for k in range(ns // 2)]
    total = half[0]
    for k in range(1, ns // 2):
        total = total + swap(half[k].astype(BF), "space", 2 * k).astype(F32)
    total = total.reshape(nf // 2, 2, rows, share)
    near = total[:, 0] + swap(total[:, 1].astype(BF), "filter", 1).astype(F32)
    result = near[0]
    for k in range(1, nf // 2):
        result = result + swap(near[k].astype(BF), "filter", 2 * k).astype(F32)
    return result


def halo(first, last):
    size = lax.axis_size("space")
    before = lax.ppermute(last, "space", [(i, i + 1) for i in range(size - 1)])
    after = lax.ppermute(first, "space", [(i + 1, i) for i in range(size - 1)])
    return before, after


def fill(pad_ref, plane, source):
    rows, width, ch = pad_ref.shape[1] - 2, pad_ref.shape[2], pad_ref.shape[3]
    pad_ref[plane, 1 : rows + 1] = source.astype(F32).reshape(rows, width, ch)
    pad_ref[plane, 0] = jnp.zeros((width, ch), F32)
    pad_ref[plane, rows + 1] = jnp.zeros((width, ch), F32)


def shifted(value, up):
    width = value.shape[0]
    index = lax.broadcasted_iota(jnp.int32, value.shape, 0)
    if up:
        return jnp.where(index == width - 1, 0.0, pltpu.roll(value, width - 1, 0))
    return jnp.where(index == 0, 0.0, pltpu.roll(value, 1, 0))


def conv_row(pad_ref, taps_ref, plane, row, flip):
    sums = [None, None, None]
    for a in range(3):
        for b in range(3):
            da, db = (1 - a, 1 - b) if flip else (a - 1, b - 1)
            line = pad_ref[plane + da, row + db]
            for e in range(3):
                term = taps_ref[pl.ds(a * 9 + b * 3 + e, 1), :] * line
                sums[e] = term if sums[e] is None else sums[e] + term
    lo, hi = (sums[2], sums[0]) if flip else (sums[0], sums[2])
    return sums[1] + shifted(lo, False) + shifted(hi, True)


def load_planes(pad_ref, refs, where, before_ref, after_ref, wanted, planes):
    for p in sorted(wanted):
        if p < 0:
            fill(pad_ref, 0, before_ref[...])
        elif p >= planes:
            fill(pad_ref, planes + 1, after_ref[...])
        else:
            which, at = where[p]
            cells = refs[which].shape[1] // len([q for q in where if where[q][0] == which])
            fill(pad_ref, p + 1, refs[which][:, at * cells : (at + 1) * cells, :])


def forward_kernel(group, where, planes, m0, m1, before, after, taps, vol, up, grad, out, pad):
    wanted = {p + a for p in group for a in (-1, 0, 1)}
    load_planes(pad, (m0, m1), where, before, after, wanted, planes)
    strips = m0.shape[0]
    cells = vol.shape[2] // len(group)
    rows = cells // WW
    for k, p in enumerate(group):

        def strip(f, carry, k=k, p=p):
            lines = [conv_row(pad, taps, p + 1, f * rows + 1 + r, False) for r in range(rows)]
            spatial = jnp.concatenate(lines, axis=0)
            sig = 1.0 / (1.0 + jnp.exp(-spatial))
            lane = slice(k * cells, (k + 1) * cells)
            cot = jnp.transpose(up[f, :, lane].astype(F32))
            slope = sig * (1.0 + spatial * (1.0 - sig))
            grad[f, lane, :] = (cot * slope).astype(BF)
            silu = jnp.transpose(spatial * sig)
            out[f, :, lane] = (vol[f, :, lane].astype(F32) + silu).astype(BF)
            return carry

        lax.fori_loop(0, strips, strip, 0)


def backward_kernel(group, where, planes, g0, g1, before, after, taps, out, pad):
    wanted = {p + a for p in group for a in (-1, 0, 1)}
    load_planes(pad, (g0, g1), where, before, after, wanted, planes)
    strips = g0.shape[0]
    cells = out.shape[1] // len(group)
    rows = cells // WW
    for k, p in enumerate(group):

        def strip(f, carry, k=k, p=p):
            lines = [conv_row(pad, taps, p + 1, f * rows + 1 + r, True) for r in range(rows)]
            out[f, k * cells : (k + 1) * cells, :] = jnp.concatenate(lines, axis=0).astype(BF)
            return carry

        lax.fori_loop(0, strips, strip, 0)


def taps_kernel(where, planes, norm, m0, m1, before, after, g0, g1, out, pad, gpad):
    load_planes(pad, (m0, m1), where, before, after, set(range(-1, planes + 1)), planes)
    load_planes(gpad, (g0, g1), where, before, after, set(range(planes)), planes)
    rows, width, ch = pad.shape[1] - 2, pad.shape[2], pad.shape[3]
    sums = tuple(jnp.zeros((8, ch), F32) for _ in range(27))

    def line(at, sums):
        p, h = at // rows, at % rows
        sums = list(sums)
        own = gpad[p + 1, h + 1]
        turned = (shifted(own, True), own, shifted(own, False))
        for a in range(3):
            for b in range(3):
                field = pad[p + a, h + b]
                for e in range(3):
                    prod = (turned[e] * field).reshape(width // 8, 8, ch)
                    sums[a * 9 + b * 3 + e] = sums[a * 9 + b * 3 + e] + jnp.sum(prod, axis=0)
        return tuple(sums)

    sums = lax.fori_loop(0, planes * rows, line, sums)
    for k in range(27):
        out[k : k + 1, :] = jnp.sum(sums[k], axis=0, keepdims=True) * norm


def call(kernel, out_shape, scratch, *args, ops=0):
    return pl.pallas_call(
        kernel,
        out_shape=out_shape,
        in_specs=[pl.BlockSpec(memory_space=pltpu.VMEM)] * len(args),
        out_specs=jax.tree.map(lambda _: pl.BlockSpec(memory_space=pltpu.VMEM), out_shape),
        scratch_shapes=scratch,
        compiler_params=pltpu.CompilerParams(vmem_limit_bytes=40 * 1024 * 1024),
        cost_estimate=pl.CostEstimate(flops=ops, bytes_accessed=4 * 1024 * 1024, transcendentals=0),
    )(*args)


def body(volume, mixing, kernel_taps, upstream):
    ch, planes, flat = volume.shape
    height = flat // WW
    nf, ns = lax.axis_size("filter"), lax.axis_size("space")
    me, me_space = lax.axis_index("filter"), lax.axis_index("space")
    cells = flat // nf
    strips = flat // (2 * WW)
    lanes = 2 * WW
    norm = 1.0 / math.sqrt(planes * ns * flat)
    edges, middle = (0, planes - 1), tuple(range(1, planes - 1))
    groups = (edges, middle)
    where = {p: (i, k) for i, g in enumerate(groups) for k, p in enumerate(g)}
    turn = me ^ (me_space * (nf // ns))

    def strips_of(field, group, count):
        part = jnp.stack([field[:, p] for p in group], axis=1)
        part = part.reshape(ch, len(group), count, flat // count).transpose(2, 0, 1, 3)
        return part.reshape(count, ch, len(group) * (flat // count))

    vol_all = []
    for g in groups:
        part = strips_of(volume, g, nf)
        got = exchange([pick(part, me ^ s) for s in range(nf)], "filter")
        vol_all.append(place(got, turn).reshape(ns, nf * ch // ns, part.shape[2]))
    weights = gather_weights(mixing, me_space)
    vol_strips = [strips_of(volume, g, strips) for g in groups]
    up_strips = [strips_of(upstream, g, strips) for g in groups]
    vol_all[0], up_strips = lax.optimization_barrier((vol_all[0], up_strips))

    mixed = []
    for part in vol_all:
        prod = lax.dot_general(
            part, weights, (((0, 1), (0, 2)), ((), ())), preferred_element_type=F32
        ).astype(BF)
        got = exchange([prod[:, s * ch : (s + 1) * ch] for s in range(nf)], "filter")
        mixed.append(restrip(place(got, me), len(groups[len(mixed)]), strips))

    taps = kernel_taps.T
    before, after = halo(mixed[0][:, :lanes], mixed[0][:, lanes:])
    pad = pltpu.VMEM((planes + 2, height + 2, WW, ch), F32)
    conv_ops = 60 * flat * ch

    def forward(i):
        g = groups[i]
        shapes = (
            jax.ShapeDtypeStruct((strips, len(g) * lanes, ch), BF),
            jax.ShapeDtypeStruct((strips, ch, len(g) * lanes), BF),
        )
        kernel = functools.partial(forward_kernel, g, where, planes)
        return call(
            kernel, shapes, [pad], mixed[0], mixed[1], before, after, taps,
            vol_strips[i], up_strips[i], ops=conv_ops * len(g),
        )

    grad_edges, out_edges = forward(0)
    grad_before, grad_after = halo(grad_edges[:, :lanes], grad_edges[:, lanes:])
    grad_middle, out_middle = forward(1)
    grads = (grad_edges, grad_middle)

    def backward(i):
        g = groups[i]
        shape = jax.ShapeDtypeStruct((strips, len(g) * lanes, ch), BF)
        kernel = functools.partial(backward_kernel, g, where, planes)
        return call(
            kernel, shape, [pad], grad_edges, grad_middle, grad_before, grad_after, taps,
            ops=conv_ops * len(g),
        )

    mg_all, back_all = [None, None], [None, None]
    for i in (1, 0):
        part = restrip(backward(i), len(groups[i]), nf)
        mg_all[i] = jnp.stack(exchange([pick(part, me ^ s) for s in range(nf)], "filter"))

    taps_part = call(
        functools.partial(taps_kernel, where, planes, norm),
        jax.ShapeDtypeStruct((27, ch), F32), [pad, pad],
        mixed[0], mixed[1], before, after, grad_edges, grad_middle,
        ops=conv_ops * planes,
    )
    taps_grad = taps_part
    step = 1
    while step < ns:
        taps_grad = taps_grad + swap(taps_grad, "space", step)
        step *= 2

    whole = [None] * planes
    for g, part in zip(groups, (out_edges, out_middle)):
        part = part.reshape(strips, ch, len(g), lanes)
        for k, p in enumerate(g):
            whole[p] = part[:, :, k].transpose(1, 0, 2).reshape(ch, flat)
    output = jnp.stack(whole, axis=1)

    whole = [None] * planes
    weights_rows = weights.reshape(ns, nf, ch, weights.shape[2])
    for i in (1, 0):
        g = groups[i]
        back = lax.dot_general(
            weights_rows, mg_all[i], (((1, 2), (0, 2)), ((), ())), preferred_element_type=F32
        ).astype(BF)
        back = back.reshape(nf, ch, len(g) * cells)
        got = exchange([pick(back, turn ^ s) for s in range(nf)], "filter")
        back_own = place(got, me).reshape(nf, ch, len(g), cells)
        for k, p in enumerate(g):
            whole[p] = back_own[:, :, k].transpose(1, 0, 2).reshape(ch, flat)
    volume_grad = (upstream.astype(F32) + jnp.stack(whole, axis=1).astype(F32)).astype(BF)

    weight_part = lax.dot_general(
        jnp.concatenate(mg_all, axis=1),
        jnp.concatenate(vol_all, axis=2).reshape(nf * ch, -1),
        (((1,), (1,)), ((), ())),
        preferred_element_type=F32,
    )
    weight_part = weight_part.reshape(nf * ch, nf * ch) * norm
    mixing_grad = scatter_weight_sum(weight_part, ch)
    return (output, volume_grad, mixing_grad, taps_grad.T)


def solution(mesh):
    in_specs = (
        P("filter", "space", None),
        P("filter", None),
        P("filter", None),
        P("filter", "space", None),
    )
    out_specs = (
        P("filter", "space", None),
        P("filter", "space", None),
        P("filter", "space"),
        P("filter", None),
    )
    return jax.shard_map(body, mesh=mesh, in_specs=in_specs, out_specs=out_specs, check_vma=False)
```

time: 241 us -> 341 us (1.41)
  waiting for transfers between devices: 68.8 us -> 157 us
  other arithmetic: 47.6 us -> 9.47 us
  starting transfers between devices: 74.2 us -> 103 us
  Pallas kernels: 0 us -> 17.7 us
    ppermute x42 -> x70, waiting for transfers between devices: 68.8 us -> 156 us  [swap(): return lax.ppermute(block, axis, [(i, i ^ step) for i in range(size)])]
    ppermute x42 -> x70, starting transfers between devices: 66.4 us -> 93.9 us  [swap(): return lax.ppermute(block, axis, [(i, i ^ step) for i in range(size)])]
    reduce_sum x2 -> x0, other arithmetic: 19.7 us -> none  [tap_grads(): columns.append(jnp.sum(wide * window.astype(jnp.float32), axis=(0, 1, 2)))]
    pallas_call x0 -> x5, Pallas kernels: none -> 17.7 us  [call(): pl.pallas_call(kernel, out_shape=out_shape, in_specs=[pl.BlockSpec(memory...]
    convert_element_type x5 -> x2, other arithmetic: 15.1 us -> 1.62 us  [the longest x1 1.34 us: body(): (upstream.astype(F32) + jnp.stack(whole, axis=1).astype(F32)).astype(BF)]
    dynamic_slice x12 -> x0, local copies, waits for them, and re-layouts: 9.83 us -> none  [the longest x2 4.44 us: scatter_weight_sum(): mine = lax.dynamic_index_in_dim(split, bit, 2, keepdims=False)]
    transpose x0 -> x8, local copies, waits for them, and re-layouts: none -> 5 us  [the longest x4 3.33 us: body(): whole[p] = part[:, :, k].transpose(1, 0, 2).reshape(ch, flat)]
    concatenate x2 -> x1, other arithmetic: 4.39 us -> 0.31 us  [scatter_weight_sum(): theirs = jnp.concatenate(split[1::2], axis=1)]
  transfers between devices with their start and end apart: 46 -> 74, of which waited for: 19 -> 38; matrix products, arithmetic and copies ran while one was open for 22% -> 12% of each run, Pallas kernels for 0% -> 1%
where the time goes in v2:
time: 341 us; the launch traced here: 340 us
  waiting for transfers between devices  157 us (46%)
  starting transfers between devices  103 us (30%)
  local copies, waits for them, and re-layouts  43.7 us (13%)
  Pallas kernels  17.7 us (5%)
  other arithmetic  9.47 us (3%)
  matrix products  7.6 us (2%)
    ppermute x70, waiting for transfers between devices, swap(): return lax.ppermute(block, axis, [(i, i ^ step) for i in range(size)])  156 us
    ppermute x70, starting transfers between devices, swap(): return lax.ppermute(block, axis, [(i, i ^ step) for i in range(size)])  93.9 us
    pallas_call x5, Pallas kernels, call(): pl.pallas_call(kernel, out_shape=out_shape, in_specs=[pl.BlockSpec(memory...  17.7 us
    unnamed x72, local copies, waits for them, and re-layouts  12.7 us
    dynamic_update_slice x45, local copies, waits for them, and re-layouts, place(): out = lax.dynamic_update_index_in_dim(out, piece, shift ^ s, 0)  7.15 us
  transfers between devices with their start and end apart: 74, of which 38 were waited for; matrix products, arithmetic and copies ran while one was open for 12% of the time, Pallas kernels for 1%

profile of v2, /device:TPU:0, one launch (start us, length us, event | category | flops | bytes accessed | tf_op | source)
XLA Modules:
  0.0 340.3 jit_solution(5600853754746645314)
XLA Ops:
  2.2 4.0 %collective-permute-start.8 = (bf16[128,256]{1,0:T(8,128)(2,1)}, bf16[128,256]{1,0:T(8,128)(2,1)S(1)}, u32[]{:S(2)}, u32[]{:S(2)}) collective-permute-start(bf16[128,256]{1,0:T(8,128)(2,1)} %constant_dynamic-slice_fusion), channel_id=1, source_target_pairs={{0,16},{4,20},{8,24},{12,28},{16,0},{20,4},{24,8},{28,12},{1,17},{... | collective-permute-start | bytes 196616 | tf_op jit(solution)/shard_map/ppermute | solution.py:18
  12.7 4.8 %collective-permute-start.26 = (bf16[128,256]{1,0:T(8,128)(2,1)}, bf16[128,256]{1,0:T(8,128)(2,1)}, u32[]{:S(2)}, u32[]{:S(2)}) collective-permute-start(bf16[128,256]{1,0:T(8,128)(2,1)} %get-tuple-element.83), channel_id=1, source_target_pairs={{0,28},{4,24},{8,20},{12,16},{16,12},{20,8},{24,4},{28,0},{1,29},{... | collective-permute-start | bytes 196616 | tf_op jit(solution)/shard_map/ppermute | solution.py:18
  32.2 4.3 %collective-permute-done.21 = bf16[128,256]{1,0:T(8,128)(2,1)S(1)} collective-permute-done((bf16[128,256]{1,0:T(8,128)(2,1)S(1)}, bf16[128,256]{1,0:T(8,128)(2,1)S(1)}, u32[]{:S(2)}, u32[]{:S(2)}) %collective-permute-start.21) | collective-permute-done | bytes 65568 | tf_op jit(solution)/shard_map/ppermute | solution.py:18
  48.9 5.2 %collective-permute-done.10 = bf16[4,128,256]{2,1,0:T(8,128)(2,1)S(1)} collective-permute-done((bf16[4,128,256]{2,1,0:T(8,128)(2,1)S(1)}, bf16[4,128,256]{2,1,0:T(8,128)(2,1)S(1)}, u32[]{:S(2)}, u32[]{:S(2)}) %collective-permute-start.10) | collective-permute-done | bytes 262176 | tf_op jit(solution)/shard_map/ppermute | solution.py:18
  55.4 3.8 %collective-permute-done.2 = bf16[128,256]{1,0:T(8,128)(2,1)S(1)} collective-permute-done((bf16[128,256]{1,0:T(8,128)(2,1)S(1)}, bf16[128,256]{1,0:T(8,128)(2,1)S(1)}, u32[]{:S(2)}, u32[]{:S(2)}) %collective-permute-start.2) | collective-permute-done | bytes 65568 | tf_op jit(solution)/shard_map/ppermute | solution.py:18
  61.5 5.4 %collective-permute-done.3 = bf16[128,256]{1,0:T(8,128)(2,1)S(1)} collective-permute-done((bf16[128,256]{1,0:T(8,128)(2,1)S(1)}, bf16[128,256]{1,0:T(8,128)(2,1)S(1)}, u32[]{:S(2)}, u32[]{:S(2)}) %collective-permute-start.3) | collective-permute-done | bytes 65568 | tf_op jit(solution)/shard_map/ppermute | solution.py:18
  70.1 5.1 %collective-permute-done.4 = bf16[128,256]{1,0:T(8,128)(2,1)S(1)} collective-permute-done((bf16[128,256]{1,0:T(8,128)(2,1)S(1)}, bf16[128,256]{1,0:T(8,128)(2,1)S(1)}, u32[]{:S(2)}, u32[]{:S(2)}) %collective-permute-start.4) | collective-permute-done | bytes 65568 | tf_op jit(solution)/shard_map/ppermute | solution.py:18
  95.4 3.8 %collective-permute-done.13 = bf16[256,128]{1,0:T(8,128)(2,1)S(1)} collective-permute-done((bf16[256,128]{1,0:T(8,128)(2,1)S(1)}, bf16[256,128]{1,0:T(8,128)(2,1)S(1)}, u32[]{:S(2)}, u32[]{:S(2)}) %collective-permute-start.13) | collective-permute-done | bytes 65568 | tf_op jit(solution)/shard_map/ppermute | solution.py:18
  99.2 4.4 %collective-permute-done.14 = bf16[256,128]{1,0:T(8,128)(2,1)S(1)} collective-permute-done((bf16[256,128]{1,0:T(8,128)(2,1)S(1)}, bf16[256,128]{1,0:T(8,128)(2,1)S(1)}, u32[]{:S(2)}, u32[]{:S(2)}) %collective-permute-start.14) | collective-permute-done | bytes 65568 | tf_op jit(solution)/shard_map/ppermute | solution.py:18
  104.5 4.4 %collective-permute-done.15 = bf16[256,128]{1,0:T(8,128)(2,1)S(1)} collective-permute-done((bf16[256,128]{1,0:T(8,128)(2,1)S(1)}, bf16[256,128]{1,0:T(8,128)(2,1)S(1)}, u32[]{:S(2)}, u32[]{:S(2)}) %collective-permute-start.15) | collective-permute-done | bytes 65568 | tf_op jit(solution)/shard_map/ppermute | solution.py:18
  110.2 4.9 %collective-permute-done.16 = bf16[256,128]{1,0:T(8,128)(2,1)S(1)} collective-permute-done((bf16[256,128]{1,0:T(8,128)(2,1)S(1)}, bf16[256,128]{1,0:T(8,128)(2,1)S(1)}, u32[]{:S(2)}, u32[]{:S(2)}) %collective-permute-start.16) | collective-permute-done | bytes 65568 | tf_op jit(solution)/shard_map/ppermute | solution.py:18
  115.4 5.8 %collective-permute-done.17 = bf16[256,128]{1,0:T(8,128)(2,1)S(1)} collective-permute-done((bf16[256,128]{1,0:T(8,128)(2,1)S(1)}, bf16[256,128]{1,0:T(8,128)(2,1)S(1)}, u32[]{:S(2)}, u32[]{:S(2)}) %collective-permute-start.17) | collective-permute-done | bytes 65568 | tf_op jit(solution)/shard_map/ppermute | solution.py:18
  123.0 4.3 %collective-permute-done.18 = bf16[256,128]{1,0:T(8,128)(2,1)S(1)} collective-permute-done((bf16[256,128]{1,0:T(8,128)(2,1)S(1)}, bf16[256,128]{1,0:T(8,128)(2,1)S(1)}, u32[]{:S(2)}, u32[]{:S(2)}) %collective-permute-start.18) | collective-permute-done | bytes 65568 | tf_op jit(solution)/shard_map/ppermute | solution.py:18
  130.0 4.3 %collective-permute-done.19 = bf16[256,128]{1,0:T(8,128)(2,1)S(1)} collective-permute-done((bf16[256,128]{1,0:T(8,128)(2,1)S(1)}, bf16[256,128]{1,0:T(8,128)(2,1)S(1)}, u32[]{:S(2)}, u32[]{:S(2)}) %collective-permute-start.19) | collective-permute-done | bytes 65568 | tf_op jit(solution)/shard_map/ppermute | solution.py:18
  138.6 4.2 %collective-permute-done.28 = bf16[256,128]{1,0:T(8,128)(2,1)S(1)} collective-permute-done((bf16[256,128]{1,0:T(8,128)(2,1)S(1)}, bf16[256,128]{1,0:T(8,128)(2,1)S(1)}, u32[]{:S(2)}, u32[]{:S(2)}) %collective-permute-start.28) | collective-permute-done | bytes 65568 | tf_op jit(solution)/shard_map/ppermute | solution.py:18
  143.4 4.6 %collective-permute-done.29 = bf16[256,128]{1,0:T(8,128)(2,1)S(1)} collective-permute-done((bf16[256,128]{1,0:T(8,128)(2,1)S(1)}, bf16[256,128]{1,0:T(8,128)(2,1)S(1)}, u32[]{:S(2)}, u32[]{:S(2)}) %collective-permute-start.29) | collective-permute-done | bytes 65568 | tf_op jit(solution)/shard_map/ppermute | solution.py:18
  153.5 3.9 %shard_map.76 = (bf16[8,256,128]{2,1,0:T(8,128)(2,1)S(1)}, bf16[8,128,256]{2,1,0:T(8,128)(2,1)S(1)}) custom-call(bf16[8,256,128]{2,1,0:T(8,128)(2,1)S(1)} %bitcast_dynamic-update-slice_fusion.42.m0, bf16[8,256,128]{2,1,0:T(8,128)(2,1)S(1)} %bitcast_dynamic-update-slice_fusion.28.m1, bf16[8,128,128]{2,1,0:T(8,128)(2,1)S(1)} %collective-permute-done.34.before, ...), custom_call_target="tpu_custom_call" | custom-call | flops 15728640 | bytes 4194304 | tf_op jit(solution)/shard_map/pallas_call | solution.py:192
  161.1 3.9 %shard_map.75 = (bf16[8,256,128]{2,1,0:T(8,128)(2,1)S(1)}, bf16[8,128,256]{2,1,0:T(8,128)(2,1)S(1)}) custom-call(bf16[8,256,128]{2,1,0:T(8,128)(2,1)S(1)} %bitcast_dynamic-update-slice_fusion.42.m0, bf16[8,256,128]{2,1,0:T(8,128)(2,1)S(1)} %bitcast_dynamic-update-slice_fusion.28.m1, bf16[8,128,128]{2,1,0:T(8,128)(2,1)S(1)} %collective-permute-done.34.before, ...), custom_call_target="tpu_custom_call" | custom-call | flops 15728640 | bytes 4194304 | tf_op jit(solution)/shard_map/pallas_call | solution.py:192
  167.9 5.4 %shard_map.79 = f32[27,128]{1,0:T(8,128)S(1)} custom-call(bf16[8,256,128]{2,1,0:T(8,128)(2,1)S(1)} %bitcast_dynamic-update-slice_fusion.42.m0, bf16[8,256,128]{2,1,0:T(8,128)(2,1)S(1)} %bitcast_dynamic-update-slice_fusion.28.m1, bf16[8,128,128]{2,1,0:T(8,128)(2,1)S(1)} %collective-permute-done.34.before, ...), custom_call_target="tpu_custom_call" | custom-call | flops 31457280 | bytes 4194304 | tf_op jit(solution)/shard_map/pallas_call | solution.py:192
  173.3 3.9 %collective-permute-start.72 = (f32[27,128]{1,0:T(8,128)S(1)}, f32[27,128]{1,0:T(8,128)S(1)}, u32[]{:S(2)}, u32[]{:S(2)}) collective-permute-start(f32[27,128]{1,0:T(8,128)S(1)} %shard_map.79), channel_id=1, source_target_pairs={{0,1},{1,0},{2,3},{3,2},{4,5},{5,4},{6,7},{7,6},{8,9},{9,8},{10,11... | collective-permute-start | bytes 41480 | tf_op jit(solution)/shard_map/ppermute | solution.py:18
  206.1 6.7 %collective-permute-done.53 = bf16[256,128]{1,0:T(8,128)(2,1)S(1)} collective-permute-done((bf16[256,128]{1,0:T(8,128)(2,1)S(1)}, bf16[256,128]{1,0:T(8,128)(2,1)S(1)}, u32[]{:S(2)}, u32[]{:S(2)}) %collective-permute-start.53) | collective-permute-done | bytes 65568 | tf_op jit(solution)/shard_map/ppermute | solution.py:18
  213.1 5.6 %collective-permute-done.54 = bf16[256,128]{1,0:T(8,128)(2,1)S(1)} collective-permute-done((bf16[256,128]{1,0:T(8,128)(2,1)S(1)}, bf16[256,128]{1,0:T(8,128)(2,1)S(1)}, u32[]{:S(2)}, u32[]{:S(2)}) %collective-permute-start.54) | collective-permute-done | bytes 65568 | tf_op jit(solution)/shard_map/ppermute | solution.py:18
  218.7 5.1 %collective-permute-done.55 = bf16[256,128]{1,0:T(8,128)(2,1)S(1)} collective-permute-done((bf16[256,128]{1,0:T(8,128)(2,1)S(1)}, bf16[256,128]{1,0:T(8,128)(2,1)S(1)}, u32[]{:S(2)}, u32[]{:S(2)}) %collective-permute-start.55) | collective-permute-done | bytes 65568 | tf_op jit(solution)/shard_map/ppermute | solution.py:18
  224.6 6.4 %collective-permute-done.56 = bf16[256,128]{1,0:T(8,128)(2,1)S(1)} collective-permute-done((bf16[256,128]{1,0:T(8,128)(2,1)S(1)}, bf16[256,128]{1,0:T(8,128)(2,1)S(1)}, u32[]{:S(2)}, u32[]{:S(2)}) %collective-permute-start.56) | collective-permute-done | bytes 65568 | tf_op jit(solution)/shard_map/ppermute | solution.py:18
  232.9 4.1 %collective-permute-done.57 = bf16[256,128]{1,0:T(8,128)(2,1)S(1)} collective-permute-done((bf16[256,128]{1,0:T(8,128)(2,1)S(1)}, bf16[256,128]{1,0:T(8,128)(2,1)S(1)}, u32[]{:S(2)}, u32[]{:S(2)}) %collective-permute-start.57) | collective-permute-done | bytes 65568 | tf_op jit(solution)/shard_map/ppermute | solution.py:18
  237.7 6.3 %collective-permute-done.58 = bf16[256,128]{1,0:T(8,128)(2,1)S(1)} collective-permute-done((bf16[256,128]{1,0:T(8,128)(2,1)S(1)}, bf16[256,128]{1,0:T(8,128)(2,1)S(1)}, u32[]{:S(2)}, u32[]{:S(2)}) %collective-permute-start.58) | collective-permute-done | bytes 65568 | tf_op jit(solution)/shard_map/ppermute | solution.py:18
  248.3 4.3 %collective-permute-done.39 = bf16[256,128]{1,0:T(8,128)(2,1)S(1)} collective-permute-done((bf16[256,128]{1,0:T(8,128)(2,1)S(1)}, bf16[256,128]{1,0:T(8,128)(2,1)S(1)}, u32[]{:S(2)}, u32[]{:S(2)}) %collective-permute-start.39) | collective-permute-done | bytes 65568 | tf_op jit(solution)/shard_map/ppermute | solution.py:18
  253.0 4.8 %collective-permute-done.40 = bf16[256,128]{1,0:T(8,128)(2,1)S(1)} collective-permute-done((bf16[256,128]{1,0:T(8,128)(2,1)S(1)}, bf16[256,128]{1,0:T(8,128)(2,1)S(1)}, u32[]{:S(2)}, u32[]{:S(2)}) %collective-permute-start.40) | collective-permute-done | bytes 65568 | tf_op jit(solution)/shard_map/ppermute | solution.py:18
  273.1 4.2 %collective-permute-done.60 = bf16[128,256]{1,0:T(8,128)(2,1)S(1)} collective-permute-done((bf16[128,256]{1,0:T(8,128)(2,1)S(1)}, bf16[128,256]{1,0:T(8,128)(2,1)S(1)}, u32[]{:S(2)}, u32[]{:S(2)}) %collective-permute-start.60) | collective-permute-done | bytes 65568 | tf_op jit(solution)/shard_map/ppermute | solution.py:18
  277.9 5.8 %collective-permute-done.62 = bf16[128,256]{1,0:T(8,128)(2,1)S(1)} collective-permute-done((bf16[128,256]{1,0:T(8,128)(2,1)S(1)}, bf16[128,256]{1,0:T(8,128)(2,1)S(1)}, u32[]{:S(2)}, u32[]{:S(2)}) %collective-permute-start.62) | collective-permute-done | bytes 65568 | tf_op jit(solution)/shard_map/ppermute | solution.py:18
  312.5 6.5 %collective-permute-done.67 = bf16[1024,256]{1,0:T(8,128)(2,1)S(1)} collective-permute-done((bf16[1024,256]{1,0:T(8,128)(2,1)S(1)}, bf16[1024,256]{1,0:T(8,128)(2,1)S(1)}, u32[]{:S(2)}, u32[]{:S(2)}) %collective-permute-start.67) | collective-permute-done | bytes 524320 | tf_op jit(solution)/shard_map/ppermute | solution.py:18
  322.7 4.7 %collective-permute-done.68 = bf16[4,128,256]{2,1,0:T(8,128)(2,1)} collective-permute-done((bf16[4,128,256]{2,1,0:T(8,128)(2,1)S(1)}, bf16[4,128,256]{2,1,0:T(8,128)(2,1)}, u32[]{:S(2)}, u32[]{:S(2)}) %collective-permute-start.68) | collective-permute-done | bytes 262176 | tf_op jit(solution)/shard_map/ppermute | solution.py:18
  (306 shorter events, 183.6 us)
Async XLA Ops:
  2.2 34.9 %collective-permute-start.8 = (bf16[128,256]{1,0:T(8,128)(2,1)}, bf16[128,256]{1,0:T(8,128)(2,1)S(1)}, u32[]{:S(2)}, u32[]{:S(2)}) collective-permute-start(bf16[128,256]{1,0:T(8,128)(2,1)} %constant_dynamic-slice_fusion), channel_id=1, source_target_pairs={{0,16},{4,20},{8,24},{12,28},{16,0},{20,4},{24,8},{28,12},{1,17},{... | collective-permute-start | bytes 196616 | tf_op jit(solution)/shard_map/ppermute | solution.py:18
  6.3 33.6 %collective-permute-start.7 = (bf16[128,256]{1,0:T(8,128)(2,1)}, bf16[128,256]{1,0:T(8,128)(2,1)S(1)}, u32[]{:S(2)}, u32[]{:S(2)}) collective-permute-start(bf16[128,256]{1,0:T(8,128)(2,1)} %constant_dynamic-slice_fusion), channel_id=1, source_target_pairs={{0,8},{4,12},{8,0},{12,4},{16,24},{20,28},{24,16},{28,20},{1,9},{5... | collective-permute-start | bytes 196616 | tf_op jit(solution)/shard_map/ppermute | solution.py:18
  7.8 34.5 %collective-permute-start.9 = (bf16[128,256]{1,0:T(8,128)(2,1)}, bf16[128,256]{1,0:T(8,128)(2,1)}, u32[]{:S(2)}, u32[]{:S(2)}) collective-permute-start(bf16[128,256]{1,0:T(8,128)(2,1)} %constant_dynamic-slice_fusion), channel_id=1, source_target_pairs={{0,24},{4,28},{8,16},{12,20},{16,8},{20,12},{24,0},{28,4},{1,25},{... | collective-permute-start | bytes 196616 | tf_op jit(solution)/shard_map/ppermute | solution.py:18
  12.7 68.7 %collective-permute-start.26 = (bf16[128,256]{1,0:T(8,128)(2,1)}, bf16[128,256]{1,0:T(8,128)(2,1)}, u32[]{:S(2)}, u32[]{:S(2)}) collective-permute-start(bf16[128,256]{1,0:T(8,128)(2,1)} %get-tuple-element.83), channel_id=1, source_target_pairs={{0,28},{4,24},{8,20},{12,16},{16,12},{20,8},{24,4},{28,0},{1,29},{... | collective-permute-start | bytes 196616 | tf_op jit(solution)/shard_map/ppermute | solution.py:18
  17.4 10.4 %collective-permute-start.20 = (bf16[128,256]{1,0:T(8,128)(2,1)}, bf16[128,256]{1,0:T(8,128)(2,1)}, u32[]{:S(2)}, u32[]{:S(2)}) collective-permute-start(bf16[128,256]{1,0:T(8,128)(2,1)} %get-tuple-element.89), channel_id=1, source_target_pairs={{0,4},{4,0},{8,12},{12,8},{16,20},{20,16},{24,28},{28,24},{1,5},{5... | collective-permute-start | bytes 196616 | tf_op jit(solution)/shard_map/ppermute | solution.py:18
  36.4 40.8 %collective-permute-start.25 = (bf16[128,256]{1,0:T(8,128)(2,1)S(1)}, bf16[128,256]{1,0:T(8,128)(2,1)S(1)}, u32[]{:S(2)}, u32[]{:S(2)}) collective-permute-start(bf16[128,256]{1,0:T(8,128)(2,1)S(1)} %copy-done.22), channel_id=1, source_target_pairs={{0,24},{4,28},{8,16},{12,20},{16,8},{20,12},{24,0},{28,4},{1,25},{... | collective-permute-start | bytes 196616 | tf_op jit(solution)/shard_map/ppermute | solution.py:18
  37.1 32.3 %collective-permute-start.24 = (bf16[128,256]{1,0:T(8,128)(2,1)S(1)}, bf16[128,256]{1,0:T(8,128)(2,1)S(1)}, u32[]{:S(2)}, u32[]{:S(2)}) collective-permute-start(bf16[128,256]{1,0:T(8,128)(2,1)S(1)} %copy-done.23), channel_id=1, source_target_pairs={{0,20},{4,16},{8,28},{12,24},{16,4},{20,0},{24,12},{28,8},{1,21},{... | collective-permute-start | bytes 196616 | tf_op jit(solution)/shard_map/ppermute | solution.py:18
  48.1 12.6 %collective-permute-start.23 = (bf16[128,256]{1,0:T(8,128)(2,1)S(1)}, bf16[128,256]{1,0:T(8,128)(2,1)S(1)}, u32[]{:S(2)}, u32[]{:S(2)}) collective-permute-start(bf16[128,256]{1,0:T(8,128)(2,1)S(1)} %copy-done.24), channel_id=1, source_target_pairs={{0,16},{4,20},{8,24},{12,28},{16,0},{20,4},{24,8},{28,12},{1,17},{... | collective-permute-start | bytes 196616 | tf_op jit(solution)/shard_map/ppermute | solution.py:18
  59.2 9.6 %collective-permute-start.11 = (bf16[1024,256]{1,0:T(8,128)(2,1)S(1)}, bf16[1024,256]{1,0:T(8,128)(2,1)S(1)}, u32[]{:S(2)}, u32[]{:S(2)}) collective-permute-start(bf16[1024,256]{1,0:T(8,128)(2,1)S(1)} %bitcast.362), channel_id=1, source_target_pairs={{0,2},{1,3},{2,0},{3,1},{4,6},{5,7},{6,4},{7,5},{8,10},{9,11},{10,... | collective-permute-start | bytes 1572872 | tf_op jit(solution)/shard_map/ppermute | solution.py:18
  66.9 14.5 %collective-permute-start.6 = (bf16[128,256]{1,0:T(8,128)(2,1)S(1)}, bf16[128,256]{1,0:T(8,128)(2,1)S(1)}, u32[]{:S(2)}, u32[]{:S(2)}) collective-permute-start(bf16[128,256]{1,0:T(8,128)(2,1)S(1)} %get-tuple-element.98), channel_id=1, source_target_pairs={{0,28},{4,24},{8,20},{12,16},{16,12},{20,8},{24,4},{28,0},{1,29},{... | collective-permute-start | bytes 196616 | tf_op jit(solution)/shard_map/ppermute | solution.py:18
  69.4 13.4 %collective-permute-start.12 = (bf16[2,1024,256]{2,1,0:T(8,128)(2,1)S(1)}, bf16[2,1024,256]{2,1,0:T(8,128)(2,1)S(1)}, u32[]{:S(2)}, u32[]{:S(2)}) collective-permute-start(bf16[2,1024,256]{2,1,0:T(8,128)(2,1)S(1)} %get-tuple-element.27), channel_id=1, source_target_pairs={{0,1},{1,0},{2,3},{3,2},{4,5},{5,4},{6,7},{7,6},{8,9},{9,8},{10,11... | collective-permute-start | bytes 3145736 | tf_op jit(solution)/shard_map/ppermute | solution.py:18
  85.6 67.1 %collective-permute-start.33 = (bf16[256,128]{1,0:T(8,128)(2,1)S(1)}, bf16[256,128]{1,0:T(8,128)(2,1)S(1)}, u32[]{:S(2)}, u32[]{:S(2)}) collective-permute-start(bf16[256,128]{1,0:T(8,128)(2,1)S(1)} %get-tuple-element.76), channel_id=1, source_target_pairs={{0,28},{4,24},{8,20},{12,16},{16,12},{20,8},{24,4},{28,0},{1,29},{... | collective-permute-start | bytes 196616 | tf_op jit(solution)/shard_map/ppermute | solution.py:18
  88.2 64.4 %collective-permute-start.32 = (bf16[256,128]{1,0:T(8,128)(2,1)S(1)}, bf16[256,128]{1,0:T(8,128)(2,1)S(1)}, u32[]{:S(2)}, u32[]{:S(2)}) collective-permute-start(bf16[256,128]{1,0:T(8,128)(2,1)S(1)} %get-tuple-element.77), channel_id=1, source_target_pairs={{0,24},{4,28},{8,16},{12,20},{16,8},{20,12},{24,0},{28,4},{1,25},{... | collective-permute-start | bytes 196616 | tf_op jit(solution)/shard_map/ppermute | solution.py:18
  90.0 62.6 %collective-permute-start.31 = (bf16[256,128]{1,0:T(8,128)(2,1)S(1)}, bf16[256,128]{1,0:T(8,128)(2,1)S(1)}, u32[]{:S(2)}, u32[]{:S(2)}) collective-permute-start(bf16[256,128]{1,0:T(8,128)(2,1)S(1)} %get-tuple-element.78), channel_id=1, source_target_pairs={{0,20},{4,16},{8,28},{12,24},{16,4},{20,0},{24,12},{28,8},{1,21},{... | collective-permute-start | bytes 196616 | tf_op jit(solution)/shard_map/ppermute | solution.py:18
  90.0 59.3 %collective-permute-start.30 = (bf16[256,128]{1,0:T(8,128)(2,1)S(1)}, bf16[256,128]{1,0:T(8,128)(2,1)S(1)}, u32[]{:S(2)}, u32[]{:S(2)}) collective-permute-start(bf16[256,128]{1,0:T(8,128)(2,1)S(1)} %get-tuple-element.79), channel_id=1, source_target_pairs={{0,16},{4,20},{8,24},{12,28},{16,0},{20,4},{24,8},{28,12},{1,17},{... | collective-permute-start | bytes 196616 | tf_op jit(solution)/shard_map/ppermute | solution.py:18
  173.3 13.5 %collective-permute-start.72 = (f32[27,128]{1,0:T(8,128)S(1)}, f32[27,128]{1,0:T(8,128)S(1)}, u32[]{:S(2)}, u32[]{:S(2)}) collective-permute-start(f32[27,128]{1,0:T(8,128)S(1)} %shard_map.79), channel_id=1, source_target_pairs={{0,1},{1,0},{2,3},{3,2},{4,5},{5,4},{6,7},{7,6},{8,9},{9,8},{10,11... | collective-permute-start | bytes 41480 | tf_op jit(solution)/shard_map/ppermute | solution.py:18
  180.1 12.7 %collective-permute-start.37 = (bf16[8,128,128]{2,1,0:T(8,128)(2,1)}, bf16[8,128,128]{2,1,0:T(8,128)(2,1)S(1)}, u32[]{:S(2)}, u32[]{:S(2)}) collective-permute-start(bf16[8,128,128]{2,1,0:T(8,128)(2,1)} %get-tuple-element.68), channel_id=1, source_target_pairs={{1,0},{2,1},{3,2},{5,4},{6,5},{7,6},{9,8},{10,9},{11,10},{13,12},{... | collective-permute-start | bytes 786440 | tf_op jit(solution)/shard_map/ppermute | solution.py:84
  181.3 11.4 %collective-permute-start.36 = (bf16[8,128,128]{2,1,0:T(8,128)(2,1)}, bf16[8,128,128]{2,1,0:T(8,128)(2,1)S(1)}, u32[]{:S(2)}, u32[]{:S(2)}) collective-permute-start(bf16[8,128,128]{2,1,0:T(8,128)(2,1)} %get-tuple-element.69), channel_id=1, source_target_pairs={{0,1},{1,2},{2,3},{4,5},{5,6},{6,7},{8,9},{9,10},{10,11},{12,13},{... | collective-permute-start | bytes 786440 | tf_op jit(solution)/shard_map/ppermute | solution.py:83
  195.1 11.0 %collective-permute-start.52 = (bf16[256,128]{1,0:T(8,128)(2,1)S(1)}, bf16[256,128]{1,0:T(8,128)(2,1)S(1)}, u32[]{:S(2)}, u32[]{:S(2)}) collective-permute-start(bf16[256,128]{1,0:T(8,128)(2,1)S(1)} %get-tuple-element.50), channel_id=1, source_target_pairs={{0,4},{4,0},{8,12},{12,8},{16,20},{20,16},{24,28},{28,24},{1,5},{5... | collective-permute-start | bytes 196616 | tf_op jit(solution)/shard_map/ppermute | solution.py:18
  198.4 59.6 %collective-permute-start.44 = (bf16[256,128]{1,0:T(8,128)(2,1)S(1)}, bf16[256,128]{1,0:T(8,128)(2,1)S(1)}, u32[]{:S(2)}, u32[]{:S(2)}) collective-permute-start(bf16[256,128]{1,0:T(8,128)(2,1)S(1)} %get-tuple-element.60), channel_id=1, source_target_pairs={{0,28},{4,24},{8,20},{12,16},{16,12},{20,8},{24,4},{28,0},{1,29},{... | collective-permute-start | bytes 196616 | tf_op jit(solution)/shard_map/ppermute | solution.py:18
  199.3 58.6 %collective-permute-start.43 = (bf16[256,128]{1,0:T(8,128)(2,1)S(1)}, bf16[256,128]{1,0:T(8,128)(2,1)S(1)}, u32[]{:S(2)}, u32[]{:S(2)}) collective-permute-start(bf16[256,128]{1,0:T(8,128)(2,1)S(1)} %get-tuple-element.61), channel_id=1, source_target_pairs={{0,24},{4,28},{8,16},{12,20},{16,8},{20,12},{24,0},{28,4},{1,25},{... | collective-permute-start | bytes 196616 | tf_op jit(solution)/shard_map/ppermute | solution.py:18
  202.9 55.0 %collective-permute-start.42 = (bf16[256,128]{1,0:T(8,128)(2,1)S(1)}, bf16[256,128]{1,0:T(8,128)(2,1)S(1)}, u32[]{:S(2)}, u32[]{:S(2)}) collective-permute-start(bf16[256,128]{1,0:T(8,128)(2,1)S(1)} %get-tuple-element.62), channel_id=1, source_target_pairs={{0,20},{4,16},{8,28},{12,24},{16,4},{20,0},{24,12},{28,8},{1,21},{... | collective-permute-start | bytes 196616 | tf_op jit(solution)/shard_map/ppermute | solution.py:18
  202.9 55.0 %collective-permute-start.41 = (bf16[256,128]{1,0:T(8,128)(2,1)S(1)}, bf16[256,128]{1,0:T(8,128)(2,1)S(1)}, u32[]{:S(2)}, u32[]{:S(2)}) collective-permute-start(bf16[256,128]{1,0:T(8,128)(2,1)S(1)} %get-tuple-element.63), channel_id=1, source_target_pairs={{0,16},{4,20},{8,24},{12,28},{16,0},{20,4},{24,8},{28,12},{1,17},{... | collective-permute-start | bytes 196616 | tf_op jit(solution)/shard_map/ppermute | solution.py:18
  260.3 27.8 %collective-permute-start.65 = (bf16[128,256]{1,0:T(8,128)(2,1)S(1)}, bf16[128,256]{1,0:T(8,128)(2,1)S(1)}, u32[]{:S(2)}, u32[]{:S(2)}) collective-permute-start(bf16[128,256]{1,0:T(8,128)(2,1)S(1)} %get-tuple-element.36), channel_id=1, source_target_pairs={{0,28},{4,24},{8,20},{12,16},{16,12},{20,8},{24,4},{28,0},{1,29},{... | collective-permute-start | bytes 196616 | tf_op jit(solution)/shard_map/ppermute | solution.py:18
  262.4 25.6 %collective-permute-start.64 = (bf16[128,256]{1,0:T(8,128)(2,1)S(1)}, bf16[128,256]{1,0:T(8,128)(2,1)S(1)}, u32[]{:S(2)}, u32[]{:S(2)}) collective-permute-start(bf16[128,256]{1,0:T(8,128)(2,1)S(1)} %get-tuple-element.37), channel_id=1, source_target_pairs={{0,24},{4,28},{8,16},{12,20},{16,8},{20,12},{24,0},{28,4},{1,25},{... | collective-permute-start | bytes 196616 | tf_op jit(solution)/shard_map/ppermute | solution.py:18
  264.6 21.5 %collective-permute-start.63 = (bf16[128,256]{1,0:T(8,128)(2,1)S(1)}, bf16[128,256]{1,0:T(8,128)(2,1)S(1)}, u32[]{:S(2)}, u32[]{:S(2)}) collective-permute-start(bf16[128,256]{1,0:T(8,128)(2,1)S(1)} %get-tuple-element.38), channel_id=1, source_target_pairs={{0,20},{4,16},{8,28},{12,24},{16,4},{20,0},{24,12},{28,8},{1,21},{... | collective-permute-start | bytes 196616 | tf_op jit(solution)/shard_map/ppermute | solution.py:18
  264.6 12.8 %collective-permute-start.61 = (bf16[128,256]{1,0:T(8,128)(2,1)S(1)}, bf16[128,256]{1,0:T(8,128)(2,1)S(1)}, u32[]{:S(2)}, u32[]{:S(2)}) collective-permute-start(bf16[128,256]{1,0:T(8,128)(2,1)S(1)} %get-tuple-element.40), channel_id=1, source_target_pairs={{0,12},{4,8},{8,4},{12,0},{16,28},{20,24},{24,20},{28,16},{1,13},{... | collective-permute-start | bytes 196616 | tf_op jit(solution)/shard_map/ppermute | solution.py:18
  277.4 30.7 %collective-permute-start.66 = (f32[1024,512]{1,0:T(8,128)S(1)}, f32[1024,512]{1,0:T(8,128)S(1)}, u32[]{:S(2)}, u32[]{:S(2)}) collective-permute-start(f32[1024,512]{1,0:T(8,128)S(1)} %pad_maximum_fusion.1), channel_id=1, source_target_pairs={{0,1},{1,0},{2,3},{3,2},{4,5},{5,4},{6,7},{7,6},{8,9},{9,8},{10,11... | collective-permute-start | bytes 6291464 | tf_op jit(solution)/shard_map/ppermute | solution.py:18
  283.7 38.6 %collective-permute-start.51 = (bf16[128,256]{1,0:T(8,128)(2,1)S(1)}, bf16[128,256]{1,0:T(8,128)(2,1)S(1)}, u32[]{:S(2)}, u32[]{:S(2)}) collective-permute-start(bf16[128,256]{1,0:T(8,128)(2,1)S(1)} %get-tuple-element.52), channel_id=1, source_target_pairs={{0,28},{4,24},{8,20},{12,16},{16,12},{20,8},{24,4},{28,0},{1,29},{... | collective-permute-start | bytes 196616 | tf_op jit(solution)/shard_map/ppermute | solution.py:18
  286.1 25.5 %collective-permute-start.50 = (bf16[128,256]{1,0:T(8,128)(2,1)S(1)}, bf16[128,256]{1,0:T(8,128)(2,1)S(1)}, u32[]{:S(2)}, u32[]{:S(2)}) collective-permute-start(bf16[128,256]{1,0:T(8,128)(2,1)S(1)} %get-tuple-element.53), channel_id=1, source_target_pairs={{0,24},{4,28},{8,16},{12,20},{16,8},{20,12},{24,0},{28,4},{1,25},{... | collective-permute-start | bytes 196616 | tf_op jit(solution)/shard_map/ppermute | solution.py:18
  288.0 23.3 %collective-permute-start.49 = (bf16[128,256]{1,0:T(8,128)(2,1)S(1)}, bf16[128,256]{1,0:T(8,128)(2,1)S(1)}, u32[]{:S(2)}, u32[]{:S(2)}) collective-permute-start(bf16[128,256]{1,0:T(8,128)(2,1)S(1)} %get-tuple-element.54), channel_id=1, source_target_pairs={{0,20},{4,16},{8,28},{12,24},{16,4},{20,0},{24,12},{28,8},{1,21},{... | collective-permute-start | bytes 196616 | tf_op jit(solution)/shard_map/ppermute | solution.py:18
  309.4 9.6 %collective-permute-start.67 = (bf16[1024,256]{1,0:T(8,128)(2,1)S(1)}, bf16[1024,256]{1,0:T(8,128)(2,1)S(1)}, u32[]{:S(2)}, u32[]{:S(2)}) collective-permute-start(bf16[1024,256]{1,0:T(8,128)(2,1)S(1)} %fusion.4), channel_id=1, source_target_pairs={{0,2},{1,3},{2,0},{3,1},{4,6},{5,7},{6,4},{7,5},{8,10},{9,11},{10,... | collective-permute-start | bytes 1572872 | tf_op jit(solution)/shard_map/ppermute | solution.py:18
  (69 other events, 579.0 us)

commit v3 on v2

--- a/solution.py
+++ b/solution.py
@@ -113,60 +113,65 @@
     return sums[1] + shifted(lo, False) + shifted(hi, True)
 
 
-def load_planes(pad_ref, refs, where, before_ref, after_ref, wanted, planes):
+def load_planes(pad_ref, refs, where, sides, wanted, planes):
+    lanes = 2 * WW
     for p in sorted(wanted):
         if p < 0:
-            fill(pad_ref, 0, before_ref[...])
+            fill(pad_ref, 0, sides[0][...])
         elif p >= planes:
-            fill(pad_ref, planes + 1, after_ref[...])
+            fill(pad_ref, planes + 1, sides[1][...])
         else:
             which, at = where[p]
-            cells = refs[which].shape[1] // len([q for q in where if where[q][0] == which])
-            fill(pad_ref, p + 1, refs[which][:, at * cells : (at + 1) * cells, :])
-
-
-def forward_kernel(group, where, planes, m0, m1, before, after, taps, vol, up, grad, out, pad):
+            fill(pad_ref, p + 1, refs[which][:, at * lanes : (at + 1) * lanes, :])
+
+
+def forward_kernel(group, at, where, planes, m, before, after, taps, vol, up, grad, out, pad):
     wanted = {p + a for p in group for a in (-1, 0, 1)}
-    load_planes(pad, (m0, m1), where, before, after, wanted, planes)
-    strips = m0.shape[0]
-    cells = vol.shape[2] // len(group)
-    rows = cells // WW
+    load_planes(pad, (m,), where, (before, after), wanted, planes)
+    lanes = 2 * WW
     for k, p in enumerate(group):
 
         def strip(f, carry, k=k, p=p):
-            lines = [conv_row(pad, taps, p + 1, f * rows + 1 + r, False) for r in range(rows)]
+            lines = [conv_row(pad, taps, p + 1, f * 2 + 1 + r, False) for r in range(2)]
             spatial = jnp.concatenate(lines, axis=0)
             sig = 1.0 / (1.0 + jnp.exp(-spatial))
-            lane = slice(k * cells, (k + 1) * cells)
-            cot = jnp.transpose(up[f, :, lane].astype(F32))
+            lane = slice(k * lanes, (k + 1) * lanes)
+            source = slice(at[p] * lanes, (at[p] + 1) * lanes)
+            cot = jnp.transpose(up[f, :, source].astype(F32))
             slope = sig * (1.0 + spatial * (1.0 - sig))
             grad[f, lane, :] = (cot * slope).astype(BF)
             silu = jnp.transpose(spatial * sig)
-            out[f, :, lane] = (vol[f, :, lane].astype(F32) + silu).astype(BF)
+            out[f, :, lane] = (vol[f, :, source].astype(F32) + silu).astype(BF)
             return carry
 
-        lax.fori_loop(0, strips, strip, 0)
+        lax.fori_loop(0, m.shape[0], strip, 0)
+
+
+def middle_forward_kernel(group, at, where, planes, m, taps, vol, up, grad, out, pad):
+    forward_kernel(group, at, where, planes, m, None, None, taps, vol, up, grad, out, pad)
 
 
 def backward_kernel(group, where, planes, g0, g1, before, after, taps, out, pad):
     wanted = {p + a for p in group for a in (-1, 0, 1)}
-    load_planes(pad, (g0, g1), where, before, after, wanted, planes)
-    strips = g0.shape[0]
-    cells = out.shape[1] // len(group)
-    rows = cells // WW
+    load_planes(pad, (g0, g1), where, (before, after), wanted, planes)
+    lanes = 2 * WW
     for k, p in enumerate(group):
 
         def strip(f, carry, k=k, p=p):
-            lines = [conv_row(pad, taps, p + 1, f * rows + 1 + r, True) for r in range(rows)]
-            out[f, k * cells : (k + 1) * cells, :] = jnp.concatenate(lines, axis=0).astype(BF)
+            lines = [conv_row(pad, taps, p + 1, f * 2 + 1 + r, True) for r in range(2)]
+            out[f, k * lanes : (k + 1) * lanes, :] = jnp.concatenate(lines, axis=0).astype(BF)
             return carry
 
-        lax.fori_loop(0, strips, strip, 0)
-
-
-def taps_kernel(where, planes, norm, m0, m1, before, after, g0, g1, out, pad, gpad):
-    load_planes(pad, (m0, m1), where, before, after, set(range(-1, planes + 1)), planes)
-    load_planes(gpad, (g0, g1), where, before, after, set(range(planes)), planes)
+        lax.fori_loop(0, g0.shape[0], strip, 0)
+
+
+def middle_backward_kernel(group, where, planes, g0, g1, taps, out, pad):
+    backward_kernel(group, where, planes, g0, g1, None, None, taps, out, pad)
+
+
+def taps_kernel(where, where_grad, planes, norm, m, before, after, g0, g1, out, pad, gpad):
+    load_planes(pad, (m,), where, (before, after), range(-1, planes + 1), planes)
+    load_planes(gpad, (g0, g1), where_grad, (), range(planes), planes)
     rows, width, ch = pad.shape[1] - 2, pad.shape[2], pad.shape[3]
     sums = tuple(jnp.zeros((8, ch), F32) for _ in range(27))
 
@@ -211,34 +216,42 @@
     norm = 1.0 / math.sqrt(planes * ns * flat)
     edges, middle = (0, planes - 1), tuple(range(1, planes - 1))
     groups = (edges, middle)
-    where = {p: (i, k) for i, g in enumerate(groups) for k, p in enumerate(g)}
+    order = edges + middle
     turn = me ^ (me_space * (nf // ns))
 
-    def strips_of(field, group, count):
-        part = jnp.stack([field[:, p] for p in group], axis=1)
-        part = part.reshape(ch, len(group), count, flat // count).transpose(2, 0, 1, 3)
-        return part.reshape(count, ch, len(group) * (flat // count))
-
-    vol_all = []
-    for g in groups:
-        part = strips_of(volume, g, nf)
-        got = exchange([pick(part, me ^ s) for s in range(nf)], "filter")
-        vol_all.append(place(got, turn).reshape(ns, nf * ch // ns, part.shape[2]))
+    def strips_of(field, count):
+        part = jnp.stack([field[:, p] for p in order], axis=1)
+        part = part.reshape(ch, planes, count, flat // count).transpose(2, 0, 1, 3)
+        return part.reshape(count, ch, planes * (flat // count))
+
+    def planes_of(part, count):
+        part = part.reshape(count, ch, planes, flat // count)
+        whole = [part[:, :, order.index(p)].transpose(1, 0, 2).reshape(ch, flat) for p in range(planes)]
+        return jnp.stack(whole, axis=1)
+
+    part = strips_of(volume, nf)
+    got = exchange([pick(part, me ^ s) for s in range(nf)], "filter")
+    vol_all = place(got, turn).reshape(ns, nf * ch // ns, planes * cells)
     weights = gather_weights(mixing, me_space)
-    vol_strips = [strips_of(volume, g, strips) for g in groups]
-    up_strips = [strips_of(upstream, g, strips) for g in groups]
-    vol_all[0], up_strips = lax.optimization_barrier((vol_all[0], up_strips))
-
-    mixed = []
-    for part in vol_all:
-        prod = lax.dot_general(
-            part, weights, (((0, 1), (0, 2)), ((), ())), preferred_element_type=F32
-        ).astype(BF)
-        got = exchange([prod[:, s * ch : (s + 1) * ch] for s in range(nf)], "filter")
-        mixed.append(restrip(place(got, me), len(groups[len(mixed)]), strips))
+    vol_strips = strips_of(volume, strips)
+    up_strips = strips_of(upstream, strips)
+    vol_all, up_strips = lax.optimization_barrier((vol_all, up_strips))
+
+    prod = lax.dot_general(
+        vol_all, weights, (((0, 1), (0, 2)), ((), ())), preferred_element_type=F32
+    ).astype(BF)
+    got = exchange([prod[:, s * ch : (s + 1) * ch] for s in range(nf)], "filter")
+    mixed = restrip(place(got, me), planes, strips)
 
     taps = kernel_taps.T
-    before, after = halo(mixed[0][:, :lanes], mixed[0][:, lanes:])
+    at = {p: k for k, p in enumerate(order)}
+    where = {p: (0, at[p]) for p in order}
+    where_grad = {p: (i, k) for i, g in enumerate(groups) for k, p in enumerate(g)}
+
+    def plane(field, p):
+        return field[:, at[p] * lanes : (at[p] + 1) * lanes]
+
+    before, after = halo(plane(mixed, 0), plane(mixed, planes - 1))
     pad = pltpu.VMEM((planes + 2, height + 2, WW, ch), F32)
     conv_ops = 60 * flat * ch
 
@@ -248,35 +261,43 @@
             jax.ShapeDtypeStruct((strips, len(g) * lanes, ch), BF),
             jax.ShapeDtypeStruct((strips, ch, len(g) * lanes), BF),
         )
-        kernel = functools.partial(forward_kernel, g, where, planes)
+        if i == 0:
+            kernel = functools.partial(forward_kernel, g, at, where, planes)
+            sides = (before, after)
+        else:
+            kernel = functools.partial(middle_forward_kernel, g, at, where, planes)
+            sides = ()
         return call(
-            kernel, shapes, [pad], mixed[0], mixed[1], before, after, taps,
-            vol_strips[i], up_strips[i], ops=conv_ops * len(g),
+            kernel, shapes, [pad], mixed, *sides, taps, vol_strips, up_strips,
+            ops=conv_ops * len(g),
         )
 
+    grad_middle, out_middle = forward(1)
     grad_edges, out_edges = forward(0)
     grad_before, grad_after = halo(grad_edges[:, :lanes], grad_edges[:, lanes:])
-    grad_middle, out_middle = forward(1)
-    grads = (grad_edges, grad_middle)
 
     def backward(i):
         g = groups[i]
         shape = jax.ShapeDtypeStruct((strips, len(g) * lanes, ch), BF)
-        kernel = functools.partial(backward_kernel, g, where, planes)
+        if i == 0:
+            kernel = functools.partial(backward_kernel, g, where_grad, planes)
+            sides = (grad_before, grad_after)
+        else:
+            kernel = functools.partial(middle_backward_kernel, g, where_grad, planes)
+            sides = ()
         return call(
-            kernel, shape, [pad], grad_edges, grad_middle, grad_before, grad_after, taps,
-            ops=conv_ops * len(g),
+            kernel, shape, [pad], grad_edges, grad_middle, *sides, taps, ops=conv_ops * len(g)
         )
 
-    mg_all, back_all = [None, None], [None, None]
-    for i in (1, 0):
-        part = restrip(backward(i), len(groups[i]), nf)
-        mg_all[i] = jnp.stack(exchange([pick(part, me ^ s) for s in range(nf)], "filter"))
+    mg_middle = backward(1)
+    mg_edges = backward(0)
+    part = restrip(jnp.concatenate([mg_edges, mg_middle], axis=1), planes, nf)
+    mg_all = jnp.stack(exchange([pick(part, me ^ s) for s in range(nf)], "filter"))
 
     taps_part = call(
-        functools.partial(taps_kernel, where, planes, norm),
+        functools.partial(taps_kernel, where, where_grad, planes, norm),
         jax.ShapeDtypeStruct((27, ch), F32), [pad, pad],
-        mixed[0], mixed[1], before, after, grad_edges, grad_middle,
+        mixed, before, after, grad_edges, grad_middle,
         ops=conv_ops * planes,
     )
     taps_grad = taps_part
@@ -284,31 +305,23 @@
     while step < ns:
         taps_grad = taps_grad + swap(taps_grad, "space", step)
         step *= 2
-
-    whole = [None] * planes
-    for g, part in zip(groups, (out_edges, out_middle)):
-        part = part.reshape(strips, ch, len(g), lanes)
-        for k, p in enumerate(g):
-            whole[p] = part[:, :, k].transpose(1, 0, 2).reshape(ch, flat)
-    output = jnp.stack(whole, axis=1)
-
-    whole = [None] * planes
-    weights_rows = weights.reshape(ns, nf, ch, weights.shape[2])
-    for i in (1, 0):
-        g = groups[i]
-        back = lax.dot_general(
-            weights_rows, mg_all[i], (((1, 2), (0, 2)), ((), ())), preferred_element_type=F32
-        ).astype(BF)
-        back = back.reshape(nf, ch, len(g) * cells)
-        got = exchange([pick(back, turn ^ s) for s in range(nf)], "filter")
-        back_own = place(got, me).reshape(nf, ch, len(g), cells)
-        for k, p in enumerate(g):
-            whole[p] = back_own[:, :, k].transpose(1, 0, 2).reshape(ch, flat)
-    volume_grad = (upstream.astype(F32) + jnp.stack(whole, axis=1).astype(F32)).astype(BF)
+    output = planes_of(jnp.concatenate([out_edges, out_middle], axis=2), strips)
+    mg_all, taps_grad, output = lax.optimization_barrier((mg_all, taps_grad, output))
+
+    back = lax.dot_general(
+        weights.reshape(ns, nf, ch, nf * ch // ns),
+        mg_all,
+        (((1, 2), (0, 2)), ((), ())),
+        preferred_element_type=F32,
+    ).astype(BF)
+    back = back.reshape(nf, ch, planes * cells)
+    got = exchange([pick(back, turn ^ s) for s in range(nf)], "filter")
+    back_own = planes_of(place(got, me), nf)
+    volume_grad = (upstream.astype(F32) + back_own.astype(F32)).astype(BF)
 
     weight_part = lax.dot_general(
-        jnp.concatenate(mg_all, axis=1),
-        jnp.concatenate(vol_all, axis=2).reshape(nf * ch, -1),
+        mg_all,
+        vol_all.reshape(nf * ch, planes * cells),
         (((1,), (1,)), ((), ())),
         preferred_element_type=F32,
     )

time: 341 us -> 216 us (0.63)
  waiting for transfers between devices: 157 us -> 59.8 us
  starting transfers between devices: 103 us -> 78.9 us
  local copies, waits for them, and re-layouts: 43.7 us -> 37.6 us
  other arithmetic: 9.47 us -> 14.8 us
    ppermute x70 -> x42, waiting for transfers between devices: 156 us -> 59.8 us  [swap(): return lax.ppermute(block, axis, [(i, i ^ step) for i in range(size)])]
    ppermute x70 -> x42, starting transfers between devices: 93.9 us -> 69.4 us  [swap(): return lax.ppermute(block, axis, [(i, i ^ step) for i in range(size)])]
    reshape x6 -> x3, local copies, waits for them, and re-layouts: 6.04 us -> 2.22 us  [the longest x1 1.34 us: planes_of(): part = part.reshape(count, ch, planes, flat // count)]
    unnamed x72 -> x47, local copies, waits for them, and re-layouts: 12.7 us -> 9.43 us
    dot_general x5 -> x3, matrix products: 7.6 us -> 5.1 us  [the longest x1 2.5 us: body(): lax.dot_general(mg_all, vol_all.reshape(nf * ch, planes * cells), (((1,),...]
    dynamic_update_slice x45 -> x23, local copies, waits for them, and re-layouts: 7.15 us -> 6.86 us  [place(): out = lax.dynamic_update_index_in_dim(out, piece, shift ^ s, 0)]
  transfers between devices with their start and end apart: 74 -> 46, of which waited for: 38 -> 15; matrix products, arithmetic and copies ran while one was open for 12% -> 20% of each run, Pallas kernels for 1% -> 6%
where the time goes in v3:
time: 216 us
  starting transfers between devices  78.9 us (37%)
  waiting for transfers between devices  59.8 us (28%)
  local copies, waits for them, and re-layouts  37.6 us (17%)
  Pallas kernels  17.7 us (8%)
  other arithmetic  14.8 us (7%)
  matrix products  5.1 us (2%)
    ppermute x42, starting transfers between devices, swap(): return lax.ppermute(block, axis, [(i, i ^ step) for i in range(size)])  69.4 us
    ppermute x42, waiting for transfers between devices, swap(): return lax.ppermute(block, axis, [(i, i ^ step) for i in range(size)])  59.8 us
    pallas_call x5, Pallas kernels, call(): pl.pallas_call(kernel, out_shape=out_shape, in_specs=[pl.BlockSpec(memory...  17.7 us
    unnamed x47, local copies, waits for them, and re-layouts  9.43 us
    ppermute x2, starting transfers between devices, halo(): before = lax.ppermute(last, 'space', [(i, i + 1) for i in range(size - 1)])  6.93 us
    dynamic_update_slice x23, local copies, waits for them, and re-layouts, place(): out = lax.dynamic_update_index_in_dim(out, piece, shift ^ s, 0)  6.86 us
    slice x4, local copies, waits for them, and re-layouts, strips_of(): part = jnp.stack([field[:, p] for p in order], axis=1)  5.6 us
    transpose x4, local copies, waits for them, and re-layouts, planes_of(): part[:, :, order.index(p)].transpose(1, 0, 2).reshape(ch, flat)  4.87 us
  transfers between devices with their start and end apart: 46, of which 15 were waited for; matrix products, arithmetic and copies ran while one was open for 20% of the time, Pallas kernels for 6%

profile of v3, /device:TPU:0, one launch (start us, length us, event | category | flops | bytes accessed | tf_op | source)
XLA Modules:
  0.0 215.6 jit_solution(15479553461451931617)
XLA Ops:
  1.6 5.1 %collective-permute-start.9 = (bf16[128,256]{1,0:T(8,128)(2,1)S(1)}, bf16[128,256]{1,0:T(8,128)(2,1)S(1)}, u32[]{:S(2)}, u32[]{:S(2)}) collective-permute-start(bf16[128,256]{1,0:T(8,128)(2,1)S(1)} %constant_dynamic-slice_fusion), channel_id=1, source_target_pairs={{0,24},{4,28},{8,16},{12,20},{16,8},{20,12},{24,0},{28,4},{1,25},{... | collective-permute-start | bytes 196616 | tf_op jit(solution)/shard_map/ppermute | solution.py:18
  9.2 2.5 %fusion.35 = (bf16[128,1,1024]{2,1,0:T(2,128)(2,1)S(1)}, bf16[128,1,1024]{2,1,0:T(2,128)(2,1)S(1)}) fusion(bf16[128,4,1024]{2,1,0:T(4,128)(2,1)} %param.4), kind=kLoop, calls=%fused_computation.119 | loop fusion | bytes 1048576 | tf_op jit(solution)/shard_map/slice | solution.py:223
  19.7 2.1 collective-permute-start.3
  23.8 7.0 %collective-permute-done.10 = bf16[4,128,256]{2,1,0:T(8,128)(2,1)S(1)} collective-permute-done((bf16[4,128,256]{2,1,0:T(8,128)(2,1)S(1)}, bf16[4,128,256]{2,1,0:T(8,128)(2,1)S(1)}, u32[]{:S(2)}, u32[]{:S(2)}) %collective-permute-start.10) | collective-permute-done | bytes 262176 | tf_op jit(solution)/shard_map/ppermute | solution.py:18
  44.1 2.8 %collective-permute-start.6 = (bf16[128,512]{1,0:T(8,128)(2,1)S(1)}, bf16[128,512]{1,0:T(8,128)(2,1)S(1)}, u32[]{:S(2)}, u32[]{:S(2)}) collective-permute-start(bf16[128,512]{1,0:T(8,128)(2,1)S(1)} %get-tuple-element.67), channel_id=1, source_target_pairs={{0,28},{4,24},{8,20},{12,16},{16,12},{20,8},{24,4},{28,0},{1,29},{... | collective-permute-start | bytes 393224 | tf_op jit(solution)/shard_map/ppermute | solution.py:18
  54.2 4.2 %collective-permute-start.14 = (bf16[512,128]{1,0:T(8,128)(2,1)S(1)}, bf16[512,128]{1,0:T(8,128)(2,1)S(1)}, u32[]{:S(2)}, u32[]{:S(2)}) collective-permute-start(bf16[512,128]{1,0:T(8,128)(2,1)S(1)} %get-tuple-element.61), channel_id=1, source_target_pairs={{0,8},{4,12},{8,0},{12,4},{16,24},{20,28},{24,16},{28,20},{1,9},{5... | collective-permute-start | bytes 393224 | tf_op jit(solution)/shard_map/ppermute | solution.py:18
  59.1 2.1 collective-permute-start.16
  62.5 2.4 %collective-permute-start.18 = (bf16[512,128]{1,0:T(8,128)(2,1)S(1)}, bf16[512,128]{1,0:T(8,128)(2,1)S(1)}, u32[]{:S(2)}, u32[]{:S(2)}) collective-permute-start(bf16[512,128]{1,0:T(8,128)(2,1)S(1)} %get-tuple-element.57), channel_id=1, source_target_pairs={{0,24},{4,28},{8,16},{12,20},{16,8},{20,12},{24,0},{28,4},{1,25},{... | collective-permute-start | bytes 393224 | tf_op jit(solution)/shard_map/ppermute | solution.py:18
  64.9 2.2 %collective-permute-start.19 = (bf16[512,128]{1,0:T(8,128)(2,1)S(1)}, bf16[512,128]{1,0:T(8,128)(2,1)S(1)}, u32[]{:S(2)}, u32[]{:S(2)}) collective-permute-start(bf16[512,128]{1,0:T(8,128)(2,1)S(1)} %get-tuple-element.56), channel_id=1, source_target_pairs={{0,28},{4,24},{8,20},{12,16},{16,12},{20,8},{24,4},{28,0},{1,29},{... | collective-permute-start | bytes 393224 | tf_op jit(solution)/shard_map/ppermute | solution.py:18
  68.3 9.1 %collective-permute-done.16 = bf16[512,128]{1,0:T(8,128)(2,1)S(1)} collective-permute-done((bf16[512,128]{1,0:T(8,128)(2,1)S(1)}, bf16[512,128]{1,0:T(8,128)(2,1)S(1)}, u32[]{:S(2)}, u32[]{:S(2)}) %collective-permute-start.16) | collective-permute-done | bytes 131104 | tf_op jit(solution)/shard_map/ppermute | solution.py:18
  77.4 2.8 %collective-permute-done.17 = bf16[512,128]{1,0:T(8,128)(2,1)S(1)} collective-permute-done((bf16[512,128]{1,0:T(8,128)(2,1)S(1)}, bf16[512,128]{1,0:T(8,128)(2,1)S(1)}, u32[]{:S(2)}, u32[]{:S(2)}) %collective-permute-start.17) | collective-permute-done | bytes 131104 | tf_op jit(solution)/shard_map/ppermute | solution.py:18
  83.1 3.9 %shard_map.76 = (bf16[8,256,128]{2,1,0:T(8,128)(2,1)S(1)}, bf16[8,128,256]{2,1,0:T(8,128)(2,1)S(1)}) custom-call(bf16[8,512,128]{2,1,0:T(8,128)(2,1)S(1)} %bitcast_dynamic-update-slice_fusion.14.m, f32[27,128]{1,0:T(8,128)S(1)} %bitcast.221, bf16[8,128,512]{2,1,0:T(8,128)(2,1)S(1)} %reshape.53.vol, bf16[8,128,512]{2,1,0:T(8,128)(2,1)S(1)} %reshape.56.up), custom_call_target="tpu_custom_call" | custom-call | flops 15728640 | bytes 4194304 | tf_op jit(solution)/shard_map/pallas_call | solution.py:197
  87.0 3.9 %shard_map.75 = (bf16[8,256,128]{2,1,0:T(8,128)(2,1)S(1)}, bf16[8,128,256]{2,1,0:T(8,128)(2,1)S(1)}) custom-call(bf16[8,512,128]{2,1,0:T(8,128)(2,1)S(1)} %bitcast_dynamic-update-slice_fusion.14.m, bf16[8,128,128]{2,1,0:T(8,128)(2,1)S(1)} %collective-permute-done.20.before, bf16[8,128,128]{2,1,0:T(8,128)(2,1)S(1)} %collective-permute-done.21.after, ...), custom_call_target="tpu_custom_call" | custom-call | flops 15728640 | bytes 4194304 | tf_op jit(solution)/shard_map/pallas_call | solution.py:197
  91.8 5.4 %collective-permute-start.22 = (bf16[8,128,128]{2,1,0:T(8,128)(2,1)}, bf16[8,128,128]{2,1,0:T(8,128)(2,1)S(1)}, u32[]{:S(2)}, u32[]{:S(2)}) collective-permute-start(bf16[8,128,128]{2,1,0:T(8,128)(2,1)} %get-tuple-element.78), channel_id=1, source_target_pairs={{0,1},{1,2},{2,3},{4,5},{5,6},{6,7},{8,9},{9,10},{10,11},{12,13},{... | collective-permute-start | bytes 786440 | tf_op jit(solution)/shard_map/ppermute | solution.py:83
  98.5 5.4 %shard_map.79 = f32[27,128]{1,0:T(8,128)S(1)} custom-call(bf16[8,512,128]{2,1,0:T(8,128)(2,1)S(1)} %bitcast_dynamic-update-slice_fusion.14.m, bf16[8,128,128]{2,1,0:T(8,128)(2,1)S(1)} %collective-permute-done.20.before, bf16[8,128,128]{2,1,0:T(8,128)(2,1)S(1)} %collective-permute-done.21.after, bf16[8,256,128]{2,1,0:T(8,128)(2,1)S(1)} %get-tuple-element.15.g0, ...), custom_call_target="tpu_custom_call" | custom-call | flops 31457280 | bytes 4194304 | tf_op jit(solution)/shard_map/pallas_call | solution.py:197
  107.5 2.8 %fusion.31 = (bf16[8,128,1,128]{3,2,1,0:T(2,128)(2,1)}, bf16[8,128,1,128]{3,2,1,0:T(2,128)(2,1)}, bf16[8,128,1,128]{3,2,1,0:T(2,128)(2,1)}, bf16[8,128,1,128]{3,2,1,0:T(2,128)(2,1)}) fusion(bf16[8,128,4,128]{3,2,1,0:T(4,128)(2,1)S(1)} %reshape.59), kind=kLoop, calls=%fused_computation.115 | loop fusion | bytes 2097152 | tf_op jit(solution)/shard_map/slice | solution.py:229
  115.2 2.2 %shard_map.78 = bf16[8,256,128]{2,1,0:T(8,128)(2,1)S(1)} custom-call(bf16[8,256,128]{2,1,0:T(8,128)(2,1)S(1)} %get-tuple-element.15.g0, bf16[8,256,128]{2,1,0:T(8,128)(2,1)S(1)} %get-tuple-element.16.g1, f32[27,128]{1,0:T(8,128)S(1)} %bitcast.223), custom_call_target="tpu_custom_call" | custom-call | flops 15728640 | bytes 4194304 | tf_op jit(solution)/shard_map/pallas_call | solution.py:197
  118.7 2.3 %shard_map.77 = bf16[8,256,128]{2,1,0:T(8,128)(2,1)S(1)} custom-call(bf16[8,256,128]{2,1,0:T(8,128)(2,1)S(1)} %get-tuple-element.15.g0, bf16[8,256,128]{2,1,0:T(8,128)(2,1)S(1)} %get-tuple-element.16.g1, bf16[8,128,128]{2,1,0:T(8,128)(2,1)S(1)} %collective-permute-done.22.before, bf16[8,128,128]{2,1,0:T(8,128)(2,1)S(1)} %collective-permute-done.23.after, ...), custom_call_target="tpu_custom_call" | custom-call | flops 15728640 | bytes 4194304 | tf_op jit(solution)/shard_map/pallas_call | solution.py:197
  123.4 4.6 %collective-permute-start.25 = (bf16[512,128]{1,0:T(8,128)(2,1)S(1)}, bf16[512,128]{1,0:T(8,128)(2,1)S(1)}, u32[]{:S(2)}, u32[]{:S(2)}) collective-permute-start(bf16[512,128]{1,0:T(8,128)(2,1)S(1)} %get-tuple-element.49), channel_id=1, source_target_pairs={{0,8},{4,12},{8,0},{12,4},{16,24},{20,28},{24,16},{28,20},{1,9},{5... | collective-permute-start | bytes 393224 | tf_op jit(solution)/shard_map/ppermute | solution.py:18
  128.0 2.2 %collective-permute-start.27 = (bf16[512,128]{1,0:T(8,128)(2,1)S(1)}, bf16[512,128]{1,0:T(8,128)(2,1)S(1)}, u32[]{:S(2)}, u32[]{:S(2)}) collective-permute-start(bf16[512,128]{1,0:T(8,128)(2,1)S(1)} %get-tuple-element.51), channel_id=1, source_target_pairs={{0,16},{4,20},{8,24},{12,28},{16,0},{20,4},{24,8},{28,12},{1,17},{... | collective-permute-start | bytes 393224 | tf_op jit(solution)/shard_map/ppermute | solution.py:18
  133.5 3.3 %collective-permute-done.25 = bf16[512,128]{1,0:T(8,128)(2,1)S(1)} collective-permute-done((bf16[512,128]{1,0:T(8,128)(2,1)S(1)}, bf16[512,128]{1,0:T(8,128)(2,1)S(1)}, u32[]{:S(2)}, u32[]{:S(2)}) %collective-permute-start.25) | collective-permute-done | bytes 131104 | tf_op jit(solution)/shard_map/ppermute | solution.py:18
  138.0 12.1 %collective-permute-done.28 = bf16[512,128]{1,0:T(8,128)(2,1)S(1)} collective-permute-done((bf16[512,128]{1,0:T(8,128)(2,1)S(1)}, bf16[512,128]{1,0:T(8,128)(2,1)S(1)}, u32[]{:S(2)}, u32[]{:S(2)}) %collective-permute-start.28) | collective-permute-done | bytes 131104 | tf_op jit(solution)/shard_map/ppermute | solution.py:18
  151.5 2.5 %convolution_multiply_fusion = f32[1024,1024]{1,0:T(8,128)S(1)} fusion(bf16[1024,512]{1,0:T(8,128)(2,1)} %bitcast.234, bf16[1024,512]{1,0:T(8,128)(2,1)S(1)} %bitcast.233), kind=kOutput, calls=%fused_computation | convolution fusion | flops 1074790400 | bytes 6291456 | tf_op jit(solution)/shard_map/dot_general | solution.py:322
  165.5 4.9 %collective-permute-start.34 = (bf16[128,512]{1,0:T(8,128)(2,1)}, bf16[128,512]{1,0:T(8,128)(2,1)S(1)}, u32[]{:S(2)}, u32[]{:S(2)}) collective-permute-start(bf16[128,512]{1,0:T(8,128)(2,1)} %get-tuple-element.39), channel_id=1, source_target_pairs={{0,8},{4,12},{8,0},{12,4},{16,24},{20,28},{24,16},{28,20},{1,9},{5... | collective-permute-start | bytes 393224 | tf_op jit(solution)/shard_map/ppermute | solution.py:18
  171.3 2.1 collective-permute-start.36
  175.2 3.6 %collective-permute-start.38 = (bf16[128,512]{1,0:T(8,128)(2,1)}, bf16[128,512]{1,0:T(8,128)(2,1)S(1)}, u32[]{:S(2)}, u32[]{:S(2)}) collective-permute-start(bf16[128,512]{1,0:T(8,128)(2,1)} %get-tuple-element.35), channel_id=1, source_target_pairs={{0,24},{4,28},{8,16},{12,20},{16,8},{20,12},{24,0},{28,4},{1,25},{... | collective-permute-start | bytes 393224 | tf_op jit(solution)/shard_map/ppermute | solution.py:18
  178.8 2.6 %collective-permute-done.35 = bf16[128,512]{1,0:T(8,128)(2,1)S(1)} collective-permute-done((bf16[128,512]{1,0:T(8,128)(2,1)}, bf16[128,512]{1,0:T(8,128)(2,1)S(1)}, u32[]{:S(2)}, u32[]{:S(2)}) %collective-permute-start.35) | collective-permute-done | bytes 131104 | tf_op jit(solution)/shard_map/ppermute | solution.py:18
  185.5 4.5 %collective-permute-done.36 = bf16[128,512]{1,0:T(8,128)(2,1)S(1)} collective-permute-done((bf16[128,512]{1,0:T(8,128)(2,1)}, bf16[128,512]{1,0:T(8,128)(2,1)S(1)}, u32[]{:S(2)}, u32[]{:S(2)}) %collective-permute-start.36) | collective-permute-done | bytes 131104 | tf_op jit(solution)/shard_map/ppermute | solution.py:18
  190.0 2.4 %collective-permute-done.37 = bf16[128,512]{1,0:T(8,128)(2,1)S(1)} collective-permute-done((bf16[128,512]{1,0:T(8,128)(2,1)}, bf16[128,512]{1,0:T(8,128)(2,1)S(1)}, u32[]{:S(2)}, u32[]{:S(2)}) %collective-permute-start.37) | collective-permute-done | bytes 131104 | tf_op jit(solution)/shard_map/ppermute | solution.py:18
  192.5 4.6 %collective-permute-done.41 = bf16[1024,256]{1,0:T(8,128)(2,1)S(1)} collective-permute-done((bf16[1024,256]{1,0:T(8,128)(2,1)S(1)}, bf16[1024,256]{1,0:T(8,128)(2,1)S(1)}, u32[]{:S(2)}, u32[]{:S(2)}) %collective-permute-start.41) | collective-permute-done | bytes 524320 | tf_op jit(solution)/shard_map/ppermute | solution.py:18
  201.8 4.5 %collective-permute-done.42 = bf16[4,128,256]{2,1,0:T(8,128)(2,1)} collective-permute-done((bf16[4,128,256]{2,1,0:T(8,128)(2,1)}, bf16[4,128,256]{2,1,0:T(8,128)(2,1)}, u32[]{:S(2)}, u32[]{:S(2)}) %collective-permute-start.42) | collective-permute-done | bytes 262176 | tf_op jit(solution)/shard_map/ppermute | solution.py:18
  209.2 2.6 %collective-permute-start.43 = (bf16[128,256]{1,0:T(8,128)(2,1)S(1)}, bf16[128,256]{1,0:T(8,128)(2,1)S(1)}, u32[]{:S(2)}, u32[]{:S(2)}) collective-permute-start(bf16[128,256]{1,0:T(8,128)(2,1)S(1)} %get-tuple-element.79), channel_id=1, source_target_pairs={{0,8},{4,12},{8,0},{12,4},{16,24},{20,28},{24,16},{28,20},{1,9},{5... | collective-permute-start | bytes 196616 | tf_op jit(solution)/shard_map/ppermute | solution.py:18
  (185 shorter events, 89.1 us)
Async XLA Ops:
  1.6 16.9 %collective-permute-start.9 = (bf16[128,256]{1,0:T(8,128)(2,1)S(1)}, bf16[128,256]{1,0:T(8,128)(2,1)S(1)}, u32[]{:S(2)}, u32[]{:S(2)}) collective-permute-start(bf16[128,256]{1,0:T(8,128)(2,1)S(1)} %constant_dynamic-slice_fusion), channel_id=1, source_target_pairs={{0,24},{4,28},{8,16},{12,20},{16,8},{20,12},{24,0},{28,4},{1,25},{... | collective-permute-start | bytes 196616 | tf_op jit(solution)/shard_map/ppermute | solution.py:18
  6.7 13.0 %collective-permute-start.8 = (bf16[128,256]{1,0:T(8,128)(2,1)S(1)}, bf16[128,256]{1,0:T(8,128)(2,1)S(1)}, u32[]{:S(2)}, u32[]{:S(2)}) collective-permute-start(bf16[128,256]{1,0:T(8,128)(2,1)S(1)} %constant_dynamic-slice_fusion), channel_id=1, source_target_pairs={{0,16},{4,20},{8,24},{12,28},{16,0},{20,4},{24,8},{28,12},{1,17},{... | collective-permute-start | bytes 196616 | tf_op jit(solution)/shard_map/ppermute | solution.py:18
  6.7 15.1 %collective-permute-start.7 = (bf16[128,256]{1,0:T(8,128)(2,1)S(1)}, bf16[128,256]{1,0:T(8,128)(2,1)S(1)}, u32[]{:S(2)}, u32[]{:S(2)}) collective-permute-start(bf16[128,256]{1,0:T(8,128)(2,1)S(1)} %constant_dynamic-slice_fusion), channel_id=1, source_target_pairs={{0,8},{4,12},{8,0},{12,4},{16,24},{20,28},{24,16},{28,20},{1,9},{5... | collective-permute-start | bytes 196616 | tf_op jit(solution)/shard_map/ppermute | solution.py:18
  15.0 20.4 %collective-permute-start = (bf16[128,512]{1,0:T(8,128)(2,1)}, bf16[128,512]{1,0:T(8,128)(2,1)}, u32[]{:S(2)}, u32[]{:S(2)}) collective-permute-start(bf16[128,512]{1,0:T(8,128)(2,1)} %get-tuple-element.73), channel_id=1, source_target_pairs={{0,4},{4,0},{8,12},{12,8},{16,20},{20,16},{24,28},{28,24},{1,5},{5... | collective-permute-start | bytes 393224 | tf_op jit(solution)/shard_map/ppermute | solution.py:18
  16.6 22.0 %collective-permute-start.1 = (bf16[128,512]{1,0:T(8,128)(2,1)}, bf16[128,512]{1,0:T(8,128)(2,1)}, u32[]{:S(2)}, u32[]{:S(2)}) collective-permute-start(bf16[128,512]{1,0:T(8,128)(2,1)} %get-tuple-element.72), channel_id=1, source_target_pairs={{0,8},{4,12},{8,0},{12,4},{16,24},{20,28},{24,16},{28,20},{1,9},{5... | collective-permute-start | bytes 393224 | tf_op jit(solution)/shard_map/ppermute | solution.py:18
  18.5 29.8 %collective-permute-start.2 = (bf16[128,512]{1,0:T(8,128)(2,1)}, bf16[128,512]{1,0:T(8,128)(2,1)}, u32[]{:S(2)}, u32[]{:S(2)}) collective-permute-start(bf16[128,512]{1,0:T(8,128)(2,1)} %get-tuple-element.71), channel_id=1, source_target_pairs={{0,12},{4,8},{8,4},{12,0},{16,28},{20,24},{24,20},{28,16},{1,13},{... | collective-permute-start | bytes 393224 | tf_op jit(solution)/shard_map/ppermute | solution.py:18
  19.7 29.6 %collective-permute-start.3 = (bf16[128,512]{1,0:T(8,128)(2,1)}, bf16[128,512]{1,0:T(8,128)(2,1)}, u32[]{:S(2)}, u32[]{:S(2)}) collective-permute-start(bf16[128,512]{1,0:T(8,128)(2,1)} %get-tuple-element.70), channel_id=1, source_target_pairs={{0,16},{4,20},{8,24},{12,28},{16,0},{20,4},{24,8},{28,12},{1,17},{... | collective-permute-start | bytes 393224 | tf_op jit(solution)/shard_map/ppermute | solution.py:18
  31.6 12.6 %collective-permute-start.11 = (bf16[1024,256]{1,0:T(8,128)(2,1)}, bf16[1024,256]{1,0:T(8,128)(2,1)}, u32[]{:S(2)}, u32[]{:S(2)}) collective-permute-start(bf16[1024,256]{1,0:T(8,128)(2,1)} %bitcast.25), channel_id=1, source_target_pairs={{0,2},{1,3},{2,0},{3,1},{4,6},{5,7},{6,4},{7,5},{8,10},{9,11},{10,... | collective-permute-start | bytes 1572872 | tf_op jit(solution)/shard_map/ppermute | solution.py:18
  35.4 14.9 %collective-permute-start.4 = (bf16[128,512]{1,0:T(8,128)(2,1)}, bf16[128,512]{1,0:T(8,128)(2,1)S(1)}, u32[]{:S(2)}, u32[]{:S(2)}) collective-permute-start(bf16[128,512]{1,0:T(8,128)(2,1)} %get-tuple-element.69), channel_id=1, source_target_pairs={{0,20},{4,16},{8,28},{12,24},{16,4},{20,0},{24,12},{28,8},{1,21},{... | collective-permute-start | bytes 393224 | tf_op jit(solution)/shard_map/ppermute | solution.py:18
  38.6 11.7 %collective-permute-start.5 = (bf16[128,512]{1,0:T(8,128)(2,1)}, bf16[128,512]{1,0:T(8,128)(2,1)S(1)}, u32[]{:S(2)}, u32[]{:S(2)}) collective-permute-start(bf16[128,512]{1,0:T(8,128)(2,1)} %get-tuple-element.68), channel_id=1, source_target_pairs={{0,24},{4,28},{8,16},{12,20},{16,8},{20,12},{24,0},{28,4},{1,25},{... | collective-permute-start | bytes 393224 | tf_op jit(solution)/shard_map/ppermute | solution.py:18
  54.2 10.7 %collective-permute-start.14 = (bf16[512,128]{1,0:T(8,128)(2,1)S(1)}, bf16[512,128]{1,0:T(8,128)(2,1)S(1)}, u32[]{:S(2)}, u32[]{:S(2)}) collective-permute-start(bf16[512,128]{1,0:T(8,128)(2,1)S(1)} %get-tuple-element.61), channel_id=1, source_target_pairs={{0,8},{4,12},{8,0},{12,4},{16,24},{20,28},{24,16},{28,20},{1,9},{5... | collective-permute-start | bytes 393224 | tf_op jit(solution)/shard_map/ppermute | solution.py:18
  59.1 18.3 %collective-permute-start.16 = (bf16[512,128]{1,0:T(8,128)(2,1)S(1)}, bf16[512,128]{1,0:T(8,128)(2,1)S(1)}, u32[]{:S(2)}, u32[]{:S(2)}) collective-permute-start(bf16[512,128]{1,0:T(8,128)(2,1)S(1)} %get-tuple-element.59), channel_id=1, source_target_pairs={{0,16},{4,20},{8,24},{12,28},{16,0},{20,4},{24,8},{28,12},{1,17},{... | collective-permute-start | bytes 393224 | tf_op jit(solution)/shard_map/ppermute | solution.py:18
  61.2 19.0 %collective-permute-start.17 = (bf16[512,128]{1,0:T(8,128)(2,1)S(1)}, bf16[512,128]{1,0:T(8,128)(2,1)S(1)}, u32[]{:S(2)}, u32[]{:S(2)}) collective-permute-start(bf16[512,128]{1,0:T(8,128)(2,1)S(1)} %get-tuple-element.58), channel_id=1, source_target_pairs={{0,20},{4,16},{8,28},{12,24},{16,4},{20,0},{24,12},{28,8},{1,21},{... | collective-permute-start | bytes 393224 | tf_op jit(solution)/shard_map/ppermute | solution.py:18
  62.5 17.7 %collective-permute-start.18 = (bf16[512,128]{1,0:T(8,128)(2,1)S(1)}, bf16[512,128]{1,0:T(8,128)(2,1)S(1)}, u32[]{:S(2)}, u32[]{:S(2)}) collective-permute-start(bf16[512,128]{1,0:T(8,128)(2,1)S(1)} %get-tuple-element.57), channel_id=1, source_target_pairs={{0,24},{4,28},{8,16},{12,20},{16,8},{20,12},{24,0},{28,4},{1,25},{... | collective-permute-start | bytes 393224 | tf_op jit(solution)/shard_map/ppermute | solution.py:18
  64.9 15.3 %collective-permute-start.19 = (bf16[512,128]{1,0:T(8,128)(2,1)S(1)}, bf16[512,128]{1,0:T(8,128)(2,1)S(1)}, u32[]{:S(2)}, u32[]{:S(2)}) collective-permute-start(bf16[512,128]{1,0:T(8,128)(2,1)S(1)} %get-tuple-element.56), channel_id=1, source_target_pairs={{0,28},{4,24},{8,20},{12,16},{16,12},{20,8},{24,4},{28,0},{1,29},{... | collective-permute-start | bytes 393224 | tf_op jit(solution)/shard_map/ppermute | solution.py:18
  91.8 26.9 %collective-permute-start.22 = (bf16[8,128,128]{2,1,0:T(8,128)(2,1)}, bf16[8,128,128]{2,1,0:T(8,128)(2,1)S(1)}, u32[]{:S(2)}, u32[]{:S(2)}) collective-permute-start(bf16[8,128,128]{2,1,0:T(8,128)(2,1)} %get-tuple-element.78), channel_id=1, source_target_pairs={{0,1},{1,2},{2,3},{4,5},{5,6},{6,7},{8,9},{9,10},{10,11},{12,13},{... | collective-permute-start | bytes 786440 | tf_op jit(solution)/shard_map/ppermute | solution.py:83
  97.2 21.5 %collective-permute-start.23 = (bf16[8,128,128]{2,1,0:T(8,128)(2,1)}, bf16[8,128,128]{2,1,0:T(8,128)(2,1)S(1)}, u32[]{:S(2)}, u32[]{:S(2)}) collective-permute-start(bf16[8,128,128]{2,1,0:T(8,128)(2,1)} %get-tuple-element.77), channel_id=1, source_target_pairs={{1,0},{2,1},{3,2},{5,4},{6,5},{7,6},{9,8},{10,9},{11,10},{13,12},{... | collective-permute-start | bytes 786440 | tf_op jit(solution)/shard_map/ppermute | solution.py:84
  103.9 13.6 %collective-permute-start.31 = (f32[27,128]{1,0:T(8,128)S(1)}, f32[27,128]{1,0:T(8,128)S(1)}, u32[]{:S(2)}, u32[]{:S(2)}) collective-permute-start(f32[27,128]{1,0:T(8,128)S(1)} %shard_map.79), channel_id=1, source_target_pairs={{0,1},{1,0},{2,3},{3,2},{4,5},{5,4},{6,7},{7,6},{8,9},{9,8},{10,11... | collective-permute-start | bytes 41480 | tf_op jit(solution)/shard_map/ppermute | solution.py:18
  121.1 10.8 %collective-permute-start.24 = (bf16[512,128]{1,0:T(8,128)(2,1)S(1)}, bf16[512,128]{1,0:T(8,128)(2,1)S(1)}, u32[]{:S(2)}, u32[]{:S(2)}) collective-permute-start(bf16[512,128]{1,0:T(8,128)(2,1)S(1)} %get-tuple-element.48), channel_id=1, source_target_pairs={{0,4},{4,0},{8,12},{12,8},{16,20},{20,16},{24,28},{28,24},{1,5},{5... | collective-permute-start | bytes 393224 | tf_op jit(solution)/shard_map/ppermute | solution.py:18
  123.4 13.4 %collective-permute-start.25 = (bf16[512,128]{1,0:T(8,128)(2,1)S(1)}, bf16[512,128]{1,0:T(8,128)(2,1)S(1)}, u32[]{:S(2)}, u32[]{:S(2)}) collective-permute-start(bf16[512,128]{1,0:T(8,128)(2,1)S(1)} %get-tuple-element.49), channel_id=1, source_target_pairs={{0,8},{4,12},{8,0},{12,4},{16,24},{20,28},{24,16},{28,20},{1,9},{5... | collective-permute-start | bytes 393224 | tf_op jit(solution)/shard_map/ppermute | solution.py:18
  128.0 10.0 %collective-permute-start.27 = (bf16[512,128]{1,0:T(8,128)(2,1)S(1)}, bf16[512,128]{1,0:T(8,128)(2,1)S(1)}, u32[]{:S(2)}, u32[]{:S(2)}) collective-permute-start(bf16[512,128]{1,0:T(8,128)(2,1)S(1)} %get-tuple-element.51), channel_id=1, source_target_pairs={{0,16},{4,20},{8,24},{12,28},{16,0},{20,4},{24,8},{28,12},{1,17},{... | collective-permute-start | bytes 393224 | tf_op jit(solution)/shard_map/ppermute | solution.py:18
  130.3 19.8 %collective-permute-start.28 = (bf16[512,128]{1,0:T(8,128)(2,1)S(1)}, bf16[512,128]{1,0:T(8,128)(2,1)S(1)}, u32[]{:S(2)}, u32[]{:S(2)}) collective-permute-start(bf16[512,128]{1,0:T(8,128)(2,1)S(1)} %get-tuple-element.53), channel_id=1, source_target_pairs={{0,20},{4,16},{8,28},{12,24},{16,4},{20,0},{24,12},{28,8},{1,21},{... | collective-permute-start | bytes 393224 | tf_op jit(solution)/shard_map/ppermute | solution.py:18
  132.0 18.2 %collective-permute-start.29 = (bf16[512,128]{1,0:T(8,128)(2,1)S(1)}, bf16[512,128]{1,0:T(8,128)(2,1)S(1)}, u32[]{:S(2)}, u32[]{:S(2)}) collective-permute-start(bf16[512,128]{1,0:T(8,128)(2,1)S(1)} %get-tuple-element.52), channel_id=1, source_target_pairs={{0,24},{4,28},{8,16},{12,20},{16,8},{20,12},{24,0},{28,4},{1,25},{... | collective-permute-start | bytes 393224 | tf_op jit(solution)/shard_map/ppermute | solution.py:18
  136.8 13.3 %collective-permute-start.30 = (bf16[512,128]{1,0:T(8,128)(2,1)S(1)}, bf16[512,128]{1,0:T(8,128)(2,1)S(1)}, u32[]{:S(2)}, u32[]{:S(2)}) collective-permute-start(bf16[512,128]{1,0:T(8,128)(2,1)S(1)} %get-tuple-element.46), channel_id=1, source_target_pairs={{0,28},{4,24},{8,20},{12,16},{16,12},{20,8},{24,4},{28,0},{1,29},{... | collective-permute-start | bytes 393224 | tf_op jit(solution)/shard_map/ppermute | solution.py:18
  158.0 25.3 %collective-permute-start.40 = (f32[1024,512]{1,0:T(8,128)}, f32[1024,512]{1,0:T(8,128)}, u32[]{:S(2)}, u32[]{:S(2)}) collective-permute-start(f32[1024,512]{1,0:T(8,128)} %pad_maximum_fusion.1), channel_id=1, source_target_pairs={{0,1},{1,0},{2,3},{3,2},{4,5},{5,4},{6,7},{7,6},{8,9},{9,8},{10,11... | collective-permute-start | bytes 6291464 | tf_op jit(solution)/shard_map/ppermute | solution.py:18
  162.2 11.3 %collective-permute-start.33 = (bf16[128,512]{1,0:T(8,128)(2,1)}, bf16[128,512]{1,0:T(8,128)(2,1)}, u32[]{:S(2)}, u32[]{:S(2)}) collective-permute-start(bf16[128,512]{1,0:T(8,128)(2,1)} %get-tuple-element.40), channel_id=1, source_target_pairs={{0,4},{4,0},{8,12},{12,8},{16,20},{20,16},{24,28},{28,24},{1,5},{5... | collective-permute-start | bytes 393224 | tf_op jit(solution)/shard_map/ppermute | solution.py:18
  170.4 11.0 %collective-permute-start.35 = (bf16[128,512]{1,0:T(8,128)(2,1)}, bf16[128,512]{1,0:T(8,128)(2,1)S(1)}, u32[]{:S(2)}, u32[]{:S(2)}) collective-permute-start(bf16[128,512]{1,0:T(8,128)(2,1)} %get-tuple-element.38), channel_id=1, source_target_pairs={{0,12},{4,8},{8,4},{12,0},{16,28},{20,24},{24,20},{28,16},{1,13},{... | collective-permute-start | bytes 393224 | tf_op jit(solution)/shard_map/ppermute | solution.py:18
  171.3 18.7 %collective-permute-start.36 = (bf16[128,512]{1,0:T(8,128)(2,1)}, bf16[128,512]{1,0:T(8,128)(2,1)S(1)}, u32[]{:S(2)}, u32[]{:S(2)}) collective-permute-start(bf16[128,512]{1,0:T(8,128)(2,1)} %get-tuple-element.37), channel_id=1, source_target_pairs={{0,16},{4,20},{8,24},{12,28},{16,0},{20,4},{24,8},{28,12},{1,17},{... | collective-permute-start | bytes 393224 | tf_op jit(solution)/shard_map/ppermute | solution.py:18
  173.5 18.9 %collective-permute-start.37 = (bf16[128,512]{1,0:T(8,128)(2,1)}, bf16[128,512]{1,0:T(8,128)(2,1)S(1)}, u32[]{:S(2)}, u32[]{:S(2)}) collective-permute-start(bf16[128,512]{1,0:T(8,128)(2,1)} %get-tuple-element.36), channel_id=1, source_target_pairs={{0,20},{4,16},{8,28},{12,24},{16,4},{20,0},{24,12},{28,8},{1,21},{... | collective-permute-start | bytes 393224 | tf_op jit(solution)/shard_map/ppermute | solution.py:18
  175.2 17.2 %collective-permute-start.38 = (bf16[128,512]{1,0:T(8,128)(2,1)}, bf16[128,512]{1,0:T(8,128)(2,1)S(1)}, u32[]{:S(2)}, u32[]{:S(2)}) collective-permute-start(bf16[128,512]{1,0:T(8,128)(2,1)} %get-tuple-element.35), channel_id=1, source_target_pairs={{0,24},{4,28},{8,16},{12,20},{16,8},{20,12},{24,0},{28,4},{1,25},{... | collective-permute-start | bytes 393224 | tf_op jit(solution)/shard_map/ppermute | solution.py:18
  181.4 19.6 %collective-permute-start.39 = (bf16[128,512]{1,0:T(8,128)(2,1)S(1)}, bf16[128,512]{1,0:T(8,128)(2,1)S(1)}, u32[]{:S(2)}, u32[]{:S(2)}) collective-permute-start(bf16[128,512]{1,0:T(8,128)(2,1)S(1)} %get-tuple-element.34), channel_id=1, source_target_pairs={{0,28},{4,24},{8,20},{12,16},{16,12},{20,8},{24,4},{28,0},{1,29},{... | collective-permute-start | bytes 393224 | tf_op jit(solution)/shard_map/ppermute | solution.py:18
  184.9 12.2 %collective-permute-start.41 = (bf16[1024,256]{1,0:T(8,128)(2,1)S(1)}, bf16[1024,256]{1,0:T(8,128)(2,1)S(1)}, u32[]{:S(2)}, u32[]{:S(2)}) collective-permute-start(bf16[1024,256]{1,0:T(8,128)(2,1)S(1)} %fusion), channel_id=1, source_target_pairs={{0,2},{1,3},{2,0},{3,1},{4,6},{5,7},{6,4},{7,5},{8,10},{9,11},{10,... | collective-permute-start | bytes 1572872 | tf_op jit(solution)/shard_map/ppermute | solution.py:18
  (33 other events, 197.2 us)

commit v4 on v3

v4 whole, which is shorter than its diff:
```python
import functools
import math

import jax
import jax.numpy as jnp
from jax import lax
from jax.experimental import pallas as pl
from jax.experimental.pallas import tpu as pltpu
from jax.sharding import PartitionSpec as P

WW = 64
BF = jnp.bfloat16
F32 = jnp.float32


def swap(block, axis, step):
    size = lax.axis_size(axis)
    return lax.ppermute(block, axis, [(i, i ^ step) for i in range(size)])


def exchange(pieces, axis):
    size = len(pieces)
    order = list(range(size // 2, size)) + list(range(1, size // 2))
    got = {0: pieces[0]}
    for s in order:
        got[s] = swap(pieces[s], axis, s)
    return [got[s] for s in range(size)]


def place(pieces, shift):
    out = jnp.zeros((len(pieces),) + pieces[0].shape, pieces[0].dtype)
    for s, piece in enumerate(pieces):
        out = lax.dynamic_update_index_in_dim(out, piece, shift ^ s, 0)
    return out


def pick(blocks, index):
    return lax.dynamic_index_in_dim(blocks, index, 0, keepdims=False)


def gather_weights(mixing, me_space, after):
    rows, cols = mixing.shape
    nf, ns = lax.axis_size("filter"), lax.axis_size("space")
    share = cols // ns
    own = lax.dynamic_slice_in_dim(mixing, me_space * share, share, axis=1)
    even = jnp.stack([own] + [swap(own, "filter", s) for s in range(2, nf, 2)])
    even, _ = lax.optimization_barrier((even, after))
    odd = swap(even, "filter", 1)
    part = jnp.stack([even, odd], axis=1).reshape(nf * rows, share)
    held = jnp.stack([part] + [swap(part, "space", s) for s in range(2, ns, 2)])
    return held, swap(held, "space", 1)


def scatter_rest(half, rows):
    nf, ns = lax.axis_size("filter"), lax.axis_size("space")
    share = 2 * half.shape[1] // ns
    half = [half[:, k * share : (k + 1) * share] for k in range(ns // 2)]
    total = half[0]
    for k in range(1, ns // 2):
        total = total + swap(half[k].astype(BF), "space", 2 * k).astype(F32)
    total = total.reshape(nf // 2, 2, rows, share)
    near = total[:, 0] + swap(total[:, 1].astype(BF), "filter", 1).astype(F32)
    result = near[0]
    for k in range(1, nf // 2):
        result = result + swap(near[k].astype(BF), "filter", 2 * k).astype(F32)
    return result


def halo(first, last):
    size = lax.axis_size("space")
    before = lax.ppermute(last, "space", [(i, i + 1) for i in range(size - 1)])
    after = lax.ppermute(first, "space", [(i + 1, i) for i in range(size - 1)])
    return before, after


def fill(pad_ref, plane, source):
    rows, width, ch = pad_ref.shape[1] - 2, pad_ref.shape[2], pad_ref.shape[3]
    pad_ref[plane, 1 : rows + 1] = source.astype(F32).reshape(rows, width, ch)
    pad_ref[plane, 0] = jnp.zeros((width, ch), F32)
    pad_ref[plane, rows + 1] = jnp.zeros((width, ch), F32)


def shifted(value, up):
    width = value.shape[0]
    index = lax.broadcasted_iota(jnp.int32, value.shape, 0)
    if up:
        return jnp.where(index == width - 1, 0.0, pltpu.roll(value, width - 1, 0))
    return jnp.where(index == 0, 0.0, pltpu.roll(value, 1, 0))


def conv_row(pad_ref, taps_ref, plane, row, flip):
    sums = [None, None, None]
    for a in range(3):
        for b in range(3):
            da, db = (1 - a, 1 - b) if flip else (a - 1, b - 1)
            line = pad_ref[plane + da, row + db]
            for e in range(3):
                term = taps_ref[pl.ds(a * 9 + b * 3 + e, 1), :] * line
                sums[e] = term if sums[e] is None else sums[e] + term
    lo, hi = (sums[2], sums[0]) if flip else (sums[0], sums[2])
    return sums[1] + shifted(lo, False) + shifted(hi, True)


def load_planes(pad_ref, refs, where, sides, wanted, planes):
    for p in sorted(wanted):
        if p < 0:
            fill(pad_ref, 0, sides[0][...])
        elif p >= planes:
            fill(pad_ref, planes + 1, sides[1][...])
        else:
            which, at = where[p]
            fill(pad_ref, p + 1, refs[which][at])


def forward_kernel(group, planes, m, before, after, taps, vol, up, grad, out, pad):
    wanted = {p + a for p in group for a in (-1, 0, 1)}
    where = {p: (0, p) for p in range(planes)}
    load_planes(pad, (m,), where, (before, after), wanted, planes)
    lanes, flat = 2 * WW, m.shape[1]
    for k, p in enumerate(group):

        def strip(f, carry, k=k, p=p):
            lines = [conv_row(pad, taps, p + 1, f * 2 + 1 + r, False) for r in range(2)]
            spatial = jnp.concatenate(lines, axis=0)
            sig = 1.0 / (1.0 + jnp.exp(-spatial))
            cells = pl.ds(pl.multiple_of(f * lanes, lanes), lanes)
            source = pl.ds(pl.multiple_of(p * flat + f * lanes, lanes), lanes)
            target = pl.ds(pl.multiple_of(k * flat + f * lanes, lanes), lanes)
            cot = jnp.transpose(up[:, source].astype(F32))
            slope = sig * (1.0 + spatial * (1.0 - sig))
            grad[k, cells, :] = (cot * slope).astype(BF)
            silu = jnp.transpose(spatial * sig)
            out[:, target] = (vol[:, source].astype(F32) + silu).astype(BF)
            return carry

        lax.fori_loop(0, flat // lanes, strip, 0)


def middle_forward_kernel(group, planes, m, taps, vol, up, grad, out, pad):
    forward_kernel(group, planes, m, None, None, taps, vol, up, grad, out, pad)


def backward_kernel(group, where, planes, g0, g1, before, after, taps, out, pad):
    wanted = {p + a for p in group for a in (-1, 0, 1)}
    load_planes(pad, (g0, g1), where, (before, after), wanted, planes)
    lanes, flat = 2 * WW, g0.shape[1]
    for k, p in enumerate(group):

        def strip(f, carry, k=k, p=p):
            lines = [conv_row(pad, taps, p + 1, f * 2 + 1 + r, True) for r in range(2)]
            cells = pl.ds(pl.multiple_of(f * lanes, lanes), lanes)
            out[k, cells, :] = jnp.concatenate(lines, axis=0).astype(BF)
            return carry

        lax.fori_loop(0, flat // lanes, strip, 0)


def middle_backward_kernel(group, where, planes, g0, g1, taps, out, pad):
    backward_kernel(group, where, planes, g0, g1, None, None, taps, out, pad)


def taps_kernel(where_grad, planes, norm, m, before, after, g0, g1, out, pad, gpad):
    where = {p: (0, p) for p in range(planes)}
    load_planes(pad, (m,), where, (before, after), range(-1, planes + 1), planes)
    load_planes(gpad, (g0, g1), where_grad, (), range(planes), planes)
    rows, width, ch = pad.shape[1] - 2, pad.shape[2], pad.shape[3]
    sums = tuple(jnp.zeros((8, ch), F32) for _ in range(27))

    def line(at, sums):
        p, h = at // rows, at % rows
        sums = list(sums)
        own = gpad[p + 1, h + 1]
        turned = (shifted(own, True), own, shifted(own, False))
        for a in range(3):
            for b in range(3):
                field = pad[p + a, h + b]
                for e in range(3):
                    prod = (turned[e] * field).reshape(width // 8, 8, ch)
                    sums[a * 9 + b * 3 + e] = sums[a * 9 + b * 3 + e] + jnp.sum(prod, axis=0)
        return tuple(sums)

    sums = lax.fori_loop(0, planes * rows, line, sums)
    for k in range(27):
        out[k : k + 1, :] = jnp.sum(sums[k], axis=0, keepdims=True) * norm


def call(kernel, out_shape, scratch, *args, ops=0):
    def place_of(arg):
        return pltpu.SMEM if arg.dtype == jnp.int32 else pltpu.VMEM

    return pl.pallas_call(
        kernel,
        out_shape=out_shape,
        in_specs=[pl.BlockSpec(memory_space=place_of(arg)) for arg in args],
        out_specs=jax.tree.map(lambda _: pl.BlockSpec(memory_space=pltpu.VMEM), out_shape),
        scratch_shapes=scratch,
        compiler_params=pltpu.CompilerParams(vmem_limit_bytes=40 * 1024 * 1024),
        cost_estimate=pl.CostEstimate(flops=ops, bytes_accessed=4 * 1024 * 1024, transcendentals=0),
    )(*args)


def mix_kernel(turn, *refs):
    nf = len(refs) - 4
    pieces, (held, other, vol_t, out) = refs[:nf], refs[nf:]
    ch = pieces[0].shape[0]
    share = held.shape[2]
    for t, piece in enumerate(pieces):
        lane = pl.ds(pl.multiple_of((turn[0] ^ t) * ch, 128), ch)
        vol_t[:, lane] = jnp.transpose(piece[...])
    for s in range(0, nf, 2):
        total = None
        for v in range(2 * held.shape[0]):
            block = (other if v % 2 else held)[v // 2, s * ch : (s + 2) * ch, :]
            term = lax.dot_general(
                vol_t[:, v * share : (v + 1) * share], block, (((1,), (1,)), ((), ())),
                preferred_element_type=F32,
            )
            total = term if total is None else total + term
        out[s] = total[:, :ch].astype(BF)
        out[s + 1] = total[:, ch:].astype(BF)


def mix(turn, pieces, held, other):
    nf, (ch, blk) = len(pieces), pieces[0].shape
    pairs, rows, share = held.shape
    if ch % 128:
        vol_t = place(pieces, turn[0]).reshape(nf * ch, blk).T
        weights = jnp.stack([held, other], axis=1).reshape(2 * pairs, rows, share)
        out = jnp.einsum(
            "cvi,voi->co", vol_t.reshape(blk, 2 * pairs, share), weights, preferred_element_type=F32
        )
        return vol_t, out.astype(BF).reshape(blk, nf, ch).transpose(1, 0, 2)
    shapes = (
        jax.ShapeDtypeStruct((blk, nf * ch), BF),
        jax.ShapeDtypeStruct((nf, blk, ch), BF),
    )
    return call(mix_kernel, shapes, [], turn, *pieces, held, other, ops=2 * blk * rows * rows)


def unmix_kernel(turn, mg, held, other, out):
    ch = out.shape[1]
    share = held.shape[2]
    for v in range(2 * held.shape[0]):
        block = (other if v % 2 else held)[v // 2]
        total = lax.dot_general(
            mg[...], block, (((1,), (0,)), ((), ())), preferred_element_type=F32
        )
        turned = jnp.transpose(total).astype(BF)
        for k in range(share // ch):
            out[(v * (share // ch) + k) ^ turn[0]] = turned[k * ch : (k + 1) * ch, :]


def unmix(turn, mg, held, other, ch):
    blk = mg.shape[0]
    pairs, rows, share = held.shape
    nf = rows // ch
    if ch % 128:
        weights = jnp.stack([held, other], axis=1).reshape(2 * pairs, rows, share)
        out = jnp.einsum("co,voi->vic", mg, weights, preferred_element_type=F32)
        out = out.astype(BF).reshape(nf, ch, blk)
        return jnp.stack([pick(out, turn[0] ^ s) for s in range(nf)])
    shape = jax.ShapeDtypeStruct((nf, ch, blk), BF)
    return call(unmix_kernel, shape, [], turn, mg, held, other, ops=2 * blk * rows * rows)


def weight_kernel(norm, mg, vol_t, mine, theirs):
    pairs = mine.shape[0]
    share = mine.shape[2]
    for v in range(2 * pairs):
        total = lax.dot_general(
            mg[...], vol_t[:, v * share : (v + 1) * share], (((0,), (0,)), ((), ())),
            preferred_element_type=F32,
        )
        if v % 2:
            theirs[v // 2] = (total * norm).astype(BF)
        else:
            mine[v // 2] = total * norm


def weight_products(mg, vol_t, norm, ns):
    rows = mg.shape[1]
    share = vol_t.shape[1] // ns
    shapes = (
        jax.ShapeDtypeStruct((ns // 2, rows, share), F32),
        jax.ShapeDtypeStruct((ns // 2, rows, share), BF),
    )
    if share % 128:
        part = lax.dot_general(mg, vol_t, (((0,), (0,)), ((), ())), preferred_element_type=F32)
        part = (part * norm).reshape(rows, ns // 2, 2, share).transpose(2, 1, 0, 3)
        return part[0], part[1].astype(BF)
    kernel = functools.partial(weight_kernel, norm)
    return call(kernel, shapes, [], mg, vol_t, ops=2 * mg.shape[0] * rows * rows)


def body(volume, mixing, kernel_taps, upstream):
    ch, planes, flat = volume.shape
    height = flat // WW
    nf, ns = lax.axis_size("filter"), lax.axis_size("space")
    me, me_space = lax.axis_index("filter"), lax.axis_index("space")
    total = planes * flat
    blk = total // nf
    norm = 1.0 / math.sqrt(ns * total)
    edges, middle = (0, planes - 1), tuple(range(1, planes - 1))
    groups = (edges, middle)
    turn = jnp.reshape(me ^ (me_space * (nf // ns)), (1,)).astype(jnp.int32)

    vol = volume.reshape(ch, total)
    send = [lax.dynamic_slice_in_dim(vol, (me ^ s) * blk, blk, axis=1) for s in range(nf)]
    pieces = exchange(send, "filter")
    held, other = gather_weights(mixing, me_space, send)
    up = upstream.reshape(ch, total)
    pieces, up, held, other = lax.optimization_barrier((pieces, up, held, other))
    vol_t, prod = mix(turn, pieces, held, other)

    got = exchange([prod[s] for s in range(nf)], "filter")
    mixed = place(got, me).reshape(planes, flat, ch)

    taps = kernel_taps.T
    before, after = halo(mixed[0], mixed[planes - 1])
    pad = pltpu.VMEM((planes + 2, height + 2, WW, ch), F32)
    conv_ops = 60 * flat * ch

    def forward(i):
        g = groups[i]
        shapes = (
            jax.ShapeDtypeStruct((len(g), flat, ch), BF),
            jax.ShapeDtypeStruct((ch, len(g) * flat), BF),
        )
        kernel = middle_forward_kernel if i else forward_kernel
        sides = () if i else (before, after)
        return call(
            functools.partial(kernel, g, planes), shapes, [pad], mixed, *sides, taps, vol, up,
            ops=conv_ops * len(g),
        )

    grad_middle, out_middle = forward(1)
    grad_edges, out_edges = forward(0)
    grad_before, grad_after = halo(grad_edges[0], grad_edges[1])
    where_grad = {p: (i, k) for i, g in enumerate(groups) for k, p in enumerate(g)}

    def backward(i):
        g = groups[i]
        shape = jax.ShapeDtypeStruct((len(g), flat, ch), BF)
        kernel = middle_backward_kernel if i else backward_kernel
        sides = () if i else (grad_before, grad_after)
        return call(
            functools.partial(kernel, g, where_grad, planes), shape, [pad],
            grad_edges, grad_middle, *sides, taps, ops=conv_ops * len(g),
        )

    mg_middle = backward(1)
    mg_edges = backward(0)
    mixed_grad = jnp.concatenate([mg_edges[:1], mg_middle, mg_edges[1:]], axis=0)
    mixed_grad = mixed_grad.reshape(nf, blk, ch)
    got = exchange([pick(mixed_grad, me ^ s) for s in range(nf)], "filter")

    late = lax.optimization_barrier((got[nf // 2], mixed, grad_edges, out_edges, out_middle))
    _, mixed, grad_edges, out_edges, out_middle = late
    taps_grad = call(
        functools.partial(taps_kernel, where_grad, planes, norm),
        jax.ShapeDtypeStruct((27, ch), F32), [pad, pad],
        mixed, before, after, grad_edges, grad_middle,
        ops=conv_ops * planes,
    )
    output = jnp.concatenate([out_edges[:, :flat], out_middle, out_edges[:, flat:]], axis=1)
    output = output.reshape(ch, planes, flat)
    got, taps_grad, output = lax.optimization_barrier((got, taps_grad, output))

    mg_all = jnp.concatenate(got, axis=1)
    mine, theirs = weight_products(mg_all, vol_t, norm, ns)
    mg_all, theirs = lax.optimization_barrier((mg_all, theirs))
    half = mine + swap(theirs, "space", 1).astype(F32)
    back = unmix(turn, mg_all, held, other, ch)
    back, half = lax.optimization_barrier((back, half))
    got = exchange([back[s] for s in range(nf)], "filter")
    back_own = jnp.zeros((ch, total), BF)
    for s, piece in enumerate(got):
        back_own = lax.dynamic_update_slice_in_dim(back_own, piece, (me ^ s) * blk, axis=1)
    back_own = back_own.reshape(ch, planes, flat)
    volume_grad = (upstream.astype(F32) + back_own.astype(F32)).astype(BF)

    half = half.transpose(1, 0, 2).reshape(nf * ch, -1)
    mixing_grad = scatter_rest(half, ch)
    step = 1
    while step < ns:
        taps_grad = taps_grad + swap(taps_grad, "space", step)
        step *= 2
    return (output, volume_grad, mixing_grad, taps_grad.T)


def solution(mesh):
    in_specs = (
        P("filter", "space", None),
        P("filter", None),
        P("filter", None),
        P("filter", "space", None),
    )
    out_specs = (
        P("filter", "space", None),
        P("filter", "space", None),
        P("filter", "space"),
        P("filter", None),
    )
    return jax.shard_map(body, mesh=mesh, in_specs=in_specs, out_specs=out_specs, check_vma=False)
```

time: 216 us -> 211 us (0.977)
  starting transfers between devices: 78.9 us -> 89.5 us
  other arithmetic: 14.8 us -> 5.98 us
  local copies, waits for them, and re-layouts: 37.6 us -> 30.1 us
  Pallas kernels: 17.7 us -> 24.7 us
  matrix products: 5.1 us -> 0 us
    ppermute x42, starting transfers between devices: 69.4 us -> 78.7 us  [swap(): return lax.ppermute(block, axis, [(i, i ^ step) for i in range(size)])]
    slice x10 -> x4, local copies, waits for them, and re-layouts: 9.8 us -> 1.4 us  [the longest x1 1.29 us: scatter_rest(): half = [half[:, k * share:(k + 1) * share] for k in range(ns // 2)]]
    pallas_call x5 -> x8, Pallas kernels: 17.7 us -> 24.7 us  [call(): pl.pallas_call(kernel, out_shape=out_shape, in_specs=[pl.BlockSpec(memory...]
    dynamic_update_slice x23 -> x7, local copies, waits for them, and re-layouts: 6.86 us -> 1.04 us  [place(): out = lax.dynamic_update_index_in_dim(out, piece, shift ^ s, 0)]
    dot_general x3 -> x0, matrix products: 5.1 us -> none  [the longest x1 2.5 us: body(): lax.dot_general(mg_all, vol_all.reshape(nf * ch, planes * cells), (((1,),...]
    ppermute x42, waiting for transfers between devices: 59.8 us -> 55.1 us  [swap(): return lax.ppermute(block, axis, [(i, i ^ step) for i in range(size)])]
    ppermute x2, waiting for transfers between devices: 0.01 us -> 3.85 us  [halo(): after = lax.ppermute(first, 'space', [(i + 1, i) for i in range(size - 1)])]
    unnamed x47 -> x63, local copies, waits for them, and re-layouts: 9.43 us -> 12.8 us
  transfers between devices with their start and end apart: 46 -> 46, of which waited for: 15 -> 16; matrix products, arithmetic and copies ran while one was open for 20% -> 8% of each run, Pallas kernels for 6% -> 7%
where the time goes in v4:
time: 211 us
  starting transfers between devices  89.5 us (42%)
  waiting for transfers between devices  58.9 us (28%)
  local copies, waits for them, and re-layouts  30.1 us (14%)
  Pallas kernels  24.7 us (12%)
  other arithmetic  5.98 us (3%)
    ppermute x42, starting transfers between devices, swap(): return lax.ppermute(block, axis, [(i, i ^ step) for i in range(size)])  78.7 us
    ppermute x42, waiting for transfers between devices, swap(): return lax.ppermute(block, axis, [(i, i ^ step) for i in range(size)])  55.1 us
    pallas_call x8, Pallas kernels, call(): pl.pallas_call(kernel, out_shape=out_shape, in_specs=[pl.BlockSpec(memory...  24.7 us
    unnamed x63, local copies, waits for them, and re-layouts  12.8 us
    ppermute x2, starting transfers between devices, halo(): before = lax.ppermute(last, 'space', [(i, i + 1) for i in range(size - 1)])  7.99 us
  transfers between devices with their start and end apart: 46, of which 16 were waited for; matrix products, arithmetic and copies ran while one was open for 8% of the time, Pallas kernels for 7%

profile of v4, /device:TPU:0, one launch (start us, length us, event | category | flops | bytes accessed | tf_op | source)
XLA Modules:
  0.0 210.7 jit_solution(16954997849944648694)
XLA Ops:
  1.6 3.1 %collective-permute-start.7 = (bf16[128,256]{1,0:T(8,128)(2,1)S(1)}, bf16[128,256]{1,0:T(8,128)(2,1)S(1)}, u32[]{:S(2)}, u32[]{:S(2)}) collective-permute-start(bf16[128,256]{1,0:T(8,128)(2,1)S(1)} %constant_dynamic-slice_fusion), channel_id=1, source_target_pairs={{0,8},{4,12},{8,0},{12,4},{16,24},{20,28},{24,16},{28,20},{1,9},{5... | collective-permute-start | bytes 196616 | tf_op jit(solution)/shard_map/ppermute | solution.py:18
  4.7 2.6 %collective-permute-start.8 = (bf16[128,256]{1,0:T(8,128)(2,1)S(1)}, bf16[128,256]{1,0:T(8,128)(2,1)S(1)}, u32[]{:S(2)}, u32[]{:S(2)}) collective-permute-start(bf16[128,256]{1,0:T(8,128)(2,1)S(1)} %constant_dynamic-slice_fusion), channel_id=1, source_target_pairs={{0,16},{4,20},{8,24},{12,28},{16,0},{20,4},{24,8},{28,12},{1,17},{... | collective-permute-start | bytes 196616 | tf_op jit(solution)/shard_map/ppermute | solution.py:18
  14.9 4.9 %collective-permute-done.10 = bf16[4,128,256]{2,1,0:T(8,128)(2,1)S(1)} collective-permute-done((bf16[4,128,256]{2,1,0:T(8,128)(2,1)S(1)}, bf16[4,128,256]{2,1,0:T(8,128)(2,1)S(1)}, u32[]{:S(2)}, u32[]{:S(2)}) %collective-permute-start.10) | collective-permute-done | bytes 262176 | tf_op jit(solution)/shard_map/ppermute | solution.py:18
  21.6 9.3 %collective-permute-done.11 = bf16[1024,256]{1,0:T(8,128)(2,1)S(1)} collective-permute-done((bf16[1024,256]{1,0:T(8,128)(2,1)S(1)}, bf16[1024,256]{1,0:T(8,128)(2,1)S(1)}, u32[]{:S(2)}, u32[]{:S(2)}) %collective-permute-start.11) | collective-permute-done | bytes 524320 | tf_op jit(solution)/shard_map/ppermute | solution.py:18
  34.6 2.7 %collective-permute-start.3 = (bf16[128,512]{1,0:T(8,128)(2,1)}, bf16[128,512]{1,0:T(8,128)(2,1)}, u32[]{:S(2)}, u32[]{:S(2)}) collective-permute-start(bf16[128,512]{1,0:T(8,128)(2,1)} %get-tuple-element.110), channel_id=1, source_target_pairs={{0,16},{4,20},{8,24},{12,28},{16,0},{20,4},{24,8},{28,12},{1,17},{... | collective-permute-start | bytes 393224 | tf_op jit(solution)/shard_map/ppermute | solution.py:18
  38.0 3.3 %collective-permute-start.4 = (bf16[128,512]{1,0:T(8,128)(2,1)}, bf16[128,512]{1,0:T(8,128)(2,1)}, u32[]{:S(2)}, u32[]{:S(2)}) collective-permute-start(bf16[128,512]{1,0:T(8,128)(2,1)} %get-tuple-element.109), channel_id=1, source_target_pairs={{0,20},{4,16},{8,28},{12,24},{16,4},{20,0},{24,12},{28,8},{1,21},{... | collective-permute-start | bytes 393224 | tf_op jit(solution)/shard_map/ppermute | solution.py:18
  42.4 3.1 %collective-permute-start.5 = (bf16[128,512]{1,0:T(8,128)(2,1)}, bf16[128,512]{1,0:T(8,128)(2,1)}, u32[]{:S(2)}, u32[]{:S(2)}) collective-permute-start(bf16[128,512]{1,0:T(8,128)(2,1)} %get-tuple-element.108), channel_id=1, source_target_pairs={{0,24},{4,28},{8,16},{12,20},{16,8},{20,12},{24,0},{28,4},{1,25},{... | collective-permute-start | bytes 393224 | tf_op jit(solution)/shard_map/ppermute | solution.py:18
  46.2 2.9 %collective-permute-start.6 = (bf16[128,512]{1,0:T(8,128)(2,1)}, bf16[128,512]{1,0:T(8,128)(2,1)}, u32[]{:S(2)}, u32[]{:S(2)}) collective-permute-start(bf16[128,512]{1,0:T(8,128)(2,1)} %get-tuple-element.107), channel_id=1, source_target_pairs={{0,28},{4,24},{8,20},{12,16},{16,12},{20,8},{24,4},{28,0},{1,29},{... | collective-permute-start | bytes 393224 | tf_op jit(solution)/shard_map/ppermute | solution.py:18
  50.8 6.4 %collective-permute-done.4.refs_5_ = bf16[128,512]{1,0:T(8,128)(2,1)} collective-permute-done((bf16[128,512]{1,0:T(8,128)(2,1)}, bf16[128,512]{1,0:T(8,128)(2,1)}, u32[]{:S(2)}, u32[]{:S(2)}) %collective-permute-start.4) | collective-permute-done | bytes 131104 | tf_op jit(solution)/shard_map/ppermute | solution.py:18
  59.9 3.1 %shard_map.75 = (bf16[512,1024]{1,0:T(8,128)(2,1)S(1)}, bf16[8,512,128]{2,1,0:T(8,128)(2,1)S(1)}) custom-call(s32[1]{0:T(128)} %bitcast.turn, bf16[128,512]{1,0:T(8,128)(2,1)S(1)} %get-tuple-element.43.refs_0_, bf16[128,512]{1,0:T(8,128)(2,1)S(1)} %copy-done.13, bf16[128,512]{1,0:T(8,128)(2,1)S(1)} %copy-done.15, bf16[128,512]{1,0:T(8,128)(2,1)S(1)} %copy-done.17, ...), custom_call_target="tpu_custom_call" | custom-call | flops 1073741824 | bytes 4194304 | tf_op jit(solution)/shard_map/pallas_call | solution.py:191
  65.7 5.1 %collective-permute-start.14 = (bf16[512,128]{1,0:T(8,128)(2,1)}, bf16[512,128]{1,0:T(8,128)(2,1)S(1)}, u32[]{:S(2)}, u32[]{:S(2)}) collective-permute-start(bf16[512,128]{1,0:T(8,128)(2,1)} %get-tuple-element.104), channel_id=1, source_target_pairs={{0,8},{4,12},{8,0},{12,4},{16,24},{20,28},{24,16},{28,20},{1,9},{5... | collective-permute-start | bytes 393224 | tf_op jit(solution)/shard_map/ppermute | solution.py:18
  70.8 2.7 %collective-permute-start.16 = (bf16[512,128]{1,0:T(8,128)(2,1)}, bf16[512,128]{1,0:T(8,128)(2,1)S(1)}, u32[]{:S(2)}, u32[]{:S(2)}) collective-permute-start(bf16[512,128]{1,0:T(8,128)(2,1)} %get-tuple-element.102), channel_id=1, source_target_pairs={{0,16},{4,20},{8,24},{12,28},{16,0},{20,4},{24,8},{28,12},{1,17},{... | collective-permute-start | bytes 393224 | tf_op jit(solution)/shard_map/ppermute | solution.py:18
  80.1 9.2 %collective-permute-done.16 = bf16[512,128]{1,0:T(8,128)(2,1)S(1)} collective-permute-done((bf16[512,128]{1,0:T(8,128)(2,1)}, bf16[512,128]{1,0:T(8,128)(2,1)S(1)}, u32[]{:S(2)}, u32[]{:S(2)}) %collective-permute-start.16) | collective-permute-done | bytes 131104 | tf_op jit(solution)/shard_map/ppermute | solution.py:18
  89.4 3.8 %collective-permute-done.17 = bf16[512,128]{1,0:T(8,128)(2,1)S(1)} collective-permute-done((bf16[512,128]{1,0:T(8,128)(2,1)}, bf16[512,128]{1,0:T(8,128)(2,1)S(1)}, u32[]{:S(2)}, u32[]{:S(2)}) %collective-permute-start.17) | collective-permute-done | bytes 131104 | tf_op jit(solution)/shard_map/ppermute | solution.py:18
  96.0 3.8 %collective-permute-done.21.after = bf16[1024,128]{1,0:T(8,128)(2,1)S(1)} collective-permute-done((bf16[1024,128]{1,0:T(8,128)(2,1)S(1)}, bf16[1024,128]{1,0:T(8,128)(2,1)S(1)}, u32[]{:S(2)}, u32[]{:S(2)}) %collective-permute-start.21) | collective-permute-done | bytes 262176 | tf_op jit(solution)/shard_map/ppermute | solution.py:72
  99.9 3.9 %shard_map.76 = (bf16[2,1024,128]{2,1,0:T(8,128)(2,1)S(1)}, bf16[128,2048]{1,0:T(8,128)(2,1)S(1)}) custom-call(bf16[4,1024,128]{2,1,0:T(8,128)(2,1)S(1)} %bitcast.112, bf16[1024,128]{1,0:T(8,128)(2,1)S(1)} %collective-permute-done.20.before, bf16[1024,128]{1,0:T(8,128)(2,1)S(1)} %collective-permute-done.21.after, f32[27,128]{1,0:T(8,128)S(1)} %bitcast.120, ...), custom_call_target="tpu_custom_call" | custom-call | flops 15728640 | bytes 4194304 | tf_op jit(solution)/shard_map/pallas_call | solution.py:191
  103.9 6.7 %collective-permute-start.22 = (bf16[1024,128]{1,0:T(8,128)(2,1)S(1)}, bf16[1024,128]{1,0:T(8,128)(2,1)S(1)}, u32[]{:S(2)}, u32[]{:S(2)}) collective-permute-start(bf16[1024,128]{1,0:T(8,128)(2,1)S(1)} %get-tuple-element.120), channel_id=1, source_target_pairs={{0,1},{1,2},{2,3},{4,5},{5,6},{6,7},{8,9},{9,10},{10,11},{12,13},{... | collective-permute-start | bytes 786440 | tf_op jit(solution)/shard_map/ppermute | solution.py:71
  112.1 3.9 %shard_map.77 = (bf16[2,1024,128]{2,1,0:T(8,128)(2,1)S(1)}, bf16[128,2048]{1,0:T(8,128)(2,1)S(1)}) custom-call(bf16[4,1024,128]{2,1,0:T(8,128)(2,1)S(1)} %bitcast.113, f32[27,128]{1,0:T(8,128)S(1)} %bitcast.121, bf16[128,4096]{1,0:T(8,128)(2,1)S(1)} %bitcast.117, bf16[128,4096]{1,0:T(8,128)(2,1)S(1)} %bitcast.119), custom_call_target="tpu_custom_call" | custom-call | flops 15728640 | bytes 4194304 | tf_op jit(solution)/shard_map/pallas_call | solution.py:191
  115.9 2.3 %shard_map.79 = bf16[2,1024,128]{2,1,0:T(8,128)(2,1)S(1)} custom-call(bf16[2,1024,128]{2,1,0:T(8,128)(2,1)S(1)} %get-tuple-element.60.g0, bf16[2,1024,128]{2,1,0:T(8,128)(2,1)S(1)} %get-tuple-element.56.g1, f32[27,128]{1,0:T(8,128)S(1)} %bitcast.122), custom_call_target="tpu_custom_call" | custom-call | flops 15728640 | bytes 4194304 | tf_op jit(solution)/shard_map/pallas_call | solution.py:191
  118.2 2.3 %shard_map.78 = bf16[2,1024,128]{2,1,0:T(8,128)(2,1)S(1)} custom-call(bf16[2,1024,128]{2,1,0:T(8,128)(2,1)S(1)} %get-tuple-element.60.g0, bf16[2,1024,128]{2,1,0:T(8,128)(2,1)S(1)} %get-tuple-element.56.g1, bf16[1024,128]{1,0:T(8,128)(2,1)S(1)} %collective-permute-done.22.before, bf16[1024,128]{1,0:T(8,128)(2,1)S(1)} %collective-permute-done.23.after, ...), custom_call_target="tpu_custom_call" | custom-call | flops 15728640 | bytes 4194304 | tf_op jit(solution)/shard_map/pallas_call | solution.py:191
  121.5 4.6 %collective-permute-start.27 = (bf16[512,128]{1,0:T(8,128)(2,1)S(1)}, bf16[512,128]{1,0:T(8,128)(2,1)S(1)}, u32[]{:S(2)}, u32[]{:S(2)}) collective-permute-start(bf16[512,128]{1,0:T(8,128)(2,1)S(1)} %get-tuple-element.92), channel_id=1, source_target_pairs={{0,16},{4,20},{8,24},{12,28},{16,0},{20,4},{24,8},{28,12},{1,17},{... | collective-permute-start | bytes 393224 | tf_op jit(solution)/shard_map/ppermute | solution.py:18
  127.4 2.2 %collective-permute-start.26 = (bf16[512,128]{1,0:T(8,128)(2,1)S(1)}, bf16[512,128]{1,0:T(8,128)(2,1)}, u32[]{:S(2)}, u32[]{:S(2)}) collective-permute-start(bf16[512,128]{1,0:T(8,128)(2,1)S(1)} %get-tuple-element.93), channel_id=1, source_target_pairs={{0,12},{4,8},{8,4},{12,0},{16,28},{20,24},{24,20},{28,16},{1,13},{... | collective-permute-start | bytes 393224 | tf_op jit(solution)/shard_map/ppermute | solution.py:18
  130.6 4.9 %collective-permute-start.29 = (bf16[512,128]{1,0:T(8,128)(2,1)S(1)}, bf16[512,128]{1,0:T(8,128)(2,1)}, u32[]{:S(2)}, u32[]{:S(2)}) collective-permute-start(bf16[512,128]{1,0:T(8,128)(2,1)S(1)} %get-tuple-element.90), channel_id=1, source_target_pairs={{0,24},{4,28},{8,16},{12,20},{16,8},{20,12},{24,0},{28,4},{1,25},{... | collective-permute-start | bytes 393224 | tf_op jit(solution)/shard_map/ppermute | solution.py:18
  138.8 2.6 %reshape.52 = bf16[128,4,1024]{2,1,0:T(4,128)(2,1)} reshape(bf16[128,4096]{1,0:T(8,128)(2,1)} %pad_maximum_fusion.2) | data formatting | bytes 2097152 | tf_op jit(solution)/shard_map/reshape | solution.py:366
  141.5 5.4 %shard_map.80 = f32[27,128]{1,0:T(8,128)S(1)} custom-call(bf16[4,1024,128]{2,1,0:T(8,128)(2,1)S(1)} %bitcast.114, bf16[1024,128]{1,0:T(8,128)(2,1)S(1)} %copy-done.8, bf16[1024,128]{1,0:T(8,128)(2,1)S(1)} %copy-done.10, bf16[2,1024,128]{2,1,0:T(8,128)(2,1)S(1)} %copy-done.2, bf16[2,1024,128]{2,1,0:T(8,128)(2,1)S(1)} %copy-done.4), custom_call_target="tpu_custom_call" | custom-call | flops 31457280 | bytes 4194304 | tf_op jit(solution)/shard_map/pallas_call | solution.py:191
  157.2 2.6 %shard_map.82 = bf16[8,128,512]{2,1,0:T(8,128)(2,1)S(1)} custom-call(s32[1]{0:T(128)} %bitcast.turn, bf16[512,1024]{1,0:T(8,128)(2,1)S(1)} %constant_dynamic-update-slice_fusion.mg, bf16[2,1024,256]{2,1,0:T(8,128)(2,1)S(1)} %copy-done.6, bf16[2,1024,256]{2,1,0:T(8,128)(2,1)} %collective-permute-done.12.refs_9_.other), custom_call_target="tpu_custom_call" | custom-call | flops 1073741824 | bytes 4194304 | tf_op jit(solution)/shard_map/pallas_call | solution.py:191
  167.1 4.3 %collective-permute-start.33 = (bf16[128,512]{1,0:T(8,128)(2,1)S(1)}, bf16[128,512]{1,0:T(8,128)(2,1)S(1)}, u32[]{:S(2)}, u32[]{:S(2)}) collective-permute-start(bf16[128,512]{1,0:T(8,128)(2,1)S(1)} %get-tuple-element.87), channel_id=1, source_target_pairs={{0,8},{4,12},{8,0},{12,4},{16,24},{20,28},{24,16},{28,20},{1,9},{5... | collective-permute-start | bytes 393224 | tf_op jit(solution)/shard_map/ppermute | solution.py:18
  171.7 3.0 %collective-permute-start.35 = (bf16[128,512]{1,0:T(8,128)(2,1)S(1)}, bf16[128,512]{1,0:T(8,128)(2,1)S(1)}, u32[]{:S(2)}, u32[]{:S(2)}) collective-permute-start(bf16[128,512]{1,0:T(8,128)(2,1)S(1)} %get-tuple-element.85), channel_id=1, source_target_pairs={{0,16},{4,20},{8,24},{12,28},{16,0},{20,4},{24,8},{28,12},{1,17},{... | collective-permute-start | bytes 393224 | tf_op jit(solution)/shard_map/ppermute | solution.py:18
  178.8 2.5 %collective-permute-done.34 = bf16[128,512]{1,0:T(8,128)(2,1)S(1)} collective-permute-done((bf16[128,512]{1,0:T(8,128)(2,1)S(1)}, bf16[128,512]{1,0:T(8,128)(2,1)S(1)}, u32[]{:S(2)}, u32[]{:S(2)}) %collective-permute-start.34) | collective-permute-done | bytes 131104 | tf_op jit(solution)/shard_map/ppermute | solution.py:18
  186.2 7.1 %collective-permute-done.36 = bf16[128,512]{1,0:T(8,128)(2,1)} collective-permute-done((bf16[128,512]{1,0:T(8,128)(2,1)}, bf16[128,512]{1,0:T(8,128)(2,1)}, u32[]{:S(2)}, u32[]{:S(2)}) %collective-permute-start.36) | collective-permute-done | bytes 131104 | tf_op jit(solution)/shard_map/ppermute | solution.py:18
  199.1 3.6 %collective-permute-start.41 = (bf16[128,256]{1,0:T(8,128)(2,1)S(1)}, bf16[128,256]{1,0:T(8,128)(2,1)S(1)}, u32[]{:S(2)}, u32[]{:S(2)}) collective-permute-start(bf16[128,256]{1,0:T(8,128)(2,1)S(1)} %get-tuple-element.121), channel_id=1, source_target_pairs={{0,8},{4,12},{8,0},{12,4},{16,24},{20,28},{24,16},{28,20},{1,9},{5... | collective-permute-start | bytes 196616 | tf_op jit(solution)/shard_map/ppermute | solution.py:18
  206.8 3.2 %collective-permute-done.42 = bf16[128,256]{1,0:T(8,128)(2,1)S(1)} collective-permute-done((bf16[128,256]{1,0:T(8,128)(2,1)S(1)}, bf16[128,256]{1,0:T(8,128)(2,1)S(1)}, u32[]{:S(2)}, u32[]{:S(2)}) %collective-permute-start.42) | collective-permute-done | bytes 65568 | tf_op jit(solution)/shard_map/ppermute | solution.py:18
  (179 shorter events, 77.9 us)
Async XLA Ops:
  20.0 10.9 %collective-permute-start.11 = (bf16[1024,256]{1,0:T(8,128)(2,1)S(1)}, bf16[1024,256]{1,0:T(8,128)(2,1)S(1)}, u32[]{:S(2)}, u32[]{:S(2)}) collective-permute-start(bf16[1024,256]{1,0:T(8,128)(2,1)S(1)} %bitcast.131), channel_id=1, source_target_pairs={{0,2},{1,3},{2,0},{3,1},{4,6},{5,7},{6,4},{7,5},{8,10},{9,11},{10,... | collective-permute-start | bytes 1572872 | tf_op jit(solution)/shard_map/ppermute | solution.py:18
  31.0 26.2 %collective-permute-start.12 = (bf16[2,1024,256]{2,1,0:T(8,128)(2,1)S(1)}, bf16[2,1024,256]{2,1,0:T(8,128)(2,1)}, u32[]{:S(2)}, u32[]{:S(2)}) collective-permute-start(bf16[2,1024,256]{2,1,0:T(8,128)(2,1)S(1)} %pad_maximum_fusion.refs_8_.held), channel_id=1, source_target_pairs={{0,1},{1,0},{2,3},{3,2},{4,5},{5,4},{6,7},{7,6},{8,9},{9,8},{10,11... | collective-permute-start | bytes 3145736 | tf_op jit(solution)/shard_map/ppermute | solution.py:18
  32.6 9.1 %collective-permute-start.1 = (bf16[128,512]{1,0:T(8,128)(2,1)S(1)}, bf16[128,512]{1,0:T(8,128)(2,1)S(1)}, u32[]{:S(2)}, u32[]{:S(2)}) collective-permute-start(bf16[128,512]{1,0:T(8,128)(2,1)S(1)} %get-tuple-element.112), channel_id=1, source_target_pairs={{0,8},{4,12},{8,0},{12,4},{16,24},{20,28},{24,16},{28,20},{1,9},{5... | collective-permute-start | bytes 393224 | tf_op jit(solution)/shard_map/ppermute | solution.py:18
  34.4 11.2 %collective-permute-start.2 = (bf16[128,512]{1,0:T(8,128)(2,1)S(1)}, bf16[128,512]{1,0:T(8,128)(2,1)S(1)}, u32[]{:S(2)}, u32[]{:S(2)}) collective-permute-start(bf16[128,512]{1,0:T(8,128)(2,1)S(1)} %get-tuple-element.111), channel_id=1, source_target_pairs={{0,12},{4,8},{8,4},{12,0},{16,28},{20,24},{24,20},{28,16},{1,13},{... | collective-permute-start | bytes 393224 | tf_op jit(solution)/shard_map/ppermute | solution.py:18
  34.6 16.1 %collective-permute-start.3 = (bf16[128,512]{1,0:T(8,128)(2,1)}, bf16[128,512]{1,0:T(8,128)(2,1)}, u32[]{:S(2)}, u32[]{:S(2)}) collective-permute-start(bf16[128,512]{1,0:T(8,128)(2,1)} %get-tuple-element.110), channel_id=1, source_target_pairs={{0,16},{4,20},{8,24},{12,28},{16,0},{20,4},{24,8},{28,12},{1,17},{... | collective-permute-start | bytes 393224 | tf_op jit(solution)/shard_map/ppermute | solution.py:18
  38.0 19.2 %collective-permute-start.4 = (bf16[128,512]{1,0:T(8,128)(2,1)}, bf16[128,512]{1,0:T(8,128)(2,1)}, u32[]{:S(2)}, u32[]{:S(2)}) collective-permute-start(bf16[128,512]{1,0:T(8,128)(2,1)} %get-tuple-element.109), channel_id=1, source_target_pairs={{0,20},{4,16},{8,28},{12,24},{16,4},{20,0},{24,12},{28,8},{1,21},{... | collective-permute-start | bytes 393224 | tf_op jit(solution)/shard_map/ppermute | solution.py:18
  42.4 14.8 %collective-permute-start.5 = (bf16[128,512]{1,0:T(8,128)(2,1)}, bf16[128,512]{1,0:T(8,128)(2,1)}, u32[]{:S(2)}, u32[]{:S(2)}) collective-permute-start(bf16[128,512]{1,0:T(8,128)(2,1)} %get-tuple-element.108), channel_id=1, source_target_pairs={{0,24},{4,28},{8,16},{12,20},{16,8},{20,12},{24,0},{28,4},{1,25},{... | collective-permute-start | bytes 393224 | tf_op jit(solution)/shard_map/ppermute | solution.py:18
  46.2 11.0 %collective-permute-start.6 = (bf16[128,512]{1,0:T(8,128)(2,1)}, bf16[128,512]{1,0:T(8,128)(2,1)}, u32[]{:S(2)}, u32[]{:S(2)}) collective-permute-start(bf16[128,512]{1,0:T(8,128)(2,1)} %get-tuple-element.107), channel_id=1, source_target_pairs={{0,28},{4,24},{8,20},{12,16},{16,12},{20,8},{24,4},{28,0},{1,29},{... | collective-permute-start | bytes 393224 | tf_op jit(solution)/shard_map/ppermute | solution.py:18
  64.2 10.4 %collective-permute-start.13 = (bf16[512,128]{1,0:T(8,128)(2,1)}, bf16[512,128]{1,0:T(8,128)(2,1)}, u32[]{:S(2)}, u32[]{:S(2)}) collective-permute-start(bf16[512,128]{1,0:T(8,128)(2,1)} %get-tuple-element.105), channel_id=1, source_target_pairs={{0,4},{4,0},{8,12},{12,8},{16,20},{20,16},{24,28},{28,24},{1,5},{5... | collective-permute-start | bytes 393224 | tf_op jit(solution)/shard_map/ppermute | solution.py:18
  65.7 11.8 %collective-permute-start.14 = (bf16[512,128]{1,0:T(8,128)(2,1)}, bf16[512,128]{1,0:T(8,128)(2,1)S(1)}, u32[]{:S(2)}, u32[]{:S(2)}) collective-permute-start(bf16[512,128]{1,0:T(8,128)(2,1)} %get-tuple-element.104), channel_id=1, source_target_pairs={{0,8},{4,12},{8,0},{12,4},{16,24},{20,28},{24,16},{28,20},{1,9},{5... | collective-permute-start | bytes 393224 | tf_op jit(solution)/shard_map/ppermute | solution.py:18
  70.8 9.3 %collective-permute-start.15 = (bf16[512,128]{1,0:T(8,128)(2,1)}, bf16[512,128]{1,0:T(8,128)(2,1)S(1)}, u32[]{:S(2)}, u32[]{:S(2)}) collective-permute-start(bf16[512,128]{1,0:T(8,128)(2,1)} %get-tuple-element.103), channel_id=1, source_target_pairs={{0,12},{4,8},{8,4},{12,0},{16,28},{20,24},{24,20},{28,16},{1,13},{... | collective-permute-start | bytes 393224 | tf_op jit(solution)/shard_map/ppermute | solution.py:18
  70.8 18.5 %collective-permute-start.16 = (bf16[512,128]{1,0:T(8,128)(2,1)}, bf16[512,128]{1,0:T(8,128)(2,1)S(1)}, u32[]{:S(2)}, u32[]{:S(2)}) collective-permute-start(bf16[512,128]{1,0:T(8,128)(2,1)} %get-tuple-element.102), channel_id=1, source_target_pairs={{0,16},{4,20},{8,24},{12,28},{16,0},{20,4},{24,8},{28,12},{1,17},{... | collective-permute-start | bytes 393224 | tf_op jit(solution)/shard_map/ppermute | solution.py:18
  73.6 19.7 %collective-permute-start.17 = (bf16[512,128]{1,0:T(8,128)(2,1)}, bf16[512,128]{1,0:T(8,128)(2,1)S(1)}, u32[]{:S(2)}, u32[]{:S(2)}) collective-permute-start(bf16[512,128]{1,0:T(8,128)(2,1)} %get-tuple-element.101), channel_id=1, source_target_pairs={{0,20},{4,16},{8,28},{12,24},{16,4},{20,0},{24,12},{28,8},{1,21},{... | collective-permute-start | bytes 393224 | tf_op jit(solution)/shard_map/ppermute | solution.py:18
  74.6 18.6 %collective-permute-start.18 = (bf16[512,128]{1,0:T(8,128)(2,1)}, bf16[512,128]{1,0:T(8,128)(2,1)S(1)}, u32[]{:S(2)}, u32[]{:S(2)}) collective-permute-start(bf16[512,128]{1,0:T(8,128)(2,1)} %get-tuple-element.100), channel_id=1, source_target_pairs={{0,24},{4,28},{8,16},{12,20},{16,8},{20,12},{24,0},{28,4},{1,25},{... | collective-permute-start | bytes 393224 | tf_op jit(solution)/shard_map/ppermute | solution.py:18
  77.5 15.8 %collective-permute-start.19 = (bf16[512,128]{1,0:T(8,128)(2,1)S(1)}, bf16[512,128]{1,0:T(8,128)(2,1)S(1)}, u32[]{:S(2)}, u32[]{:S(2)}) collective-permute-start(bf16[512,128]{1,0:T(8,128)(2,1)S(1)} %get-tuple-element.99), channel_id=1, source_target_pairs={{0,28},{4,24},{8,20},{12,16},{16,12},{20,8},{24,4},{28,0},{1,29},{... | collective-permute-start | bytes 393224 | tf_op jit(solution)/shard_map/ppermute | solution.py:18
  103.9 14.3 %collective-permute-start.22 = (bf16[1024,128]{1,0:T(8,128)(2,1)S(1)}, bf16[1024,128]{1,0:T(8,128)(2,1)S(1)}, u32[]{:S(2)}, u32[]{:S(2)}) collective-permute-start(bf16[1024,128]{1,0:T(8,128)(2,1)S(1)} %get-tuple-element.120), channel_id=1, source_target_pairs={{0,1},{1,2},{2,3},{4,5},{5,6},{6,7},{8,9},{9,10},{10,11},{12,13},{... | collective-permute-start | bytes 786440 | tf_op jit(solution)/shard_map/ppermute | solution.py:71
  121.5 9.1 %collective-permute-start.27 = (bf16[512,128]{1,0:T(8,128)(2,1)S(1)}, bf16[512,128]{1,0:T(8,128)(2,1)S(1)}, u32[]{:S(2)}, u32[]{:S(2)}) collective-permute-start(bf16[512,128]{1,0:T(8,128)(2,1)S(1)} %get-tuple-element.92), channel_id=1, source_target_pairs={{0,16},{4,20},{8,24},{12,28},{16,0},{20,4},{24,8},{28,12},{1,17},{... | collective-permute-start | bytes 393224 | tf_op jit(solution)/shard_map/ppermute | solution.py:18
  126.1 9.4 %collective-permute-start.24 = (bf16[512,128]{1,0:T(8,128)(2,1)S(1)}, bf16[512,128]{1,0:T(8,128)(2,1)S(1)}, u32[]{:S(2)}, u32[]{:S(2)}) collective-permute-start(bf16[512,128]{1,0:T(8,128)(2,1)S(1)} %get-tuple-element.95), channel_id=1, source_target_pairs={{0,4},{4,0},{8,12},{12,8},{16,20},{20,16},{24,28},{28,24},{1,5},{5... | collective-permute-start | bytes 393224 | tf_op jit(solution)/shard_map/ppermute | solution.py:18
  127.4 19.4 %collective-permute-start.25 = (bf16[512,128]{1,0:T(8,128)(2,1)}, bf16[512,128]{1,0:T(8,128)(2,1)}, u32[]{:S(2)}, u32[]{:S(2)}) collective-permute-start(bf16[512,128]{1,0:T(8,128)(2,1)} %get-tuple-element.94), channel_id=1, source_target_pairs={{0,8},{4,12},{8,0},{12,4},{16,24},{20,28},{24,16},{28,20},{1,9},{5... | collective-permute-start | bytes 393224 | tf_op jit(solution)/shard_map/ppermute | solution.py:18
  127.4 19.4 %collective-permute-start.26 = (bf16[512,128]{1,0:T(8,128)(2,1)S(1)}, bf16[512,128]{1,0:T(8,128)(2,1)}, u32[]{:S(2)}, u32[]{:S(2)}) collective-permute-start(bf16[512,128]{1,0:T(8,128)(2,1)S(1)} %get-tuple-element.93), channel_id=1, source_target_pairs={{0,12},{4,8},{8,4},{12,0},{16,28},{20,24},{24,20},{28,16},{1,13},{... | collective-permute-start | bytes 393224 | tf_op jit(solution)/shard_map/ppermute | solution.py:18
  129.6 17.3 %collective-permute-start.28 = (bf16[512,128]{1,0:T(8,128)(2,1)S(1)}, bf16[512,128]{1,0:T(8,128)(2,1)}, u32[]{:S(2)}, u32[]{:S(2)}) collective-permute-start(bf16[512,128]{1,0:T(8,128)(2,1)S(1)} %get-tuple-element.91), channel_id=1, source_target_pairs={{0,20},{4,16},{8,28},{12,24},{16,4},{20,0},{24,12},{28,8},{1,21},{... | collective-permute-start | bytes 393224 | tf_op jit(solution)/shard_map/ppermute | solution.py:18
  130.6 16.3 %collective-permute-start.29 = (bf16[512,128]{1,0:T(8,128)(2,1)S(1)}, bf16[512,128]{1,0:T(8,128)(2,1)}, u32[]{:S(2)}, u32[]{:S(2)}) collective-permute-start(bf16[512,128]{1,0:T(8,128)(2,1)S(1)} %get-tuple-element.90), channel_id=1, source_target_pairs={{0,24},{4,28},{8,16},{12,20},{16,8},{20,12},{24,0},{28,4},{1,25},{... | collective-permute-start | bytes 393224 | tf_op jit(solution)/shard_map/ppermute | solution.py:18
  135.5 11.3 %collective-permute-start.30 = (bf16[512,128]{1,0:T(8,128)(2,1)S(1)}, bf16[512,128]{1,0:T(8,128)(2,1)}, u32[]{:S(2)}, u32[]{:S(2)}) collective-permute-start(bf16[512,128]{1,0:T(8,128)(2,1)S(1)} %get-tuple-element.89), channel_id=1, source_target_pairs={{0,28},{4,24},{8,20},{12,16},{16,12},{20,8},{24,4},{28,0},{1,29},{... | collective-permute-start | bytes 393224 | tf_op jit(solution)/shard_map/ppermute | solution.py:18
  163.9 19.7 %collective-permute-start.39 = (bf16[1024,256]{0,1:T(8,128)(2,1)S(1)}, bf16[1024,256]{0,1:T(8,128)(2,1)S(1)}, u32[]{:S(2)}, u32[]{:S(2)}) collective-permute-start(bf16[1024,256]{0,1:T(8,128)(2,1)S(1)} %slice.183), channel_id=1, source_target_pairs={{0,2},{1,3},{2,0},{3,1},{4,6},{5,7},{6,4},{7,5},{8,10},{9,11},{10,... | collective-permute-start | bytes 1572872 | tf_op jit(solution)/shard_map/ppermute | solution.py:18
  165.8 9.0 %collective-permute-start.32 = (bf16[128,512]{1,0:T(8,128)(2,1)S(1)}, bf16[128,512]{1,0:T(8,128)(2,1)S(1)}, u32[]{:S(2)}, u32[]{:S(2)}) collective-permute-start(bf16[128,512]{1,0:T(8,128)(2,1)S(1)} %get-tuple-element.88), channel_id=1, source_target_pairs={{0,4},{4,0},{8,12},{12,8},{16,20},{20,16},{24,28},{28,24},{1,5},{5... | collective-permute-start | bytes 393224 | tf_op jit(solution)/shard_map/ppermute | solution.py:18
  167.1 11.0 %collective-permute-start.33 = (bf16[128,512]{1,0:T(8,128)(2,1)S(1)}, bf16[128,512]{1,0:T(8,128)(2,1)S(1)}, u32[]{:S(2)}, u32[]{:S(2)}) collective-permute-start(bf16[128,512]{1,0:T(8,128)(2,1)S(1)} %get-tuple-element.87), channel_id=1, source_target_pairs={{0,8},{4,12},{8,0},{12,4},{16,24},{20,28},{24,16},{28,20},{1,9},{5... | collective-permute-start | bytes 393224 | tf_op jit(solution)/shard_map/ppermute | solution.py:18
  171.5 9.9 %collective-permute-start.34 = (bf16[128,512]{1,0:T(8,128)(2,1)S(1)}, bf16[128,512]{1,0:T(8,128)(2,1)S(1)}, u32[]{:S(2)}, u32[]{:S(2)}) collective-permute-start(bf16[128,512]{1,0:T(8,128)(2,1)S(1)} %get-tuple-element.86), channel_id=1, source_target_pairs={{0,12},{4,8},{8,4},{12,0},{16,28},{20,24},{24,20},{28,16},{1,13},{... | collective-permute-start | bytes 393224 | tf_op jit(solution)/shard_map/ppermute | solution.py:18
  171.7 11.7 %collective-permute-start.35 = (bf16[128,512]{1,0:T(8,128)(2,1)S(1)}, bf16[128,512]{1,0:T(8,128)(2,1)S(1)}, u32[]{:S(2)}, u32[]{:S(2)}) collective-permute-start(bf16[128,512]{1,0:T(8,128)(2,1)S(1)} %get-tuple-element.85), channel_id=1, source_target_pairs={{0,16},{4,20},{8,24},{12,28},{16,0},{20,4},{24,8},{28,12},{1,17},{... | collective-permute-start | bytes 393224 | tf_op jit(solution)/shard_map/ppermute | solution.py:18
  174.8 18.5 %collective-permute-start.36 = (bf16[128,512]{1,0:T(8,128)(2,1)}, bf16[128,512]{1,0:T(8,128)(2,1)}, u32[]{:S(2)}, u32[]{:S(2)}) collective-permute-start(bf16[128,512]{1,0:T(8,128)(2,1)} %get-tuple-element.84), channel_id=1, source_target_pairs={{0,20},{4,16},{8,28},{12,24},{16,4},{20,0},{24,12},{28,8},{1,21},{... | collective-permute-start | bytes 393224 | tf_op jit(solution)/shard_map/ppermute | solution.py:18
  178.0 16.2 %collective-permute-start.37 = (bf16[128,512]{1,0:T(8,128)(2,1)}, bf16[128,512]{1,0:T(8,128)(2,1)}, u32[]{:S(2)}, u32[]{:S(2)}) collective-permute-start(bf16[128,512]{1,0:T(8,128)(2,1)} %get-tuple-element.83), channel_id=1, source_target_pairs={{0,24},{4,28},{8,16},{12,20},{16,8},{20,12},{24,0},{28,4},{1,25},{... | collective-permute-start | bytes 393224 | tf_op jit(solution)/shard_map/ppermute | solution.py:18
  181.4 13.7 %collective-permute-start.38 = (bf16[128,512]{1,0:T(8,128)(2,1)S(1)}, bf16[128,512]{1,0:T(8,128)(2,1)}, u32[]{:S(2)}, u32[]{:S(2)}) collective-permute-start(bf16[128,512]{1,0:T(8,128)(2,1)S(1)} %get-tuple-element.82), channel_id=1, source_target_pairs={{0,28},{4,24},{8,20},{12,16},{16,12},{20,8},{24,4},{28,0},{1,29},{... | collective-permute-start | bytes 393224 | tf_op jit(solution)/shard_map/ppermute | solution.py:18
  184.9 12.9 %collective-permute-start.40 = (bf16[4,128,256]{2,1,0:T(8,128)(2,1)}, bf16[4,128,256]{2,1,0:T(8,128)(2,1)}, u32[]{:S(2)}, u32[]{:S(2)}) collective-permute-start(bf16[4,128,256]{2,1,0:T(8,128)(2,1)} %fusion.1), channel_id=1, source_target_pairs={{0,4},{4,0},{8,12},{12,8},{16,20},{20,16},{24,28},{28,24},{1,5},{5... | collective-permute-start | bytes 786440 | tf_op jit(solution)/shard_map/ppermute | solution.py:18
  (41 other events, 283.8 us)

commit v5 on v4

--- a/solution.py
+++ b/solution.py
@@ -38,27 +38,27 @@
     return lax.dynamic_index_in_dim(blocks, index, 0, keepdims=False)
 
 
-def gather_weights(mixing, me_space, after):
+def gather_weights(mixing, me_space, send, pieces):
     rows, cols = mixing.shape
     nf, ns = lax.axis_size("filter"), lax.axis_size("space")
     share = cols // ns
     own = lax.dynamic_slice_in_dim(mixing, me_space * share, share, axis=1)
     even = jnp.stack([own] + [swap(own, "filter", s) for s in range(2, nf, 2)])
-    even, _ = lax.optimization_barrier((even, after))
+    even, _ = lax.optimization_barrier((even, send))
     odd = swap(even, "filter", 1)
     part = jnp.stack([even, odd], axis=1).reshape(nf * rows, share)
+    part, _ = lax.optimization_barrier((part, pieces[nf // 2]))
     held = jnp.stack([part] + [swap(part, "space", s) for s in range(2, ns, 2)])
+    held, _ = lax.optimization_barrier((held, pieces[nf // 2 :]))
     return held, swap(held, "space", 1)
 
 
 def scatter_rest(half, rows):
-    nf, ns = lax.axis_size("filter"), lax.axis_size("space")
-    share = 2 * half.shape[1] // ns
-    half = [half[:, k * share : (k + 1) * share] for k in range(ns // 2)]
+    nf = lax.axis_size("filter")
     total = half[0]
-    for k in range(1, ns // 2):
+    for k in range(1, len(half)):
         total = total + swap(half[k].astype(BF), "space", 2 * k).astype(F32)
-    total = total.reshape(nf // 2, 2, rows, share)
+    total = total.reshape(nf // 2, 2, rows, total.shape[1])
     near = total[:, 0] + swap(total[:, 1].astype(BF), "filter", 1).astype(F32)
     result = near[0]
     for k in range(1, nf // 2):
@@ -66,11 +66,15 @@
     return result
 
 
-def halo(first, last):
+def halo(field):
     size = lax.axis_size("space")
-    before = lax.ppermute(last, "space", [(i, i + 1) for i in range(size - 1)])
-    after = lax.ppermute(first, "space", [(i + 1, i) for i in range(size - 1)])
-    return before, after
+    odd = lax.axis_index("space") & 1
+    planes = field.shape[0]
+    inner = [(i, i ^ 1) for i in range(size)]
+    outer = [(i, ((i + 1) ^ 1) - 1) for i in range(1, size - 1)]
+    near = lax.ppermute(pick(field, (1 - odd) * (planes - 1)), "space", inner)
+    far = lax.ppermute(pick(field, odd * (planes - 1)), "space", outer)
+    return jnp.where(odd == 1, near, far), jnp.where(odd == 1, far, near)
 
 
 def fill(pad_ref, plane, source):
@@ -194,14 +198,14 @@
         in_specs=[pl.BlockSpec(memory_space=place_of(arg)) for arg in args],
         out_specs=jax.tree.map(lambda _: pl.BlockSpec(memory_space=pltpu.VMEM), out_shape),
         scratch_shapes=scratch,
-        compiler_params=pltpu.CompilerParams(vmem_limit_bytes=40 * 1024 * 1024),
+        compiler_params=pltpu.CompilerParams(vmem_limit_bytes=20 * 1024 * 1024),
         cost_estimate=pl.CostEstimate(flops=ops, bytes_accessed=4 * 1024 * 1024, transcendentals=0),
     )(*args)
 
 
 def mix_kernel(turn, *refs):
-    nf = len(refs) - 4
-    pieces, (held, other, vol_t, out) = refs[:nf], refs[nf:]
+    nf = (len(refs) - 3) // 2
+    pieces, (held, other, vol_t), out = refs[:nf], refs[nf : nf + 3], refs[nf + 3 :]
     ch = pieces[0].shape[0]
     share = held.shape[2]
     for t, piece in enumerate(pieces):
@@ -216,8 +220,8 @@
                 preferred_element_type=F32,
             )
             total = term if total is None else total + term
-        out[s] = total[:, :ch].astype(BF)
-        out[s + 1] = total[:, ch:].astype(BF)
+        out[s][...] = total[:, :ch].astype(BF)
+        out[s + 1][...] = total[:, ch:].astype(BF)
 
 
 def mix(turn, pieces, held, other):
@@ -228,18 +232,21 @@
         weights = jnp.stack([held, other], axis=1).reshape(2 * pairs, rows, share)
         out = jnp.einsum(
             "cvi,voi->co", vol_t.reshape(blk, 2 * pairs, share), weights, preferred_element_type=F32
-        )
-        return vol_t, out.astype(BF).reshape(blk, nf, ch).transpose(1, 0, 2)
-    shapes = (
-        jax.ShapeDtypeStruct((blk, nf * ch), BF),
-        jax.ShapeDtypeStruct((nf, blk, ch), BF),
-    )
-    return call(mix_kernel, shapes, [], turn, *pieces, held, other, ops=2 * blk * rows * rows)
-
-
-def unmix_kernel(turn, mg, held, other, out):
-    ch = out.shape[1]
+        ).astype(BF)
+        return vol_t, [out[:, s * ch : (s + 1) * ch] for s in range(nf)]
+    shapes = [jax.ShapeDtypeStruct((blk, nf * ch), BF)] + [jax.ShapeDtypeStruct((blk, ch), BF)] * nf
+    got = call(mix_kernel, shapes, [], turn, *pieces, held, other, ops=2 * blk * rows * rows)
+    return got[0], got[1:]
+
+
+def unmix_kernel(turn, *refs):
+    nf = (len(refs) - 4) // 2
+    pieces, (held, other), out = refs[:nf], refs[nf : nf + 2], refs[nf + 2 : 2 * nf + 2]
+    mg, back = refs[2 * nf + 2 :]
+    ch = out[0].shape[0]
     share = held.shape[2]
+    for r, piece in enumerate(pieces):
+        mg[:, r * ch : (r + 1) * ch] = piece[...]
     for v in range(2 * held.shape[0]):
         block = (other if v % 2 else held)[v // 2]
         total = lax.dot_general(
@@ -247,49 +254,62 @@
         )
         turned = jnp.transpose(total).astype(BF)
         for k in range(share // ch):
-            out[(v * (share // ch) + k) ^ turn[0]] = turned[k * ch : (k + 1) * ch, :]
-
-
-def unmix(turn, mg, held, other, ch):
-    blk = mg.shape[0]
+            back[v * (share // ch) + k] = turned[k * ch : (k + 1) * ch, :]
+    for s in range(nf):
+        out[s][...] = back[turn[0] ^ s]
+
+
+def unmix(turn, pieces, held, other):
+    nf, (blk, ch) = len(pieces), pieces[0].shape
     pairs, rows, share = held.shape
-    nf = rows // ch
     if ch % 128:
         weights = jnp.stack([held, other], axis=1).reshape(2 * pairs, rows, share)
+        mg = jnp.concatenate(pieces, axis=1)
         out = jnp.einsum("co,voi->vic", mg, weights, preferred_element_type=F32)
         out = out.astype(BF).reshape(nf, ch, blk)
-        return jnp.stack([pick(out, turn[0] ^ s) for s in range(nf)])
-    shape = jax.ShapeDtypeStruct((nf, ch, blk), BF)
-    return call(unmix_kernel, shape, [], turn, mg, held, other, ops=2 * blk * rows * rows)
-
-
-def weight_kernel(norm, mg, vol_t, mine, theirs):
-    pairs = mine.shape[0]
-    share = mine.shape[2]
-    for v in range(2 * pairs):
-        total = lax.dot_general(
-            mg[...], vol_t[:, v * share : (v + 1) * share], (((0,), (0,)), ((), ())),
-            preferred_element_type=F32,
-        )
-        if v % 2:
-            theirs[v // 2] = (total * norm).astype(BF)
-        else:
-            mine[v // 2] = total * norm
-
-
-def weight_products(mg, vol_t, norm, ns):
-    rows = mg.shape[1]
+        return [pick(out, turn[0] ^ s) for s in range(nf)]
+    shapes = [jax.ShapeDtypeStruct((ch, blk), BF)] * nf
+    scratch = [pltpu.VMEM((blk, nf * ch), BF), pltpu.VMEM((nf, ch, blk), BF)]
+    return call(unmix_kernel, shapes, scratch, turn, *pieces, held, other, ops=2 * blk * rows * rows)
+
+
+def weight_products(pieces, vol_t, norm, ns):
+    nf, (blk, ch) = len(pieces), pieces[0].shape
     share = vol_t.shape[1] // ns
-    shapes = (
-        jax.ShapeDtypeStruct((ns // 2, rows, share), F32),
-        jax.ShapeDtypeStruct((ns // 2, rows, share), BF),
-    )
-    if share % 128:
+    pairs = ns // 2
+    if ch % 128 or share % 128:
+        mg = jnp.concatenate(pieces, axis=1)
         part = lax.dot_general(mg, vol_t, (((0,), (0,)), ((), ())), preferred_element_type=F32)
-        part = (part * norm).reshape(rows, ns // 2, 2, share).transpose(2, 1, 0, 3)
-        return part[0], part[1].astype(BF)
-    kernel = functools.partial(weight_kernel, norm)
-    return call(kernel, shapes, [], mg, vol_t, ops=2 * mg.shape[0] * rows * rows)
+        part = (part * norm).reshape(nf * ch, pairs, 2, share)
+        return [part[:, k, 0] for k in range(pairs)], part[:, :, 1].transpose(1, 0, 2).astype(BF)
+
+    def kernel(*refs):
+        parts, vol, mine, theirs = refs[:nf], refs[nf], refs[nf + 1 : nf + 1 + pairs], refs[-1]
+        for r, piece in enumerate(parts):
+            turned = jnp.transpose(piece[...])
+            for v in range(ns):
+                total = norm * lax.dot_general(
+                    turned, vol[:, v * share : (v + 1) * share], (((1,), (0,)), ((), ())),
+                    preferred_element_type=F32,
+                )
+                row = slice(r * ch, (r + 1) * ch)
+                if v % 2:
+                    theirs[v // 2, row, :] = total.astype(BF)
+                else:
+                    mine[v // 2][row, :] = total
+
+    shapes = [jax.ShapeDtypeStruct((nf * ch, share), F32)] * pairs
+    shapes.append(jax.ShapeDtypeStruct((pairs, nf * ch, share), BF))
+    got = call(kernel, shapes, [], *pieces, vol_t, ops=2 * blk * (nf * ch) ** 2)
+    return got[:-1], got[-1]
+
+
+def finish_kernel(me, *refs):
+    pieces, (up, out) = refs[:-2], refs[-2:]
+    blk = pieces[0].shape[1]
+    for s, piece in enumerate(pieces):
+        lane = pl.ds(pl.multiple_of((me[0] ^ s) * blk, 128), blk)
+        out[:, lane] = (up[:, lane].astype(F32) + piece[...].astype(F32)).astype(BF)
 
 
 def body(volume, mixing, kernel_taps, upstream):
@@ -307,16 +327,16 @@
     vol = volume.reshape(ch, total)
     send = [lax.dynamic_slice_in_dim(vol, (me ^ s) * blk, blk, axis=1) for s in range(nf)]
     pieces = exchange(send, "filter")
-    held, other = gather_weights(mixing, me_space, send)
+    held, other = gather_weights(mixing, me_space, send, pieces)
     up = upstream.reshape(ch, total)
     pieces, up, held, other = lax.optimization_barrier((pieces, up, held, other))
     vol_t, prod = mix(turn, pieces, held, other)
 
-    got = exchange([prod[s] for s in range(nf)], "filter")
+    got = exchange(prod, "filter")
     mixed = place(got, me).reshape(planes, flat, ch)
 
     taps = kernel_taps.T
-    before, after = halo(mixed[0], mixed[planes - 1])
+    before, after = halo(mixed)
     pad = pltpu.VMEM((planes + 2, height + 2, WW, ch), F32)
     conv_ops = 60 * flat * ch
 
@@ -335,7 +355,7 @@
 
     grad_middle, out_middle = forward(1)
     grad_edges, out_edges = forward(0)
-    grad_before, grad_after = halo(grad_edges[0], grad_edges[1])
+    grad_before, grad_after = halo(grad_edges)
     where_grad = {p: (i, k) for i, g in enumerate(groups) for k, p in enumerate(g)}
 
     def backward(i):
@@ -364,27 +384,23 @@
     )
     output = jnp.concatenate([out_edges[:, :flat], out_middle, out_edges[:, flat:]], axis=1)
     output = output.reshape(ch, planes, flat)
-    got, taps_grad, output = lax.optimization_barrier((got, taps_grad, output))
-
-    mg_all = jnp.concatenate(got, axis=1)
-    mine, theirs = weight_products(mg_all, vol_t, norm, ns)
-    mg_all, theirs = lax.optimization_barrier((mg_all, theirs))
-    half = mine + swap(theirs, "space", 1).astype(F32)
-    back = unmix(turn, mg_all, held, other, ch)
-    back, half = lax.optimization_barrier((back, half))
-    got = exchange([back[s] for s in range(nf)], "filter")
-    back_own = jnp.zeros((ch, total), BF)
-    for s, piece in enumerate(got):
-        back_own = lax.dynamic_update_slice_in_dim(back_own, piece, (me ^ s) * blk, axis=1)
-    back_own = back_own.reshape(ch, planes, flat)
-    volume_grad = (upstream.astype(F32) + back_own.astype(F32)).astype(BF)
-
-    half = half.transpose(1, 0, 2).reshape(nf * ch, -1)
-    mixing_grad = scatter_rest(half, ch)
     step = 1
     while step < ns:
         taps_grad = taps_grad + swap(taps_grad, "space", step)
         step *= 2
+    got, taps_grad, output = lax.optimization_barrier((got, taps_grad, output))
+
+    mine, theirs = weight_products(got, vol_t, norm, ns)
+    got, theirs = lax.optimization_barrier((got, theirs))
+    theirs = swap(theirs, "space", 1)
+    half = [mine[k] + theirs[k].astype(F32) for k in range(ns // 2)]
+    mixing_grad = scatter_rest(half, ch)
+    got = exchange(unmix(turn, got, held, other), "filter")
+    got, mixing_grad = lax.optimization_barrier((got, mixing_grad))
+    volume_grad = call(
+        finish_kernel, jax.ShapeDtypeStruct((ch, total), BF), [],
+        jnp.reshape(me, (1,)).astype(jnp.int32), *got, up, ops=total * ch,
+    ).reshape(ch, planes, flat)
     return (output, volume_grad, mixing_grad, taps_grad.T)
 
 

time: 211 us -> 213 us (level)
  waiting for transfers between devices: 58.9 us -> 86 us
  starting transfers between devices: 89.5 us -> 71.7 us
  local copies, waits for them, and re-layouts: 30.1 us -> 22.9 us
  Pallas kernels: 24.7 us -> 22 us
    ppermute x42, waiting for transfers between devices: 55.1 us -> 84.5 us  [swap(): return lax.ppermute(block, axis, [(i, i ^ step) for i in range(size)])]
    ppermute x42, starting transfers between devices: 78.7 us -> 62.4 us  [swap(): return lax.ppermute(block, axis, [(i, i ^ step) for i in range(size)])]
    pallas_call x0 -> x1, other arithmetic: none -> 4.05 us  [call(): pl.pallas_call(kernel, out_shape=out_shape, in_specs=[pl.BlockSpec(memory...]
    unnamed x63 -> x64, local copies, waits for them, and re-layouts: 12.8 us -> 15.6 us
    dynamic_update_slice x8 -> x0, local copies, waits for them, and re-layouts: 2.83 us -> none  [body(): lax.dynamic_update_slice_in_dim(back_own, piece, (me ^ s) * blk, axis=1)]
    pallas_call x8, Pallas kernels: 24.7 us -> 22 us  [call(): pl.pallas_call(kernel, out_shape=out_shape, in_specs=[pl.BlockSpec(memory...]
    ppermute x4, waiting for transfers between devices: 3.86 us -> 1.51 us  [the longest x2 1.5 us: halo(): near = lax.ppermute(pick(field, (1 - odd) * (planes - 1)), 'space', inner)]
  transfers between devices with their start and end apart: 46 -> 46, of which waited for: 16 -> 21; matrix products, arithmetic and copies ran while one was open for 8% -> 4% of each run, Pallas kernels for 7% -> 4%
where the time goes in v5:
time: 213 us; the launch traced here: 212 us
  waiting for transfers between devices  86 us (40%)
  starting transfers between devices  71.7 us (34%)
  local copies, waits for them, and re-layouts  22.9 us (11%)
  Pallas kernels  22 us (10%)
  other arithmetic  8.11 us (4%)
    ppermute x42, waiting for transfers between devices, swap(): return lax.ppermute(block, axis, [(i, i ^ step) for i in range(size)])  84.5 us
    ppermute x42, starting transfers between devices, swap(): return lax.ppermute(block, axis, [(i, i ^ step) for i in range(size)])  62.4 us
    pallas_call x8, Pallas kernels, call(): pl.pallas_call(kernel, out_shape=out_shape, in_specs=[pl.BlockSpec(memory...  22 us
    unnamed x64, local copies, waits for them, and re-layouts  15.6 us
    ppermute x2, starting transfers between devices, halo(): near = lax.ppermute(pick(field, (1 - odd) * (planes - 1)), 'space', inner)  7.05 us
  transfers between devices with their start and end apart: 46, of which 21 were waited for; matrix products, arithmetic and copies ran while one was open for 4% of the time, Pallas kernels for 4%

profile of v5, /device:TPU:0, one launch (start us, length us, event | category | flops | bytes accessed | tf_op | source)
XLA Modules:
  0.0 211.8 jit_solution(10865169553799296662)
XLA Ops:
  1.6 4.1 %collective-permute-start.8 = (bf16[128,256]{1,0:T(8,128)(2,1)S(1)}, bf16[128,256]{1,0:T(8,128)(2,1)S(1)}, u32[]{:S(2)}, u32[]{:S(2)}) collective-permute-start(bf16[128,256]{1,0:T(8,128)(2,1)S(1)} %constant_dynamic-slice_fusion), channel_id=1, source_target_pairs={{0,16},{4,20},{8,24},{12,28},{16,0},{20,4},{24,8},{28,12},{1,17},{... | collective-permute-start | bytes 196616 | tf_op jit(solution)/shard_map/ppermute | solution.py:18
  10.0 3.4 %collective-permute-done.9 = bf16[128,256]{1,0:T(8,128)(2,1)S(1)} collective-permute-done((bf16[128,256]{1,0:T(8,128)(2,1)S(1)}, bf16[128,256]{1,0:T(8,128)(2,1)S(1)}, u32[]{:S(2)}, u32[]{:S(2)}) %collective-permute-start.9) | collective-permute-done | bytes 65568 | tf_op jit(solution)/shard_map/ppermute | solution.py:18
  16.2 3.6 %collective-permute-done.10 = bf16[4,128,256]{2,1,0:T(8,128)(2,1)S(1)} collective-permute-done((bf16[4,128,256]{2,1,0:T(8,128)(2,1)S(1)}, bf16[4,128,256]{2,1,0:T(8,128)(2,1)S(1)}, u32[]{:S(2)}, u32[]{:S(2)}) %collective-permute-start.10) | collective-permute-done | bytes 262176 | tf_op jit(solution)/shard_map/ppermute | solution.py:18
  27.4 8.3 %collective-permute-done.11 = bf16[1024,256]{1,0:T(8,128)(2,1)S(1)} collective-permute-done((bf16[1024,256]{1,0:T(8,128)(2,1)S(1)}, bf16[1024,256]{1,0:T(8,128)(2,1)S(1)}, u32[]{:S(2)}, u32[]{:S(2)}) %collective-permute-start.11) | collective-permute-done | bytes 524320 | tf_op jit(solution)/shard_map/ppermute | solution.py:18
  35.9 5.6 %collective-permute-done.4 = bf16[128,512]{1,0:T(8,128)(2,1)S(1)} collective-permute-done((bf16[128,512]{1,0:T(8,128)(2,1)S(1)}, bf16[128,512]{1,0:T(8,128)(2,1)S(1)}, u32[]{:S(2)}, u32[]{:S(2)}) %collective-permute-start.4) | collective-permute-done | bytes 131104 | tf_op jit(solution)/shard_map/ppermute | solution.py:18
  42.1 2.4 %collective-permute-start.1 = (bf16[128,512]{1,0:T(8,128)(2,1)}, bf16[128,512]{1,0:T(8,128)(2,1)}, u32[]{:S(2)}, u32[]{:S(2)}) collective-permute-start(bf16[128,512]{1,0:T(8,128)(2,1)} %get-tuple-element.179), channel_id=1, source_target_pairs={{0,8},{4,12},{8,0},{12,4},{16,24},{20,28},{24,16},{28,20},{1,9},{5... | collective-permute-start | bytes 393224 | tf_op jit(solution)/shard_map/ppermute | solution.py:18
  46.7 2.4 %collective-permute-done.2 = bf16[128,512]{1,0:T(8,128)(2,1)} collective-permute-done((bf16[128,512]{1,0:T(8,128)(2,1)}, bf16[128,512]{1,0:T(8,128)(2,1)}, u32[]{:S(2)}, u32[]{:S(2)}) %collective-permute-start.2) | collective-permute-done | bytes 131104 | tf_op jit(solution)/shard_map/ppermute | solution.py:18
  49.1 2.4 %collective-permute-done.1 = bf16[128,512]{1,0:T(8,128)(2,1)} collective-permute-done((bf16[128,512]{1,0:T(8,128)(2,1)}, bf16[128,512]{1,0:T(8,128)(2,1)}, u32[]{:S(2)}, u32[]{:S(2)}) %collective-permute-start.1) | collective-permute-done | bytes 131104 | tf_op jit(solution)/shard_map/ppermute | solution.py:18
  51.7 4.1 %shard_map.83 = (bf16[8,512,128]{2,1,0:T(8,128)(2,1)S(1)}, bf16[512,128]{1,0:T(8,128)(2,1)}, bf16[512,128]{1,0:T(8,128)(2,1)}, bf16[512,128]{1,0:T(8,128)(2,1)},...) fusion(bf16[8,512,128]{2,1,0:T(8,128)(2,1)S(1)} %broadcast_in_d, ...), kind=kCustom, calls=%fused_computation.34 | custom fusion | flops 1073741824 | bytes 5242888 | tf_op jit(solution)/shard_map/pallas_call | solution.py:195
  60.6 2.4 %collective-permute-start.17 = (bf16[512,128]{1,0:T(8,128)(2,1)}, bf16[512,128]{1,0:T(8,128)(2,1)S(1)}, u32[]{:S(2)}, u32[]{:S(2)}) collective-permute-start(bf16[512,128]{1,0:T(8,128)(2,1)} %get-tuple-element.155), channel_id=1, source_target_pairs={{0,20},{4,16},{8,28},{12,24},{16,4},{20,0},{24,12},{28,8},{1,21},{... | collective-permute-start | bytes 393224 | tf_op jit(solution)/shard_map/ppermute | solution.py:18
  63.0 2.6 %collective-permute-start.18 = (bf16[512,128]{1,0:T(8,128)(2,1)}, bf16[512,128]{1,0:T(8,128)(2,1)S(1)}, u32[]{:S(2)}, u32[]{:S(2)}) collective-permute-start(bf16[512,128]{1,0:T(8,128)(2,1)} %get-tuple-element.157), channel_id=1, source_target_pairs={{0,24},{4,28},{8,16},{12,20},{16,8},{20,12},{24,0},{28,4},{1,25},{... | collective-permute-start | bytes 393224 | tf_op jit(solution)/shard_map/ppermute | solution.py:18
  68.5 9.2 %collective-permute-done.16 = bf16[512,128]{1,0:T(8,128)(2,1)S(1)} collective-permute-done((bf16[512,128]{1,0:T(8,128)(2,1)}, bf16[512,128]{1,0:T(8,128)(2,1)S(1)}, u32[]{:S(2)}, u32[]{:S(2)}) %collective-permute-start.16) | collective-permute-done | bytes 131104 | tf_op jit(solution)/shard_map/ppermute | solution.py:18
  77.8 3.9 %collective-permute-done.17 = bf16[512,128]{1,0:T(8,128)(2,1)S(1)} collective-permute-done((bf16[512,128]{1,0:T(8,128)(2,1)}, bf16[512,128]{1,0:T(8,128)(2,1)S(1)}, u32[]{:S(2)}, u32[]{:S(2)}) %collective-permute-start.17) | collective-permute-done | bytes 131104 | tf_op jit(solution)/shard_map/ppermute | solution.py:18
  87.8 4.0 %shard_map.75 = (bf16[2,1024,128]{2,1,0:T(8,128)(2,1)S(1)}, bf16[128,2048]{1,0:T(8,128)(2,1)S(1)}) custom-call(bf16[4,1024,128]{2,1,0:T(8,128)(2,1)S(1)} %bitcast.93, bf16[1024,128]{1,0:T(8,128)(2,1)S(1)} %get-tuple-element.191.before, bf16[1024,128]{1,0:T(8,128)(2,1)S(1)} %get-tuple-element.190.after, f32[27,128]{1,0:T(8,128)S(1)} %bitcast.102, ...), custom_call_target="tpu_custom_call" | custom-call | flops 15728640 | bytes 4194304 | tf_op jit(solution)/shard_map/pallas_call | solution.py:195
  92.7 5.8 %collective-permute-start.22 = (bf16[1024,128]{1,0:T(8,128)(2,1)S(1)}, bf16[1024,128]{1,0:T(8,128)(2,1)S(1)}, u32[]{:S(2)}, u32[]{:S(2)}) collective-permute-start(bf16[1024,128]{1,0:T(8,128)(2,1)S(1)} %get-tuple-element.189), channel_id=1, source_target_pairs={{0,1},{1,0},{2,3},{3,2},{4,5},{5,4},{6,7},{7,6},{8,9},{9,8},{10,11... | collective-permute-start | bytes 786440 | tf_op jit(solution)/shard_map/ppermute | solution.py:75
  98.5 3.9 %shard_map.76 = (bf16[2,1024,128]{2,1,0:T(8,128)(2,1)S(1)}, bf16[128,2048]{1,0:T(8,128)(2,1)S(1)}) custom-call(bf16[4,1024,128]{2,1,0:T(8,128)(2,1)S(1)} %bitcast.94, f32[27,128]{1,0:T(8,128)S(1)} %bitcast.103, bf16[128,4096]{1,0:T(8,128)(2,1)S(1)} %bitcast.101, bf16[128,4096]{1,0:T(8,128)(2,1)S(1)} %bitcast.97), custom_call_target="tpu_custom_call" | custom-call | flops 15728640 | bytes 4194304 | tf_op jit(solution)/shard_map/pallas_call | solution.py:195
  108.0 5.4 %collective-permute-start.27 = (bf16[512,128]{1,0:T(8,128)(2,1)S(1)}, bf16[512,128]{1,0:T(8,128)(2,1)S(1)}, u32[]{:S(2)}, u32[]{:S(2)}) collective-permute-start(bf16[512,128]{1,0:T(8,128)(2,1)S(1)} %get-tuple-element.167), channel_id=1, source_target_pairs={{0,16},{4,20},{8,24},{12,28},{16,0},{20,4},{24,8},{28,12},{1,17},{... | collective-permute-start | bytes 393224 | tf_op jit(solution)/shard_map/ppermute | solution.py:18
  113.4 6.5 %collective-permute-done.27.refs_4_ = bf16[512,128]{1,0:T(8,128)(2,1)S(1)} collective-permute-done((bf16[512,128]{1,0:T(8,128)(2,1)S(1)}, bf16[512,128]{1,0:T(8,128)(2,1)S(1)}, u32[]{:S(2)}, u32[]{:S(2)}) %collective-permute-start.27) | collective-permute-done | bytes 131104 | tf_op jit(solution)/shard_map/ppermute | solution.py:18
  119.9 5.4 %shard_map.79 = f32[27,128]{1,0:T(8,128)S(1)} custom-call(bf16[4,1024,128]{2,1,0:T(8,128)(2,1)S(1)} %bitcast.95, bf16[1024,128]{1,0:T(8,128)(2,1)S(1)} %get-tuple-element.191.before, bf16[1024,128]{1,0:T(8,128)(2,1)S(1)} %get-tuple-element.190.after, bf16[2,1024,128]{2,1,0:T(8,128)(2,1)S(1)} %get-tuple-element.101.g0, ...), custom_call_target="tpu_custom_call" | custom-call | flops 31457280 | bytes 4194304 | tf_op jit(solution)/shard_map/pallas_call | solution.py:195
  129.2 3.1 %collective-permute-start.26 = (bf16[512,128]{1,0:T(8,128)(2,1)}, bf16[512,128]{1,0:T(8,128)(2,1)S(1)}, u32[]{:S(2)}, u32[]{:S(2)}) collective-permute-start(bf16[512,128]{1,0:T(8,128)(2,1)} %get-tuple-element.168), channel_id=1, source_target_pairs={{0,12},{4,8},{8,4},{12,0},{16,28},{20,24},{24,20},{28,16},{1,13},{... | collective-permute-start | bytes 393224 | tf_op jit(solution)/shard_map/ppermute | solution.py:18
  135.2 3.1 %collective-permute-start.25 = (bf16[512,128]{1,0:T(8,128)(2,1)}, bf16[512,128]{1,0:T(8,128)(2,1)S(1)}, u32[]{:S(2)}, u32[]{:S(2)}) collective-permute-start(bf16[512,128]{1,0:T(8,128)(2,1)} %get-tuple-element.169), channel_id=1, source_target_pairs={{0,8},{4,12},{8,0},{12,4},{16,24},{20,28},{24,16},{28,20},{1,9},{5... | collective-permute-start | bytes 393224 | tf_op jit(solution)/shard_map/ppermute | solution.py:18
  141.1 2.7 %reshape.52 = bf16[128,4,1024]{2,1,0:T(4,128)(2,1)} reshape(bf16[128,4096]{1,0:T(8,128)(2,1)} %pad_maximum_fusion.2) | data formatting | bytes 2097152 | tf_op jit(solution)/shard_map/reshape | solution.py:386
  155.5 2.6 %collective-permute-done.40 = bf16[2,1024,256]{2,1,0:T(8,128)(2,1)S(1)} collective-permute-done((bf16[2,1024,256]{2,1,0:T(8,128)(2,1)S(1)}, bf16[2,1024,256]{2,1,0:T(8,128)(2,1)S(1)}, u32[]{:S(2)}, u32[]{:S(2)}) %collective-permute-start.40) | collective-permute-done | bytes 1048608 | tf_op jit(solution)/shard_map/ppermute | solution.py:18
  158.7 13.6 %collective-permute-done.41 = bf16[1024,256]{1,0:T(8,128)(2,1)S(1)} collective-permute-done((bf16[1024,256]{1,0:T(8,128)(2,1)S(1)}, bf16[1024,256]{1,0:T(8,128)(2,1)S(1)}, u32[]{:S(2)}, u32[]{:S(2)}) %collective-permute-start.41) | collective-permute-done | bytes 524320 | tf_op jit(solution)/shard_map/ppermute | solution.py:18
  173.7 2.7 %shard_map.81 = (bf16[128,512]{1,0:T(8,128)(2,1)S(1)}, bf16[128,512]{1,0:T(8,128)(2,1)S(1)}, bf16[128,512]{1,0:T(8,128)(2,1)S(1)}, bf16[128,512]{1,0:T(8,128)(2,...) custom-call(s32[1]{0:T(128)} %bitcast.turn, ...), custom_call_target="tpu_custom_call" | custom-call | flops 1073741824 | bytes 4194304 | tf_op jit(solution)/shard_map/pallas_call | solution.py:195
  177.4 4.1 %collective-permute-done.42 = bf16[4,128,256]{2,1,0:T(8,128)(2,1)S(1)} collective-permute-done((bf16[4,128,256]{2,1,0:T(8,128)(2,1)S(1)}, bf16[4,128,256]{2,1,0:T(8,128)(2,1)S(1)}, u32[]{:S(2)}, u32[]{:S(2)}) %collective-permute-start.42) | collective-permute-done | bytes 262176 | tf_op jit(solution)/shard_map/ppermute | solution.py:18
  181.7 4.2 %collective-permute-start.45 = (bf16[128,256]{1,0:T(8,128)(2,1)S(1)}, bf16[128,256]{1,0:T(8,128)(2,1)S(1)}, u32[]{:S(2)}, u32[]{:S(2)}) collective-permute-start(bf16[128,256]{1,0:T(8,128)(2,1)S(1)} %get-tuple-element.193), channel_id=1, source_target_pairs={{0,24},{4,28},{8,16},{12,20},{16,8},{20,12},{24,0},{28,4},{1,25},{... | collective-permute-start | bytes 196616 | tf_op jit(solution)/shard_map/ppermute | solution.py:18
  187.6 2.9 %collective-permute-start.36 = (bf16[128,512]{1,0:T(8,128)(2,1)S(1)}, bf16[128,512]{1,0:T(8,128)(2,1)S(1)}, u32[]{:S(2)}, u32[]{:S(2)}) collective-permute-start(bf16[128,512]{1,0:T(8,128)(2,1)S(1)} %get-tuple-element.127), channel_id=1, source_target_pairs={{0,16},{4,20},{8,24},{12,28},{16,0},{20,4},{24,8},{28,12},{1,17},{... | collective-permute-start | bytes 393224 | tf_op jit(solution)/shard_map/ppermute | solution.py:18
  190.8 3.3 %collective-permute-start.38 = (bf16[128,512]{1,0:T(8,128)(2,1)S(1)}, bf16[128,512]{1,0:T(8,128)(2,1)S(1)}, u32[]{:S(2)}, u32[]{:S(2)}) collective-permute-start(bf16[128,512]{1,0:T(8,128)(2,1)S(1)} %get-tuple-element.129), channel_id=1, source_target_pairs={{0,24},{4,28},{8,16},{12,20},{16,8},{20,12},{24,0},{28,4},{1,25},{... | collective-permute-start | bytes 393224 | tf_op jit(solution)/shard_map/ppermute | solution.py:18
  194.1 8.2 %collective-permute-done.44 = bf16[128,256]{1,0:T(8,128)(2,1)S(1)} collective-permute-done((bf16[128,256]{1,0:T(8,128)(2,1)S(1)}, bf16[128,256]{1,0:T(8,128)(2,1)S(1)}, u32[]{:S(2)}, u32[]{:S(2)}) %collective-permute-start.44) | collective-permute-done | bytes 65568 | tf_op jit(solution)/shard_map/ppermute | solution.py:18
  202.2 2.9 %collective-permute-start.39 = (bf16[128,512]{1,0:T(8,128)(2,1)S(1)}, bf16[128,512]{1,0:T(8,128)(2,1)S(1)}, u32[]{:S(2)}, u32[]{:S(2)}) collective-permute-start(bf16[128,512]{1,0:T(8,128)(2,1)S(1)} %get-tuple-element.130), channel_id=1, source_target_pairs={{0,28},{4,24},{8,20},{12,16},{16,12},{20,8},{24,4},{28,0},{1,29},{... | collective-permute-start | bytes 393224 | tf_op jit(solution)/shard_map/ppermute | solution.py:18
  205.8 2.7 %collective-permute-done.37.refs_5_ = bf16[128,512]{1,0:T(8,128)(2,1)S(1)} collective-permute-done((bf16[128,512]{1,0:T(8,128)(2,1)S(1)}, bf16[128,512]{1,0:T(8,128)(2,1)S(1)}, u32[]{:S(2)}, u32[]{:S(2)}) %collective-permute-start.37) | collective-permute-done | bytes 131104 | tf_op jit(solution)/shard_map/ppermute | solution.py:18
  (167 shorter events, 69.3 us)
Async XLA Ops:
  22.1 13.6 %collective-permute-start.11 = (bf16[1024,256]{1,0:T(8,128)(2,1)S(1)}, bf16[1024,256]{1,0:T(8,128)(2,1)S(1)}, u32[]{:S(2)}, u32[]{:S(2)}) collective-permute-start(bf16[1024,256]{1,0:T(8,128)(2,1)S(1)} %bitcast.109), channel_id=1, source_target_pairs={{0,2},{1,3},{2,0},{3,1},{4,6},{5,7},{6,4},{7,5},{8,10},{9,11},{10,... | collective-permute-start | bytes 1572872 | tf_op jit(solution)/shard_map/ppermute | solution.py:18
  23.6 12.2 %collective-permute-start.6 = (bf16[128,512]{1,0:T(8,128)(2,1)S(1)}, bf16[128,512]{1,0:T(8,128)(2,1)S(1)}, u32[]{:S(2)}, u32[]{:S(2)}) collective-permute-start(bf16[128,512]{1,0:T(8,128)(2,1)S(1)} %get-tuple-element.174), channel_id=1, source_target_pairs={{0,28},{4,24},{8,20},{12,16},{16,12},{20,8},{24,4},{28,0},{1,29},{... | collective-permute-start | bytes 393224 | tf_op jit(solution)/shard_map/ppermute | solution.py:18
  25.7 10.1 %collective-permute-start.5 = (bf16[128,512]{1,0:T(8,128)(2,1)S(1)}, bf16[128,512]{1,0:T(8,128)(2,1)S(1)}, u32[]{:S(2)}, u32[]{:S(2)}) collective-permute-start(bf16[128,512]{1,0:T(8,128)(2,1)S(1)} %get-tuple-element.175), channel_id=1, source_target_pairs={{0,24},{4,28},{8,16},{12,20},{16,8},{20,12},{24,0},{28,4},{1,25},{... | collective-permute-start | bytes 393224 | tf_op jit(solution)/shard_map/ppermute | solution.py:18
  27.4 14.1 %collective-permute-start.4 = (bf16[128,512]{1,0:T(8,128)(2,1)S(1)}, bf16[128,512]{1,0:T(8,128)(2,1)S(1)}, u32[]{:S(2)}, u32[]{:S(2)}) collective-permute-start(bf16[128,512]{1,0:T(8,128)(2,1)S(1)} %get-tuple-element.176), channel_id=1, source_target_pairs={{0,20},{4,16},{8,28},{12,24},{16,4},{20,0},{24,12},{28,8},{1,21},{... | collective-permute-start | bytes 393224 | tf_op jit(solution)/shard_map/ppermute | solution.py:18
  41.5 10.0 %collective-permute-start.12 = (bf16[2,1024,256]{2,1,0:T(8,128)(2,1)S(1)}, bf16[2,1024,256]{2,1,0:T(8,128)(2,1)}, u32[]{:S(2)}, u32[]{:S(2)}) collective-permute-start(bf16[2,1024,256]{2,1,0:T(8,128)(2,1)S(1)} %pad_maximum_fusion.refs_8_), channel_id=1, source_target_pairs={{0,1},{1,0},{2,3},{3,2},{4,5},{5,4},{6,7},{7,6},{8,9},{9,8},{10,11... | collective-permute-start | bytes 3145736 | tf_op jit(solution)/shard_map/ppermute | solution.py:18
  42.1 9.4 %collective-permute-start.1 = (bf16[128,512]{1,0:T(8,128)(2,1)}, bf16[128,512]{1,0:T(8,128)(2,1)}, u32[]{:S(2)}, u32[]{:S(2)}) collective-permute-start(bf16[128,512]{1,0:T(8,128)(2,1)} %get-tuple-element.179), channel_id=1, source_target_pairs={{0,8},{4,12},{8,0},{12,4},{16,24},{20,28},{24,16},{28,20},{1,9},{5... | collective-permute-start | bytes 393224 | tf_op jit(solution)/shard_map/ppermute | solution.py:18
  57.1 10.4 %collective-permute-start.14 = (bf16[512,128]{1,0:T(8,128)(2,1)}, bf16[512,128]{1,0:T(8,128)(2,1)S(1)}, u32[]{:S(2)}, u32[]{:S(2)}) collective-permute-start(bf16[512,128]{1,0:T(8,128)(2,1)} %get-tuple-element.149), channel_id=1, source_target_pairs={{0,8},{4,12},{8,0},{12,4},{16,24},{20,28},{24,16},{28,20},{1,9},{5... | collective-permute-start | bytes 393224 | tf_op jit(solution)/shard_map/ppermute | solution.py:18
  57.1 11.4 %collective-permute-start.15 = (bf16[512,128]{1,0:T(8,128)(2,1)}, bf16[512,128]{1,0:T(8,128)(2,1)S(1)}, u32[]{:S(2)}, u32[]{:S(2)}) collective-permute-start(bf16[512,128]{1,0:T(8,128)(2,1)} %get-tuple-element.151), channel_id=1, source_target_pairs={{0,12},{4,8},{8,4},{12,0},{16,28},{20,24},{24,20},{28,16},{1,13},{... | collective-permute-start | bytes 393224 | tf_op jit(solution)/shard_map/ppermute | solution.py:18
  59.2 18.5 %collective-permute-start.16 = (bf16[512,128]{1,0:T(8,128)(2,1)}, bf16[512,128]{1,0:T(8,128)(2,1)S(1)}, u32[]{:S(2)}, u32[]{:S(2)}) collective-permute-start(bf16[512,128]{1,0:T(8,128)(2,1)} %get-tuple-element.153), channel_id=1, source_target_pairs={{0,16},{4,20},{8,24},{12,28},{16,0},{20,4},{24,8},{28,12},{1,17},{... | collective-permute-start | bytes 393224 | tf_op jit(solution)/shard_map/ppermute | solution.py:18
  60.6 21.1 %collective-permute-start.17 = (bf16[512,128]{1,0:T(8,128)(2,1)}, bf16[512,128]{1,0:T(8,128)(2,1)S(1)}, u32[]{:S(2)}, u32[]{:S(2)}) collective-permute-start(bf16[512,128]{1,0:T(8,128)(2,1)} %get-tuple-element.155), channel_id=1, source_target_pairs={{0,20},{4,16},{8,28},{12,24},{16,4},{20,0},{24,12},{28,8},{1,21},{... | collective-permute-start | bytes 393224 | tf_op jit(solution)/shard_map/ppermute | solution.py:18
  63.0 18.7 %collective-permute-start.18 = (bf16[512,128]{1,0:T(8,128)(2,1)}, bf16[512,128]{1,0:T(8,128)(2,1)S(1)}, u32[]{:S(2)}, u32[]{:S(2)}) collective-permute-start(bf16[512,128]{1,0:T(8,128)(2,1)} %get-tuple-element.157), channel_id=1, source_target_pairs={{0,24},{4,28},{8,16},{12,20},{16,8},{20,12},{24,0},{28,4},{1,25},{... | collective-permute-start | bytes 393224 | tf_op jit(solution)/shard_map/ppermute | solution.py:18
  67.5 14.2 %collective-permute-start.19 = (bf16[512,128]{1,0:T(8,128)(2,1)}, bf16[512,128]{1,0:T(8,128)(2,1)S(1)}, u32[]{:S(2)}, u32[]{:S(2)}) collective-permute-start(bf16[512,128]{1,0:T(8,128)(2,1)} %get-tuple-element.159), channel_id=1, source_target_pairs={{0,28},{4,24},{8,20},{12,16},{16,12},{20,8},{24,4},{28,0},{1,29},{... | collective-permute-start | bytes 393224 | tf_op jit(solution)/shard_map/ppermute | solution.py:18
  91.8 12.8 %collective-permute-start.23 = (bf16[1024,128]{1,0:T(8,128)(2,1)S(1)}, bf16[1024,128]{1,0:T(8,128)(2,1)S(1)}, u32[]{:S(2)}, u32[]{:S(2)}) collective-permute-start(bf16[1024,128]{1,0:T(8,128)(2,1)S(1)} %get-tuple-element.188), channel_id=1, source_target_pairs={{1,2},{2,1},{5,6},{6,5},{9,10},{10,9},{13,14},{14,13},{17,18},{18,... | collective-permute-start | bytes 786440 | tf_op jit(solution)/shard_map/ppermute | solution.py:76
  92.7 12.0 %collective-permute-start.22 = (bf16[1024,128]{1,0:T(8,128)(2,1)S(1)}, bf16[1024,128]{1,0:T(8,128)(2,1)S(1)}, u32[]{:S(2)}, u32[]{:S(2)}) collective-permute-start(bf16[1024,128]{1,0:T(8,128)(2,1)S(1)} %get-tuple-element.189), channel_id=1, source_target_pairs={{0,1},{1,0},{2,3},{3,2},{4,5},{5,4},{6,7},{7,6},{8,9},{9,8},{10,11... | collective-permute-start | bytes 786440 | tf_op jit(solution)/shard_map/ppermute | solution.py:75
  108.0 11.8 %collective-permute-start.27 = (bf16[512,128]{1,0:T(8,128)(2,1)S(1)}, bf16[512,128]{1,0:T(8,128)(2,1)S(1)}, u32[]{:S(2)}, u32[]{:S(2)}) collective-permute-start(bf16[512,128]{1,0:T(8,128)(2,1)S(1)} %get-tuple-element.167), channel_id=1, source_target_pairs={{0,16},{4,20},{8,24},{12,28},{16,0},{20,4},{24,8},{28,12},{1,17},{... | collective-permute-start | bytes 393224 | tf_op jit(solution)/shard_map/ppermute | solution.py:18
  125.3 9.3 %collective-permute-start.30 = (bf16[512,128]{1,0:T(8,128)(2,1)S(1)}, bf16[512,128]{1,0:T(8,128)(2,1)S(1)}, u32[]{:S(2)}, u32[]{:S(2)}) collective-permute-start(bf16[512,128]{1,0:T(8,128)(2,1)S(1)} %get-tuple-element.164), channel_id=1, source_target_pairs={{0,28},{4,24},{8,20},{12,16},{16,12},{20,8},{24,4},{28,0},{1,29},{... | collective-permute-start | bytes 393224 | tf_op jit(solution)/shard_map/ppermute | solution.py:18
  127.1 17.4 %collective-permute-start.29 = (bf16[512,128]{1,0:T(8,128)(2,1)}, bf16[512,128]{1,0:T(8,128)(2,1)S(1)}, u32[]{:S(2)}, u32[]{:S(2)}) collective-permute-start(bf16[512,128]{1,0:T(8,128)(2,1)} %get-tuple-element.165), channel_id=1, source_target_pairs={{0,24},{4,28},{8,16},{12,20},{16,8},{20,12},{24,0},{28,4},{1,25},{... | collective-permute-start | bytes 393224 | tf_op jit(solution)/shard_map/ppermute | solution.py:18
  129.2 15.9 %collective-permute-start.28 = (bf16[512,128]{1,0:T(8,128)(2,1)}, bf16[512,128]{1,0:T(8,128)(2,1)S(1)}, u32[]{:S(2)}, u32[]{:S(2)}) collective-permute-start(bf16[512,128]{1,0:T(8,128)(2,1)} %get-tuple-element.166), channel_id=1, source_target_pairs={{0,20},{4,16},{8,28},{12,24},{16,4},{20,0},{24,12},{28,8},{1,21},{... | collective-permute-start | bytes 393224 | tf_op jit(solution)/shard_map/ppermute | solution.py:18
  129.2 16.6 %collective-permute-start.26 = (bf16[512,128]{1,0:T(8,128)(2,1)}, bf16[512,128]{1,0:T(8,128)(2,1)S(1)}, u32[]{:S(2)}, u32[]{:S(2)}) collective-permute-start(bf16[512,128]{1,0:T(8,128)(2,1)} %get-tuple-element.168), channel_id=1, source_target_pairs={{0,12},{4,8},{8,4},{12,0},{16,28},{20,24},{24,20},{28,16},{1,13},{... | collective-permute-start | bytes 393224 | tf_op jit(solution)/shard_map/ppermute | solution.py:18
  135.2 11.2 %collective-permute-start.25 = (bf16[512,128]{1,0:T(8,128)(2,1)}, bf16[512,128]{1,0:T(8,128)(2,1)S(1)}, u32[]{:S(2)}, u32[]{:S(2)}) collective-permute-start(bf16[512,128]{1,0:T(8,128)(2,1)} %get-tuple-element.169), channel_id=1, source_target_pairs={{0,8},{4,12},{8,0},{12,4},{16,24},{20,28},{24,16},{28,20},{1,9},{5... | collective-permute-start | bytes 393224 | tf_op jit(solution)/shard_map/ppermute | solution.py:18
  138.4 8.7 %collective-permute-start.24 = (bf16[512,128]{1,0:T(8,128)(2,1)S(1)}, bf16[512,128]{1,0:T(8,128)(2,1)S(1)}, u32[]{:S(2)}, u32[]{:S(2)}) collective-permute-start(bf16[512,128]{1,0:T(8,128)(2,1)S(1)} %get-tuple-element.170), channel_id=1, source_target_pairs={{0,4},{4,0},{8,12},{12,8},{16,20},{20,16},{24,28},{28,24},{1,5},{5... | collective-permute-start | bytes 393224 | tf_op jit(solution)/shard_map/ppermute | solution.py:18
  158.2 14.0 %collective-permute-start.41 = (bf16[1024,256]{1,0:T(8,128)(2,1)S(1)}, bf16[1024,256]{1,0:T(8,128)(2,1)S(1)}, u32[]{:S(2)}, u32[]{:S(2)}) collective-permute-start(bf16[1024,256]{1,0:T(8,128)(2,1)S(1)} %fusion), channel_id=1, source_target_pairs={{0,2},{1,3},{2,0},{3,1},{4,6},{5,7},{6,4},{7,5},{8,10},{9,11},{10,... | collective-permute-start | bytes 1572872 | tf_op jit(solution)/shard_map/ppermute | solution.py:18
  172.5 9.0 %collective-permute-start.42 = (bf16[4,128,256]{2,1,0:T(8,128)(2,1)S(1)}, bf16[4,128,256]{2,1,0:T(8,128)(2,1)S(1)}, u32[]{:S(2)}, u32[]{:S(2)}) collective-permute-start(bf16[4,128,256]{2,1,0:T(8,128)(2,1)S(1)} %fusion.3), channel_id=1, source_target_pairs={{0,4},{4,0},{8,12},{12,8},{16,20},{20,16},{24,28},{28,24},{1,5},{5... | collective-permute-start | bytes 786440 | tf_op jit(solution)/shard_map/ppermute | solution.py:18
  176.4 10.0 %collective-permute-start.33 = (bf16[128,512]{1,0:T(8,128)(2,1)S(1)}, bf16[128,512]{1,0:T(8,128)(2,1)S(1)}, u32[]{:S(2)}, u32[]{:S(2)}) collective-permute-start(bf16[128,512]{1,0:T(8,128)(2,1)S(1)} %get-tuple-element.124), channel_id=1, source_target_pairs={{0,4},{4,0},{8,12},{12,8},{16,20},{20,16},{24,28},{28,24},{1,5},{5... | collective-permute-start | bytes 393224 | tf_op jit(solution)/shard_map/ppermute | solution.py:18
  177.4 10.2 %collective-permute-start.34 = (bf16[128,512]{1,0:T(8,128)(2,1)S(1)}, bf16[128,512]{1,0:T(8,128)(2,1)S(1)}, u32[]{:S(2)}, u32[]{:S(2)}) collective-permute-start(bf16[128,512]{1,0:T(8,128)(2,1)S(1)} %get-tuple-element.125), channel_id=1, source_target_pairs={{0,8},{4,12},{8,0},{12,4},{16,24},{20,28},{24,16},{28,20},{1,9},{5... | collective-permute-start | bytes 393224 | tf_op jit(solution)/shard_map/ppermute | solution.py:18
  181.6 9.0 %collective-permute-start.43 = (bf16[128,256]{1,0:T(8,128)(2,1)S(1)}, bf16[128,256]{1,0:T(8,128)(2,1)S(1)}, u32[]{:S(2)}, u32[]{:S(2)}) collective-permute-start(bf16[128,256]{1,0:T(8,128)(2,1)S(1)} %get-tuple-element.192), channel_id=1, source_target_pairs={{0,8},{4,12},{8,0},{12,4},{16,24},{20,28},{24,16},{28,20},{1,9},{5... | collective-permute-start | bytes 196616 | tf_op jit(solution)/shard_map/ppermute | solution.py:18
  181.7 9.1 %collective-permute-start.45 = (bf16[128,256]{1,0:T(8,128)(2,1)S(1)}, bf16[128,256]{1,0:T(8,128)(2,1)S(1)}, u32[]{:S(2)}, u32[]{:S(2)}) collective-permute-start(bf16[128,256]{1,0:T(8,128)(2,1)S(1)} %get-tuple-element.193), channel_id=1, source_target_pairs={{0,24},{4,28},{8,16},{12,20},{16,8},{20,12},{24,0},{28,4},{1,25},{... | collective-permute-start | bytes 196616 | tf_op jit(solution)/shard_map/ppermute | solution.py:18
  185.9 16.4 %collective-permute-start.44 = (bf16[128,256]{1,0:T(8,128)(2,1)S(1)}, bf16[128,256]{1,0:T(8,128)(2,1)S(1)}, u32[]{:S(2)}, u32[]{:S(2)}) collective-permute-start(bf16[128,256]{1,0:T(8,128)(2,1)S(1)} %get-tuple-element.194), channel_id=1, source_target_pairs={{0,16},{4,20},{8,24},{12,28},{16,0},{20,4},{24,8},{28,12},{1,17},{... | collective-permute-start | bytes 196616 | tf_op jit(solution)/shard_map/ppermute | solution.py:18
  186.3 19.5 %collective-permute-start.35 = (bf16[128,512]{1,0:T(8,128)(2,1)S(1)}, bf16[128,512]{1,0:T(8,128)(2,1)S(1)}, u32[]{:S(2)}, u32[]{:S(2)}) collective-permute-start(bf16[128,512]{1,0:T(8,128)(2,1)S(1)} %get-tuple-element.126), channel_id=1, source_target_pairs={{0,12},{4,8},{8,4},{12,0},{16,28},{20,24},{24,20},{28,16},{1,13},{... | collective-permute-start | bytes 393224 | tf_op jit(solution)/shard_map/ppermute | solution.py:18
  187.6 18.2 %collective-permute-start.36 = (bf16[128,512]{1,0:T(8,128)(2,1)S(1)}, bf16[128,512]{1,0:T(8,128)(2,1)S(1)}, u32[]{:S(2)}, u32[]{:S(2)}) collective-permute-start(bf16[128,512]{1,0:T(8,128)(2,1)S(1)} %get-tuple-element.127), channel_id=1, source_target_pairs={{0,16},{4,20},{8,24},{12,28},{16,0},{20,4},{24,8},{28,12},{1,17},{... | collective-permute-start | bytes 393224 | tf_op jit(solution)/shard_map/ppermute | solution.py:18
  190.6 18.0 %collective-permute-start.37 = (bf16[128,512]{1,0:T(8,128)(2,1)S(1)}, bf16[128,512]{1,0:T(8,128)(2,1)S(1)}, u32[]{:S(2)}, u32[]{:S(2)}) collective-permute-start(bf16[128,512]{1,0:T(8,128)(2,1)S(1)} %get-tuple-element.128), channel_id=1, source_target_pairs={{0,20},{4,16},{8,28},{12,24},{16,4},{20,0},{24,12},{28,8},{1,21},{... | collective-permute-start | bytes 393224 | tf_op jit(solution)/shard_map/ppermute | solution.py:18
  190.8 17.8 %collective-permute-start.38 = (bf16[128,512]{1,0:T(8,128)(2,1)S(1)}, bf16[128,512]{1,0:T(8,128)(2,1)S(1)}, u32[]{:S(2)}, u32[]{:S(2)}) collective-permute-start(bf16[128,512]{1,0:T(8,128)(2,1)S(1)} %get-tuple-element.129), channel_id=1, source_target_pairs={{0,24},{4,28},{8,16},{12,20},{16,8},{20,12},{24,0},{28,4},{1,25},{... | collective-permute-start | bytes 393224 | tf_op jit(solution)/shard_map/ppermute | solution.py:18
  (45 other events, 164.0 us)

commit v6 on v5

v6 whole, which is shorter than its diff:
```python
import functools
import math

import jax
import jax.numpy as jnp
from jax import lax
from jax.experimental import pallas as pl
from jax.experimental.pallas import tpu as pltpu
from jax.sharding import PartitionSpec as P

WW = 64
BF = jnp.bfloat16
F32 = jnp.float32
VM = 16


def swap(block, axis, step):
    size = lax.axis_size(axis)
    return lax.ppermute(block, axis, [(i, i ^ step) for i in range(size)])


def exchange(pieces, axis):
    size = len(pieces)
    order = list(range(size // 2, size)) + list(range(1, size // 2))
    got = {0: pieces[0]}
    for s in order:
        got[s] = swap(pieces[s], axis, s)
    return [got[s] for s in range(size)]


def place(pieces, shift):
    out = jnp.zeros((len(pieces),) + pieces[0].shape, pieces[0].dtype)
    for s, piece in enumerate(pieces):
        out = lax.dynamic_update_index_in_dim(out, piece, shift ^ s, 0)
    return out


def pick(blocks, index):
    return lax.dynamic_index_in_dim(blocks, index, 0, keepdims=False)


def join(parts, after, us=0.4):
    def kernel(*refs):
        for k in range(len(parts)):
            refs[-1][k] = refs[k][...]

    shape = jax.ShapeDtypeStruct((len(parts),) + parts[0].shape, parts[0].dtype)
    return call(kernel, shape, [], *parts, us=us, after=after)


def gather_weights(mixing, me_space, send, pieces):
    rows, cols = mixing.shape
    nf, ns = lax.axis_size("filter"), lax.axis_size("space")
    share, pairs = cols // ns, ns // 2
    own = lax.dynamic_slice_in_dim(mixing, me_space * share, share, axis=1)
    even = join([own] + [swap(own, "filter", s) for s in range(2, nf, 2)], send[nf // 2 :])
    first = [even] + [swap(even, "space", s) for s in range(2, ns, 2)]
    odd = join([swap(even, "filter", 1)], pieces[nf // 2 : nf // 2 + 2])[0]
    second = [odd] + [swap(odd, "space", s) for s in range(2, ns, 2)]

    def kernel(*refs):
        for k in range(pairs):
            for r in range(nf):
                source = refs[pairs * (r % 2) + k]
                refs[-1][k, r * rows : (r + 1) * rows, :] = source[r // 2]

    shape = jax.ShapeDtypeStruct((pairs, nf * rows, share), BF)
    after = pieces[nf // 2 + 2 : nf // 2 + 3]
    held = call(kernel, shape, [], *first, *second, us=0.6, after=after)
    return held, swap(held, "space", 1)


def scatter_rest(mine, theirs, rows, back, pieces):
    nf, pairs, share = lax.axis_size("filter"), len(mine), theirs.shape[2]

    def near_half(*refs):
        kept, sent = refs[-pairs], refs[len(refs) - pairs + 1 :]
        got = refs[pairs]
        kept[...] = refs[0][...] + got[0].astype(F32)
        for k in range(1, pairs):
            sent[k - 1][...] = (refs[k][...] + got[k].astype(F32)).astype(BF)

    flat = jax.ShapeDtypeStruct((nf * rows, share), BF)
    shapes = [jax.ShapeDtypeStruct((nf * rows, share), F32)] + [flat] * (pairs - 1)
    half = call(near_half, shapes, [], *mine, theirs, us=0.8, after=(back,))
    got = [swap(half[k], "space", 2 * k) for k in range(1, pairs)]

    def rows_half(*refs):
        kept, sent = refs[-2:]
        for r in range(nf):
            row = slice(r * rows, (r + 1) * rows)
            total = refs[0][row, :]
            for k in range(1, pairs):
                total = total + refs[k][row, :].astype(F32)
            if r % 2:
                sent[r // 2] = total.astype(BF)
            else:
                kept[r // 2] = total

    shapes = (
        jax.ShapeDtypeStruct((nf // 2, rows, share), F32),
        jax.ShapeDtypeStruct((nf // 2, rows, share), BF),
    )
    after = pieces[nf // 2 : nf // 2 + 2]
    kept, sent = call(rows_half, shapes, [], half[0], *got, us=0.6, after=after)
    got = swap(sent, "filter", 1)

    def rows_rest(*refs):
        kept, sent = refs[-nf // 2], refs[len(refs) - nf // 2 + 1 :]
        kept[...] = refs[0][0] + refs[1][0].astype(F32)
        for k in range(1, nf // 2):
            sent[k - 1][...] = (refs[0][k] + refs[1][k].astype(F32)).astype(BF)

    one = jax.ShapeDtypeStruct((rows, share), BF)
    shapes = [jax.ShapeDtypeStruct((rows, share), F32)] + [one] * (nf // 2 - 1)
    after = pieces[nf // 2 + 2 : nf // 2 + 3]
    rest = call(rows_rest, shapes, [], kept, got, us=0.4, after=after)
    result = rest[0]
    for k in range(1, nf // 2):
        result = result + swap(rest[k], "filter", 2 * k).astype(F32)
    return result


def halo(near, far):
    size = lax.axis_size("space")
    inner = [(i, i ^ 1) for i in range(size)]
    outer = [(i, ((i + 1) ^ 1) - 1) for i in range(1, size - 1)]
    return lax.ppermute(near, "space", inner), lax.ppermute(far, "space", outer)


def fill(pad_ref, plane, source):
    rows, width, ch = pad_ref.shape[1] - 2, pad_ref.shape[2], pad_ref.shape[3]
    pad_ref[plane, 1 : rows + 1] = source.astype(F32).reshape(rows, width, ch)
    pad_ref[plane, 0] = jnp.zeros((width, ch), F32)
    pad_ref[plane, rows + 1] = jnp.zeros((width, ch), F32)


def shifted(value, up):
    width = value.shape[0]
    index = lax.broadcasted_iota(jnp.int32, value.shape, 0)
    if up:
        return jnp.where(index == width - 1, 0.0, pltpu.roll(value, width - 1, 0))
    return jnp.where(index == 0, 0.0, pltpu.roll(value, 1, 0))


def conv_row(pad_ref, taps_ref, plane, row, flip):
    sums = [None, None, None]
    for a in range(3):
        for b in range(3):
            da, db = (1 - a, 1 - b) if flip else (a - 1, b - 1)
            line = pad_ref[plane + da, row + db]
            for e in range(3):
                term = taps_ref[pl.ds(a * 9 + b * 3 + e, 1), :] * line
                sums[e] = term if sums[e] is None else sums[e] + term
    lo, hi = (sums[2], sums[0]) if flip else (sums[0], sums[2])
    return sums[1] + shifted(lo, False) + shifted(hi, True)


def load_planes(pad_ref, refs, where, sides, wanted, planes):
    for p in sorted(wanted):
        if p < 0:
            fill(pad_ref, 0, jnp.where(sides[0][0] == 1, sides[1][...], sides[2][...]))
        elif p >= planes:
            fill(pad_ref, planes + 1, jnp.where(sides[0][0] == 1, sides[2][...], sides[1][...]))
        else:
            which, at = where[p]
            fill(pad_ref, p + 1, refs[which][at])


def forward_planes(group, planes, sides, m, taps, vol, up, grad, out, pad):
    wanted = {p + a for p in group for a in (-1, 0, 1)}
    where = {p: (0, p) for p in range(planes)}
    load_planes(pad, (m,), where, sides, wanted, planes)
    lanes, flat = 2 * WW, m.shape[1]
    for k, p in enumerate(group):

        def strip(f, carry, k=k, p=p):
            lines = [conv_row(pad, taps, p + 1, f * 2 + 1 + r, False) for r in range(2)]
            spatial = jnp.concatenate(lines, axis=0)
            sig = 1.0 / (1.0 + jnp.exp(-spatial))
            cells = pl.ds(pl.multiple_of(f * lanes, lanes), lanes)
            source = pl.ds(pl.multiple_of(p * flat + f * lanes, lanes), lanes)
            target = pl.ds(pl.multiple_of(k * flat + f * lanes, lanes), lanes)
            cot = jnp.transpose(up[:, source].astype(F32))
            slope = sig * (1.0 + spatial * (1.0 - sig))
            grad[k, cells, :] = (cot * slope).astype(BF)
            silu = jnp.transpose(spatial * sig)
            out[:, target] = (vol[:, source].astype(F32) + silu).astype(BF)
            return carry

        lax.fori_loop(0, flat // lanes, strip, 0)


def forward_middle(group, planes, m, taps, vol, up, grad, out, pad):
    forward_planes(group, planes, (), m, taps, vol, up, grad, out, pad)


def forward_edges(planes, odd, m, near, far, taps, vol, up, grad, out, to_near, to_far, pad):
    sides = (odd, near, far)
    forward_planes((0, planes - 1), planes, sides, m, taps, vol, up, grad, out, pad)
    to_near[...] = jnp.where(odd[0] == 1, grad[0], grad[1])
    to_far[...] = jnp.where(odd[0] == 1, grad[1], grad[0])


def backward_planes(group, where, planes, sides, g0, g1, taps, put, pad):
    wanted = {p + a for p in group for a in (-1, 0, 1)}
    load_planes(pad, (g0, g1), where, sides, wanted, planes)
    lanes, flat = 2 * WW, g0.shape[1]
    for k, p in enumerate(group):

        def strip(f, carry, k=k, p=p):
            lines = [conv_row(pad, taps, p + 1, f * 2 + 1 + r, True) for r in range(2)]
            put(k, p, pl.multiple_of(f * lanes, lanes), jnp.concatenate(lines, axis=0).astype(BF))
            return carry

        lax.fori_loop(0, flat // lanes, strip, 0)


def backward_middle(group, where, planes, g0, g1, taps, out, pad):
    def put(k, p, cell, value):
        out[k, pl.ds(cell, value.shape[0]), :] = value

    backward_planes(group, where, planes, (), g0, g1, taps, put, pad)


def backward_edges(where, planes, me, odd, g0, g1, near, far, taps, inner, *refs):
    out, (whole, pad) = refs[:-2], refs[-2:]
    flat = g0.shape[1]

    def put(k, p, cell, value):
        whole[pl.ds(p * flat + cell, value.shape[0]), :] = value

    backward_planes((0, planes - 1), where, planes, (odd, near, far), g0, g1, taps, put, pad)
    for k in range(1, planes - 1):
        whole[k * flat : (k + 1) * flat, :] = inner[k - 1]
    blk = out[0].shape[0]
    for s in range(len(out)):
        out[s][...] = whole[pl.ds(pl.multiple_of((me[0] ^ s) * blk, blk), blk), :]


def taps_kernel(where_grad, planes, norm, odd, m, near, far, g0, g1, o0, o1, *refs):
    out, output, pad, gpad = refs[-4:]
    flat = m.shape[1]
    output[:, :flat] = o0[:, :flat]
    output[:, flat:-flat] = o1[...]
    output[:, -flat:] = o0[:, flat:]
    where = {p: (0, p) for p in range(planes)}
    load_planes(pad, (m,), where, (odd, near, far), range(-1, planes + 1), planes)
    load_planes(gpad, (g0, g1), where_grad, (), range(planes), planes)
    rows, width, ch = pad.shape[1] - 2, pad.shape[2], pad.shape[3]
    sums = tuple(jnp.zeros((8, ch), F32) for _ in range(27))

    def line(at, sums):
        p, h = at // rows, at % rows
        sums = list(sums)
        own = gpad[p + 1, h + 1]
        turned = (shifted(own, True), own, shifted(own, False))
        for a in range(3):
            for b in range(3):
                field = pad[p + a, h + b]
                for e in range(3):
                    prod = (turned[e] * field).reshape(width // 8, 8, ch)
                    sums[a * 9 + b * 3 + e] = sums[a * 9 + b * 3 + e] + jnp.sum(prod, axis=0)
        return tuple(sums)

    sums = lax.fori_loop(0, planes * rows, line, sums)
    for k in range(27):
        out[k : k + 1, :] = jnp.sum(sums[k], axis=0, keepdims=True) * norm


def call(kernel, out_shape, scratch, *args, us=1.0, vmem=VM, fetched=0, after=(), kept_out=()):
    def place_of(k, arg):
        if k >= len(args) - fetched:
            return pltpu.HBM
        return pltpu.SMEM if arg.dtype == jnp.int32 else pltpu.VMEM

    specs = [pl.BlockSpec(memory_space=place_of(k, arg)) for k, arg in enumerate(args)]
    many = isinstance(out_shape, (list, tuple))
    out_specs = [
        pl.BlockSpec(memory_space=pltpu.HBM if k in kept_out else pltpu.VMEM)
        for k in range(len(out_shape) if many else 1)
    ]

    def wrapped(*refs):
        kernel(*refs[: len(args)], *refs[len(args) + len(after) :])

    return pl.pallas_call(
        wrapped,
        out_shape=out_shape,
        in_specs=specs + [pl.BlockSpec(memory_space=pl.ANY)] * len(after),
        out_specs=type(out_shape)(out_specs) if many else out_specs[0],
        scratch_shapes=scratch,
        compiler_params=pltpu.CompilerParams(vmem_limit_bytes=vmem * 1024 * 1024),
        cost_estimate=pl.CostEstimate(
            flops=int(us * 1.15e9), bytes_accessed=1024 * 1024, transcendentals=0
        ),
    )(*args, *after)


def fetch(pieces, held, sems):
    copies = [pltpu.make_async_copy(p, held.at[t], sems.at[t]) for t, p in enumerate(pieces)]
    for copy in copies:
        copy.start()
    return copies


def fetched(pieces):
    nf = len(pieces)
    return [pltpu.VMEM((nf,) + pieces[0].shape, BF), pltpu.SemaphoreType.DMA((nf,))]


def mix_kernel(turn, held, other, *refs):
    nf = (len(refs) - 1) // 2
    pieces, vol_t, out = refs[:nf], refs[nf], refs[nf + 1 :]
    ch = pieces[0].shape[0]
    share = held.shape[2]
    for t, piece in enumerate(pieces):
        lane = pl.ds(pl.multiple_of((turn[0] ^ t) * ch, 128), ch)
        vol_t[:, lane] = jnp.transpose(piece[...])
    for s in range(0, nf, 2):
        total = None
        for v in range(2 * held.shape[0]):
            block = (other if v % 2 else held)[v // 2, s * ch : (s + 2) * ch, :]
            term = lax.dot_general(
                vol_t[:, v * share : (v + 1) * share], block, (((1,), (1,)), ((), ())),
                preferred_element_type=F32,
            )
            total = term if total is None else total + term
        out[s][...] = total[:, :ch].astype(BF)
        out[s + 1][...] = total[:, ch:].astype(BF)


def mix(turn, pieces, held, other, after):
    nf, (ch, blk) = len(pieces), pieces[0].shape
    pairs, rows, share = held.shape
    if ch % 128:
        vol_t = place(pieces, turn[0]).reshape(nf * ch, blk).T
        weights = jnp.stack([held, other], axis=1).reshape(2 * pairs, rows, share)
        out = jnp.einsum(
            "cvi,voi->co", vol_t.reshape(blk, 2 * pairs, share), weights, preferred_element_type=F32
        ).astype(BF)
        return vol_t, [out[:, s * ch : (s + 1) * ch] for s in range(nf)]
    shapes = [jax.ShapeDtypeStruct((blk, nf * ch), BF)] + [jax.ShapeDtypeStruct((blk, ch), BF)] * nf
    got = call(mix_kernel, shapes, [], turn, held, other, *pieces, us=3.0, after=after)
    return got[0], got[1:]


def unmix_kernel(turn, mg, held, other, *refs):
    out, back = refs[:-1], refs[-1]
    nf, ch = len(out), out[0].shape[0]
    share = held.shape[2]
    for v in range(2 * held.shape[0]):
        block = (other if v % 2 else held)[v // 2]
        total = lax.dot_general(
            mg[...], block, (((1,), (0,)), ((), ())), preferred_element_type=F32
        )
        turned = jnp.transpose(total).astype(BF)
        for k in range(share // ch):
            back[v * (share // ch) + k] = turned[k * ch : (k + 1) * ch, :]
    for s in range(nf):
        out[s][...] = back[turn[0] ^ s]


def unmix(turn, mg, held, other, ch):
    blk = mg.shape[0]
    pairs, rows, share = held.shape
    nf = rows // ch
    if ch % 128:
        weights = jnp.stack([held, other], axis=1).reshape(2 * pairs, rows, share)
        out = jnp.einsum("co,voi->vic", mg, weights, preferred_element_type=F32)
        out = out.astype(BF).reshape(nf, ch, blk)
        return [pick(out, turn[0] ^ s) for s in range(nf)]
    shapes = [jax.ShapeDtypeStruct((ch, blk), BF)] * nf
    scratch = [pltpu.VMEM((nf, ch, blk), BF)]
    return call(unmix_kernel, shapes, scratch, turn, mg, held, other, us=2.6)


def weight_products(pieces, vol_t, norm, ns, after):
    nf, (blk, ch) = len(pieces), pieces[0].shape
    share = vol_t.shape[1] // ns
    pairs = ns // 2
    if ch % 128 or share % 128:
        mg = jnp.concatenate(pieces, axis=1)
        part = lax.dot_general(mg, vol_t, (((0,), (0,)), ((), ())), preferred_element_type=F32)
        part = (part * norm).reshape(nf * ch, pairs, 2, share)
        return [part[:, k, 0] for k in range(pairs)], part[:, :, 1].transpose(1, 0, 2).astype(BF), mg

    def kernel(*refs):
        parts, vol, refs = refs[:nf], refs[nf], refs[nf + 1 :]
        mine, (theirs, mg) = refs[:pairs], refs[pairs:]
        for r, part in enumerate(parts):
            row = slice(r * ch, (r + 1) * ch)
            mg[:, row] = part[...]
            turned = jnp.transpose(part[...])
            for v in range(ns):
                total = norm * lax.dot_general(
                    turned, vol[:, v * share : (v + 1) * share], (((1,), (0,)), ((), ())),
                    preferred_element_type=F32,
                )
                if v % 2:
                    theirs[v // 2, row, :] = total.astype(BF)
                else:
                    mine[v // 2][row, :] = total

    shapes = [jax.ShapeDtypeStruct((nf * ch, share), F32)] * pairs
    shapes.append(jax.ShapeDtypeStruct((pairs, nf * ch, share), BF))
    shapes.append(jax.ShapeDtypeStruct((blk, nf * ch), BF))
    got = call(
        kernel, shapes, [], *pieces, vol_t, us=3.0, after=after,
    )
    return got[:-2], got[-2], got[-1]


def assemble_kernel(me, odd, *refs):
    pieces, (out, near, far, sems) = refs[:-4], refs[-4:]
    nf, flat = len(pieces), near.shape[0]
    copies = [
        pltpu.make_async_copy(p, out.at[me[0] ^ s], sems.at[s]) for s, p in enumerate(pieces)
    ]
    for copy in copies:
        copy.start()
    for copy in copies:
        copy.wait()
    blk = pieces[0].shape[0]
    for k in range(flat // blk):
        first = out[k]
        last = out[nf - flat // blk + k]
        near[k * blk : (k + 1) * blk, :] = jnp.where(odd[0] == 1, first, last)
        far[k * blk : (k + 1) * blk, :] = jnp.where(odd[0] == 1, last, first)


def assemble(me, odd, pieces, planes):
    nf, (blk, ch) = len(pieces), pieces[0].shape
    edge = jax.ShapeDtypeStruct((nf * blk // planes, ch), BF)
    shapes = (jax.ShapeDtypeStruct((nf, blk, ch), BF), edge, edge)
    got = call(
        assemble_kernel, shapes, [pltpu.SemaphoreType.DMA((nf,))], me, odd, *pieces,
        us=1.2, fetched=nf,
    )
    return got[0].reshape(planes, nf * blk // planes, ch), got[1], got[2]


def finish_kernel(me, up, *refs):
    pieces, out = refs[:-1], refs[-1]
    blk = pieces[0].shape[1]
    for s, piece in enumerate(pieces):
        lane = pl.ds(pl.multiple_of((me[0] ^ s) * blk, 128), blk)
        out[:, lane] = (up[:, lane].astype(F32) + piece[...].astype(F32)).astype(BF)


def body(volume, mixing, kernel_taps, upstream):
    ch, planes, flat = volume.shape
    height = flat // WW
    nf, ns = lax.axis_size("filter"), lax.axis_size("space")
    me, me_space = lax.axis_index("filter"), lax.axis_index("space")
    total = planes * flat
    blk = total // nf
    norm = 1.0 / math.sqrt(ns * total)
    edges, middle = (0, planes - 1), tuple(range(1, planes - 1))
    groups = (edges, middle)
    turn = jnp.reshape(me ^ (me_space * (nf // ns)), (1,)).astype(jnp.int32)

    odd = jnp.reshape(me_space & 1, (1,)).astype(jnp.int32)
    own = jnp.reshape(me, (1,)).astype(jnp.int32)

    vol = volume.reshape(ch, total)
    send = [lax.dynamic_slice_in_dim(vol, (me ^ s) * blk, blk, axis=1) for s in range(nf)]
    pieces = exchange(send, "filter")
    held, other = gather_weights(mixing, me_space, send, pieces)
    up = upstream.reshape(ch, total)
    vol_t, prod = mix(turn, pieces, held, other, (up,))

    got = exchange(prod, "filter")
    mixed, near, far = assemble(own, odd, got, planes)
    near, far = halo(near, far)

    taps = kernel_taps.T
    pad = pltpu.VMEM((planes + 2, height + 2, WW, ch), F32)

    def grad_shapes(g):
        return (
            jax.ShapeDtypeStruct((len(g), flat, ch), BF),
            jax.ShapeDtypeStruct((ch, len(g) * flat), BF),
        )

    edge = jax.ShapeDtypeStruct((flat, ch), BF)
    grad_middle, out_middle = call(
        functools.partial(forward_middle, middle, planes), grad_shapes(middle), [pad],
        mixed, taps, vol, up, us=4.0,
    )
    grad_edges, out_edges, to_near, to_far = call(
        functools.partial(forward_edges, planes), grad_shapes(edges) + (edge, edge), [pad],
        odd, mixed, near, far, taps, vol, up, us=4.0, after=(grad_middle,),
    )
    grad_near, grad_far = halo(to_near, to_far)
    where = {p: (i, k) for i, g in enumerate(groups) for k, p in enumerate(g)}
    mg_middle = call(
        functools.partial(backward_middle, middle, where, planes),
        jax.ShapeDtypeStruct((len(middle), flat, ch), BF), [pad],
        grad_edges, grad_middle, taps, us=2.3,
    )
    send = call(
        functools.partial(backward_edges, where, planes),
        [jax.ShapeDtypeStruct((blk, ch), BF)] * nf,
        [pltpu.VMEM((total, ch), BF), pad],
        own, odd, grad_edges, grad_middle, grad_near, grad_far, taps, mg_middle,
        us=2.8,
    )
    got = exchange(send, "filter")

    after = got[nf // 2 : nf // 2 + 2]
    taps_grad, output = call(
        functools.partial(taps_kernel, where, planes, norm),
        (jax.ShapeDtypeStruct((27, ch), F32), jax.ShapeDtypeStruct((ch, total), BF)), [pad, pad],
        odd, mixed, near, far, grad_edges, grad_middle, out_edges, out_middle,
        us=5.8, after=after,
    )
    output = output.reshape(ch, planes, flat)

    mine, theirs, mg_all = weight_products(got, vol_t, norm, ns, (taps_grad, output))
    theirs = swap(theirs, "space", 1)
    back = unmix(turn, mg_all, held, other, ch)
    got = exchange(back, "filter")
    mixing_grad = scatter_rest(mine, theirs, ch, back[1], got)
    volume_grad = call(
        finish_kernel, jax.ShapeDtypeStruct((ch, total), BF), [],
        own, up, *got, us=1.6,
    ).reshape(ch, planes, flat)
    step = 1
    while step < ns:
        taps_grad = taps_grad + swap(taps_grad, "space", step)
        step *= 2
    return (output, volume_grad, mixing_grad, taps_grad.T)


def solution(mesh):
    in_specs = (
        P("filter", "space", None),
        P("filter", None),
        P("filter", None),
        P("filter", "space", None),
    )
    out_specs = (
        P("filter", "space", None),
        P("filter", "space", None),
        P("filter", "space"),
        P("filter", None),
    )
    return jax.shard_map(body, mesh=mesh, in_specs=in_specs, out_specs=out_specs, check_vma=False)
```

time: 213 us -> 190 us (0.89)
  waiting for transfers between devices: 86 us -> 67.9 us
  Pallas kernels: 22 us -> 32 us
  other arithmetic: 8.11 us -> 1.3 us
  starting transfers between devices: 71.7 us -> 67.5 us
  local copies, waits for them, and re-layouts: 22.9 us -> 19.9 us
    ppermute x42 -> x43, waiting for transfers between devices: 84.5 us -> 67.9 us  [swap(): return lax.ppermute(block, axis, [(i, i ^ step) for i in range(size)])]
    pallas_call x8 -> x16, Pallas kernels: 22 us -> 32 us  [call(): pl.pallas_call(wrapped, out_shape=out_shape, in_specs=specs + [pl.BlockSp...]
    pallas_call x1 -> x0, other arithmetic: 4.05 us -> none  [call(): pl.pallas_call(kernel, out_shape=out_shape, in_specs=[pl.BlockSpec(memory...]
    ppermute x4, starting transfers between devices: 9.28 us -> 5.23 us  [the longest x2 3.71 us: halo(): lax.ppermute(near, 'space', inner)]
    unnamed x64 -> x40, local copies, waits for them, and re-layouts: 15.6 us -> 16.7 us
    ppermute x42 -> x43, starting transfers between devices: 62.4 us -> 62.2 us  [swap(): return lax.ppermute(block, axis, [(i, i ^ step) for i in range(size)])]
  transfers between devices with their start and end apart: 46 -> 47, of which waited for: 21 -> 21; matrix products, arithmetic and copies ran while one was open for 4% -> 4% of each run, Pallas kernels for 4% -> 8%
where the time goes in v6:
time: 190 us
  waiting for transfers between devices  67.9 us (36%)
  starting transfers between devices  67.5 us (36%)
  Pallas kernels  32 us (17%)
  local copies, waits for them, and re-layouts  19.9 us (10%)
    ppermute x43, waiting for transfers between devices, swap(): return lax.ppermute(block, axis, [(i, i ^ step) for i in range(size)])  67.9 us
    ppermute x43, starting transfers between devices, swap(): return lax.ppermute(block, axis, [(i, i ^ step) for i in range(size)])  62.2 us
    pallas_call x16, Pallas kernels, call(): pl.pallas_call(wrapped, out_shape=out_shape, in_specs=specs + [pl.BlockSp...  32 us
    unnamed x40, local copies, waits for them, and re-layouts  16.7 us
  transfers between devices with their start and end apart: 47, of which 21 were waited for; matrix products, arithmetic and copies ran while one was open for 4% of the time, Pallas kernels for 8%

profile of v6, /device:TPU:0, one launch (start us, length us, event | category | flops | bytes accessed | tf_op | source)
XLA Modules:
  0.0 189.6 jit_solution(15054689978633492145)
XLA Ops:
  1.6 3.1 %collective-permute-start = (bf16[128,256]{1,0:T(8,128)(2,1)S(1)}, bf16[128,256]{1,0:T(8,128)(2,1)S(1)}, u32[]{:S(2)}, u32[]{:S(2)}) collective-permute-start(bf16[128,256]{1,0:T(8,128)(2,1)S(1)} %constant_dynamic-slice_fusion.8.refs_0_), channel_id=1, source_target_pairs={{0,8},{4,12},{8,0},{12,4},{16,24},{20,28},{24,16},{28,20},{1,9},{5... | collective-permute-start | bytes 196616 | tf_op jit(solution)/shard_map/ppermute | solution.py:19
  4.7 2.6 %collective-permute-start.1 = (bf16[128,256]{1,0:T(8,128)(2,1)S(1)}, bf16[128,256]{1,0:T(8,128)(2,1)S(1)}, u32[]{:S(2)}, u32[]{:S(2)}) collective-permute-start(bf16[128,256]{1,0:T(8,128)(2,1)S(1)} %constant_dynamic-slice_fusion.8.refs_0_), channel_id=1, source_target_pairs={{0,16},{4,20},{8,24},{12,28},{16,0},{20,4},{24,8},{28,12},{1,17},{... | collective-permute-start | bytes 196616 | tf_op jit(solution)/shard_map/ppermute | solution.py:19
  9.7 2.2 %collective-permute-done.1.refs_2_ = bf16[128,256]{1,0:T(8,128)(2,1)S(1)} collective-permute-done((bf16[128,256]{1,0:T(8,128)(2,1)S(1)}, bf16[128,256]{1,0:T(8,128)(2,1)S(1)}, u32[]{:S(2)}, u32[]{:S(2)}) %collective-permute-start.1) | collective-permute-done | bytes 65568 | tf_op jit(solution)/shard_map/ppermute | solution.py:19
  19.3 5.6 %collective-permute-done.5.refs_1_.refs_7_ = bf16[128,512]{1,0:T(8,128)(2,1)S(1)} collective-permute-done((bf16[128,512]{1,0:T(8,128)(2,1)S(1)}, bf16[128,512]{1,0:T(8,128)(2,1)S(1)}, u32[]{:S(2)}, u32[]{:S(2)}) %collective-permute-start.5) | collective-permute-done | bytes 131104 | tf_op jit(solution)/shard_map/ppermute | solution.py:19
  25.0 2.6 %collective-permute-done.6.refs_2_.refs_8_ = bf16[128,512]{1,0:T(8,128)(2,1)S(1)} collective-permute-done((bf16[128,512]{1,0:T(8,128)(2,1)S(1)}, bf16[128,512]{1,0:T(8,128)(2,1)S(1)}, u32[]{:S(2)}, u32[]{:S(2)}) %collective-permute-start.6) | collective-permute-done | bytes 131104 | tf_op jit(solution)/shard_map/ppermute | solution.py:19
  30.7 5.3 %collective-permute-done.8.refs_4_.refs_9_ = bf16[128,512]{1,0:T(8,128)(2,1)S(1)} collective-permute-done((bf16[128,512]{1,0:T(8,128)(2,1)S(1)}, bf16[128,512]{1,0:T(8,128)(2,1)S(1)}, u32[]{:S(2)}, u32[]{:S(2)}) %collective-permute-start.8) | collective-permute-done | bytes 131104 | tf_op jit(solution)/shard_map/ppermute | solution.py:19
  47.8 3.3 %collective-permute-done.13.refs_10_ = bf16[128,512]{1,0:T(8,128)(2,1)S(1)} collective-permute-done((bf16[128,512]{1,0:T(8,128)(2,1)S(1)}, bf16[128,512]{1,0:T(8,128)(2,1)S(1)}, u32[]{:S(2)}, u32[]{:S(2)}) %collective-permute-start.13) | collective-permute-done | bytes 131104 | tf_op jit(solution)/shard_map/ppermute | solution.py:19
  55.4 3.1 %shard_map.78 = (bf16[512,1024]{1,0:T(8,128)(2,1)S(1)}, bf16[512,128]{1,0:T(8,128)(2,1)S(1)}, bf16[512,128]{1,0:T(8,128)(2,1)S(1)}, bf16[512,128]{1,0:T(8,128)(2...) custom-call(s32[1]{0:T(128)} %bitcast.2.refs_0_, ...), custom_call_target="tpu_custom_call" | custom-call | flops 3449999872 | bytes 1048576 | tf_op jit(solution)/shard_map/pallas_call | solution.py:287
  61.4 2.2 %collective-permute-start.16 = (bf16[512,128]{1,0:T(8,128)(2,1)S(1)}, bf16[512,128]{1,0:T(8,128)(2,1)S(1)}, u32[]{:S(2)}, u32[]{:S(2)}) collective-permute-start(bf16[512,128]{1,0:T(8,128)(2,1)S(1)} %get-tuple-element.55), channel_id=1, source_target_pairs={{0,12},{4,8},{8,4},{12,0},{16,28},{20,24},{24,20},{28,16},{1,13},{... | collective-permute-start | bytes 393224 | tf_op jit(solution)/shard_map/ppermute | solution.py:19
  64.6 2.7 %collective-permute-start.18 = (bf16[512,128]{1,0:T(8,128)(2,1)S(1)}, bf16[512,128]{1,0:T(8,128)(2,1)}, u32[]{:S(2)}, u32[]{:S(2)}) collective-permute-start(bf16[512,128]{1,0:T(8,128)(2,1)S(1)} %get-tuple-element.57), channel_id=1, source_target_pairs={{0,20},{4,16},{8,28},{12,24},{16,4},{20,0},{24,12},{28,8},{1,21},{... | collective-permute-start | bytes 393224 | tf_op jit(solution)/shard_map/ppermute | solution.py:19
  67.3 2.6 %collective-permute-start.19 = (bf16[512,128]{1,0:T(8,128)(2,1)S(1)}, bf16[512,128]{1,0:T(8,128)(2,1)}, u32[]{:S(2)}, u32[]{:S(2)}) collective-permute-start(bf16[512,128]{1,0:T(8,128)(2,1)S(1)} %get-tuple-element.58), channel_id=1, source_target_pairs={{0,24},{4,28},{8,16},{12,20},{16,8},{20,12},{24,0},{28,4},{1,25},{... | collective-permute-start | bytes 393224 | tf_op jit(solution)/shard_map/ppermute | solution.py:19
  72.1 10.0 %collective-permute-done.17.refs_6_ = bf16[512,128]{1,0:T(8,128)(2,1)S(1)} collective-permute-done((bf16[512,128]{1,0:T(8,128)(2,1)S(1)}, bf16[512,128]{1,0:T(8,128)(2,1)S(1)}, u32[]{:S(2)}, u32[]{:S(2)}) %collective-permute-start.17) | collective-permute-done | bytes 131104 | tf_op jit(solution)/shard_map/ppermute | solution.py:19
  82.2 3.2 %collective-permute-done.18.refs_7_ = bf16[512,128]{1,0:T(8,128)(2,1)} collective-permute-done((bf16[512,128]{1,0:T(8,128)(2,1)S(1)}, bf16[512,128]{1,0:T(8,128)(2,1)}, u32[]{:S(2)}, u32[]{:S(2)}) %collective-permute-start.18) | collective-permute-done | bytes 131104 | tf_op jit(solution)/shard_map/ppermute | solution.py:19
  89.1 3.9 %shard_map.80 = (bf16[2,1024,128]{2,1,0:T(8,128)(2,1)S(1)}, bf16[128,2048]{1,0:T(8,128)(2,1)S(1)}) custom-call(bf16[4,1024,128]{2,1,0:T(8,128)(2,1)S(1)} %bitcast.25, f32[27,128]{1,0:T(8,128)S(1)} %bitcast.21, bf16[128,4096]{1,0:T(8,128)(2,1)S(1)} %bitcast.13, bf16[128,4096]{1,0:T(8,128)(2,1)S(1)} %bitcast.16), custom_call_target="tpu_custom_call" | custom-call | flops 4600000000 | bytes 1048576 | tf_op jit(solution)/shard_map/pallas_call | solution.py:287
  93.0 4.1 %shard_map.81 = (bf16[2,1024,128]{2,1,0:T(8,128)(2,1)S(1)}, bf16[128,2048]{1,0:T(8,128)(2,1)S(1)}, bf16[1024,128]{1,0:T(8,128)(2,1)S(1)}, bf16[1024,128]{1,0:T(8,128)(2,1)S(1)}) custom-call(s32[1]{0:T(128)} %bitcast.refs_1_.refs_0_, bf16[4,1024,128]{2,1,0:T(8,128)(2,1)S(1)} %bitcast.26, bf16[1024,128]{1,0:T(8,128)(2,1)S(1)} %collective-permute-done.21.refs_2_, ...), custom_call_target="tpu_custom_call" | custom-call | flops 4600000000 | bytes 1048576 | tf_op jit(solution)/shard_map/pallas_call | solution.py:287
  97.1 3.6 %collective-permute-start.23 = (bf16[1024,128]{1,0:T(8,128)(2,1)S(1)}, bf16[1024,128]{1,0:T(8,128)(2,1)S(1)}, u32[]{:S(2)}, u32[]{:S(2)}) collective-permute-start(bf16[1024,128]{1,0:T(8,128)(2,1)S(1)} %get-tuple-element.67), channel_id=1, source_target_pairs={{0,1},{1,0},{2,3},{3,2},{4,5},{5,4},{6,7},{7,6},{8,9},{9,8},{10,11... | collective-permute-start | bytes 786440 | tf_op jit(solution)/shard_map/ppermute | solution.py:128
  101.6 2.3 %shard_map.82.refs_7_ = bf16[2,1024,128]{2,1,0:T(8,128)(2,1)S(1)} custom-call(bf16[2,1024,128]{2,1,0:T(8,128)(2,1)S(1)} %get-tuple-element.64.refs_0_.refs_2_.refs_4_, bf16[2,1024,128]{2,1,0:T(8,128)(2,1)S(1)} %get-tuple-element.63.refs_7_.refs_1_.refs_3_.refs_5_, f32[27,128]{1,0:T(8,128)S(1)} %bitcast.23), custom_call_target="tpu_custom_call" | custom-call | flops 2644999936 | bytes 1048576 | tf_op jit(solution)/shard_map/pallas_call | solution.py:287
  103.9 3.2 %shard_map.83 = (bf16[512,128]{1,0:T(8,128)(2,1)S(1)}, bf16[512,128]{1,0:T(8,128)(2,1)}, bf16[512,128]{1,0:T(8,128)(2,1)}, bf16[512,128]{1,0:T(8,128)(2,1)}, bf1...) custom-call(s32[1]{0:T(128)} %bitcast.1.refs_0_, ...), custom_call_target="tpu_custom_call" | custom-call | flops 3220000000 | bytes 1048576 | tf_op jit(solution)/shard_map/pallas_call | solution.py:287
  107.8 5.6 %collective-permute-start.25 = (bf16[512,128]{1,0:T(8,128)(2,1)S(1)}, bf16[512,128]{1,0:T(8,128)(2,1)S(1)}, u32[]{:S(2)}, u32[]{:S(2)}) collective-permute-start(bf16[512,128]{1,0:T(8,128)(2,1)S(1)} %get-tuple-element.69), channel_id=1, source_target_pairs={{0,16},{4,20},{8,24},{12,28},{16,0},{20,4},{24,8},{28,12},{1,17},{... | collective-permute-start | bytes 393224 | tf_op jit(solution)/shard_map/ppermute | solution.py:19
  119.2 5.5 %collective-permute-done.26.refs_9_.refs_5_ = bf16[512,128]{1,0:T(8,128)(2,1)S(1)} collective-permute-done((bf16[512,128]{1,0:T(8,128)(2,1)S(1)}, bf16[512,128]{1,0:T(8,128)(2,1)S(1)}, u32[]{:S(2)}, u32[]{:S(2)}) %collective-permute-start.26) | collective-permute-done | bytes 131104 | tf_op jit(solution)/shard_map/ppermute | solution.py:19
  124.7 2.5 %collective-permute-start.31 = (bf16[512,128]{1,0:T(8,128)(2,1)}, bf16[512,128]{1,0:T(8,128)(2,1)}, u32[]{:S(2)}, u32[]{:S(2)}) collective-permute-start(bf16[512,128]{1,0:T(8,128)(2,1)} %get-tuple-element.77), channel_id=1, source_target_pairs={{0,28},{4,24},{8,20},{12,16},{16,12},{20,8},{24,4},{28,0},{1,29},{... | collective-permute-start | bytes 393224 | tf_op jit(solution)/shard_map/ppermute | solution.py:19
  127.2 5.5 %shard_map.84 = (f32[27,128]{1,0:T(8,128)S(1)}, bf16[128,4096]{1,0:T(8,128)(2,1)S(1)}) custom-call(s32[1]{0:T(128)} %bitcast.refs_1_.refs_0_, bf16[4,1024,128]{2,1,0:T(8,128)(2,1)S(1)} %bitcast.27, bf16[1024,128]{1,0:T(8,128)(2,1)S(1)} %collective-permute-done.21.refs_2_, bf16[1024,128]{1,0:T(8,128)(2,1)S(1)} %collective-permute-done.22.refs_3_, ...), custom_call_target="tpu_custom_call" | custom-call | flops 6670000128 | bytes 1048576 | tf_op jit(solution)/shard_map/pallas_call | solution.py:287
  136.7 2.7 %shard_map.85 = (f32[1024,256]{1,0:T(8,128)S(1)}, f32[1024,256]{1,0:T(8,128)S(1)}, bf16[2,1024,256]{2,1,0:T(8,128)(2,1)S(1)}, bf16[512,1024]{1,0:T(8,128)(2,1)S(1)}) custom-call(bf16[512,128]{1,0:T(8,128)(2,1)S(1)} %copy-done.18, bf16[512,128]{1,0:T(8,128)(2,1)} %collective-permute-done.27.refs_1_, bf16[512,128]{1,0:T(8,128)(2,1)} %collective-permute-done.28.refs_2_, ...), custom_call_target="tpu_custom_call" | custom-call | flops 3449999872 | bytes 1048576 | tf_op jit(solution)/shard_map/pallas_call | solution.py:287
  139.5 4.7 %collective-permute-start.39 = (bf16[2,1024,256]{2,1,0:T(8,128)(2,1)S(1)}, bf16[2,1024,256]{2,1,0:T(8,128)(2,1)S(1)}, u32[]{:S(2)}, u32[]{:S(2)}) collective-permute-start(bf16[2,1024,256]{2,1,0:T(8,128)(2,1)S(1)} %get-tuple-element.91), channel_id=1, source_target_pairs={{0,1},{1,0},{2,3},{3,2},{4,5},{5,4},{6,7},{7,6},{8,9},{9,8},{10,11... | collective-permute-start | bytes 3145736 | tf_op jit(solution)/shard_map/ppermute | solution.py:19
  144.2 3.0 %shard_map.86 = (bf16[128,512]{1,0:T(8,128)(2,1)S(1)}, bf16[128,512]{1,0:T(8,128)(2,1)S(1)}, bf16[128,512]{1,0:T(8,128)(2,1)S(1)}, bf16[128,512]{1,0:T(8,128)(2,...) custom-call(s32[1]{0:T(128)} %bitcast.2.refs_0_, ...), custom_call_target="tpu_custom_call" | custom-call | flops 2990000128 | bytes 1048576 | tf_op jit(solution)/shard_map/pallas_call | solution.py:287
  147.3 2.3 %collective-permute-start.40 = (bf16[1024,256]{1,0:T(8,128)(2,1)S(1)}, bf16[1024,256]{1,0:T(8,128)(2,1)S(1)}, u32[]{:S(2)}, u32[]{:S(2)}) collective-permute-start(bf16[1024,256]{1,0:T(8,128)(2,1)S(1)} %get-tuple-element.93), channel_id=1, source_target_pairs={{0,2},{1,3},{2,0},{3,1},{4,6},{5,7},{6,4},{7,5},{8,10},{9,11},{10,... | collective-permute-start | bytes 1572872 | tf_op jit(solution)/shard_map/ppermute | solution.py:19
  149.6 2.9 %collective-permute-start.36 = (bf16[128,512]{1,0:T(8,128)(2,1)S(1)}, bf16[128,512]{1,0:T(8,128)(2,1)S(1)}, u32[]{:S(2)}, u32[]{:S(2)}) collective-permute-start(bf16[128,512]{1,0:T(8,128)(2,1)S(1)} %get-tuple-element.86), channel_id=1, source_target_pairs={{0,20},{4,16},{8,28},{12,24},{16,4},{20,0},{24,12},{28,8},{1,21},{... | collective-permute-start | bytes 393224 | tf_op jit(solution)/shard_map/ppermute | solution.py:19
  154.6 9.5 %collective-permute-done.35.refs_6_.refs_2_ = bf16[128,512]{1,0:T(8,128)(2,1)S(1)} collective-permute-done((bf16[128,512]{1,0:T(8,128)(2,1)S(1)}, bf16[128,512]{1,0:T(8,128)(2,1)S(1)}, u32[]{:S(2)}, u32[]{:S(2)}) %collective-permute-start.35) | collective-permute-done | bytes 131104 | tf_op jit(solution)/shard_map/ppermute | solution.py:19
  164.1 2.7 %collective-permute-done.36.refs_7_.refs_3_ = bf16[128,512]{1,0:T(8,128)(2,1)S(1)} collective-permute-done((bf16[128,512]{1,0:T(8,128)(2,1)S(1)}, bf16[128,512]{1,0:T(8,128)(2,1)S(1)}, u32[]{:S(2)}, u32[]{:S(2)}) %collective-permute-start.36) | collective-permute-done | bytes 131104 | tf_op jit(solution)/shard_map/ppermute | solution.py:19
  170.5 2.9 %collective-permute-done.46 = f32[27,128]{1,0:T(8,128)S(1)} collective-permute-done((f32[27,128]{1,0:T(8,128)S(1)}, f32[27,128]{1,0:T(8,128)S(1)}, u32[]{:S(2)}, u32[]{:S(2)}) %collective-permute-start.46) | collective-permute-done | bytes 13856 | tf_op jit(solution)/shard_map/ppermute | solution.py:19
  175.9 3.6 %collective-permute-done.41.refs_1_ = bf16[4,128,256]{2,1,0:T(8,128)(2,1)S(1)} collective-permute-done((bf16[4,128,256]{2,1,0:T(8,128)(2,1)S(1)}, bf16[4,128,256]{2,1,0:T(8,128)(2,1)S(1)}, u32[]{:S(2)}, u32[]{:S(2)}) %collective-permute-start.41) | collective-permute-done | bytes 262176 | tf_op jit(solution)/shard_map/ppermute | solution.py:19
  183.6 2.3 %collective-permute-start.42 = (bf16[128,256]{1,0:T(8,128)(2,1)S(1)}, bf16[128,256]{1,0:T(8,128)(2,1)S(1)}, u32[]{:S(2)}, u32[]{:S(2)}) collective-permute-start(bf16[128,256]{1,0:T(8,128)(2,1)S(1)} %get-tuple-element.97), channel_id=1, source_target_pairs={{0,8},{4,12},{8,0},{12,4},{16,24},{20,28},{24,16},{28,20},{1,9},{5... | collective-permute-start | bytes 196616 | tf_op jit(solution)/shard_map/ppermute | solution.py:19
  (125 shorter events, 67.2 us)
Async XLA Ops:
  1.6 8.1 %collective-permute-start = (bf16[128,256]{1,0:T(8,128)(2,1)S(1)}, bf16[128,256]{1,0:T(8,128)(2,1)S(1)}, u32[]{:S(2)}, u32[]{:S(2)}) collective-permute-start(bf16[128,256]{1,0:T(8,128)(2,1)S(1)} %constant_dynamic-slice_fusion.8.refs_0_), channel_id=1, source_target_pairs={{0,8},{4,12},{8,0},{12,4},{16,24},{20,28},{24,16},{28,20},{1,9},{5... | collective-permute-start | bytes 196616 | tf_op jit(solution)/shard_map/ppermute | solution.py:19
  13.4 14.2 %collective-permute-start.4 = (bf16[4,128,256]{2,1,0:T(8,128)(2,1)S(1)}, bf16[4,128,256]{2,1,0:T(8,128)(2,1)S(1)}, u32[]{:S(2)}, u32[]{:S(2)}) collective-permute-start(bf16[4,128,256]{2,1,0:T(8,128)(2,1)S(1)} %shard_map.75.refs_0_), channel_id=1, source_target_pairs={{0,4},{4,0},{8,12},{12,8},{16,20},{20,16},{24,28},{28,24},{1,5},{5... | collective-permute-start | bytes 786440 | tf_op jit(solution)/shard_map/ppermute | solution.py:19
  14.9 10.0 %collective-permute-start.5 = (bf16[128,512]{1,0:T(8,128)(2,1)S(1)}, bf16[128,512]{1,0:T(8,128)(2,1)S(1)}, u32[]{:S(2)}, u32[]{:S(2)}) collective-permute-start(bf16[128,512]{1,0:T(8,128)(2,1)S(1)} %get-tuple-element.107.refs_4_), channel_id=1, source_target_pairs={{0,16},{4,20},{8,24},{12,28},{16,0},{20,4},{24,8},{28,12},{1,17},{... | collective-permute-start | bytes 393224 | tf_op jit(solution)/shard_map/ppermute | solution.py:19
  16.5 11.1 %collective-permute-start.6 = (bf16[128,512]{1,0:T(8,128)(2,1)S(1)}, bf16[128,512]{1,0:T(8,128)(2,1)S(1)}, u32[]{:S(2)}, u32[]{:S(2)}) collective-permute-start(bf16[128,512]{1,0:T(8,128)(2,1)S(1)} %get-tuple-element.106.refs_5_), channel_id=1, source_target_pairs={{0,20},{4,16},{8,28},{12,24},{16,4},{20,0},{24,12},{28,8},{1,21},{... | collective-permute-start | bytes 393224 | tf_op jit(solution)/shard_map/ppermute | solution.py:19
  17.8 18.1 %collective-permute-start.3 = (bf16[4,128,256]{2,1,0:T(8,128)(2,1)S(1)}, bf16[4,128,256]{2,1,0:T(8,128)(2,1)S(1)}, u32[]{:S(2)}, u32[]{:S(2)}) collective-permute-start(bf16[4,128,256]{2,1,0:T(8,128)(2,1)S(1)} %shard_map.75.refs_0_), channel_id=1, source_target_pairs={{0,2},{1,3},{2,0},{3,1},{4,6},{5,7},{6,4},{7,5},{8,10},{9,11},{10,... | collective-permute-start | bytes 786440 | tf_op jit(solution)/shard_map/ppermute | solution.py:19
  27.6 8.4 %collective-permute-start.7 = (bf16[4,128,256]{2,1,0:T(8,128)(2,1)S(1)}, bf16[4,128,256]{2,1,0:T(8,128)(2,1)S(1)}, u32[]{:S(2)}, u32[]{:S(2)}) collective-permute-start(bf16[4,128,256]{2,1,0:T(8,128)(2,1)S(1)} %bitcast.19), channel_id=1, source_target_pairs={{0,2},{1,3},{2,0},{3,1},{4,6},{5,7},{6,4},{7,5},{8,10},{9,11},{10,... | collective-permute-start | bytes 786440 | tf_op jit(solution)/shard_map/ppermute | solution.py:19
  37.0 14.8 %collective-permute-start.9 = (bf16[2,1024,256]{2,1,0:T(8,128)(2,1)}, bf16[2,1024,256]{2,1,0:T(8,128)(2,1)}, u32[]{:S(2)}, u32[]{:S(2)}) collective-permute-start(bf16[2,1024,256]{2,1,0:T(8,128)(2,1)} %shard_map.77.refs_1_.refs_2_), channel_id=1, source_target_pairs={{0,1},{1,0},{2,3},{3,2},{4,5},{5,4},{6,7},{7,6},{8,9},{9,8},{10,11... | collective-permute-start | bytes 3145736 | tf_op jit(solution)/shard_map/ppermute | solution.py:19
  38.6 8.6 %collective-permute-start.12 = (bf16[128,512]{1,0:T(8,128)(2,1)}, bf16[128,512]{1,0:T(8,128)(2,1)S(1)}, u32[]{:S(2)}, u32[]{:S(2)}) collective-permute-start(bf16[128,512]{1,0:T(8,128)(2,1)} %get-tuple-element.100), channel_id=1, source_target_pairs={{0,12},{4,8},{8,4},{12,0},{16,28},{20,24},{24,20},{28,16},{1,13},{... | collective-permute-start | bytes 393224 | tf_op jit(solution)/shard_map/ppermute | solution.py:19
  40.5 10.6 %collective-permute-start.13 = (bf16[128,512]{1,0:T(8,128)(2,1)S(1)}, bf16[128,512]{1,0:T(8,128)(2,1)S(1)}, u32[]{:S(2)}, u32[]{:S(2)}) collective-permute-start(bf16[128,512]{1,0:T(8,128)(2,1)S(1)} %get-tuple-element.104.refs_7_), channel_id=1, source_target_pairs={{0,28},{4,24},{8,20},{12,16},{16,12},{20,8},{24,4},{28,0},{1,29},{... | collective-permute-start | bytes 393224 | tf_op jit(solution)/shard_map/ppermute | solution.py:19
  61.4 9.7 %collective-permute-start.15 = (bf16[512,128]{1,0:T(8,128)(2,1)S(1)}, bf16[512,128]{1,0:T(8,128)(2,1)S(1)}, u32[]{:S(2)}, u32[]{:S(2)}) collective-permute-start(bf16[512,128]{1,0:T(8,128)(2,1)S(1)} %get-tuple-element.54), channel_id=1, source_target_pairs={{0,8},{4,12},{8,0},{12,4},{16,24},{20,28},{24,16},{28,20},{1,9},{5... | collective-permute-start | bytes 393224 | tf_op jit(solution)/shard_map/ppermute | solution.py:19
  61.4 10.7 %collective-permute-start.16 = (bf16[512,128]{1,0:T(8,128)(2,1)S(1)}, bf16[512,128]{1,0:T(8,128)(2,1)S(1)}, u32[]{:S(2)}, u32[]{:S(2)}) collective-permute-start(bf16[512,128]{1,0:T(8,128)(2,1)S(1)} %get-tuple-element.55), channel_id=1, source_target_pairs={{0,12},{4,8},{8,4},{12,0},{16,28},{20,24},{24,20},{28,16},{1,13},{... | collective-permute-start | bytes 393224 | tf_op jit(solution)/shard_map/ppermute | solution.py:19
  63.7 18.5 %collective-permute-start.17 = (bf16[512,128]{1,0:T(8,128)(2,1)S(1)}, bf16[512,128]{1,0:T(8,128)(2,1)S(1)}, u32[]{:S(2)}, u32[]{:S(2)}) collective-permute-start(bf16[512,128]{1,0:T(8,128)(2,1)S(1)} %get-tuple-element.56), channel_id=1, source_target_pairs={{0,16},{4,20},{8,24},{12,28},{16,0},{20,4},{24,8},{28,12},{1,17},{... | collective-permute-start | bytes 393224 | tf_op jit(solution)/shard_map/ppermute | solution.py:19
  64.6 20.8 %collective-permute-start.18 = (bf16[512,128]{1,0:T(8,128)(2,1)S(1)}, bf16[512,128]{1,0:T(8,128)(2,1)}, u32[]{:S(2)}, u32[]{:S(2)}) collective-permute-start(bf16[512,128]{1,0:T(8,128)(2,1)S(1)} %get-tuple-element.57), channel_id=1, source_target_pairs={{0,20},{4,16},{8,28},{12,24},{16,4},{20,0},{24,12},{28,8},{1,21},{... | collective-permute-start | bytes 393224 | tf_op jit(solution)/shard_map/ppermute | solution.py:19
  67.3 18.1 %collective-permute-start.19 = (bf16[512,128]{1,0:T(8,128)(2,1)S(1)}, bf16[512,128]{1,0:T(8,128)(2,1)}, u32[]{:S(2)}, u32[]{:S(2)}) collective-permute-start(bf16[512,128]{1,0:T(8,128)(2,1)S(1)} %get-tuple-element.58), channel_id=1, source_target_pairs={{0,24},{4,28},{8,16},{12,20},{16,8},{20,12},{24,0},{28,4},{1,25},{... | collective-permute-start | bytes 393224 | tf_op jit(solution)/shard_map/ppermute | solution.py:19
  71.1 14.3 %collective-permute-start.20 = (bf16[512,128]{1,0:T(8,128)(2,1)S(1)}, bf16[512,128]{1,0:T(8,128)(2,1)}, u32[]{:S(2)}, u32[]{:S(2)}) collective-permute-start(bf16[512,128]{1,0:T(8,128)(2,1)S(1)} %get-tuple-element.59), channel_id=1, source_target_pairs={{0,28},{4,24},{8,20},{12,16},{16,12},{20,8},{24,4},{28,0},{1,29},{... | collective-permute-start | bytes 393224 | tf_op jit(solution)/shard_map/ppermute | solution.py:19
  107.8 11.4 %collective-permute-start.25 = (bf16[512,128]{1,0:T(8,128)(2,1)S(1)}, bf16[512,128]{1,0:T(8,128)(2,1)S(1)}, u32[]{:S(2)}, u32[]{:S(2)}) collective-permute-start(bf16[512,128]{1,0:T(8,128)(2,1)S(1)} %get-tuple-element.69), channel_id=1, source_target_pairs={{0,16},{4,20},{8,24},{12,28},{16,0},{20,4},{24,8},{28,12},{1,17},{... | collective-permute-start | bytes 393224 | tf_op jit(solution)/shard_map/ppermute | solution.py:19
  113.3 11.3 %collective-permute-start.26 = (bf16[512,128]{1,0:T(8,128)(2,1)S(1)}, bf16[512,128]{1,0:T(8,128)(2,1)S(1)}, u32[]{:S(2)}, u32[]{:S(2)}) collective-permute-start(bf16[512,128]{1,0:T(8,128)(2,1)S(1)} %get-tuple-element.70), channel_id=1, source_target_pairs={{0,20},{4,16},{8,28},{12,24},{16,4},{20,0},{24,12},{28,8},{1,21},{... | collective-permute-start | bytes 393224 | tf_op jit(solution)/shard_map/ppermute | solution.py:19
  113.3 20.1 %collective-permute-start.27 = (bf16[512,128]{1,0:T(8,128)(2,1)}, bf16[512,128]{1,0:T(8,128)(2,1)}, u32[]{:S(2)}, u32[]{:S(2)}) collective-permute-start(bf16[512,128]{1,0:T(8,128)(2,1)} %get-tuple-element.73), channel_id=1, source_target_pairs={{0,4},{4,0},{8,12},{12,8},{16,20},{20,16},{24,28},{28,24},{1,5},{5... | collective-permute-start | bytes 393224 | tf_op jit(solution)/shard_map/ppermute | solution.py:19
  114.8 18.7 %collective-permute-start.28 = (bf16[512,128]{1,0:T(8,128)(2,1)}, bf16[512,128]{1,0:T(8,128)(2,1)}, u32[]{:S(2)}, u32[]{:S(2)}) collective-permute-start(bf16[512,128]{1,0:T(8,128)(2,1)} %get-tuple-element.74), channel_id=1, source_target_pairs={{0,8},{4,12},{8,0},{12,4},{16,24},{20,28},{24,16},{28,20},{1,9},{5... | collective-permute-start | bytes 393224 | tf_op jit(solution)/shard_map/ppermute | solution.py:19
  116.7 16.8 %collective-permute-start.29 = (bf16[512,128]{1,0:T(8,128)(2,1)}, bf16[512,128]{1,0:T(8,128)(2,1)}, u32[]{:S(2)}, u32[]{:S(2)}) collective-permute-start(bf16[512,128]{1,0:T(8,128)(2,1)} %get-tuple-element.75), channel_id=1, source_target_pairs={{0,12},{4,8},{8,4},{12,0},{16,28},{20,24},{24,20},{28,16},{1,13},{... | collective-permute-start | bytes 393224 | tf_op jit(solution)/shard_map/ppermute | solution.py:19
  119.2 14.3 %collective-permute-start.30 = (bf16[512,128]{1,0:T(8,128)(2,1)}, bf16[512,128]{1,0:T(8,128)(2,1)}, u32[]{:S(2)}, u32[]{:S(2)}) collective-permute-start(bf16[512,128]{1,0:T(8,128)(2,1)} %get-tuple-element.76), channel_id=1, source_target_pairs={{0,24},{4,28},{8,16},{12,20},{16,8},{20,12},{24,0},{28,4},{1,25},{... | collective-permute-start | bytes 393224 | tf_op jit(solution)/shard_map/ppermute | solution.py:19
  124.7 8.8 %collective-permute-start.31 = (bf16[512,128]{1,0:T(8,128)(2,1)}, bf16[512,128]{1,0:T(8,128)(2,1)}, u32[]{:S(2)}, u32[]{:S(2)}) collective-permute-start(bf16[512,128]{1,0:T(8,128)(2,1)} %get-tuple-element.77), channel_id=1, source_target_pairs={{0,28},{4,24},{8,20},{12,16},{16,12},{20,8},{24,4},{28,0},{1,29},{... | collective-permute-start | bytes 393224 | tf_op jit(solution)/shard_map/ppermute | solution.py:19
  139.5 7.7 %collective-permute-start.39 = (bf16[2,1024,256]{2,1,0:T(8,128)(2,1)S(1)}, bf16[2,1024,256]{2,1,0:T(8,128)(2,1)S(1)}, u32[]{:S(2)}, u32[]{:S(2)}) collective-permute-start(bf16[2,1024,256]{2,1,0:T(8,128)(2,1)S(1)} %get-tuple-element.91), channel_id=1, source_target_pairs={{0,1},{1,0},{2,3},{3,2},{4,5},{5,4},{6,7},{7,6},{8,9},{9,8},{10,11... | collective-permute-start | bytes 3145736 | tf_op jit(solution)/shard_map/ppermute | solution.py:19
  147.3 19.5 %collective-permute-start.40 = (bf16[1024,256]{1,0:T(8,128)(2,1)S(1)}, bf16[1024,256]{1,0:T(8,128)(2,1)S(1)}, u32[]{:S(2)}, u32[]{:S(2)}) collective-permute-start(bf16[1024,256]{1,0:T(8,128)(2,1)S(1)} %get-tuple-element.93), channel_id=1, source_target_pairs={{0,2},{1,3},{2,0},{3,1},{4,6},{5,7},{6,4},{7,5},{8,10},{9,11},{10,... | collective-permute-start | bytes 1572872 | tf_op jit(solution)/shard_map/ppermute | solution.py:19
  149.6 14.5 %collective-permute-start.35 = (bf16[128,512]{1,0:T(8,128)(2,1)S(1)}, bf16[128,512]{1,0:T(8,128)(2,1)S(1)}, u32[]{:S(2)}, u32[]{:S(2)}) collective-permute-start(bf16[128,512]{1,0:T(8,128)(2,1)S(1)} %get-tuple-element.85), channel_id=1, source_target_pairs={{0,16},{4,20},{8,24},{12,28},{16,0},{20,4},{24,8},{28,12},{1,17},{... | collective-permute-start | bytes 393224 | tf_op jit(solution)/shard_map/ppermute | solution.py:19
  149.6 17.2 %collective-permute-start.36 = (bf16[128,512]{1,0:T(8,128)(2,1)S(1)}, bf16[128,512]{1,0:T(8,128)(2,1)S(1)}, u32[]{:S(2)}, u32[]{:S(2)}) collective-permute-start(bf16[128,512]{1,0:T(8,128)(2,1)S(1)} %get-tuple-element.86), channel_id=1, source_target_pairs={{0,20},{4,16},{8,28},{12,24},{16,4},{20,0},{24,12},{28,8},{1,21},{... | collective-permute-start | bytes 393224 | tf_op jit(solution)/shard_map/ppermute | solution.py:19
  152.5 21.1 %collective-permute-start.37 = (bf16[128,512]{1,0:T(8,128)(2,1)S(1)}, bf16[128,512]{1,0:T(8,128)(2,1)S(1)}, u32[]{:S(2)}, u32[]{:S(2)}) collective-permute-start(bf16[128,512]{1,0:T(8,128)(2,1)S(1)} %get-tuple-element.87), channel_id=1, source_target_pairs={{0,24},{4,28},{8,16},{12,20},{16,8},{20,12},{24,0},{28,4},{1,25},{... | collective-permute-start | bytes 393224 | tf_op jit(solution)/shard_map/ppermute | solution.py:19
  166.9 12.7 %collective-permute-start.41 = (bf16[4,128,256]{2,1,0:T(8,128)(2,1)S(1)}, bf16[4,128,256]{2,1,0:T(8,128)(2,1)S(1)}, u32[]{:S(2)}, u32[]{:S(2)}) collective-permute-start(bf16[4,128,256]{2,1,0:T(8,128)(2,1)S(1)} %get-tuple-element.95), channel_id=1, source_target_pairs={{0,4},{4,0},{8,12},{12,8},{16,20},{20,16},{24,28},{28,24},{1,5},{5... | collective-permute-start | bytes 786440 | tf_op jit(solution)/shard_map/ppermute | solution.py:19
  170.1 13.5 %collective-permute-start.32 = (bf16[128,512]{1,0:T(8,128)(2,1)S(1)}, bf16[128,512]{1,0:T(8,128)(2,1)S(1)}, u32[]{:S(2)}, u32[]{:S(2)}) collective-permute-start(bf16[128,512]{1,0:T(8,128)(2,1)S(1)} %get-tuple-element.82.refs_3_), channel_id=1, source_target_pairs={{0,4},{4,0},{8,12},{12,8},{16,20},{20,16},{24,28},{28,24},{1,5},{5... | collective-permute-start | bytes 393224 | tf_op jit(solution)/shard_map/ppermute | solution.py:19
  170.5 13.1 %collective-permute-start.33 = (bf16[128,512]{1,0:T(8,128)(2,1)S(1)}, bf16[128,512]{1,0:T(8,128)(2,1)S(1)}, u32[]{:S(2)}, u32[]{:S(2)}) collective-permute-start(bf16[128,512]{1,0:T(8,128)(2,1)S(1)} %get-tuple-element.83), channel_id=1, source_target_pairs={{0,8},{4,12},{8,0},{12,4},{16,24},{20,28},{24,16},{28,20},{1,9},{5... | collective-permute-start | bytes 393224 | tf_op jit(solution)/shard_map/ppermute | solution.py:19
  173.5 12.4 %collective-permute-start.34 = (bf16[128,512]{1,0:T(8,128)(2,1)S(1)}, bf16[128,512]{1,0:T(8,128)(2,1)S(1)}, u32[]{:S(2)}, u32[]{:S(2)}) collective-permute-start(bf16[128,512]{1,0:T(8,128)(2,1)S(1)} %get-tuple-element.84), channel_id=1, source_target_pairs={{0,12},{4,8},{8,4},{12,0},{16,28},{20,24},{24,20},{28,16},{1,13},{... | collective-permute-start | bytes 393224 | tf_op jit(solution)/shard_map/ppermute | solution.py:19
  173.5 12.3 %collective-permute-start.38 = (bf16[128,512]{1,0:T(8,128)(2,1)S(1)}, bf16[128,512]{1,0:T(8,128)(2,1)S(1)}, u32[]{:S(2)}, u32[]{:S(2)}) collective-permute-start(bf16[128,512]{1,0:T(8,128)(2,1)S(1)} %get-tuple-element.88), channel_id=1, source_target_pairs={{0,28},{4,24},{8,20},{12,16},{16,12},{20,8},{24,4},{28,0},{1,29},{... | collective-permute-start | bytes 393224 | tf_op jit(solution)/shard_map/ppermute | solution.py:19
  (34 other events, 113.6 us)

commit v7 on v6

v7 whole, which is shorter than its diff:
```python
import functools
import math

import jax
import jax.numpy as jnp
from jax import lax
from jax.experimental import pallas as pl
from jax.experimental.pallas import tpu as pltpu
from jax.sharding import PartitionSpec as P

WW = 64
BF = jnp.bfloat16
F32 = jnp.float32


def swap(block, axis, step):
    size = lax.axis_size(axis)
    return lax.ppermute(block, axis, [(i, i ^ step) for i in range(size)])


def exchange(pieces, axis):
    size = len(pieces)
    order = list(range(size // 2, size)) + list(range(1, size // 2))
    got = {0: pieces[0]}
    for s in order:
        got[s] = swap(pieces[s], axis, s)
    return [got[s] for s in range(size)]


def place(pieces, shift):
    out = jnp.zeros((len(pieces),) + pieces[0].shape, pieces[0].dtype)
    for s, piece in enumerate(pieces):
        out = lax.dynamic_update_index_in_dim(out, piece, shift ^ s, 0)
    return out


def pick(blocks, index):
    return lax.dynamic_index_in_dim(blocks, index, 0, keepdims=False)


def join(parts, after, us=0.4):
    def kernel(*refs):
        for k in range(len(parts)):
            refs[-1][k] = refs[k][...]

    shape = jax.ShapeDtypeStruct((len(parts),) + parts[0].shape, parts[0].dtype)
    return call(kernel, shape, [], *parts, us=us, after=after)


def gather_weights(mixing, me_space, send, first_in, second_in):
    rows, cols = mixing.shape
    nf, ns = lax.axis_size("filter"), lax.axis_size("space")
    share, pairs = cols // ns, ns // 2
    own = lax.dynamic_slice_in_dim(mixing, me_space * share, share, axis=1)
    even = join([own] + [swap(own, "filter", s) for s in range(2, nf, 2)], send[nf // 2 :])
    first = [even] + [swap(even, "space", s) for s in range(2, ns, 2)]
    odd = join([swap(even, "filter", 1)], (first_in,))[0]
    second = [odd] + [swap(odd, "space", s) for s in range(2, ns, 2)]

    def kernel(*refs):
        for k in range(pairs):
            for r in range(nf):
                source = refs[pairs * (r % 2) + k]
                refs[-1][k, r * rows : (r + 1) * rows, :] = source[r // 2]

    shape = jax.ShapeDtypeStruct((pairs, nf * rows, share), BF)
    held = call(kernel, shape, [], *first, *second, us=0.6, after=(second_in,))
    return held, swap(held, "space", 1)


def halved(ch, share, ns):
    return ns == 4 and share == 2 * ch and ch % 128 == 0


def halves_first(rows, nf, mine0, mine1, got, taps, a_keep, a_send, b_keep, b_next, b_send, sums):
    h, count = a_keep.shape[1], taps.shape[0]
    total = joined(*split(taps[...])) + joined(got[0, nf * rows :, :h], got[1, nf * rows :, :h])
    high, low = split(total)
    a_send[nf * rows : nf * rows + count, :] = high
    a_send[nf * rows + count :, :] = low
    sums[...] = joined(high, low)
    for r in range(nf):
        row = slice(r * rows, (r + 1) * rows)
        own = mine0[row, :] + got[0, row, :].astype(F32)
        step = mine1[row, :] + got[1, row, :].astype(F32)
        a_keep[row, :] = own[:, :h]
        a_send[row, :] = step[:, :h].astype(BF)
        if r % 2:
            b_send[0, r // 2] = own[:, h:].astype(BF)
            b_send[1, r // 2] = step[:, h:].astype(BF)
        else:
            b_keep[r // 2] = own[:, h:]
            b_next[r // 2] = step[:, h:]


def halves_second(rows, nf, a_keep, a_got, b_keep, b_next, b_got, sums, near, a_send, far, b_send, taps):
    count = taps.shape[0]
    high, low = a_got[nf * rows : nf * rows + count, :], a_got[nf * rows + count :, :]
    taps[...] = sums[...] + joined(high, low)
    for r in range(nf):
        row = slice(r * rows, (r + 1) * rows)
        own = a_keep[row, :] + a_got[row, :].astype(F32)
        if r % 2:
            a_send[r // 2] = own.astype(BF)
        else:
            near[r // 2] = own
    far[...] = b_keep[...] + b_got[0].astype(F32)
    b_send[...] = (b_next[...] + b_got[1].astype(F32)).astype(BF)


def halves_third(near, a_got, far, b_got, keep, *send):
    h = near.shape[2]
    for k in range(near.shape[0]):
        left = near[k] + a_got[k].astype(F32)
        right = far[k] + b_got[k].astype(F32)
        if k:
            send[k - 1][:, :h] = left.astype(BF)
            send[k - 1][:, h:] = right.astype(BF)
        else:
            keep[:, :h] = left
            keep[:, h:] = right


def scatter_rest(mine, theirs, taps, rows, first_in, second_in):
    nf, ns = lax.axis_size("filter"), lax.axis_size("space")
    pairs, share = ns // 2, theirs.shape[2]
    theirs = swap(theirs, "space", 1)
    if halved(rows, share, ns):
        h, n, count = share // 2, nf // 2, taps.shape[0]
        shapes = (
            jax.ShapeDtypeStruct((nf * rows, h), F32),
            jax.ShapeDtypeStruct((nf * rows + 2 * count, h), BF),
            jax.ShapeDtypeStruct((n, rows, h), F32), jax.ShapeDtypeStruct((n, rows, h), F32),
            jax.ShapeDtypeStruct((2, n, rows, h), BF), jax.ShapeDtypeStruct((count, h), F32),
        )
        kernel = functools.partial(halves_first, rows, nf)
        a_keep, a_send, b_keep, b_next, b_send, sums = call(
            kernel, shapes, [], *mine, theirs, taps, us=0.8
        )
        a_got = swap(a_send, "space", 2)
        b_got = swap(b_send, "filter", 1)
        shapes = (
            jax.ShapeDtypeStruct((n, rows, h), F32), jax.ShapeDtypeStruct((n, rows, h), BF),
            jax.ShapeDtypeStruct((n, rows, h), F32), jax.ShapeDtypeStruct((n, rows, h), BF),
            jax.ShapeDtypeStruct((count, h), F32),
        )
        kernel = functools.partial(halves_second, rows, nf)
        near, a_send, far, b_send, taps = call(
            kernel, shapes, [], a_keep, a_got, b_keep, b_next, b_got, sums,
            us=0.6, after=(first_in,),
        )
        a_got = swap(a_send, "filter", 1)
        b_got = swap(b_send, "space", 2)
        shapes = [jax.ShapeDtypeStruct((rows, share), F32)]
        shapes += [jax.ShapeDtypeStruct((rows, share), BF)] * (n - 1)
        keep, *rest = call(
            halves_third, shapes, [], near, a_got, far, b_got, us=0.5, after=(second_in,)
        )
    else:
        step = 1
        while step < ns:
            taps = taps + swap(taps, "space", step)
            step *= 2
        total = mine[0] + theirs[0].astype(F32)
        for k in range(1, pairs):
            send = (mine[k] + theirs[k].astype(F32)).astype(BF)
            total = total + swap(send, "space", 2 * k).astype(F32)
        total = total.reshape(nf // 2, 2, rows, share)
        near = total[:, 0] + swap(total[:, 1].astype(BF), "filter", 1).astype(F32)
        keep, rest = near[0], [near[k].astype(BF) for k in range(1, nf // 2)]
    for k, part in enumerate(rest):
        keep = keep + swap(part, "filter", 2 * (k + 1)).astype(F32)
    return keep, taps


def halo(near, far):
    size = lax.axis_size("space")
    inner = [(i, i ^ 1) for i in range(size)]
    outer = [(i, ((i + 1) ^ 1) - 1) for i in range(1, size - 1)]
    return lax.ppermute(near, "space", inner), lax.ppermute(far, "space", outer)


def fill(pad_ref, plane, source):
    rows, width, ch = pad_ref.shape[1] - 2, pad_ref.shape[2], pad_ref.shape[3]
    pad_ref[plane, 1 : rows + 1] = source.astype(F32).reshape(rows, width, ch)
    pad_ref[plane, 0] = jnp.zeros((width, ch), F32)
    pad_ref[plane, rows + 1] = jnp.zeros((width, ch), F32)


def shifted(value, up):
    width = value.shape[0]
    index = lax.broadcasted_iota(jnp.int32, value.shape, 0)
    if up:
        return jnp.where(index == width - 1, 0.0, pltpu.roll(value, width - 1, 0))
    return jnp.where(index == 0, 0.0, pltpu.roll(value, 1, 0))


def conv_row(pad_ref, taps_ref, plane, row, flip):
    sums = [None, None, None]
    for a in range(3):
        for b in range(3):
            da, db = (1 - a, 1 - b) if flip else (a - 1, b - 1)
            line = pad_ref[plane + da, row + db]
            for e in range(3):
                term = taps_ref[pl.ds(a * 9 + b * 3 + e, 1), :] * line
                sums[e] = term if sums[e] is None else sums[e] + term
    lo, hi = (sums[2], sums[0]) if flip else (sums[0], sums[2])
    return sums[1] + shifted(lo, False) + shifted(hi, True)


def load_planes(pad_ref, refs, where, sides, wanted, planes):
    for p in sorted(wanted):
        if p < 0:
            fill(pad_ref, 0, jnp.where(sides[0][0] == 1, sides[1][...], sides[2][...]))
        elif p >= planes:
            fill(pad_ref, planes + 1, jnp.where(sides[0][0] == 1, sides[2][...], sides[1][...]))
        else:
            which, at = where[p]
            fill(pad_ref, p + 1, refs[which][at])


def forward_planes(group, planes, sides, m, taps, vol, up, grad, out, pad):
    wanted = {p + a for p in group for a in (-1, 0, 1)}
    where = {p: (0, p) for p in range(planes)}
    load_planes(pad, (m,), where, sides, wanted, planes)
    lanes, flat = 2 * WW, m.shape[1]
    for k, p in enumerate(group):

        def strip(f, carry, k=k, p=p):
            lines = [conv_row(pad, taps, p + 1, f * 2 + 1 + r, False) for r in range(2)]
            spatial = jnp.concatenate(lines, axis=0)
            sig = 1.0 / (1.0 + jnp.exp(-spatial))
            cells = pl.ds(pl.multiple_of(f * lanes, lanes), lanes)
            source = pl.ds(pl.multiple_of(p * flat + f * lanes, lanes), lanes)
            target = pl.ds(pl.multiple_of(k * flat + f * lanes, lanes), lanes)
            cot = jnp.transpose(up[:, source].astype(F32))
            slope = sig * (1.0 + spatial * (1.0 - sig))
            grad[k, cells, :] = (cot * slope).astype(BF)
            silu = jnp.transpose(spatial * sig)
            out[:, target] = (vol[:, source].astype(F32) + silu).astype(BF)
            return carry

        lax.fori_loop(0, flat // lanes, strip, 0)


def forward_middle(group, planes, m, taps, vol, up, grad, out, pad):
    forward_planes(group, planes, (), m, taps, vol, up, grad, out, pad)


def forward_edges(planes, odd, m, near, far, taps, vol, up, grad, out, to_near, to_far, pad):
    sides = (odd, near, far)
    forward_planes((0, planes - 1), planes, sides, m, taps, vol, up, grad, out, pad)
    to_near[...] = jnp.where(odd[0] == 1, grad[0], grad[1])
    to_far[...] = jnp.where(odd[0] == 1, grad[1], grad[0])


def backward_planes(group, where, planes, sides, g0, g1, taps, put, pad):
    wanted = {p + a for p in group for a in (-1, 0, 1)}
    load_planes(pad, (g0, g1), where, sides, wanted, planes)
    lanes, flat = 2 * WW, g0.shape[1]
    for k, p in enumerate(group):

        def strip(f, carry, k=k, p=p):
            lines = [conv_row(pad, taps, p + 1, f * 2 + 1 + r, True) for r in range(2)]
            put(k, p, pl.multiple_of(f * lanes, lanes), jnp.concatenate(lines, axis=0).astype(BF))
            return carry

        lax.fori_loop(0, flat // lanes, strip, 0)


def backward_middle(group, where, planes, g0, g1, taps, out, pad):
    def put(k, p, cell, value):
        out[k, pl.ds(cell, value.shape[0]), :] = value

    backward_planes(group, where, planes, (), g0, g1, taps, put, pad)


def backward_edges(where, planes, steps, me, odd, g0, g1, near, far, taps, inner, whole, *refs):
    out, pad = refs[:-1], refs[-1]
    flat = g0.shape[1]

    def put(k, p, cell, value):
        whole[pl.ds(p * flat + cell, value.shape[0]), :] = value

    backward_planes((0, planes - 1), where, planes, (odd, near, far), g0, g1, taps, put, pad)
    for k in range(1, planes - 1):
        whole[k * flat : (k + 1) * flat, :] = inner[k - 1]
    blk = out[0].shape[0]
    for s, block in zip(steps, out):
        block[...] = whole[pl.ds(pl.multiple_of((me[0] ^ s) * blk, blk), blk), :]


def blocks(me, whole, blk, steps, after):
    def kernel(me, whole, *out):
        for s, block in zip(steps, out):
            block[...] = whole[pl.ds(pl.multiple_of((me[0] ^ s) * blk, blk), blk), :]

    shapes = [jax.ShapeDtypeStruct((blk, whole.shape[1]), BF)] * len(steps)
    return call(kernel, shapes, [], me, whole, us=0.3, after=after)


def taps_kernel(where_grad, planes, norm, steps, odd, m, near, far, g0, g1, o0, o1, *refs):
    parts, refs = refs[: len(steps)], refs[len(steps) :]
    out, output, pad, gpad = refs[0], refs[1], refs[-2], refs[-1]
    for r, part in zip(steps, parts):
        refs[2][:, r * part.shape[1] : (r + 1) * part.shape[1]] = part[...]
    flat = m.shape[1]
    output[:, :flat] = o0[:, :flat]
    output[:, flat:-flat] = o1[...]
    output[:, -flat:] = o0[:, flat:]
    where = {p: (0, p) for p in range(planes)}
    load_planes(pad, (m,), where, (odd, near, far), range(-1, planes + 1), planes)
    load_planes(gpad, (g0, g1), where_grad, (), range(planes), planes)
    rows, width, ch = pad.shape[1] - 2, pad.shape[2], pad.shape[3]
    sums = tuple(jnp.zeros((8, ch), F32) for _ in range(27))

    def line(at, sums):
        p, h = at // rows, at % rows
        sums = list(sums)
        own = gpad[p + 1, h + 1]
        turned = (shifted(own, True), own, shifted(own, False))
        for a in range(3):
            for b in range(3):
                field = pad[p + a, h + b]
                for e in range(3):
                    prod = (turned[e] * field).reshape(width // 8, 8, ch)
                    sums[a * 9 + b * 3 + e] = sums[a * 9 + b * 3 + e] + jnp.sum(prod, axis=0)
        return tuple(sums)

    sums = lax.fori_loop(0, planes * rows, line, sums)
    for k in range(27):
        out[k : k + 1, :] = jnp.sum(sums[k], axis=0, keepdims=True) * norm
    out[27:, :] = jnp.zeros((5, ch), F32)


def call(kernel, out_shape, scratch, *args, us=1.0, after=(), alias=None):
    specs = [
        pl.BlockSpec(memory_space=pltpu.SMEM if arg.dtype == jnp.int32 else pltpu.VMEM)
        for arg in args
    ]

    def wrapped(*refs):
        kernel(*refs[: len(args)], *refs[len(args) + len(after) :])

    return pl.pallas_call(
        wrapped,
        out_shape=out_shape,
        in_specs=specs + [pl.BlockSpec(memory_space=pl.ANY)] * len(after),
        out_specs=jax.tree.map(lambda _: pl.BlockSpec(memory_space=pltpu.VMEM), out_shape),
        scratch_shapes=scratch,
        input_output_aliases={} if alias is None else {alias: 0},
        compiler_params=pltpu.CompilerParams(vmem_limit_bytes=32 * 1024 * 1024),
        cost_estimate=pl.CostEstimate(
            flops=int(us * 1.15e9), bytes_accessed=1024 * 1024, transcendentals=0
        ),
    )(*args, *after)


def in_place(kernel, shape, leading, base, pieces, us):
    if base is None:
        return call(kernel, shape, [], *leading, *pieces, us=us)

    def wrapped(*refs):
        kernel(*refs[: len(leading)], *refs[len(leading) + 1 :])

    return call(wrapped, shape, [], *leading, base, *pieces, us=us, alias=len(leading))


def fold_volume(turn, base, pieces, steps):
    nf, (ch, blk) = lax.axis_size("filter"), pieces[0].shape
    if ch % 128:
        out = jnp.zeros((nf, ch, blk), BF) if base is None else base
        for t, piece in zip(steps, pieces):
            out = lax.dynamic_update_index_in_dim(out, piece, turn[0] ^ t, 0)
        return out

    def kernel(turn, *refs):
        for t, piece in zip(steps, refs[:-1]):
            lane = pl.ds(pl.multiple_of((turn[0] ^ t) * ch, 128), ch)
            refs[-1][:, lane] = jnp.transpose(piece[...])

    shape = jax.ShapeDtypeStruct((blk, nf * ch), BF)
    return in_place(kernel, shape, (turn,), base, pieces, 0.3 * len(pieces))


def mix_kernel(held, other, vol_t, *out):
    nf, ch, share = len(out), out[0].shape[1], held.shape[2]
    for s in range(0, nf, 2):
        total = None
        for v in range(2 * held.shape[0]):
            block = (other if v % 2 else held)[v // 2, s * ch : (s + 2) * ch, :]
            term = lax.dot_general(
                vol_t[:, v * share : (v + 1) * share], block, (((1,), (1,)), ((), ())),
                preferred_element_type=F32,
            )
            total = term if total is None else total + term
        out[s][...] = total[:, :ch].astype(BF)
        out[s + 1][...] = total[:, ch:].astype(BF)


def mix(vol, held, other, ch, after):
    pairs, rows, share = held.shape
    nf = rows // ch
    if ch % 128:
        vol_t = vol.reshape(rows, vol.shape[2]).T
        weights = jnp.stack([held, other], axis=1).reshape(2 * pairs, rows, share)
        out = jnp.einsum(
            "cvi,voi->co", vol_t.reshape(-1, 2 * pairs, share), weights, preferred_element_type=F32
        ).astype(BF)
        return vol_t, [out[:, s * ch : (s + 1) * ch] for s in range(nf)]
    shapes = [jax.ShapeDtypeStruct((vol.shape[0], ch), BF)] * nf
    return vol, call(mix_kernel, shapes, [], held, other, vol, us=2.6, after=after)


def unmix(turn, base, pieces, steps, held, other, ch, after):
    blk = pieces[0].shape[0]
    pairs, rows, share = held.shape
    nf = rows // ch
    if ch % 128:
        weights = jnp.stack([held, other], axis=1).reshape(2 * pairs, rows, share)
        mg = jnp.concatenate([part for _, part in sorted(list(base.items()) + list(zip(steps, pieces)))], axis=1)
        out = jnp.einsum("co,voi->vic", mg, weights, preferred_element_type=F32)
        out = out.astype(BF).reshape(nf, ch, blk)
        return mg, [pick(out, turn[0] ^ s) for s in range(nf)]

    def kernel(turn, base, held, other, *refs):
        parts, mg, out, back = refs[: len(steps)], refs[len(steps)], refs[-nf - 1 : -1], refs[-1]
        mg[...] = base[...]
        for r, part in zip(steps, parts):
            mg[:, r * ch : (r + 1) * ch] = part[...]
        for v in range(2 * pairs):
            block = (other if v % 2 else held)[v // 2]
            total = lax.dot_general(
                mg[...], block, (((1,), (0,)), ((), ())), preferred_element_type=F32
            )
            turned = jnp.transpose(total).astype(BF)
            for k in range(share // ch):
                back[v * (share // ch) + k] = turned[k * ch : (k + 1) * ch, :]
        for s in range(nf):
            out[s][...] = back[turn[0] ^ s]

    shapes = [jax.ShapeDtypeStruct((blk, rows), BF)] + [jax.ShapeDtypeStruct((ch, blk), BF)] * nf
    got = call(
        kernel, shapes, [pltpu.VMEM((nf, ch, blk), BF)], turn, base, held, other, *pieces,
        us=3.0, after=after,
    )
    return got[0], got[1:]


def split(value):
    high = value.astype(BF)
    return high, (value - high.astype(F32)).astype(BF)


def joined(high, low):
    return high.astype(F32) + low.astype(F32)


def weight_products(mg, vol_t, taps, ch, norm, ns):
    rows, share, pairs = mg.shape[1], vol_t.shape[1] // ns, ns // 2
    if halved(ch, share, ns):
        count = taps.shape[0]

        def kernel(mg, vol, taps, *refs):
            mine, theirs = refs[:pairs], refs[-1]
            for r in range(rows // ch):
                row = slice(r * ch, (r + 1) * ch)
                turned = jnp.transpose(mg[:, row])
                for v in range(ns):
                    total = norm * lax.dot_general(
                        turned, vol[:, v * share : (v + 1) * share], (((1,), (0,)), ((), ())),
                        preferred_element_type=F32,
                    )
                    if v % 2:
                        theirs[v // 2, row, :] = total.astype(BF)
                    else:
                        mine[v // 2][row, :] = total
            high, low = split(taps[...])
            theirs[0, rows:, :ch] = high
            theirs[1, rows:, :ch] = low

        shapes = [jax.ShapeDtypeStruct((rows, share), F32)] * pairs
        shapes.append(jax.ShapeDtypeStruct((pairs, rows + count, share), BF))
        got = call(kernel, shapes, [], mg, vol_t, taps, us=2.5)
        return got[:-1], got[-1]
    part = lax.dot_general(mg, vol_t, (((0,), (0,)), ((), ())), preferred_element_type=F32)
    part = (part * norm).reshape(rows, pairs, 2, share)
    return [part[:, k, 0] for k in range(pairs)], part[:, :, 1].transpose(1, 0, 2).astype(BF)


def assemble(me, base, pieces, steps):
    blk, ch = pieces[0].shape

    def kernel(me, *refs):
        for s, piece in zip(steps, refs[:-1]):
            refs[-1][me[0] ^ s] = piece[...]

    shape = jax.ShapeDtypeStruct((lax.axis_size("filter"), blk, ch), BF)
    return in_place(kernel, shape, (me,), base, pieces, 0.5)


def assemble_last(me, odd, base, pieces, steps, planes):
    nf, blk, ch = base.shape
    flat = nf * blk // planes

    def kernel(me, odd, base, *refs):
        out, near, far = refs[-3:]
        for s, piece in zip(steps, refs[:-3]):
            out[me[0] ^ s] = piece[...]
        for k in range(flat // blk):
            first, last = out[k], out[nf - flat // blk + k]
            near[k * blk : (k + 1) * blk, :] = jnp.where(odd[0] == 1, first, last)
            far[k * blk : (k + 1) * blk, :] = jnp.where(odd[0] == 1, last, first)

    edge = jax.ShapeDtypeStruct((flat, ch), BF)
    shapes = (jax.ShapeDtypeStruct((nf, blk, ch), BF), edge, edge)
    out, near, far = call(kernel, shapes, [], me, odd, base, *pieces, us=0.8, alias=2)
    return out.reshape(planes, flat, ch), near, far


def finish(me, up, base, pieces, steps):
    blk = pieces[0].shape[1]

    def kernel(me, up, *refs):
        for s, piece in zip(steps, refs[:-1]):
            lane = pl.ds(pl.multiple_of((me[0] ^ s) * blk, 128), blk)
            refs[-1][:, lane] = (up[:, lane].astype(F32) + piece[...].astype(F32)).astype(BF)

    shape = jax.ShapeDtypeStruct(up.shape, BF)
    return in_place(kernel, shape, (me, up), base, pieces, 0.25 * len(pieces))


def body(volume, mixing, kernel_taps, upstream):
    ch, planes, flat = volume.shape
    height = flat // WW
    nf, ns = lax.axis_size("filter"), lax.axis_size("space")
    me, me_space = lax.axis_index("filter"), lax.axis_index("space")
    total = planes * flat
    blk = total // nf
    norm = 1.0 / math.sqrt(ns * total)
    edges, middle = (0, planes - 1), tuple(range(1, planes - 1))
    groups = (edges, middle)
    turn = jnp.reshape(me ^ (me_space * (nf // ns)), (1,)).astype(jnp.int32)

    odd = jnp.reshape(me_space & 1, (1,)).astype(jnp.int32)
    own = jnp.reshape(me, (1,)).astype(jnp.int32)

    vol = volume.reshape(ch, total)
    mid = nf // 2
    early = [0, mid]
    later = [s for s in range(mid + 1, nf)]
    last = list(range(1, mid))

    def some(parts, steps):
        return [parts[s] for s in steps]

    send = [lax.dynamic_slice_in_dim(vol, (me ^ s) * blk, blk, axis=1) for s in range(nf)]
    pieces = exchange(send, "filter")
    steps = early + [mid + 1]
    vol_1 = fold_volume(turn, None, some(pieces, steps), steps)
    vol_2 = fold_volume(turn, vol_1, some(pieces, [mid + 2, 1]), [mid + 2, 1])
    rest = later[2:] + last[1:]
    vol_3 = fold_volume(turn, vol_2, some(pieces, rest), rest)
    held, other = gather_weights(mixing, me_space, send, vol_1, vol_2)
    up = upstream.reshape(ch, total)
    vol_t, prod = mix(vol_3, held, other, ch, (up,))

    got = exchange(prod, "filter")
    near_steps, cross = list(range(2, mid)), list(range(mid, nf))
    mixed = assemble(own, None, some(got, [0, 1]), [0, 1])
    mixed = assemble(own, mixed, some(got, near_steps), near_steps)
    mixed, near, far = assemble_last(own, odd, mixed, some(got, cross), cross, planes)
    near, far = halo(near, far)

    taps = kernel_taps.T
    pad = pltpu.VMEM((planes + 2, height + 2, WW, ch), F32)

    def grad_shapes(g):
        return (
            jax.ShapeDtypeStruct((len(g), flat, ch), BF),
            jax.ShapeDtypeStruct((ch, len(g) * flat), BF),
        )

    edge = jax.ShapeDtypeStruct((flat, ch), BF)
    grad_middle, out_middle = call(
        functools.partial(forward_middle, middle, planes), grad_shapes(middle), [pad],
        mixed, taps, vol, up, us=4.0,
    )
    grad_edges, out_edges, to_near, to_far = call(
        functools.partial(forward_edges, planes), grad_shapes(edges) + (edge, edge), [pad],
        odd, mixed, near, far, taps, vol, up, us=4.0, after=(grad_middle,),
    )
    grad_near, grad_far = halo(to_near, to_far)
    where = {p: (i, k) for i, g in enumerate(groups) for k, p in enumerate(g)}
    mg_middle = call(
        functools.partial(backward_middle, middle, where, planes),
        jax.ShapeDtypeStruct((len(middle), flat, ch), BF), [pad],
        grad_edges, grad_middle, taps, us=2.3,
    )
    steps = [0, 1] + cross
    whole, *send = call(
        functools.partial(backward_edges, where, planes, steps),
        [jax.ShapeDtypeStruct((total, ch), BF)] + [jax.ShapeDtypeStruct((blk, ch), BF)] * len(steps),
        [pad], own, odd, grad_edges, grad_middle, grad_near, grad_far, taps, mg_middle, us=2.8,
    )
    got = {s: swap(block, "filter", s) if s else block for s, block in zip(steps, send)}

    wide = ch % 128 == 0
    side = some(got, [0, 1])
    shapes = (jax.ShapeDtypeStruct((32, ch), F32), jax.ShapeDtypeStruct((ch, total), BF))
    shapes += (jax.ShapeDtypeStruct((blk, nf * ch), BF),) if wide else ()
    kernel = functools.partial(taps_kernel, where, planes, norm, [0, 1] if wide else [])
    taps_grad, output, *mg = call(
        kernel, shapes, [pad, pad],
        odd, mixed, near, far, grad_edges, grad_middle, out_edges, out_middle,
        *(side if wide else []), us=5.8,
    )
    output = output.reshape(ch, planes, flat)
    send = blocks(own, whole, blk, near_steps, (taps_grad,))
    got.update((s, swap(block, "filter", s)) for s, block in zip(near_steps, send))
    base = mg[0] if wide else dict(zip([0, 1], side))
    rest = cross + near_steps
    mg_all, back = unmix(
        turn, base, some(got, rest), rest, held, other, ch, ()
    )
    got = exchange(back, "filter")
    mine, theirs = weight_products(mg_all, vol_t, taps_grad, ch, norm, ns)
    volume_grad_1 = finish(own, up, None, some(got, early), early)
    volume_grad_2 = finish(own, up, volume_grad_1, some(got, later), later)
    mixing_grad, taps_grad = scatter_rest(
        mine, theirs, taps_grad, ch, volume_grad_1, volume_grad_2
    )
    volume_grad = finish(own, up, volume_grad_2, some(got, last), last)
    volume_grad = volume_grad.reshape(ch, planes, flat)
    return (output, volume_grad, mixing_grad, taps_grad[:27].T)


def solution(mesh):
    in_specs = (
        P("filter", "space", None),
        P("filter", None),
        P("filter", None),
        P("filter", "space", None),
    )
    out_specs = (
        P("filter", "space", None),
        P("filter", "space", None),
        P("filter", "space"),
        P("filter", None),
    )
    return jax.shard_map(body, mesh=mesh, in_specs=in_specs, out_specs=out_specs, check_vma=False)
```

time: 190 us -> 175 us (0.921)
  waiting for transfers between devices: 67.9 us -> 57.6 us
  local copies, waits for them, and re-layouts: 19.9 us -> 14.4 us
  starting transfers between devices: 67.5 us -> 71.3 us
  Pallas kernels: 32 us -> 30 us
    ppermute x43, waiting for transfers between devices: 67.9 us -> 57.6 us  [swap(): return lax.ppermute(block, axis, [(i, i ^ step) for i in range(size)])]
    unnamed x40 -> x58, local copies, waits for them, and re-layouts: 16.7 us -> 9.77 us
    ppermute x43, starting transfers between devices: 62.2 us -> 66.1 us  [swap(): return lax.ppermute(block, axis, [(i, i ^ step) for i in range(size)])]
    pallas_call x16 -> x24, Pallas kernels: 32 us -> 30 us  [call(): pl.pallas_call(wrapped, out_shape=out_shape, in_specs=specs + [pl.BlockSp...]
  transfers between devices with their start and end apart: 47 -> 47, of which waited for: 21 -> 19; matrix products, arithmetic and copies ran while one was open for 4% -> 4% of each run, Pallas kernels for 8% -> 9%
where the time goes in v7:
time: 175 us
  starting transfers between devices  71.3 us (41%)
  waiting for transfers between devices  57.6 us (33%)
  Pallas kernels  30 us (17%)
  local copies, waits for them, and re-layouts  14.4 us (8%)
    ppermute x43, starting transfers between devices, swap(): return lax.ppermute(block, axis, [(i, i ^ step) for i in range(size)])  66.1 us
    ppermute x43, waiting for transfers between devices, swap(): return lax.ppermute(block, axis, [(i, i ^ step) for i in range(size)])  57.6 us
    pallas_call x24, Pallas kernels, call(): pl.pallas_call(wrapped, out_shape=out_shape, in_specs=specs + [pl.BlockSp...  30 us
    unnamed x58, local copies, waits for them, and re-layouts  9.77 us
    ppermute x2, starting transfers between devices, halo(): lax.ppermute(near, 'space', inner)  3.64 us
  transfers between devices with their start and end apart: 47, of which 19 were waited for; matrix products, arithmetic and copies ran while one was open for 4% of the time, Pallas kernels for 9%

profile of v7, /device:TPU:0, one launch (start us, length us, event | category | flops | bytes accessed | tf_op | source)
XLA Modules:
  0.0 175.2 jit_solution(3500310115406685570)
XLA Ops:
  1.6 5.1 %collective-permute-start.2 = (bf16[128,256]{1,0:T(8,128)(2,1)S(1)}, bf16[128,256]{1,0:T(8,128)(2,1)S(1)}, u32[]{:S(2)}, u32[]{:S(2)}) collective-permute-start(bf16[128,256]{1,0:T(8,128)(2,1)S(1)} %constant_dynamic-slice_fusion.8.refs_0_), channel_id=1, source_target_pairs={{0,24},{4,28},{8,16},{12,20},{16,8},{20,12},{24,0},{28,4},{1,25},{... | collective-permute-start | bytes 196616 | tf_op jit(solution)/shard_map/ppermute | solution.py:18
  9.8 2.5 %collective-permute-done.1.refs_2_ = bf16[128,256]{1,0:T(8,128)(2,1)S(1)} collective-permute-done((bf16[128,256]{1,0:T(8,128)(2,1)S(1)}, bf16[128,256]{1,0:T(8,128)(2,1)S(1)}, u32[]{:S(2)}, u32[]{:S(2)}) %collective-permute-start.1) | collective-permute-done | bytes 65568 | tf_op jit(solution)/shard_map/ppermute | solution.py:18
  18.3 7.8 %collective-permute-done.6.refs_3_ = bf16[128,512]{1,0:T(8,128)(2,1)S(1)} collective-permute-done((bf16[128,512]{1,0:T(8,128)(2,1)S(1)}, bf16[128,512]{1,0:T(8,128)(2,1)S(1)}, u32[]{:S(2)}, u32[]{:S(2)}) %collective-permute-start.6) | collective-permute-done | bytes 131104 | tf_op jit(solution)/shard_map/ppermute | solution.py:18
  34.3 3.3 %collective-permute-done.8.refs_2_ = bf16[128,512]{1,0:T(8,128)(2,1)S(1)} collective-permute-done((bf16[128,512]{1,0:T(8,128)(2,1)S(1)}, bf16[128,512]{1,0:T(8,128)(2,1)S(1)}, u32[]{:S(2)}, u32[]{:S(2)}) %collective-permute-start.8) | collective-permute-done | bytes 131104 | tf_op jit(solution)/shard_map/ppermute | solution.py:18
  40.6 2.6 %collective-permute-start.11 = (bf16[128,512]{1,0:T(8,128)(2,1)S(1)}, bf16[128,512]{1,0:T(8,128)(2,1)S(1)}, u32[]{:S(2)}, u32[]{:S(2)}) collective-permute-start(bf16[128,512]{1,0:T(8,128)(2,1)S(1)} %get-tuple-element.120.refs_7_), channel_id=1, source_target_pairs={{0,28},{4,24},{8,20},{12,16},{16,12},{20,8},{24,4},{28,0},{1,29},{... | collective-permute-start | bytes 393224 | tf_op jit(solution)/shard_map/ppermute | solution.py:18
  43.6 2.5 %collective-permute-done.13.refs_4_ = bf16[128,512]{1,0:T(8,128)(2,1)S(1)} collective-permute-done((bf16[128,512]{1,0:T(8,128)(2,1)S(1)}, bf16[128,512]{1,0:T(8,128)(2,1)S(1)}, u32[]{:S(2)}, u32[]{:S(2)}) %collective-permute-start.13) | collective-permute-done | bytes 131104 | tf_op jit(solution)/shard_map/ppermute | solution.py:18
  47.5 2.1 %collective-permute-done.11.refs_2_ = bf16[128,512]{1,0:T(8,128)(2,1)S(1)} collective-permute-done((bf16[128,512]{1,0:T(8,128)(2,1)S(1)}, bf16[128,512]{1,0:T(8,128)(2,1)S(1)}, u32[]{:S(2)}, u32[]{:S(2)}) %collective-permute-start.11) | collective-permute-done | bytes 131104 | tf_op jit(solution)/shard_map/ppermute | solution.py:18
  49.8 2.1 %shard_map.81 = (bf16[512,128]{1,0:T(8,128)(2,1)S(1)}, bf16[512,128]{1,0:T(8,128)(2,1)S(1)}, bf16[512,128]{1,0:T(8,128)(2,1)S(1)}, bf16[512,128]{1,0:T(8,128)(2,...) custom-call(bf16[2,1024,256]{2,1,0:T(8,128)(2,1)S(1)} %shard_map.79., ...), custom_call_target="tpu_custom_call" | custom-call | flops 2990000128 | bytes 1048576 | tf_op jit(solution)/shard_map/pallas_call | solution.py:345
  53.9 2.2 %collective-permute-start.16 = (bf16[512,128]{1,0:T(8,128)(2,1)}, bf16[512,128]{1,0:T(8,128)(2,1)}, u32[]{:S(2)}, u32[]{:S(2)}) collective-permute-start(bf16[512,128]{1,0:T(8,128)(2,1)} %get-tuple-element.63), channel_id=1, source_target_pairs={{0,12},{4,8},{8,4},{12,0},{16,28},{20,24},{24,20},{28,16},{1,13},{... | collective-permute-start | bytes 393224 | tf_op jit(solution)/shard_map/ppermute | solution.py:18
  56.5 3.2 %collective-permute-start.18 = (bf16[512,128]{1,0:T(8,128)(2,1)}, bf16[512,128]{1,0:T(8,128)(2,1)}, u32[]{:S(2)}, u32[]{:S(2)}) collective-permute-start(bf16[512,128]{1,0:T(8,128)(2,1)} %get-tuple-element.65), channel_id=1, source_target_pairs={{0,20},{4,16},{8,28},{12,24},{16,4},{20,0},{24,12},{28,8},{1,21},{... | collective-permute-start | bytes 393224 | tf_op jit(solution)/shard_map/ppermute | solution.py:18
  67.1 7.3 %collective-permute-done.17.refs_3_ = bf16[512,128]{1,0:T(8,128)(2,1)} collective-permute-done((bf16[512,128]{1,0:T(8,128)(2,1)}, bf16[512,128]{1,0:T(8,128)(2,1)}, u32[]{:S(2)}, u32[]{:S(2)}) %collective-permute-start.17) | collective-permute-done | bytes 131104 | tf_op jit(solution)/shard_map/ppermute | solution.py:18
  74.4 3.4 %collective-permute-done.18.refs_4_ = bf16[512,128]{1,0:T(8,128)(2,1)} collective-permute-done((bf16[512,128]{1,0:T(8,128)(2,1)}, bf16[512,128]{1,0:T(8,128)(2,1)}, u32[]{:S(2)}, u32[]{:S(2)}) %collective-permute-start.18) | collective-permute-done | bytes 131104 | tf_op jit(solution)/shard_map/ppermute | solution.py:18
  79.8 3.9 %shard_map.85 = (bf16[2,1024,128]{2,1,0:T(8,128)(2,1)S(1)}, bf16[128,2048]{1,0:T(8,128)(2,1)S(1)}) custom-call(bf16[4,1024,128]{2,1,0:T(8,128)(2,1)S(1)} %bitcast.21, f32[27,128]{1,0:T(8,128)S(1)} %bitcast.26, bf16[128,4096]{1,0:T(8,128)(2,1)S(1)} %bitcast.19, bf16[128,4096]{1,0:T(8,128)(2,1)S(1)} %bitcast.13), custom_call_target="tpu_custom_call" | custom-call | flops 4600000000 | bytes 1048576 | tf_op jit(solution)/shard_map/pallas_call | solution.py:345
  83.7 4.2 %shard_map.86 = (bf16[2,1024,128]{2,1,0:T(8,128)(2,1)S(1)}, bf16[128,2048]{1,0:T(8,128)(2,1)S(1)}, bf16[1024,128]{1,0:T(8,128)(2,1)S(1)}, bf16[1024,128]{1,0:T(8,128)(2,1)S(1)}) custom-call(s32[1]{0:T(128)} %bitcast.refs_1_.refs_0_, bf16[4,1024,128]{2,1,0:T(8,128)(2,1)S(1)} %bitcast.22, bf16[1024,128]{1,0:T(8,128)(2,1)S(1)} %collective-permute-done.21.refs_2_, ...), custom_call_target="tpu_custom_call" | custom-call | flops 4600000000 | bytes 1048576 | tf_op jit(solution)/shard_map/pallas_call | solution.py:345
  87.9 3.6 %collective-permute-start.23 = (bf16[1024,128]{1,0:T(8,128)(2,1)S(1)}, bf16[1024,128]{1,0:T(8,128)(2,1)S(1)}, u32[]{:S(2)}, u32[]{:S(2)}) collective-permute-start(bf16[1024,128]{1,0:T(8,128)(2,1)S(1)} %get-tuple-element.75), channel_id=1, source_target_pairs={{0,1},{1,0},{2,3},{3,2},{4,5},{5,4},{6,7},{7,6},{8,9},{9,8},{10,11... | collective-permute-start | bytes 786440 | tf_op jit(solution)/shard_map/ppermute | solution.py:180
  92.4 2.3 %shard_map.87.refs_7_ = bf16[2,1024,128]{2,1,0:T(8,128)(2,1)S(1)} custom-call(bf16[2,1024,128]{2,1,0:T(8,128)(2,1)S(1)} %get-tuple-element.72.refs_0_.refs_2_.refs_4_, bf16[2,1024,128]{2,1,0:T(8,128)(2,1)S(1)} %get-tuple-element.71.refs_7_.refs_1_.refs_3_.refs_5_, f32[27,128]{1,0:T(8,128)S(1)} %bitcast.28), custom_call_target="tpu_custom_call" | custom-call | flops 2644999936 | bytes 1048576 | tf_op jit(solution)/shard_map/pallas_call | solution.py:345
  94.7 2.5 %shard_map.88 = (bf16[4096,128]{1,0:T(8,128)(2,1)S(1)}, bf16[512,128]{1,0:T(8,128)(2,1)S(1)}, bf16[512,128]{1,0:T(8,128)(2,1)S(1)}, bf16[512,128]{1,0:T(8,128)(2...) custom-call(s32[1]{0:T(128)} %bitcast.1.refs_0_, ...), custom_call_target="tpu_custom_call" | custom-call | flops 3220000000 | bytes 1048576 | tf_op jit(solution)/shard_map/pallas_call | solution.py:345
  98.2 4.3 %collective-permute-start.26 = (bf16[512,128]{1,0:T(8,128)(2,1)S(1)}, bf16[512,128]{1,0:T(8,128)(2,1)S(1)}, u32[]{:S(2)}, u32[]{:S(2)}) collective-permute-start(bf16[512,128]{1,0:T(8,128)(2,1)S(1)} %get-tuple-element.81), channel_id=1, source_target_pairs={{0,16},{4,20},{8,24},{12,28},{16,0},{20,4},{24,8},{28,12},{1,17},{... | collective-permute-start | bytes 393224 | tf_op jit(solution)/shard_map/ppermute | solution.py:18
  105.4 2.1 %collective-permute-start.29 = (bf16[512,128]{1,0:T(8,128)(2,1)S(1)}, bf16[512,128]{1,0:T(8,128)(2,1)S(1)}, u32[]{:S(2)}, u32[]{:S(2)}) collective-permute-start(bf16[512,128]{1,0:T(8,128)(2,1)S(1)} %get-tuple-element.84), channel_id=1, source_target_pairs={{0,28},{4,24},{8,20},{12,16},{16,12},{20,8},{24,4},{28,0},{1,29},{... | collective-permute-start | bytes 393224 | tf_op jit(solution)/shard_map/ppermute | solution.py:18
  107.5 5.5 %shard_map.89 = (f32[32,128]{1,0:T(8,128)S(1)}, bf16[128,4096]{1,0:T(8,128)(2,1)S(1)}, bf16[512,1024]{1,0:T(8,128)(2,1)S(1)}) custom-call(s32[1]{0:T(128)} %bitcast.refs_1_.refs_0_, bf16[4,1024,128]{2,1,0:T(8,128)(2,1)S(1)} %bitcast.23, bf16[1024,128]{1,0:T(8,128)(2,1)S(1)} %collective-permute-done.21.refs_2_, ...), custom_call_target="tpu_custom_call" | custom-call | flops 6670000128 | bytes 1048576 | tf_op jit(solution)/shard_map/pallas_call | solution.py:345
  114.7 2.3 %collective-permute-start.31 = (bf16[512,128]{1,0:T(8,128)(2,1)S(1)}, bf16[512,128]{1,0:T(8,128)(2,1)S(1)}, u32[]{:S(2)}, u32[]{:S(2)}) collective-permute-start(bf16[512,128]{1,0:T(8,128)(2,1)S(1)} %get-tuple-element.88), channel_id=1, source_target_pairs={{0,12},{4,8},{8,4},{12,0},{16,28},{20,24},{24,20},{28,16},{1,13},{... | collective-permute-start | bytes 393224 | tf_op jit(solution)/shard_map/ppermute | solution.py:18
  117.0 3.9 %collective-permute-done.27.refs_5_ = bf16[512,128]{1,0:T(8,128)(2,1)S(1)} collective-permute-done((bf16[512,128]{1,0:T(8,128)(2,1)S(1)}, bf16[512,128]{1,0:T(8,128)(2,1)S(1)}, u32[]{:S(2)}, u32[]{:S(2)}) %collective-permute-start.27) | collective-permute-done | bytes 131104 | tf_op jit(solution)/shard_map/ppermute | solution.py:18
  121.0 3.3 %collective-permute-done.30.refs_8_ = bf16[512,128]{1,0:T(8,128)(2,1)S(1)} collective-permute-done((bf16[512,128]{1,0:T(8,128)(2,1)S(1)}, bf16[512,128]{1,0:T(8,128)(2,1)S(1)}, u32[]{:S(2)}, u32[]{:S(2)}) %collective-permute-start.30) | collective-permute-done | bytes 131104 | tf_op jit(solution)/shard_map/ppermute | solution.py:18
  124.3 3.6 %collective-permute-done.31.refs_9_ = bf16[512,128]{1,0:T(8,128)(2,1)S(1)} collective-permute-done((bf16[512,128]{1,0:T(8,128)(2,1)S(1)}, bf16[512,128]{1,0:T(8,128)(2,1)S(1)}, u32[]{:S(2)}, u32[]{:S(2)}) %collective-permute-start.31) | collective-permute-done | bytes 131104 | tf_op jit(solution)/shard_map/ppermute | solution.py:18
  127.9 2.1 %shard_map.91 = (bf16[512,1024]{1,0:T(8,128)(2,1)S(1)}, bf16[128,512]{1,0:T(8,128)(2,1)S(1)}, bf16[128,512]{1,0:T(8,128)(2,1)S(1)}, bf16[128,512]{1,0:T(8,128)(2...) custom-call(s32[1]{0:T(128)} %bitcast.2.refs_0_, ...), custom_call_target="tpu_custom_call" | custom-call | flops 3449999872 | bytes 1048576 | tf_op jit(solution)/shard_map/pallas_call | solution.py:345
  132.2 2.6 %collective-permute-done.39.refs_2_ = bf16[2,1056,256]{2,1,0:T(8,128)(2,1)S(1)} collective-permute-done((bf16[2,1056,256]{2,1,0:T(8,128)(2,1)S(1)}, bf16[2,1056,256]{2,1,0:T(8,128)(2,1)S(1)}, u32[]{:S(2)}, u32[]{:S(2)}) %collective-permute-start.39) | collective-permute-done | bytes 1081376 | tf_op jit(solution)/shard_map/ppermute | solution.py:18
  140.7 2.3 %collective-permute-start.33 = (bf16[128,512]{1,0:T(8,128)(2,1)}, bf16[128,512]{1,0:T(8,128)(2,1)S(1)}, u32[]{:S(2)}, u32[]{:S(2)}) collective-permute-start(bf16[128,512]{1,0:T(8,128)(2,1)} %copy-done.19), channel_id=1, source_target_pairs={{0,20},{4,16},{8,28},{12,24},{16,4},{20,0},{24,12},{28,8},{1,21},{... | collective-permute-start | bytes 393224 | tf_op jit(solution)/shard_map/ppermute | solution.py:18
  143.0 2.2 %collective-permute-start.34 = (bf16[128,512]{1,0:T(8,128)(2,1)}, bf16[128,512]{1,0:T(8,128)(2,1)S(1)}, u32[]{:S(2)}, u32[]{:S(2)}) collective-permute-start(bf16[128,512]{1,0:T(8,128)(2,1)} %copy-done.18), channel_id=1, source_target_pairs={{0,24},{4,28},{8,16},{12,20},{16,8},{20,12},{24,0},{28,4},{1,25},{... | collective-permute-start | bytes 393224 | tf_op jit(solution)/shard_map/ppermute | solution.py:18
  145.2 7.8 %collective-permute-done.32.refs_3_ = bf16[128,512]{1,0:T(8,128)(2,1)} collective-permute-done((bf16[128,512]{1,0:T(8,128)(2,1)}, bf16[128,512]{1,0:T(8,128)(2,1)}, u32[]{:S(2)}, u32[]{:S(2)}) %collective-permute-start.32) | collective-permute-done | bytes 131104 | tf_op jit(solution)/shard_map/ppermute | solution.py:18
  153.0 2.5 %collective-permute-start.35 = (bf16[128,512]{1,0:T(8,128)(2,1)}, bf16[128,512]{1,0:T(8,128)(2,1)S(1)}, u32[]{:S(2)}, u32[]{:S(2)}) collective-permute-start(bf16[128,512]{1,0:T(8,128)(2,1)} %copy-done.17), channel_id=1, source_target_pairs={{0,28},{4,24},{8,20},{12,16},{16,12},{20,8},{24,4},{28,0},{1,29},{... | collective-permute-start | bytes 393224 | tf_op jit(solution)/shard_map/ppermute | solution.py:18
  162.2 3.2 %collective-permute-start.38 = (bf16[128,512]{1,0:T(8,128)(2,1)S(1)}, bf16[128,512]{1,0:T(8,128)(2,1)S(1)}, u32[]{:S(2)}, u32[]{:S(2)}) collective-permute-start(bf16[128,512]{1,0:T(8,128)(2,1)S(1)} %copy-done.12), channel_id=1, source_target_pairs={{0,12},{4,8},{8,4},{12,0},{16,28},{20,24},{24,20},{28,16},{1,13},{... | collective-permute-start | bytes 393224 | tf_op jit(solution)/shard_map/ppermute | solution.py:18
  165.7 2.3 %collective-permute-start.45 = (bf16[128,256]{1,0:T(8,128)(2,1)S(1)}, bf16[128,256]{1,0:T(8,128)(2,1)S(1)}, u32[]{:S(2)}, u32[]{:S(2)}) collective-permute-start(bf16[128,256]{1,0:T(8,128)(2,1)S(1)} %get-tuple-element.113), channel_id=1, source_target_pairs={{0,16},{4,20},{8,24},{12,28},{16,0},{20,4},{24,8},{28,12},{1,17},{... | collective-permute-start | bytes 196616 | tf_op jit(solution)/shard_map/ppermute | solution.py:18
  (150 shorter events, 63.3 us)
Async XLA Ops:
  1.6 8.2 %collective-permute-start.2 = (bf16[128,256]{1,0:T(8,128)(2,1)S(1)}, bf16[128,256]{1,0:T(8,128)(2,1)S(1)}, u32[]{:S(2)}, u32[]{:S(2)}) collective-permute-start(bf16[128,256]{1,0:T(8,128)(2,1)S(1)} %constant_dynamic-slice_fusion.8.refs_0_), channel_id=1, source_target_pairs={{0,24},{4,28},{8,16},{12,20},{16,8},{20,12},{24,0},{28,4},{1,25},{... | collective-permute-start | bytes 196616 | tf_op jit(solution)/shard_map/ppermute | solution.py:18
  12.3 15.4 %collective-permute-start.4 = (bf16[4,128,256]{2,1,0:T(8,128)(2,1)S(1)}, bf16[4,128,256]{2,1,0:T(8,128)(2,1)S(1)}, u32[]{:S(2)}, u32[]{:S(2)}) collective-permute-start(bf16[4,128,256]{2,1,0:T(8,128)(2,1)S(1)} %shard_map.75.refs_0_), channel_id=1, source_target_pairs={{0,4},{4,0},{8,12},{12,8},{16,20},{20,16},{24,28},{28,24},{1,5},{5... | collective-permute-start | bytes 786440 | tf_op jit(solution)/shard_map/ppermute | solution.py:18
  13.9 12.2 %collective-permute-start.6 = (bf16[128,512]{1,0:T(8,128)(2,1)S(1)}, bf16[128,512]{1,0:T(8,128)(2,1)S(1)}, u32[]{:S(2)}, u32[]{:S(2)}) collective-permute-start(bf16[128,512]{1,0:T(8,128)(2,1)S(1)} %get-tuple-element.122.refs_5_), channel_id=1, source_target_pairs={{0,20},{4,16},{8,28},{12,24},{16,4},{20,0},{24,12},{28,8},{1,21},{... | collective-permute-start | bytes 393224 | tf_op jit(solution)/shard_map/ppermute | solution.py:18
  15.5 12.1 %collective-permute-start.5 = (bf16[128,512]{1,0:T(8,128)(2,1)S(1)}, bf16[128,512]{1,0:T(8,128)(2,1)S(1)}, u32[]{:S(2)}, u32[]{:S(2)}) collective-permute-start(bf16[128,512]{1,0:T(8,128)(2,1)S(1)} %get-tuple-element.123.refs_4_), channel_id=1, source_target_pairs={{0,16},{4,20},{8,24},{12,28},{16,0},{20,4},{24,8},{28,12},{1,17},{... | collective-permute-start | bytes 393224 | tf_op jit(solution)/shard_map/ppermute | solution.py:18
  16.8 21.0 %collective-permute-start.3 = (bf16[4,128,256]{2,1,0:T(8,128)(2,1)S(1)}, bf16[4,128,256]{2,1,0:T(8,128)(2,1)S(1)}, u32[]{:S(2)}, u32[]{:S(2)}) collective-permute-start(bf16[4,128,256]{2,1,0:T(8,128)(2,1)S(1)} %shard_map.75.refs_0_), channel_id=1, source_target_pairs={{0,2},{1,3},{2,0},{3,1},{4,6},{5,7},{6,4},{7,5},{8,10},{9,11},{10,... | collective-permute-start | bytes 786440 | tf_op jit(solution)/shard_map/ppermute | solution.py:18
  27.8 10.0 %collective-permute-start.7 = (bf16[4,128,256]{2,1,0:T(8,128)(2,1)S(1)}, bf16[4,128,256]{2,1,0:T(8,128)(2,1)S(1)}, u32[]{:S(2)}, u32[]{:S(2)}) collective-permute-start(bf16[4,128,256]{2,1,0:T(8,128)(2,1)S(1)} %bitcast.24), channel_id=1, source_target_pairs={{0,2},{1,3},{2,0},{3,1},{4,6},{5,7},{6,4},{7,5},{8,10},{9,11},{10,... | collective-permute-start | bytes 786440 | tf_op jit(solution)/shard_map/ppermute | solution.py:18
  37.9 11.9 %collective-permute-start.10 = (bf16[2,1024,256]{2,1,0:T(8,128)(2,1)S(1)}, bf16[2,1024,256]{2,1,0:T(8,128)(2,1)S(1)}, u32[]{:S(2)}, u32[]{:S(2)}) collective-permute-start(bf16[2,1024,256]{2,1,0:T(8,128)(2,1)S(1)} %shard_map.79.refs_0_.refs_2_), channel_id=1, source_target_pairs={{0,1},{1,0},{2,3},{3,2},{4,5},{5,4},{6,7},{7,6},{8,9},{9,8},{10,11... | collective-permute-start | bytes 3145736 | tf_op jit(solution)/shard_map/ppermute | solution.py:18
  38.7 8.8 %collective-permute-start.12 = (bf16[128,512]{1,0:T(8,128)(2,1)S(1)}, bf16[128,512]{1,0:T(8,128)(2,1)S(1)}, u32[]{:S(2)}, u32[]{:S(2)}) collective-permute-start(bf16[128,512]{1,0:T(8,128)(2,1)S(1)} %copy-done.26), channel_id=1, source_target_pairs={{0,8},{4,12},{8,0},{12,4},{16,24},{20,28},{24,16},{28,20},{1,9},{5... | collective-permute-start | bytes 393224 | tf_op jit(solution)/shard_map/ppermute | solution.py:18
  40.6 9.0 %collective-permute-start.11 = (bf16[128,512]{1,0:T(8,128)(2,1)S(1)}, bf16[128,512]{1,0:T(8,128)(2,1)S(1)}, u32[]{:S(2)}, u32[]{:S(2)}) collective-permute-start(bf16[128,512]{1,0:T(8,128)(2,1)S(1)} %get-tuple-element.120.refs_7_), channel_id=1, source_target_pairs={{0,28},{4,24},{8,20},{12,16},{16,12},{20,8},{24,4},{28,0},{1,29},{... | collective-permute-start | bytes 393224 | tf_op jit(solution)/shard_map/ppermute | solution.py:18
  53.9 8.7 %collective-permute-start.15 = (bf16[512,128]{1,0:T(8,128)(2,1)S(1)}, bf16[512,128]{1,0:T(8,128)(2,1)S(1)}, u32[]{:S(2)}, u32[]{:S(2)}) collective-permute-start(bf16[512,128]{1,0:T(8,128)(2,1)S(1)} %get-tuple-element.62), channel_id=1, source_target_pairs={{0,8},{4,12},{8,0},{12,4},{16,24},{20,28},{24,16},{28,20},{1,9},{5... | collective-permute-start | bytes 393224 | tf_op jit(solution)/shard_map/ppermute | solution.py:18
  53.9 12.3 %collective-permute-start.16 = (bf16[512,128]{1,0:T(8,128)(2,1)}, bf16[512,128]{1,0:T(8,128)(2,1)}, u32[]{:S(2)}, u32[]{:S(2)}) collective-permute-start(bf16[512,128]{1,0:T(8,128)(2,1)} %get-tuple-element.63), channel_id=1, source_target_pairs={{0,12},{4,8},{8,4},{12,0},{16,28},{20,24},{24,20},{28,16},{1,13},{... | collective-permute-start | bytes 393224 | tf_op jit(solution)/shard_map/ppermute | solution.py:18
  56.1 18.3 %collective-permute-start.17 = (bf16[512,128]{1,0:T(8,128)(2,1)}, bf16[512,128]{1,0:T(8,128)(2,1)}, u32[]{:S(2)}, u32[]{:S(2)}) collective-permute-start(bf16[512,128]{1,0:T(8,128)(2,1)} %get-tuple-element.64), channel_id=1, source_target_pairs={{0,16},{4,20},{8,24},{12,28},{16,0},{20,4},{24,8},{28,12},{1,17},{... | collective-permute-start | bytes 393224 | tf_op jit(solution)/shard_map/ppermute | solution.py:18
  56.5 21.2 %collective-permute-start.18 = (bf16[512,128]{1,0:T(8,128)(2,1)}, bf16[512,128]{1,0:T(8,128)(2,1)}, u32[]{:S(2)}, u32[]{:S(2)}) collective-permute-start(bf16[512,128]{1,0:T(8,128)(2,1)} %get-tuple-element.65), channel_id=1, source_target_pairs={{0,20},{4,16},{8,28},{12,24},{16,4},{20,0},{24,12},{28,8},{1,21},{... | collective-permute-start | bytes 393224 | tf_op jit(solution)/shard_map/ppermute | solution.py:18
  60.4 17.4 %collective-permute-start.19 = (bf16[512,128]{1,0:T(8,128)(2,1)}, bf16[512,128]{1,0:T(8,128)(2,1)}, u32[]{:S(2)}, u32[]{:S(2)}) collective-permute-start(bf16[512,128]{1,0:T(8,128)(2,1)} %get-tuple-element.66), channel_id=1, source_target_pairs={{0,24},{4,28},{8,16},{12,20},{16,8},{20,12},{24,0},{28,4},{1,25},{... | collective-permute-start | bytes 393224 | tf_op jit(solution)/shard_map/ppermute | solution.py:18
  62.6 15.2 %collective-permute-start.20 = (bf16[512,128]{1,0:T(8,128)(2,1)}, bf16[512,128]{1,0:T(8,128)(2,1)}, u32[]{:S(2)}, u32[]{:S(2)}) collective-permute-start(bf16[512,128]{1,0:T(8,128)(2,1)} %get-tuple-element.67), channel_id=1, source_target_pairs={{0,28},{4,24},{8,20},{12,16},{16,12},{20,8},{24,4},{28,0},{1,29},{... | collective-permute-start | bytes 393224 | tf_op jit(solution)/shard_map/ppermute | solution.py:18
  97.2 10.3 %collective-permute-start.25 = (bf16[512,128]{1,0:T(8,128)(2,1)S(1)}, bf16[512,128]{1,0:T(8,128)(2,1)S(1)}, u32[]{:S(2)}, u32[]{:S(2)}) collective-permute-start(bf16[512,128]{1,0:T(8,128)(2,1)S(1)} %get-tuple-element.78), channel_id=1, source_target_pairs={{0,4},{4,0},{8,12},{12,8},{16,20},{20,16},{24,28},{28,24},{1,5},{5... | collective-permute-start | bytes 393224 | tf_op jit(solution)/shard_map/ppermute | solution.py:18
  98.2 16.5 %collective-permute-start.26 = (bf16[512,128]{1,0:T(8,128)(2,1)S(1)}, bf16[512,128]{1,0:T(8,128)(2,1)S(1)}, u32[]{:S(2)}, u32[]{:S(2)}) collective-permute-start(bf16[512,128]{1,0:T(8,128)(2,1)S(1)} %get-tuple-element.81), channel_id=1, source_target_pairs={{0,16},{4,20},{8,24},{12,28},{16,0},{20,4},{24,8},{28,12},{1,17},{... | collective-permute-start | bytes 393224 | tf_op jit(solution)/shard_map/ppermute | solution.py:18
  102.5 18.4 %collective-permute-start.27 = (bf16[512,128]{1,0:T(8,128)(2,1)S(1)}, bf16[512,128]{1,0:T(8,128)(2,1)S(1)}, u32[]{:S(2)}, u32[]{:S(2)}) collective-permute-start(bf16[512,128]{1,0:T(8,128)(2,1)S(1)} %get-tuple-element.82), channel_id=1, source_target_pairs={{0,20},{4,16},{8,28},{12,24},{16,4},{20,0},{24,12},{28,8},{1,21},{... | collective-permute-start | bytes 393224 | tf_op jit(solution)/shard_map/ppermute | solution.py:18
  103.7 17.3 %collective-permute-start.28 = (bf16[512,128]{1,0:T(8,128)(2,1)S(1)}, bf16[512,128]{1,0:T(8,128)(2,1)S(1)}, u32[]{:S(2)}, u32[]{:S(2)}) collective-permute-start(bf16[512,128]{1,0:T(8,128)(2,1)S(1)} %get-tuple-element.83), channel_id=1, source_target_pairs={{0,24},{4,28},{8,16},{12,20},{16,8},{20,12},{24,0},{28,4},{1,25},{... | collective-permute-start | bytes 393224 | tf_op jit(solution)/shard_map/ppermute | solution.py:18
  105.4 15.6 %collective-permute-start.29 = (bf16[512,128]{1,0:T(8,128)(2,1)S(1)}, bf16[512,128]{1,0:T(8,128)(2,1)S(1)}, u32[]{:S(2)}, u32[]{:S(2)}) collective-permute-start(bf16[512,128]{1,0:T(8,128)(2,1)S(1)} %get-tuple-element.84), channel_id=1, source_target_pairs={{0,28},{4,24},{8,20},{12,16},{16,12},{20,8},{24,4},{28,0},{1,29},{... | collective-permute-start | bytes 393224 | tf_op jit(solution)/shard_map/ppermute | solution.py:18
  114.0 10.3 %collective-permute-start.30 = (bf16[512,128]{1,0:T(8,128)(2,1)S(1)}, bf16[512,128]{1,0:T(8,128)(2,1)S(1)}, u32[]{:S(2)}, u32[]{:S(2)}) collective-permute-start(bf16[512,128]{1,0:T(8,128)(2,1)S(1)} %get-tuple-element.87), channel_id=1, source_target_pairs={{0,8},{4,12},{8,0},{12,4},{16,24},{20,28},{24,16},{28,20},{1,9},{5... | collective-permute-start | bytes 393224 | tf_op jit(solution)/shard_map/ppermute | solution.py:18
  114.7 13.2 %collective-permute-start.31 = (bf16[512,128]{1,0:T(8,128)(2,1)S(1)}, bf16[512,128]{1,0:T(8,128)(2,1)S(1)}, u32[]{:S(2)}, u32[]{:S(2)}) collective-permute-start(bf16[512,128]{1,0:T(8,128)(2,1)S(1)} %get-tuple-element.88), channel_id=1, source_target_pairs={{0,12},{4,8},{8,4},{12,0},{16,28},{20,24},{24,20},{28,16},{1,13},{... | collective-permute-start | bytes 393224 | tf_op jit(solution)/shard_map/ppermute | solution.py:18
  137.1 19.5 %collective-permute-start.40 = (bf16[1088,128]{1,0:T(8,128)(2,1)}, bf16[1088,128]{1,0:T(8,128)(2,1)S(1)}, u32[]{:S(2)}, u32[]{:S(2)}) collective-permute-start(bf16[1088,128]{1,0:T(8,128)(2,1)} %get-tuple-element.102), channel_id=1, source_target_pairs={{0,2},{1,3},{2,0},{3,1},{4,6},{5,7},{6,4},{7,5},{8,10},{9,11},{10,... | collective-permute-start | bytes 835592 | tf_op jit(solution)/shard_map/ppermute | solution.py:18
  137.1 19.5 %collective-permute-start.41 = (bf16[2,4,128,128]{3,2,1,0:T(8,128)(2,1)}, bf16[2,4,128,128]{3,2,1,0:T(8,128)(2,1)}, u32[]{:S(2)}, u32[]{:S(2)}) collective-permute-start(bf16[2,4,128,128]{3,2,1,0:T(8,128)(2,1)} %get-tuple-element.105), channel_id=1, source_target_pairs={{0,4},{4,0},{8,12},{12,8},{16,20},{20,16},{24,28},{28,24},{1,5},{5... | collective-permute-start | bytes 786440 | tf_op jit(solution)/shard_map/ppermute | solution.py:18
  137.8 15.2 %collective-permute-start.32 = (bf16[128,512]{1,0:T(8,128)(2,1)}, bf16[128,512]{1,0:T(8,128)(2,1)}, u32[]{:S(2)}, u32[]{:S(2)}) collective-permute-start(bf16[128,512]{1,0:T(8,128)(2,1)} %get-tuple-element.90), channel_id=1, source_target_pairs={{0,16},{4,20},{8,24},{12,28},{16,0},{20,4},{24,8},{28,12},{1,17},{... | collective-permute-start | bytes 393224 | tf_op jit(solution)/shard_map/ppermute | solution.py:18
  140.7 19.7 %collective-permute-start.33 = (bf16[128,512]{1,0:T(8,128)(2,1)}, bf16[128,512]{1,0:T(8,128)(2,1)S(1)}, u32[]{:S(2)}, u32[]{:S(2)}) collective-permute-start(bf16[128,512]{1,0:T(8,128)(2,1)} %copy-done.19), channel_id=1, source_target_pairs={{0,20},{4,16},{8,28},{12,24},{16,4},{20,0},{24,12},{28,8},{1,21},{... | collective-permute-start | bytes 393224 | tf_op jit(solution)/shard_map/ppermute | solution.py:18
  143.0 19.1 %collective-permute-start.34 = (bf16[128,512]{1,0:T(8,128)(2,1)}, bf16[128,512]{1,0:T(8,128)(2,1)S(1)}, u32[]{:S(2)}, u32[]{:S(2)}) collective-permute-start(bf16[128,512]{1,0:T(8,128)(2,1)} %copy-done.18), channel_id=1, source_target_pairs={{0,24},{4,28},{8,16},{12,20},{16,8},{20,12},{24,0},{28,4},{1,25},{... | collective-permute-start | bytes 393224 | tf_op jit(solution)/shard_map/ppermute | solution.py:18
  153.0 9.2 %collective-permute-start.35 = (bf16[128,512]{1,0:T(8,128)(2,1)}, bf16[128,512]{1,0:T(8,128)(2,1)S(1)}, u32[]{:S(2)}, u32[]{:S(2)}) collective-permute-start(bf16[128,512]{1,0:T(8,128)(2,1)} %copy-done.17), channel_id=1, source_target_pairs={{0,28},{4,24},{8,20},{12,16},{16,12},{20,8},{24,4},{28,0},{1,29},{... | collective-permute-start | bytes 393224 | tf_op jit(solution)/shard_map/ppermute | solution.py:18
  162.2 7.9 %collective-permute-start.37 = (bf16[128,512]{1,0:T(8,128)(2,1)S(1)}, bf16[128,512]{1,0:T(8,128)(2,1)S(1)}, u32[]{:S(2)}, u32[]{:S(2)}) collective-permute-start(bf16[128,512]{1,0:T(8,128)(2,1)S(1)} %copy-done.14), channel_id=1, source_target_pairs={{0,8},{4,12},{8,0},{12,4},{16,24},{20,28},{24,16},{28,20},{1,9},{5... | collective-permute-start | bytes 393224 | tf_op jit(solution)/shard_map/ppermute | solution.py:18
  162.2 9.3 %collective-permute-start.38 = (bf16[128,512]{1,0:T(8,128)(2,1)S(1)}, bf16[128,512]{1,0:T(8,128)(2,1)S(1)}, u32[]{:S(2)}, u32[]{:S(2)}) collective-permute-start(bf16[128,512]{1,0:T(8,128)(2,1)S(1)} %copy-done.12), channel_id=1, source_target_pairs={{0,12},{4,8},{8,4},{12,0},{16,28},{20,24},{24,20},{28,16},{1,13},{... | collective-permute-start | bytes 393224 | tf_op jit(solution)/shard_map/ppermute | solution.py:18
  165.6 7.9 %collective-permute-start.44 = (bf16[128,256]{1,0:T(8,128)(2,1)S(1)}, bf16[128,256]{1,0:T(8,128)(2,1)S(1)}, u32[]{:S(2)}, u32[]{:S(2)}) collective-permute-start(bf16[128,256]{1,0:T(8,128)(2,1)S(1)} %get-tuple-element.112), channel_id=1, source_target_pairs={{0,8},{4,12},{8,0},{12,4},{16,24},{20,28},{24,16},{28,20},{1,9},{5... | collective-permute-start | bytes 196616 | tf_op jit(solution)/shard_map/ppermute | solution.py:18
  165.7 7.8 %collective-permute-start.45 = (bf16[128,256]{1,0:T(8,128)(2,1)S(1)}, bf16[128,256]{1,0:T(8,128)(2,1)S(1)}, u32[]{:S(2)}, u32[]{:S(2)}) collective-permute-start(bf16[128,256]{1,0:T(8,128)(2,1)S(1)} %get-tuple-element.113), channel_id=1, source_target_pairs={{0,16},{4,20},{8,24},{12,28},{16,0},{20,4},{24,8},{28,12},{1,17},{... | collective-permute-start | bytes 196616 | tf_op jit(solution)/shard_map/ppermute | solution.py:18
  (43 other events, 153.9 us)

commit v8 on v7

--- a/solution.py
+++ b/solution.py
@@ -177,7 +177,8 @@
     size = lax.axis_size("space")
     inner = [(i, i ^ 1) for i in range(size)]
     outer = [(i, ((i + 1) ^ 1) - 1) for i in range(1, size - 1)]
-    return lax.ppermute(near, "space", inner), lax.ppermute(far, "space", outer)
+    far = lax.ppermute(far, "space", outer)
+    return lax.ppermute(near, "space", inner), far
 
 
 def fill(pad_ref, plane, source):
@@ -219,7 +220,7 @@
             fill(pad_ref, p + 1, refs[which][at])
 
 
-def forward_planes(group, planes, sides, m, taps, vol, up, grad, out, pad):
+def forward_planes(group, planes, sides, m, taps, up, grad, silu, pad):
     wanted = {p + a for p in group for a in (-1, 0, 1)}
     where = {p: (0, p) for p in range(planes)}
     load_planes(pad, (m,), where, sides, wanted, planes)
@@ -232,24 +233,21 @@
             sig = 1.0 / (1.0 + jnp.exp(-spatial))
             cells = pl.ds(pl.multiple_of(f * lanes, lanes), lanes)
             source = pl.ds(pl.multiple_of(p * flat + f * lanes, lanes), lanes)
-            target = pl.ds(pl.multiple_of(k * flat + f * lanes, lanes), lanes)
-            cot = jnp.transpose(up[:, source].astype(F32))
             slope = sig * (1.0 + spatial * (1.0 - sig))
-            grad[k, cells, :] = (cot * slope).astype(BF)
-            silu = jnp.transpose(spatial * sig)
-            out[:, target] = (vol[:, source].astype(F32) + silu).astype(BF)
+            grad[k, cells, :] = (up[source, :].astype(F32) * slope).astype(BF)
+            silu[k, cells, :] = spatial * sig
             return carry
 
         lax.fori_loop(0, flat // lanes, strip, 0)
 
 
-def forward_middle(group, planes, m, taps, vol, up, grad, out, pad):
-    forward_planes(group, planes, (), m, taps, vol, up, grad, out, pad)
-
-
-def forward_edges(planes, odd, m, near, far, taps, vol, up, grad, out, to_near, to_far, pad):
+def forward_middle(group, planes, m, taps, up, grad, silu, pad):
+    forward_planes(group, planes, (), m, taps, up, grad, silu, pad)
+
+
+def forward_edges(planes, odd, m, near, far, taps, up, grad, silu, to_near, to_far, pad):
     sides = (odd, near, far)
-    forward_planes((0, planes - 1), planes, sides, m, taps, vol, up, grad, out, pad)
+    forward_planes((0, planes - 1), planes, sides, m, taps, up, grad, silu, pad)
     to_near[...] = jnp.where(odd[0] == 1, grad[0], grad[1])
     to_far[...] = jnp.where(odd[0] == 1, grad[1], grad[0])
 
@@ -299,15 +297,24 @@
     return call(kernel, shapes, [], me, whole, us=0.3, after=after)
 
 
-def taps_kernel(where_grad, planes, norm, steps, odd, m, near, far, g0, g1, o0, o1, *refs):
+def taps_kernel(where_grad, planes, norm, steps, odd, m, near, far, g0, g1, s0, s1, vol, *refs):
     parts, refs = refs[: len(steps)], refs[len(steps) :]
     out, output, pad, gpad = refs[0], refs[1], refs[-2], refs[-1]
     for r, part in zip(steps, parts):
         refs[2][:, r * part.shape[1] : (r + 1) * part.shape[1]] = part[...]
-    flat = m.shape[1]
-    output[:, :flat] = o0[:, :flat]
-    output[:, flat:-flat] = o1[...]
-    output[:, -flat:] = o0[:, flat:]
+    flat, lanes = m.shape[1], 2 * WW
+    for p in range(planes):
+        which, at = where_grad[p]
+        silu = (s0, s1)[which]
+
+        def strip(f, carry, p=p, at=at, silu=silu):
+            cells = pl.ds(pl.multiple_of(f * lanes, lanes), lanes)
+            lane = pl.ds(pl.multiple_of(p * flat + f * lanes, lanes), lanes)
+            turned = jnp.transpose(silu[at, cells, :])
+            output[:, lane] = (vol[:, lane].astype(F32) + turned).astype(BF)
+            return carry
+
+        lax.fori_loop(0, flat // lanes, strip, 0)
     where = {p: (0, p) for p in range(planes)}
     load_planes(pad, (m,), where, (odd, near, far), range(-1, planes + 1), planes)
     load_planes(gpad, (g0, g1), where_grad, (), range(planes), planes)
@@ -412,22 +419,32 @@
     return vol, call(mix_kernel, shapes, [], held, other, vol, us=2.6, after=after)
 
 
-def unmix(turn, base, pieces, steps, held, other, ch, after):
-    blk = pieces[0].shape[0]
+def turned(field):
+    def kernel(field, out):
+        step = 2 * WW
+
+        def strip(f, carry):
+            cells = pl.ds(pl.multiple_of(f * step, step), step)
+            out[cells, :] = jnp.transpose(field[:, cells])
+            return carry
+
+        lax.fori_loop(0, field.shape[1] // step, strip, 0)
+
+    return call(kernel, jax.ShapeDtypeStruct(field.shape[::-1], BF), [], field, us=1.2)
+
+
+def unmix(turn, mg, held, other, ch):
+    blk = mg.shape[0]
     pairs, rows, share = held.shape
     nf = rows // ch
     if ch % 128:
         weights = jnp.stack([held, other], axis=1).reshape(2 * pairs, rows, share)
-        mg = jnp.concatenate([part for _, part in sorted(list(base.items()) + list(zip(steps, pieces)))], axis=1)
         out = jnp.einsum("co,voi->vic", mg, weights, preferred_element_type=F32)
         out = out.astype(BF).reshape(nf, ch, blk)
-        return mg, [pick(out, turn[0] ^ s) for s in range(nf)]
-
-    def kernel(turn, base, held, other, *refs):
-        parts, mg, out, back = refs[: len(steps)], refs[len(steps)], refs[-nf - 1 : -1], refs[-1]
-        mg[...] = base[...]
-        for r, part in zip(steps, parts):
-            mg[:, r * ch : (r + 1) * ch] = part[...]
+        return [pick(out, turn[0] ^ s) for s in range(nf)]
+
+    def kernel(turn, mg, held, other, *refs):
+        out, back = refs[:-1], refs[-1]
         for v in range(2 * pairs):
             block = (other if v % 2 else held)[v // 2]
             total = lax.dot_general(
@@ -439,12 +456,10 @@
         for s in range(nf):
             out[s][...] = back[turn[0] ^ s]
 
-    shapes = [jax.ShapeDtypeStruct((blk, rows), BF)] + [jax.ShapeDtypeStruct((ch, blk), BF)] * nf
-    got = call(
-        kernel, shapes, [pltpu.VMEM((nf, ch, blk), BF)], turn, base, held, other, *pieces,
-        us=3.0, after=after,
-    )
-    return got[0], got[1:]
+    shapes = [jax.ShapeDtypeStruct((ch, blk), BF)] * nf
+    return call(
+        kernel, shapes, [pltpu.VMEM((nf, ch, blk), BF)], turn, mg, held, other, us=2.2
+    )
 
 
 def split(value):
@@ -456,13 +471,17 @@
     return high.astype(F32) + low.astype(F32)
 
 
-def weight_products(mg, vol_t, taps, ch, norm, ns):
-    rows, share, pairs = mg.shape[1], vol_t.shape[1] // ns, ns // 2
+def weight_products(base, pieces, steps, vol_t, taps, ch, norm, ns):
+    rows, pairs = vol_t.shape[1], ns // 2
+    share = rows // ns
     if halved(ch, share, ns):
         count = taps.shape[0]
 
-        def kernel(mg, vol, taps, *refs):
-            mine, theirs = refs[:pairs], refs[-1]
+        def kernel(base, vol, taps, *refs):
+            parts, mg, mine, theirs = refs[: len(steps)], refs[len(steps)], refs[-1 - pairs : -1], refs[-1]
+            mg[...] = base[...]
+            for r, part in zip(steps, parts):
+                mg[:, r * ch : (r + 1) * ch] = part[...]
             for r in range(rows // ch):
                 row = slice(r * ch, (r + 1) * ch)
                 turned = jnp.transpose(mg[:, row])
@@ -479,13 +498,22 @@
             theirs[0, rows:, :ch] = high
             theirs[1, rows:, :ch] = low
 
-        shapes = [jax.ShapeDtypeStruct((rows, share), F32)] * pairs
+        shapes = [jax.ShapeDtypeStruct(vol_t.shape, BF)]
+        shapes += [jax.ShapeDtypeStruct((rows, share), F32)] * pairs
         shapes.append(jax.ShapeDtypeStruct((pairs, rows + count, share), BF))
-        got = call(kernel, shapes, [], mg, vol_t, taps, us=2.5)
-        return got[:-1], got[-1]
+        got = call(kernel, shapes, [], base, vol_t, taps, *pieces, us=2.5)
+        return got[0], got[1:-1], got[-1]
+    if isinstance(base, dict):
+        parts = {**base, **dict(zip(steps, pieces))}
+        mg = jnp.concatenate([parts[r] for r in sorted(parts)], axis=1)
+    else:
+        mg = base
+        for r, part in zip(steps, pieces):
+            mg = lax.dynamic_update_slice_in_dim(mg, part, r * ch, axis=1)
     part = lax.dot_general(mg, vol_t, (((0,), (0,)), ((), ())), preferred_element_type=F32)
     part = (part * norm).reshape(rows, pairs, 2, share)
-    return [part[:, k, 0] for k in range(pairs)], part[:, :, 1].transpose(1, 0, 2).astype(BF)
+    theirs = part[:, :, 1].transpose(1, 0, 2).astype(BF)
+    return mg, [part[:, k, 0] for k in range(pairs)], theirs
 
 
 def assemble(me, base, pieces, steps):
@@ -563,7 +591,8 @@
     vol_3 = fold_volume(turn, vol_2, some(pieces, rest), rest)
     held, other = gather_weights(mixing, me_space, send, vol_1, vol_2)
     up = upstream.reshape(ch, total)
-    vol_t, prod = mix(vol_3, held, other, ch, (up,))
+    up_t = turned(up)
+    vol_t, prod = mix(vol_3, held, other, ch, (up_t,))
 
     got = exchange(prod, "filter")
     near_steps, cross = list(range(2, mid)), list(range(mid, nf))
@@ -578,17 +607,17 @@
     def grad_shapes(g):
         return (
             jax.ShapeDtypeStruct((len(g), flat, ch), BF),
-            jax.ShapeDtypeStruct((ch, len(g) * flat), BF),
+            jax.ShapeDtypeStruct((len(g), flat, ch), F32),
         )
 
     edge = jax.ShapeDtypeStruct((flat, ch), BF)
-    grad_middle, out_middle = call(
+    grad_middle, silu_middle = call(
         functools.partial(forward_middle, middle, planes), grad_shapes(middle), [pad],
-        mixed, taps, vol, up, us=4.0,
-    )
-    grad_edges, out_edges, to_near, to_far = call(
+        mixed, taps, up_t, us=3.2,
+    )
+    grad_edges, silu_edges, to_near, to_far = call(
         functools.partial(forward_edges, planes), grad_shapes(edges) + (edge, edge), [pad],
-        odd, mixed, near, far, taps, vol, up, us=4.0, after=(grad_middle,),
+        odd, mixed, near, far, taps, up_t, us=3.2, after=(grad_middle,),
     )
     grad_near, grad_far = halo(to_near, to_far)
     where = {p: (i, k) for i, g in enumerate(groups) for k, p in enumerate(g)}
@@ -612,7 +641,7 @@
     kernel = functools.partial(taps_kernel, where, planes, norm, [0, 1] if wide else [])
     taps_grad, output, *mg = call(
         kernel, shapes, [pad, pad],
-        odd, mixed, near, far, grad_edges, grad_middle, out_edges, out_middle,
+        odd, mixed, near, far, grad_edges, grad_middle, silu_edges, silu_middle, vol,
         *(side if wide else []), us=5.8,
     )
     output = output.reshape(ch, planes, flat)
@@ -620,17 +649,17 @@
     got.update((s, swap(block, "filter", s)) for s, block in zip(near_steps, send))
     base = mg[0] if wide else dict(zip([0, 1], side))
     rest = cross + near_steps
-    mg_all, back = unmix(
-        turn, base, some(got, rest), rest, held, other, ch, ()
-    )
+    mg_all, mine, theirs = weight_products(
+        base, some(got, rest), rest, vol_t, taps_grad, ch, norm, ns
+    )
+    back = unmix(turn, mg_all, held, other, ch)
     got = exchange(back, "filter")
-    mine, theirs = weight_products(mg_all, vol_t, taps_grad, ch, norm, ns)
-    volume_grad_1 = finish(own, up, None, some(got, early), early)
-    volume_grad_2 = finish(own, up, volume_grad_1, some(got, later), later)
+    volume_grad_1 = finish(own, up, None, some(got, [0, 1]), [0, 1])
+    volume_grad_2 = finish(own, up, volume_grad_1, some(got, cross), cross)
     mixing_grad, taps_grad = scatter_rest(
         mine, theirs, taps_grad, ch, volume_grad_1, volume_grad_2
     )
-    volume_grad = finish(own, up, volume_grad_2, some(got, last), last)
+    volume_grad = finish(own, up, volume_grad_2, some(got, near_steps), near_steps)
     volume_grad = volume_grad.reshape(ch, planes, flat)
     return (output, volume_grad, mixing_grad, taps_grad[:27].T)
 

time: 175 us -> 174 us (level)
  waiting for transfers between devices: 57.6 us -> 49.1 us
  Pallas kernels: 30 us -> 33.5 us
  starting transfers between devices: 71.3 us -> 73.9 us
    ppermute x43, waiting for transfers between devices: 57.6 us -> 49.1 us  [swap(): return lax.ppermute(block, axis, [(i, i ^ step) for i in range(size)])]
    pallas_call x24 -> x25, Pallas kernels: 30 us -> 33.5 us  [call(): pl.pallas_call(wrapped, out_shape=out_shape, in_specs=specs + [pl.BlockSp...]
    unnamed x58 -> x50, local copies, waits for them, and re-layouts: 9.77 us -> 10.8 us
  transfers between devices with their start and end apart: 47 -> 47, of which waited for: 19 -> 18; matrix products, arithmetic and copies ran while one was open for 4% -> 4% of each run, Pallas kernels for 9% -> 13%
where the time goes in v8:
time: 174 us
  starting transfers between devices  73.9 us (42%)
  waiting for transfers between devices  49.1 us (28%)
  Pallas kernels  33.5 us (19%)
  local copies, waits for them, and re-layouts  15.4 us (9%)
    ppermute x43, starting transfers between devices, swap(): return lax.ppermute(block, axis, [(i, i ^ step) for i in range(size)])  67.6 us
    ppermute x43, waiting for transfers between devices, swap(): return lax.ppermute(block, axis, [(i, i ^ step) for i in range(size)])  49.1 us
    pallas_call x25, Pallas kernels, call(): pl.pallas_call(wrapped, out_shape=out_shape, in_specs=specs + [pl.BlockSp...  33.5 us
    unnamed x50, local copies, waits for them, and re-layouts  10.8 us
    ppermute x2, starting transfers between devices, halo(): return (lax.ppermute(near, 'space', inner), far)  4.72 us
  transfers between devices with their start and end apart: 47, of which 18 were waited for; matrix products, arithmetic and copies ran while one was open for 4% of the time, Pallas kernels for 13%

profile of v8, /device:TPU:0, one launch (start us, length us, event | category | flops | bytes accessed | tf_op | source)
XLA Modules:
  0.0 173.7 jit_solution(14909791105002675846)
XLA Ops:
  1.6 5.1 %collective-permute-start.2 = (bf16[128,256]{1,0:T(8,128)(2,1)S(1)}, bf16[128,256]{1,0:T(8,128)(2,1)S(1)}, u32[]{:S(2)}, u32[]{:S(2)}) collective-permute-start(bf16[128,256]{1,0:T(8,128)(2,1)S(1)} %constant_dynamic-slice_fusion.8.refs_0_), channel_id=1, source_target_pairs={{0,24},{4,28},{8,16},{12,20},{16,8},{20,12},{24,0},{28,4},{1,25},{... | collective-permute-start | bytes 196616 | tf_op jit(solution)/shard_map/ppermute | solution.py:18
  9.8 2.5 %collective-permute-done.1.refs_2_ = bf16[128,256]{1,0:T(8,128)(2,1)S(1)} collective-permute-done((bf16[128,256]{1,0:T(8,128)(2,1)S(1)}, bf16[128,256]{1,0:T(8,128)(2,1)S(1)}, u32[]{:S(2)}, u32[]{:S(2)}) %collective-permute-start.1) | collective-permute-done | bytes 65568 | tf_op jit(solution)/shard_map/ppermute | solution.py:18
  18.3 7.8 %collective-permute-done.6.refs_3_ = bf16[128,512]{1,0:T(8,128)(2,1)S(1)} collective-permute-done((bf16[128,512]{1,0:T(8,128)(2,1)S(1)}, bf16[128,512]{1,0:T(8,128)(2,1)S(1)}, u32[]{:S(2)}, u32[]{:S(2)}) %collective-permute-start.6) | collective-permute-done | bytes 131104 | tf_op jit(solution)/shard_map/ppermute | solution.py:18
  34.3 3.3 %collective-permute-done.8.refs_2_ = bf16[128,512]{1,0:T(8,128)(2,1)S(1)} collective-permute-done((bf16[128,512]{1,0:T(8,128)(2,1)S(1)}, bf16[128,512]{1,0:T(8,128)(2,1)S(1)}, u32[]{:S(2)}, u32[]{:S(2)}) %collective-permute-start.8) | collective-permute-done | bytes 131104 | tf_op jit(solution)/shard_map/ppermute | solution.py:18
  38.7 1.9 %collective-permute-start.12 = (bf16[128,512]{1,0:T(8,128)(2,1)S(1)}, bf16[128,512]{1,0:T(8,128)(2,1)S(1)}, u32[]{:S(2)}, u32[]{:S(2)}) collective-permute-start(bf16[128,512]{1,0:T(8,128)(2,1)S(1)} %copy-done.22), channel_id=1, source_target_pairs={{0,8},{4,12},{8,0},{12,4},{16,24},{20,28},{24,16},{28,20},{1,9},{5... | collective-permute-start | bytes 393224 | tf_op jit(solution)/shard_map/ppermute | solution.py:18
  40.6 2.6 %collective-permute-start.11 = (bf16[128,512]{1,0:T(8,128)(2,1)S(1)}, bf16[128,512]{1,0:T(8,128)(2,1)S(1)}, u32[]{:S(2)}, u32[]{:S(2)}) collective-permute-start(bf16[128,512]{1,0:T(8,128)(2,1)S(1)} %get-tuple-element.120.refs_7_), channel_id=1, source_target_pairs={{0,28},{4,24},{8,20},{12,16},{16,12},{20,8},{24,4},{28,0},{1,29},{... | collective-permute-start | bytes 393224 | tf_op jit(solution)/shard_map/ppermute | solution.py:18
  43.6 2.3 %shard_map.81.refs_3_.refs_2_.refs_5_ = bf16[4096,128]{1,0:T(8,128)(2,1)S(1)} custom-call(bf16[128,4096]{1,0:T(8,128)(2,1)S(1)} %bitcast.12), custom_call_target="tpu_custom_call" | custom-call | flops 1380000000 | bytes 1048576 | tf_op jit(solution)/shard_map/pallas_call | solution.py:352
  47.5 2.1 %collective-permute-done.11.refs_2_ = bf16[128,512]{1,0:T(8,128)(2,1)S(1)} collective-permute-done((bf16[128,512]{1,0:T(8,128)(2,1)S(1)}, bf16[128,512]{1,0:T(8,128)(2,1)S(1)}, u32[]{:S(2)}, u32[]{:S(2)}) %collective-permute-start.11) | collective-permute-done | bytes 131104 | tf_op jit(solution)/shard_map/ppermute | solution.py:18
  49.8 2.1 %shard_map.82 = (bf16[512,128]{1,0:T(8,128)(2,1)S(1)}, bf16[512,128]{1,0:T(8,128)(2,1)S(1)}, bf16[512,128]{1,0:T(8,128)(2,1)S(1)}, bf16[512,128]{1,0:T(8,128)(2,...) custom-call(bf16[2,1024,256]{2,1,0:T(8,128)(2,1)S(1)} %shard_map.79., ...), custom_call_target="tpu_custom_call" | custom-call | flops 2990000128 | bytes 1048576 | tf_op jit(solution)/shard_map/pallas_call | solution.py:352
  53.9 2.2 %collective-permute-start.16 = (bf16[512,128]{1,0:T(8,128)(2,1)}, bf16[512,128]{1,0:T(8,128)(2,1)}, u32[]{:S(2)}, u32[]{:S(2)}) collective-permute-start(bf16[512,128]{1,0:T(8,128)(2,1)} %get-tuple-element.63), channel_id=1, source_target_pairs={{0,12},{4,8},{8,4},{12,0},{16,28},{20,24},{24,20},{28,16},{1,13},{... | collective-permute-start | bytes 393224 | tf_op jit(solution)/shard_map/ppermute | solution.py:18
  56.5 3.2 %collective-permute-start.18 = (bf16[512,128]{1,0:T(8,128)(2,1)}, bf16[512,128]{1,0:T(8,128)(2,1)}, u32[]{:S(2)}, u32[]{:S(2)}) collective-permute-start(bf16[512,128]{1,0:T(8,128)(2,1)} %get-tuple-element.65), channel_id=1, source_target_pairs={{0,20},{4,16},{8,28},{12,24},{16,4},{20,0},{24,12},{28,8},{1,21},{... | collective-permute-start | bytes 393224 | tf_op jit(solution)/shard_map/ppermute | solution.py:18
  60.4 2.1 %collective-permute-start.19 = (bf16[512,128]{1,0:T(8,128)(2,1)}, bf16[512,128]{1,0:T(8,128)(2,1)}, u32[]{:S(2)}, u32[]{:S(2)}) collective-permute-start(bf16[512,128]{1,0:T(8,128)(2,1)} %get-tuple-element.66), channel_id=1, source_target_pairs={{0,24},{4,28},{8,16},{12,20},{16,8},{20,12},{24,0},{28,4},{1,25},{... | collective-permute-start | bytes 393224 | tf_op jit(solution)/shard_map/ppermute | solution.py:18
  67.1 7.2 %collective-permute-done.17.refs_3_ = bf16[512,128]{1,0:T(8,128)(2,1)} collective-permute-done((bf16[512,128]{1,0:T(8,128)(2,1)}, bf16[512,128]{1,0:T(8,128)(2,1)}, u32[]{:S(2)}, u32[]{:S(2)}) %collective-permute-start.17) | collective-permute-done | bytes 131104 | tf_op jit(solution)/shard_map/ppermute | solution.py:18
  74.4 3.3 %collective-permute-done.18.refs_4_ = bf16[512,128]{1,0:T(8,128)(2,1)} collective-permute-done((bf16[512,128]{1,0:T(8,128)(2,1)}, bf16[512,128]{1,0:T(8,128)(2,1)}, u32[]{:S(2)}, u32[]{:S(2)}) %collective-permute-start.18) | collective-permute-done | bytes 131104 | tf_op jit(solution)/shard_map/ppermute | solution.py:18
  79.9 2.9 %shard_map.86 = (bf16[2,1024,128]{2,1,0:T(8,128)(2,1)S(1)}, f32[2,1024,128]{2,1,0:T(8,128)S(1)}) custom-call(bf16[4,1024,128]{2,1,0:T(8,128)(2,1)S(1)} %bitcast.18, f32[27,128]{1,0:T(8,128)S(1)} %bitcast.23, bf16[4096,128]{1,0:T(8,128)(2,1)S(1)} %copy-done.20), custom_call_target="tpu_custom_call" | custom-call | flops 3680000000 | bytes 1048576 | tf_op jit(solution)/shard_map/pallas_call | solution.py:352
  82.8 3.1 %shard_map.87 = (bf16[2,1024,128]{2,1,0:T(8,128)(2,1)S(1)}, f32[2,1024,128]{2,1,0:T(8,128)S(1)}, bf16[1024,128]{1,0:T(8,128)(2,1)S(1)}, bf16[1024,128]{1,0:T(8,128)(2,1)S(1)}) custom-call(s32[1]{0:T(128)} %bitcast.refs_1_.refs_0_, bf16[4,1024,128]{2,1,0:T(8,128)(2,1)S(1)} %bitcast.19, bf16[1024,128]{1,0:T(8,128)(2,1)S(1)} %collective-permute-done.21.refs_2_, ...), custom_call_target="tpu_custom_call" | custom-call | flops 3680000000 | bytes 1048576 | tf_op jit(solution)/shard_map/pallas_call | solution.py:352
  85.9 4.6 %collective-permute-start.23 = (bf16[1024,128]{1,0:T(8,128)(2,1)S(1)}, bf16[1024,128]{1,0:T(8,128)(2,1)S(1)}, u32[]{:S(2)}, u32[]{:S(2)}) collective-permute-start(bf16[1024,128]{1,0:T(8,128)(2,1)S(1)} %get-tuple-element.75), channel_id=1, source_target_pairs={{0,1},{1,0},{2,3},{3,2},{4,5},{5,4},{6,7},{7,6},{8,9},{9,8},{10,11... | collective-permute-start | bytes 786440 | tf_op jit(solution)/shard_map/ppermute | solution.py:181
  91.4 2.3 %shard_map.88.refs_7_ = bf16[2,1024,128]{2,1,0:T(8,128)(2,1)S(1)} custom-call(bf16[2,1024,128]{2,1,0:T(8,128)(2,1)S(1)} %get-tuple-element.72.refs_0_.refs_2_.refs_4_, bf16[2,1024,128]{2,1,0:T(8,128)(2,1)S(1)} %get-tuple-element.71.refs_6_.refs_1_.refs_3_.refs_5_, f32[27,128]{1,0:T(8,128)S(1)} %bitcast.25), custom_call_target="tpu_custom_call" | custom-call | flops 2644999936 | bytes 1048576 | tf_op jit(solution)/shard_map/pallas_call | solution.py:352
  93.6 2.4 %shard_map.89 = (bf16[4096,128]{1,0:T(8,128)(2,1)S(1)}, bf16[512,128]{1,0:T(8,128)(2,1)S(1)}, bf16[512,128]{1,0:T(8,128)(2,1)S(1)}, bf16[512,128]{1,0:T(8,128)(2...) custom-call(s32[1]{0:T(128)} %bitcast.1.refs_0_, ...), custom_call_target="tpu_custom_call" | custom-call | flops 3220000000 | bytes 1048576 | tf_op jit(solution)/shard_map/pallas_call | solution.py:352
  97.1 4.3 %collective-permute-start.26 = (bf16[512,128]{1,0:T(8,128)(2,1)S(1)}, bf16[512,128]{1,0:T(8,128)(2,1)S(1)}, u32[]{:S(2)}, u32[]{:S(2)}) collective-permute-start(bf16[512,128]{1,0:T(8,128)(2,1)S(1)} %get-tuple-element.82), channel_id=1, source_target_pairs={{0,16},{4,20},{8,24},{12,28},{16,0},{20,4},{24,8},{28,12},{1,17},{... | collective-permute-start | bytes 393224 | tf_op jit(solution)/shard_map/ppermute | solution.py:18
  104.3 2.1 %collective-permute-start.29 = (bf16[512,128]{1,0:T(8,128)(2,1)S(1)}, bf16[512,128]{1,0:T(8,128)(2,1)S(1)}, u32[]{:S(2)}, u32[]{:S(2)}) collective-permute-start(bf16[512,128]{1,0:T(8,128)(2,1)S(1)} %get-tuple-element.85), channel_id=1, source_target_pairs={{0,28},{4,24},{8,20},{12,16},{16,12},{20,8},{24,4},{28,0},{1,29},{... | collective-permute-start | bytes 393224 | tf_op jit(solution)/shard_map/ppermute | solution.py:18
  106.4 8.7 %shard_map.90 = (f32[32,128]{1,0:T(8,128)S(1)}, bf16[128,4096]{1,0:T(8,128)(2,1)S(1)}, bf16[512,1024]{1,0:T(8,128)(2,1)S(1)}) custom-call(s32[1]{0:T(128)} %bitcast.refs_1_.refs_0_, bf16[4,1024,128]{2,1,0:T(8,128)(2,1)S(1)} %bitcast.20, bf16[1024,128]{1,0:T(8,128)(2,1)S(1)} %collective-permute-done.21.refs_2_, ...), custom_call_target="tpu_custom_call" | custom-call | flops 6670000128 | bytes 1048576 | tf_op jit(solution)/shard_map/pallas_call | solution.py:352
  116.8 2.3 %collective-permute-start.31 = (bf16[512,128]{1,0:T(8,128)(2,1)S(1)}, bf16[512,128]{1,0:T(8,128)(2,1)S(1)}, u32[]{:S(2)}, u32[]{:S(2)}) collective-permute-start(bf16[512,128]{1,0:T(8,128)(2,1)S(1)} %get-tuple-element.88), channel_id=1, source_target_pairs={{0,12},{4,8},{8,4},{12,0},{16,28},{20,24},{24,20},{28,16},{1,13},{... | collective-permute-start | bytes 393224 | tf_op jit(solution)/shard_map/ppermute | solution.py:18
  119.8 2.4 %collective-permute-done.30.refs_7_ = bf16[512,128]{1,0:T(8,128)(2,1)S(1)} collective-permute-done((bf16[512,128]{1,0:T(8,128)(2,1)S(1)}, bf16[512,128]{1,0:T(8,128)(2,1)S(1)}, u32[]{:S(2)}, u32[]{:S(2)}) %collective-permute-start.30) | collective-permute-done | bytes 131104 | tf_op jit(solution)/shard_map/ppermute | solution.py:18
  122.2 3.6 %collective-permute-done.31.refs_8_ = bf16[512,128]{1,0:T(8,128)(2,1)S(1)} collective-permute-done((bf16[512,128]{1,0:T(8,128)(2,1)S(1)}, bf16[512,128]{1,0:T(8,128)(2,1)S(1)}, u32[]{:S(2)}, u32[]{:S(2)}) %collective-permute-start.31) | collective-permute-done | bytes 131104 | tf_op jit(solution)/shard_map/ppermute | solution.py:18
  128.7 2.3 %collective-permute-done.39.refs_2_ = bf16[2,1056,256]{2,1,0:T(8,128)(2,1)S(1)} collective-permute-done((bf16[2,1056,256]{2,1,0:T(8,128)(2,1)S(1)}, bf16[2,1056,256]{2,1,0:T(8,128)(2,1)S(1)}, u32[]{:S(2)}, u32[]{:S(2)}) %collective-permute-start.39) | collective-permute-done | bytes 1081376 | tf_op jit(solution)/shard_map/ppermute | solution.py:18
  133.1 2.1 %shard_map.93 = (bf16[128,512]{1,0:T(8,128)(2,1)S(1)}, bf16[128,512]{1,0:T(8,128)(2,1)S(1)}, bf16[128,512]{1,0:T(8,128)(2,1)S(1)}, bf16[128,512]{1,0:T(8,128)(2,...) custom-call(s32[1]{0:T(128)} %bitcast.2.refs_0_, ...), custom_call_target="tpu_custom_call" | custom-call | flops 2529999872 | bytes 1048576 | tf_op jit(solution)/shard_map/pallas_call | solution.py:352
  139.6 3.0 %collective-permute-done.32.refs_3_ = bf16[128,512]{1,0:T(8,128)(2,1)S(1)} collective-permute-done((bf16[128,512]{1,0:T(8,128)(2,1)S(1)}, bf16[128,512]{1,0:T(8,128)(2,1)S(1)}, u32[]{:S(2)}, u32[]{:S(2)}) %collective-permute-start.32) | collective-permute-done | bytes 131104 | tf_op jit(solution)/shard_map/ppermute | solution.py:18
  150.3 3.7 %collective-permute-done.33.refs_3_ = bf16[128,512]{1,0:T(8,128)(2,1)S(1)} collective-permute-done((bf16[128,512]{1,0:T(8,128)(2,1)S(1)}, bf16[128,512]{1,0:T(8,128)(2,1)S(1)}, u32[]{:S(2)}, u32[]{:S(2)}) %collective-permute-start.33) | collective-permute-done | bytes 131104 | tf_op jit(solution)/shard_map/ppermute | solution.py:18
  157.6 3.3 %collective-permute-start.38 = (bf16[128,512]{1,0:T(8,128)(2,1)S(1)}, bf16[128,512]{1,0:T(8,128)(2,1)S(1)}, u32[]{:S(2)}, u32[]{:S(2)}) collective-permute-start(bf16[128,512]{1,0:T(8,128)(2,1)S(1)} %get-tuple-element.97), channel_id=1, source_target_pairs={{0,12},{4,8},{8,4},{12,0},{16,28},{20,24},{24,20},{28,16},{1,13},{... | collective-permute-start | bytes 393224 | tf_op jit(solution)/shard_map/ppermute | solution.py:18
  166.6 2.0 %collective-permute-start.46 = (bf16[128,256]{1,0:T(8,128)(2,1)S(1)}, bf16[128,256]{1,0:T(8,128)(2,1)S(1)}, u32[]{:S(2)}, u32[]{:S(2)}) collective-permute-start(bf16[128,256]{1,0:T(8,128)(2,1)S(1)} %get-tuple-element.114), channel_id=1, source_target_pairs={{0,24},{4,28},{8,16},{12,20},{16,8},{20,12},{24,0},{28,4},{1,25},{... | collective-permute-start | bytes 196616 | tf_op jit(solution)/shard_map/ppermute | solution.py:18
  170.8 2.1 %collective-permute-done.45 = bf16[128,256]{1,0:T(8,128)(2,1)S(1)} collective-permute-done((bf16[128,256]{1,0:T(8,128)(2,1)S(1)}, bf16[128,256]{1,0:T(8,128)(2,1)S(1)}, u32[]{:S(2)}, u32[]{:S(2)}) %collective-permute-start.45) | collective-permute-done | bytes 65568 | tf_op jit(solution)/shard_map/ppermute | solution.py:18
  (143 shorter events, 67.3 us)
Async XLA Ops:
  1.6 8.2 %collective-permute-start.2 = (bf16[128,256]{1,0:T(8,128)(2,1)S(1)}, bf16[128,256]{1,0:T(8,128)(2,1)S(1)}, u32[]{:S(2)}, u32[]{:S(2)}) collective-permute-start(bf16[128,256]{1,0:T(8,128)(2,1)S(1)} %constant_dynamic-slice_fusion.8.refs_0_), channel_id=1, source_target_pairs={{0,24},{4,28},{8,16},{12,20},{16,8},{20,12},{24,0},{28,4},{1,25},{... | collective-permute-start | bytes 196616 | tf_op jit(solution)/shard_map/ppermute | solution.py:18
  12.3 15.4 %collective-permute-start.4 = (bf16[4,128,256]{2,1,0:T(8,128)(2,1)S(1)}, bf16[4,128,256]{2,1,0:T(8,128)(2,1)S(1)}, u32[]{:S(2)}, u32[]{:S(2)}) collective-permute-start(bf16[4,128,256]{2,1,0:T(8,128)(2,1)S(1)} %shard_map.75.refs_0_), channel_id=1, source_target_pairs={{0,4},{4,0},{8,12},{12,8},{16,20},{20,16},{24,28},{28,24},{1,5},{5... | collective-permute-start | bytes 786440 | tf_op jit(solution)/shard_map/ppermute | solution.py:18
  13.9 12.2 %collective-permute-start.6 = (bf16[128,512]{1,0:T(8,128)(2,1)S(1)}, bf16[128,512]{1,0:T(8,128)(2,1)S(1)}, u32[]{:S(2)}, u32[]{:S(2)}) collective-permute-start(bf16[128,512]{1,0:T(8,128)(2,1)S(1)} %get-tuple-element.122.refs_5_), channel_id=1, source_target_pairs={{0,20},{4,16},{8,28},{12,24},{16,4},{20,0},{24,12},{28,8},{1,21},{... | collective-permute-start | bytes 393224 | tf_op jit(solution)/shard_map/ppermute | solution.py:18
  15.5 12.1 %collective-permute-start.5 = (bf16[128,512]{1,0:T(8,128)(2,1)S(1)}, bf16[128,512]{1,0:T(8,128)(2,1)S(1)}, u32[]{:S(2)}, u32[]{:S(2)}) collective-permute-start(bf16[128,512]{1,0:T(8,128)(2,1)S(1)} %get-tuple-element.123.refs_4_), channel_id=1, source_target_pairs={{0,16},{4,20},{8,24},{12,28},{16,0},{20,4},{24,8},{28,12},{1,17},{... | collective-permute-start | bytes 393224 | tf_op jit(solution)/shard_map/ppermute | solution.py:18
  16.8 21.0 %collective-permute-start.3 = (bf16[4,128,256]{2,1,0:T(8,128)(2,1)S(1)}, bf16[4,128,256]{2,1,0:T(8,128)(2,1)S(1)}, u32[]{:S(2)}, u32[]{:S(2)}) collective-permute-start(bf16[4,128,256]{2,1,0:T(8,128)(2,1)S(1)} %shard_map.75.refs_0_), channel_id=1, source_target_pairs={{0,2},{1,3},{2,0},{3,1},{4,6},{5,7},{6,4},{7,5},{8,10},{9,11},{10,... | collective-permute-start | bytes 786440 | tf_op jit(solution)/shard_map/ppermute | solution.py:18
  27.8 10.0 %collective-permute-start.7 = (bf16[4,128,256]{2,1,0:T(8,128)(2,1)S(1)}, bf16[4,128,256]{2,1,0:T(8,128)(2,1)S(1)}, u32[]{:S(2)}, u32[]{:S(2)}) collective-permute-start(bf16[4,128,256]{2,1,0:T(8,128)(2,1)S(1)} %bitcast.21), channel_id=1, source_target_pairs={{0,2},{1,3},{2,0},{3,1},{4,6},{5,7},{6,4},{7,5},{8,10},{9,11},{10,... | collective-permute-start | bytes 786440 | tf_op jit(solution)/shard_map/ppermute | solution.py:18
  37.9 11.9 %collective-permute-start.10 = (bf16[2,1024,256]{2,1,0:T(8,128)(2,1)S(1)}, bf16[2,1024,256]{2,1,0:T(8,128)(2,1)S(1)}, u32[]{:S(2)}, u32[]{:S(2)}) collective-permute-start(bf16[2,1024,256]{2,1,0:T(8,128)(2,1)S(1)} %shard_map.79.refs_0_.refs_2_), channel_id=1, source_target_pairs={{0,1},{1,0},{2,3},{3,2},{4,5},{5,4},{6,7},{7,6},{8,9},{9,8},{10,11... | collective-permute-start | bytes 3145736 | tf_op jit(solution)/shard_map/ppermute | solution.py:18
  38.7 8.8 %collective-permute-start.12 = (bf16[128,512]{1,0:T(8,128)(2,1)S(1)}, bf16[128,512]{1,0:T(8,128)(2,1)S(1)}, u32[]{:S(2)}, u32[]{:S(2)}) collective-permute-start(bf16[128,512]{1,0:T(8,128)(2,1)S(1)} %copy-done.22), channel_id=1, source_target_pairs={{0,8},{4,12},{8,0},{12,4},{16,24},{20,28},{24,16},{28,20},{1,9},{5... | collective-permute-start | bytes 393224 | tf_op jit(solution)/shard_map/ppermute | solution.py:18
  40.6 9.0 %collective-permute-start.11 = (bf16[128,512]{1,0:T(8,128)(2,1)S(1)}, bf16[128,512]{1,0:T(8,128)(2,1)S(1)}, u32[]{:S(2)}, u32[]{:S(2)}) collective-permute-start(bf16[128,512]{1,0:T(8,128)(2,1)S(1)} %get-tuple-element.120.refs_7_), channel_id=1, source_target_pairs={{0,28},{4,24},{8,20},{12,16},{16,12},{20,8},{24,4},{28,0},{1,29},{... | collective-permute-start | bytes 393224 | tf_op jit(solution)/shard_map/ppermute | solution.py:18
  53.9 8.7 %collective-permute-start.15 = (bf16[512,128]{1,0:T(8,128)(2,1)S(1)}, bf16[512,128]{1,0:T(8,128)(2,1)S(1)}, u32[]{:S(2)}, u32[]{:S(2)}) collective-permute-start(bf16[512,128]{1,0:T(8,128)(2,1)S(1)} %get-tuple-element.62), channel_id=1, source_target_pairs={{0,8},{4,12},{8,0},{12,4},{16,24},{20,28},{24,16},{28,20},{1,9},{5... | collective-permute-start | bytes 393224 | tf_op jit(solution)/shard_map/ppermute | solution.py:18
  53.9 12.3 %collective-permute-start.16 = (bf16[512,128]{1,0:T(8,128)(2,1)}, bf16[512,128]{1,0:T(8,128)(2,1)}, u32[]{:S(2)}, u32[]{:S(2)}) collective-permute-start(bf16[512,128]{1,0:T(8,128)(2,1)} %get-tuple-element.63), channel_id=1, source_target_pairs={{0,12},{4,8},{8,4},{12,0},{16,28},{20,24},{24,20},{28,16},{1,13},{... | collective-permute-start | bytes 393224 | tf_op jit(solution)/shard_map/ppermute | solution.py:18
  56.1 18.3 %collective-permute-start.17 = (bf16[512,128]{1,0:T(8,128)(2,1)}, bf16[512,128]{1,0:T(8,128)(2,1)}, u32[]{:S(2)}, u32[]{:S(2)}) collective-permute-start(bf16[512,128]{1,0:T(8,128)(2,1)} %get-tuple-element.64), channel_id=1, source_target_pairs={{0,16},{4,20},{8,24},{12,28},{16,0},{20,4},{24,8},{28,12},{1,17},{... | collective-permute-start | bytes 393224 | tf_op jit(solution)/shard_map/ppermute | solution.py:18
  56.5 21.2 %collective-permute-start.18 = (bf16[512,128]{1,0:T(8,128)(2,1)}, bf16[512,128]{1,0:T(8,128)(2,1)}, u32[]{:S(2)}, u32[]{:S(2)}) collective-permute-start(bf16[512,128]{1,0:T(8,128)(2,1)} %get-tuple-element.65), channel_id=1, source_target_pairs={{0,20},{4,16},{8,28},{12,24},{16,4},{20,0},{24,12},{28,8},{1,21},{... | collective-permute-start | bytes 393224 | tf_op jit(solution)/shard_map/ppermute | solution.py:18
  60.4 17.3 %collective-permute-start.19 = (bf16[512,128]{1,0:T(8,128)(2,1)}, bf16[512,128]{1,0:T(8,128)(2,1)}, u32[]{:S(2)}, u32[]{:S(2)}) collective-permute-start(bf16[512,128]{1,0:T(8,128)(2,1)} %get-tuple-element.66), channel_id=1, source_target_pairs={{0,24},{4,28},{8,16},{12,20},{16,8},{20,12},{24,0},{28,4},{1,25},{... | collective-permute-start | bytes 393224 | tf_op jit(solution)/shard_map/ppermute | solution.py:18
  62.6 15.1 %collective-permute-start.20 = (bf16[512,128]{1,0:T(8,128)(2,1)}, bf16[512,128]{1,0:T(8,128)(2,1)}, u32[]{:S(2)}, u32[]{:S(2)}) collective-permute-start(bf16[512,128]{1,0:T(8,128)(2,1)} %get-tuple-element.67), channel_id=1, source_target_pairs={{0,28},{4,24},{8,20},{12,16},{16,12},{20,8},{24,4},{28,0},{1,29},{... | collective-permute-start | bytes 393224 | tf_op jit(solution)/shard_map/ppermute | solution.py:18
  85.9 7.8 %collective-permute-start.23 = (bf16[1024,128]{1,0:T(8,128)(2,1)S(1)}, bf16[1024,128]{1,0:T(8,128)(2,1)S(1)}, u32[]{:S(2)}, u32[]{:S(2)}) collective-permute-start(bf16[1024,128]{1,0:T(8,128)(2,1)S(1)} %get-tuple-element.75), channel_id=1, source_target_pairs={{0,1},{1,0},{2,3},{3,2},{4,5},{5,4},{6,7},{7,6},{8,9},{9,8},{10,11... | collective-permute-start | bytes 786440 | tf_op jit(solution)/shard_map/ppermute | solution.py:181
  96.1 10.3 %collective-permute-start.25 = (bf16[512,128]{1,0:T(8,128)(2,1)S(1)}, bf16[512,128]{1,0:T(8,128)(2,1)S(1)}, u32[]{:S(2)}, u32[]{:S(2)}) collective-permute-start(bf16[512,128]{1,0:T(8,128)(2,1)S(1)} %get-tuple-element.78), channel_id=1, source_target_pairs={{0,4},{4,0},{8,12},{12,8},{16,20},{20,16},{24,28},{28,24},{1,5},{5... | collective-permute-start | bytes 393224 | tf_op jit(solution)/shard_map/ppermute | solution.py:18
  97.1 19.7 %collective-permute-start.26 = (bf16[512,128]{1,0:T(8,128)(2,1)S(1)}, bf16[512,128]{1,0:T(8,128)(2,1)S(1)}, u32[]{:S(2)}, u32[]{:S(2)}) collective-permute-start(bf16[512,128]{1,0:T(8,128)(2,1)S(1)} %get-tuple-element.82), channel_id=1, source_target_pairs={{0,16},{4,20},{8,24},{12,28},{16,0},{20,4},{24,8},{28,12},{1,17},{... | collective-permute-start | bytes 393224 | tf_op jit(solution)/shard_map/ppermute | solution.py:18
  101.4 18.3 %collective-permute-start.27 = (bf16[512,128]{1,0:T(8,128)(2,1)S(1)}, bf16[512,128]{1,0:T(8,128)(2,1)S(1)}, u32[]{:S(2)}, u32[]{:S(2)}) collective-permute-start(bf16[512,128]{1,0:T(8,128)(2,1)S(1)} %get-tuple-element.83), channel_id=1, source_target_pairs={{0,20},{4,16},{8,28},{12,24},{16,4},{20,0},{24,12},{28,8},{1,21},{... | collective-permute-start | bytes 393224 | tf_op jit(solution)/shard_map/ppermute | solution.py:18
  102.6 17.2 %collective-permute-start.28 = (bf16[512,128]{1,0:T(8,128)(2,1)S(1)}, bf16[512,128]{1,0:T(8,128)(2,1)S(1)}, u32[]{:S(2)}, u32[]{:S(2)}) collective-permute-start(bf16[512,128]{1,0:T(8,128)(2,1)S(1)} %get-tuple-element.84), channel_id=1, source_target_pairs={{0,24},{4,28},{8,16},{12,20},{16,8},{20,12},{24,0},{28,4},{1,25},{... | collective-permute-start | bytes 393224 | tf_op jit(solution)/shard_map/ppermute | solution.py:18
  104.3 15.5 %collective-permute-start.29 = (bf16[512,128]{1,0:T(8,128)(2,1)S(1)}, bf16[512,128]{1,0:T(8,128)(2,1)S(1)}, u32[]{:S(2)}, u32[]{:S(2)}) collective-permute-start(bf16[512,128]{1,0:T(8,128)(2,1)S(1)} %get-tuple-element.85), channel_id=1, source_target_pairs={{0,28},{4,24},{8,20},{12,16},{16,12},{20,8},{24,4},{28,0},{1,29},{... | collective-permute-start | bytes 393224 | tf_op jit(solution)/shard_map/ppermute | solution.py:18
  116.8 9.0 %collective-permute-start.31 = (bf16[512,128]{1,0:T(8,128)(2,1)S(1)}, bf16[512,128]{1,0:T(8,128)(2,1)S(1)}, u32[]{:S(2)}, u32[]{:S(2)}) collective-permute-start(bf16[512,128]{1,0:T(8,128)(2,1)S(1)} %get-tuple-element.88), channel_id=1, source_target_pairs={{0,12},{4,8},{8,4},{12,0},{16,28},{20,24},{24,20},{28,16},{1,13},{... | collective-permute-start | bytes 393224 | tf_op jit(solution)/shard_map/ppermute | solution.py:18
  131.2 13.4 %collective-permute-start.41 = (bf16[2,4,128,128]{3,2,1,0:T(8,128)(2,1)S(1)}, bf16[2,4,128,128]{3,2,1,0:T(8,128)(2,1)S(1)}, u32[]{:S(2)}, u32[]{:S(2)}) collective-permute-start(bf16[2,4,128,128]{3,2,1,0:T(8,128)(2,1)S(1)} %get-tuple-element.105), channel_id=1, source_target_pairs={{0,4},{4,0},{8,12},{12,8},{16,20},{20,16},{24,28},{28,24},{1,5},{5... | collective-permute-start | bytes 786440 | tf_op jit(solution)/shard_map/ppermute | solution.py:18
  131.9 14.7 %collective-permute-start.40 = (bf16[1088,128]{1,0:T(8,128)(2,1)S(1)}, bf16[1088,128]{1,0:T(8,128)(2,1)S(1)}, u32[]{:S(2)}, u32[]{:S(2)}) collective-permute-start(bf16[1088,128]{1,0:T(8,128)(2,1)S(1)} %get-tuple-element.102), channel_id=1, source_target_pairs={{0,2},{1,3},{2,0},{3,1},{4,6},{5,7},{6,4},{7,5},{8,10},{9,11},{10,... | collective-permute-start | bytes 835592 | tf_op jit(solution)/shard_map/ppermute | solution.py:18
  136.7 17.2 %collective-permute-start.33 = (bf16[128,512]{1,0:T(8,128)(2,1)S(1)}, bf16[128,512]{1,0:T(8,128)(2,1)S(1)}, u32[]{:S(2)}, u32[]{:S(2)}) collective-permute-start(bf16[128,512]{1,0:T(8,128)(2,1)S(1)} %get-tuple-element.92), channel_id=1, source_target_pairs={{0,16},{4,20},{8,24},{12,28},{16,0},{20,4},{24,8},{28,12},{1,17},{... | collective-permute-start | bytes 393224 | tf_op jit(solution)/shard_map/ppermute | solution.py:18
  137.8 19.8 %collective-permute-start.34 = (bf16[128,512]{1,0:T(8,128)(2,1)}, bf16[128,512]{1,0:T(8,128)(2,1)}, u32[]{:S(2)}, u32[]{:S(2)}) collective-permute-start(bf16[128,512]{1,0:T(8,128)(2,1)} %get-tuple-element.93), channel_id=1, source_target_pairs={{0,20},{4,16},{8,28},{12,24},{16,4},{20,0},{24,12},{28,8},{1,21},{... | collective-permute-start | bytes 393224 | tf_op jit(solution)/shard_map/ppermute | solution.py:18
  142.7 14.9 %collective-permute-start.35 = (bf16[128,512]{1,0:T(8,128)(2,1)}, bf16[128,512]{1,0:T(8,128)(2,1)}, u32[]{:S(2)}, u32[]{:S(2)}) collective-permute-start(bf16[128,512]{1,0:T(8,128)(2,1)} %get-tuple-element.94), channel_id=1, source_target_pairs={{0,24},{4,28},{8,16},{12,20},{16,8},{20,12},{24,0},{28,4},{1,25},{... | collective-permute-start | bytes 393224 | tf_op jit(solution)/shard_map/ppermute | solution.py:18
  144.6 16.4 %collective-permute-start.36 = (bf16[128,512]{1,0:T(8,128)(2,1)}, bf16[128,512]{1,0:T(8,128)(2,1)}, u32[]{:S(2)}, u32[]{:S(2)}) collective-permute-start(bf16[128,512]{1,0:T(8,128)(2,1)} %get-tuple-element.95), channel_id=1, source_target_pairs={{0,28},{4,24},{8,20},{12,16},{16,12},{20,8},{24,4},{28,0},{1,29},{... | collective-permute-start | bytes 393224 | tf_op jit(solution)/shard_map/ppermute | solution.py:18
  148.8 14.2 %collective-permute-start.42 = (bf16[4,128,128]{2,1,0:T(8,128)(2,1)}, bf16[4,128,128]{2,1,0:T(8,128)(2,1)}, u32[]{:S(2)}, u32[]{:S(2)}) collective-permute-start(bf16[4,128,128]{2,1,0:T(8,128)(2,1)} %get-tuple-element.108), channel_id=1, source_target_pairs={{0,4},{4,0},{8,12},{12,8},{16,20},{20,16},{24,28},{28,24},{1,5},{5... | collective-permute-start | bytes 393224 | tf_op jit(solution)/shard_map/ppermute | solution.py:18
  154.6 8.5 %collective-permute-start.43 = (bf16[4,128,128]{2,1,0:T(8,128)(2,1)}, bf16[4,128,128]{2,1,0:T(8,128)(2,1)}, u32[]{:S(2)}, u32[]{:S(2)}) collective-permute-start(bf16[4,128,128]{2,1,0:T(8,128)(2,1)} %get-tuple-element.110), channel_id=1, source_target_pairs={{0,2},{1,3},{2,0},{3,1},{4,6},{5,7},{6,4},{7,5},{8,10},{9,11},{10,... | collective-permute-start | bytes 393224 | tf_op jit(solution)/shard_map/ppermute | solution.py:18
  157.6 11.6 %collective-permute-start.37 = (bf16[128,512]{1,0:T(8,128)(2,1)}, bf16[128,512]{1,0:T(8,128)(2,1)S(1)}, u32[]{:S(2)}, u32[]{:S(2)}) collective-permute-start(bf16[128,512]{1,0:T(8,128)(2,1)} %copy-done.11), channel_id=1, source_target_pairs={{0,8},{4,12},{8,0},{12,4},{16,24},{20,28},{24,16},{28,20},{1,9},{5... | collective-permute-start | bytes 393224 | tf_op jit(solution)/shard_map/ppermute | solution.py:18
  157.6 11.5 %collective-permute-start.38 = (bf16[128,512]{1,0:T(8,128)(2,1)S(1)}, bf16[128,512]{1,0:T(8,128)(2,1)S(1)}, u32[]{:S(2)}, u32[]{:S(2)}) collective-permute-start(bf16[128,512]{1,0:T(8,128)(2,1)S(1)} %get-tuple-element.97), channel_id=1, source_target_pairs={{0,12},{4,8},{8,4},{12,0},{16,28},{20,24},{24,20},{28,16},{1,13},{... | collective-permute-start | bytes 393224 | tf_op jit(solution)/shard_map/ppermute | solution.py:18
  (39 other events, 156.5 us)

commit v9 on v8

--- a/solution.py
+++ b/solution.py
@@ -47,14 +47,14 @@
     return call(kernel, shape, [], *parts, us=us, after=after)
 
 
-def gather_weights(mixing, me_space, send, first_in, second_in):
+def gather_weights(mixing, me_space, send, arrived):
     rows, cols = mixing.shape
     nf, ns = lax.axis_size("filter"), lax.axis_size("space")
     share, pairs = cols // ns, ns // 2
     own = lax.dynamic_slice_in_dim(mixing, me_space * share, share, axis=1)
     even = join([own] + [swap(own, "filter", s) for s in range(2, nf, 2)], send[nf // 2 :])
     first = [even] + [swap(even, "space", s) for s in range(2, ns, 2)]
-    odd = join([swap(even, "filter", 1)], (first_in,))[0]
+    odd = swap(even, "filter", 1)
     second = [odd] + [swap(odd, "space", s) for s in range(2, ns, 2)]
 
     def kernel(*refs):
@@ -64,7 +64,7 @@
                 refs[-1][k, r * rows : (r + 1) * rows, :] = source[r // 2]
 
     shape = jax.ShapeDtypeStruct((pairs, nf * rows, share), BF)
-    held = call(kernel, shape, [], *first, *second, us=0.6, after=(second_in,))
+    held = call(kernel, shape, [], *first, *second, us=0.6, after=(arrived,))
     return held, swap(held, "space", 1)
 
 
@@ -586,10 +586,10 @@
     pieces = exchange(send, "filter")
     steps = early + [mid + 1]
     vol_1 = fold_volume(turn, None, some(pieces, steps), steps)
-    vol_2 = fold_volume(turn, vol_1, some(pieces, [mid + 2, 1]), [mid + 2, 1])
-    rest = later[2:] + last[1:]
+    vol_2 = fold_volume(turn, vol_1, some(pieces, [mid + 2, 1, 2]), [mid + 2, 1, 2])
+    rest = later[2:] + last[2:]
     vol_3 = fold_volume(turn, vol_2, some(pieces, rest), rest)
-    held, other = gather_weights(mixing, me_space, send, vol_1, vol_2)
+    held, other = gather_weights(mixing, me_space, send, vol_2)
     up = upstream.reshape(ch, total)
     up_t = turned(up)
     vol_t, prod = mix(vol_3, held, other, ch, (up_t,))

time: 174 us -> 171 us (0.983)
  waiting for transfers between devices: 49.1 us -> 45.4 us
    ppermute x43, waiting for transfers between devices: 49.1 us -> 45.4 us  [swap(): return lax.ppermute(block, axis, [(i, i ^ step) for i in range(size)])]
    pallas_call x25 -> x24, Pallas kernels: 33.5 us -> 33.9 us  [call(): pl.pallas_call(wrapped, out_shape=out_shape, in_specs=specs + [pl.BlockSp...]
    unnamed x50 -> x48, local copies, waits for them, and re-layouts: 10.8 us -> 10.7 us
  transfers between devices with their start and end apart: 47 -> 47, of which waited for: 18 -> 19; matrix products, arithmetic and copies ran while one was open for 4% -> 4% of each run, Pallas kernels for 13% -> 13%
where the time goes in v9:
time: 171 us
  starting transfers between devices  74.6 us (44%)
  waiting for transfers between devices  45.4 us (27%)
  Pallas kernels  33.9 us (20%)
  local copies, waits for them, and re-layouts  15.3 us (9%)
    ppermute x43, starting transfers between devices, swap(): return lax.ppermute(block, axis, [(i, i ^ step) for i in range(size)])  68.5 us
    ppermute x43, waiting for transfers between devices, swap(): return lax.ppermute(block, axis, [(i, i ^ step) for i in range(size)])  45.4 us
    pallas_call x24, Pallas kernels, call(): pl.pallas_call(wrapped, out_shape=out_shape, in_specs=specs + [pl.BlockSp...  33.9 us
    unnamed x48, local copies, waits for them, and re-layouts  10.7 us
    ppermute x2, starting transfers between devices, halo(): return (lax.ppermute(near, 'space', inner), far)  4.67 us
  transfers between devices with their start and end apart: 47, of which 19 were waited for; matrix products, arithmetic and copies ran while one was open for 4% of the time, Pallas kernels for 13%

profile of v9, /device:TPU:0, one launch (start us, length us, event | category | flops | bytes accessed | tf_op | source)
XLA Modules:
  0.0 171.0 jit_solution(13080555104026169324)
XLA Ops:
  1.6 5.1 %collective-permute-start.2 = (bf16[128,256]{1,0:T(8,128)(2,1)S(1)}, bf16[128,256]{1,0:T(8,128)(2,1)S(1)}, u32[]{:S(2)}, u32[]{:S(2)}) collective-permute-start(bf16[128,256]{1,0:T(8,128)(2,1)S(1)} %constant_dynamic-slice_fusion.8.refs_0_), channel_id=1, source_target_pairs={{0,24},{4,28},{8,16},{12,20},{16,8},{20,12},{24,0},{28,4},{1,25},{... | collective-permute-start | bytes 196616 | tf_op jit(solution)/shard_map/ppermute | solution.py:18
  9.8 2.5 %collective-permute-done.1.refs_2_ = bf16[128,256]{1,0:T(8,128)(2,1)S(1)} collective-permute-done((bf16[128,256]{1,0:T(8,128)(2,1)S(1)}, bf16[128,256]{1,0:T(8,128)(2,1)S(1)}, u32[]{:S(2)}, u32[]{:S(2)}) %collective-permute-start.1) | collective-permute-done | bytes 65568 | tf_op jit(solution)/shard_map/ppermute | solution.py:18
  18.3 2.3 %collective-permute-done.4.refs_2_ = bf16[4,128,256]{2,1,0:T(8,128)(2,1)S(1)} collective-permute-done((bf16[4,128,256]{2,1,0:T(8,128)(2,1)S(1)}, bf16[4,128,256]{2,1,0:T(8,128)(2,1)S(1)}, u32[]{:S(2)}, u32[]{:S(2)}) %collective-permute-start.4) | collective-permute-done | bytes 262176 | tf_op jit(solution)/shard_map/ppermute | solution.py:18
  22.4 2.4 %collective-permute-start.10 = (bf16[128,512]{1,0:T(8,128)(2,1)}, bf16[128,512]{1,0:T(8,128)(2,1)S(1)}, u32[]{:S(2)}, u32[]{:S(2)}) collective-permute-start(bf16[128,512]{1,0:T(8,128)(2,1)} %get-tuple-element.117), channel_id=1, source_target_pairs={{0,8},{4,12},{8,0},{12,4},{16,24},{20,28},{24,16},{28,20},{1,9},{5... | collective-permute-start | bytes 393224 | tf_op jit(solution)/shard_map/ppermute | solution.py:18
  31.2 3.3 %collective-permute-done.8.refs_2_ = bf16[128,512]{1,0:T(8,128)(2,1)S(1)} collective-permute-done((bf16[128,512]{1,0:T(8,128)(2,1)S(1)}, bf16[128,512]{1,0:T(8,128)(2,1)S(1)}, u32[]{:S(2)}, u32[]{:S(2)}) %collective-permute-start.8) | collective-permute-done | bytes 131104 | tf_op jit(solution)/shard_map/ppermute | solution.py:18
  35.5 2.6 %collective-permute-start.12 = (bf16[128,512]{1,0:T(8,128)(2,1)S(1)}, bf16[128,512]{1,0:T(8,128)(2,1)S(1)}, u32[]{:S(2)}, u32[]{:S(2)}) collective-permute-start(bf16[128,512]{1,0:T(8,128)(2,1)S(1)} %get-tuple-element.120.refs_7_), channel_id=1, source_target_pairs={{0,28},{4,24},{8,20},{12,16},{16,12},{20,8},{24,4},{28,0},{1,29},{... | collective-permute-start | bytes 393224 | tf_op jit(solution)/shard_map/ppermute | solution.py:18
  38.5 2.3 %shard_map.80.refs_3_.refs_2_.refs_5_ = bf16[4096,128]{1,0:T(8,128)(2,1)S(1)} custom-call(bf16[128,4096]{1,0:T(8,128)(2,1)S(1)} %bitcast.11), custom_call_target="tpu_custom_call" | custom-call | flops 1380000000 | bytes 1048576 | tf_op jit(solution)/shard_map/pallas_call | solution.py:352
  44.6 2.1 %shard_map.81 = (bf16[512,128]{1,0:T(8,128)(2,1)S(1)}, bf16[512,128]{1,0:T(8,128)(2,1)S(1)}, bf16[512,128]{1,0:T(8,128)(2,1)S(1)}, bf16[512,128]{1,0:T(8,128)(2,...) custom-call(bf16[2,1024,256]{2,1,0:T(8,128)(2,1)S(1)} %shard_map.78., ...), custom_call_target="tpu_custom_call" | custom-call | flops 2990000128 | bytes 1048576 | tf_op jit(solution)/shard_map/pallas_call | solution.py:352
  51.4 2.3 %collective-permute-start.17 = (bf16[512,128]{1,0:T(8,128)(2,1)}, bf16[512,128]{1,0:T(8,128)(2,1)}, u32[]{:S(2)}, u32[]{:S(2)}) collective-permute-start(bf16[512,128]{1,0:T(8,128)(2,1)} %get-tuple-element.64), channel_id=1, source_target_pairs={{0,16},{4,20},{8,24},{12,28},{16,0},{20,4},{24,8},{28,12},{1,17},{... | collective-permute-start | bytes 393224 | tf_op jit(solution)/shard_map/ppermute | solution.py:18
  57.0 2.8 %collective-permute-start.20 = (bf16[512,128]{1,0:T(8,128)(2,1)}, bf16[512,128]{1,0:T(8,128)(2,1)}, u32[]{:S(2)}, u32[]{:S(2)}) collective-permute-start(bf16[512,128]{1,0:T(8,128)(2,1)} %get-tuple-element.67), channel_id=1, source_target_pairs={{0,28},{4,24},{8,20},{12,16},{16,12},{20,8},{24,4},{28,0},{1,29},{... | collective-permute-start | bytes 393224 | tf_op jit(solution)/shard_map/ppermute | solution.py:18
  62.6 7.2 %collective-permute-done.17.refs_3_ = bf16[512,128]{1,0:T(8,128)(2,1)} collective-permute-done((bf16[512,128]{1,0:T(8,128)(2,1)}, bf16[512,128]{1,0:T(8,128)(2,1)}, u32[]{:S(2)}, u32[]{:S(2)}) %collective-permute-start.17) | collective-permute-done | bytes 131104 | tf_op jit(solution)/shard_map/ppermute | solution.py:18
  69.8 3.5 %collective-permute-done.18.refs_4_ = bf16[512,128]{1,0:T(8,128)(2,1)} collective-permute-done((bf16[512,128]{1,0:T(8,128)(2,1)}, bf16[512,128]{1,0:T(8,128)(2,1)}, u32[]{:S(2)}, u32[]{:S(2)}) %collective-permute-start.18) | collective-permute-done | bytes 131104 | tf_op jit(solution)/shard_map/ppermute | solution.py:18
  75.4 2.9 %shard_map.85 = (bf16[2,1024,128]{2,1,0:T(8,128)(2,1)S(1)}, f32[2,1024,128]{2,1,0:T(8,128)S(1)}) custom-call(bf16[4,1024,128]{2,1,0:T(8,128)(2,1)S(1)} %bitcast.17, f32[27,128]{1,0:T(8,128)S(1)} %bitcast.20, bf16[4096,128]{1,0:T(8,128)(2,1)S(1)} %copy-done.20), custom_call_target="tpu_custom_call" | custom-call | flops 3680000000 | bytes 1048576 | tf_op jit(solution)/shard_map/pallas_call | solution.py:352
  78.3 3.2 %shard_map.86 = (bf16[2,1024,128]{2,1,0:T(8,128)(2,1)S(1)}, f32[2,1024,128]{2,1,0:T(8,128)S(1)}, bf16[1024,128]{1,0:T(8,128)(2,1)S(1)}, bf16[1024,128]{1,0:T(8,128)(2,1)S(1)}) custom-call(s32[1]{0:T(128)} %bitcast.refs_1_.refs_0_, bf16[4,1024,128]{2,1,0:T(8,128)(2,1)S(1)} %bitcast.18, bf16[1024,128]{1,0:T(8,128)(2,1)S(1)} %collective-permute-done.21.refs_2_, ...), custom_call_target="tpu_custom_call" | custom-call | flops 3680000000 | bytes 1048576 | tf_op jit(solution)/shard_map/pallas_call | solution.py:352
  81.5 4.6 %collective-permute-start.23 = (bf16[1024,128]{1,0:T(8,128)(2,1)S(1)}, bf16[1024,128]{1,0:T(8,128)(2,1)S(1)}, u32[]{:S(2)}, u32[]{:S(2)}) collective-permute-start(bf16[1024,128]{1,0:T(8,128)(2,1)S(1)} %get-tuple-element.75), channel_id=1, source_target_pairs={{0,1},{1,0},{2,3},{3,2},{4,5},{5,4},{6,7},{7,6},{8,9},{9,8},{10,11... | collective-permute-start | bytes 786440 | tf_op jit(solution)/shard_map/ppermute | solution.py:181
  86.9 2.3 %shard_map.87.refs_7_ = bf16[2,1024,128]{2,1,0:T(8,128)(2,1)S(1)} custom-call(bf16[2,1024,128]{2,1,0:T(8,128)(2,1)S(1)} %get-tuple-element.72.refs_0_.refs_2_.refs_4_, bf16[2,1024,128]{2,1,0:T(8,128)(2,1)S(1)} %get-tuple-element.71.refs_6_.refs_1_.refs_3_.refs_5_, f32[27,128]{1,0:T(8,128)S(1)} %bitcast.22), custom_call_target="tpu_custom_call" | custom-call | flops 2644999936 | bytes 1048576 | tf_op jit(solution)/shard_map/pallas_call | solution.py:352
  89.3 2.5 %shard_map.88 = (bf16[4096,128]{1,0:T(8,128)(2,1)S(1)}, bf16[512,128]{1,0:T(8,128)(2,1)S(1)}, bf16[512,128]{1,0:T(8,128)(2,1)S(1)}, bf16[512,128]{1,0:T(8,128)(2...) custom-call(s32[1]{0:T(128)} %bitcast.1.refs_0_, ...), custom_call_target="tpu_custom_call" | custom-call | flops 3220000000 | bytes 1048576 | tf_op jit(solution)/shard_map/pallas_call | solution.py:352
  92.6 5.2 %collective-permute-start.26 = (bf16[512,128]{1,0:T(8,128)(2,1)S(1)}, bf16[512,128]{1,0:T(8,128)(2,1)S(1)}, u32[]{:S(2)}, u32[]{:S(2)}) collective-permute-start(bf16[512,128]{1,0:T(8,128)(2,1)S(1)} %get-tuple-element.82), channel_id=1, source_target_pairs={{0,16},{4,20},{8,24},{12,28},{16,0},{20,4},{24,8},{28,12},{1,17},{... | collective-permute-start | bytes 393224 | tf_op jit(solution)/shard_map/ppermute | solution.py:18
  100.4 2.2 %collective-permute-start.29 = (bf16[512,128]{1,0:T(8,128)(2,1)S(1)}, bf16[512,128]{1,0:T(8,128)(2,1)S(1)}, u32[]{:S(2)}, u32[]{:S(2)}) collective-permute-start(bf16[512,128]{1,0:T(8,128)(2,1)S(1)} %get-tuple-element.85), channel_id=1, source_target_pairs={{0,28},{4,24},{8,20},{12,16},{16,12},{20,8},{24,4},{28,0},{1,29},{... | collective-permute-start | bytes 393224 | tf_op jit(solution)/shard_map/ppermute | solution.py:18
  102.5 8.7 %shard_map.89 = (f32[32,128]{1,0:T(8,128)S(1)}, bf16[128,4096]{1,0:T(8,128)(2,1)S(1)}, bf16[512,1024]{1,0:T(8,128)(2,1)S(1)}) custom-call(s32[1]{0:T(128)} %bitcast.refs_1_.refs_0_, bf16[4,1024,128]{2,1,0:T(8,128)(2,1)S(1)} %bitcast.19, bf16[1024,128]{1,0:T(8,128)(2,1)S(1)} %collective-permute-done.21.refs_2_, ...), custom_call_target="tpu_custom_call" | custom-call | flops 6670000128 | bytes 1048576 | tf_op jit(solution)/shard_map/pallas_call | solution.py:352
  112.7 2.2 %collective-permute-start.31 = (bf16[512,128]{1,0:T(8,128)(2,1)S(1)}, bf16[512,128]{1,0:T(8,128)(2,1)S(1)}, u32[]{:S(2)}, u32[]{:S(2)}) collective-permute-start(bf16[512,128]{1,0:T(8,128)(2,1)S(1)} %get-tuple-element.88), channel_id=1, source_target_pairs={{0,12},{4,8},{8,4},{12,0},{16,28},{20,24},{24,20},{28,16},{1,13},{... | collective-permute-start | bytes 393224 | tf_op jit(solution)/shard_map/ppermute | solution.py:18
  115.9 2.3 %collective-permute-done.30.refs_7_ = bf16[512,128]{1,0:T(8,128)(2,1)S(1)} collective-permute-done((bf16[512,128]{1,0:T(8,128)(2,1)S(1)}, bf16[512,128]{1,0:T(8,128)(2,1)S(1)}, u32[]{:S(2)}, u32[]{:S(2)}) %collective-permute-start.30) | collective-permute-done | bytes 131104 | tf_op jit(solution)/shard_map/ppermute | solution.py:18
  118.3 3.6 %collective-permute-done.31.refs_8_ = bf16[512,128]{1,0:T(8,128)(2,1)S(1)} collective-permute-done((bf16[512,128]{1,0:T(8,128)(2,1)S(1)}, bf16[512,128]{1,0:T(8,128)(2,1)S(1)}, u32[]{:S(2)}, u32[]{:S(2)}) %collective-permute-start.31) | collective-permute-done | bytes 131104 | tf_op jit(solution)/shard_map/ppermute | solution.py:18
  124.7 2.3 %collective-permute-done.39.refs_2_ = bf16[2,1056,256]{2,1,0:T(8,128)(2,1)S(1)} collective-permute-done((bf16[2,1056,256]{2,1,0:T(8,128)(2,1)S(1)}, bf16[2,1056,256]{2,1,0:T(8,128)(2,1)S(1)}, u32[]{:S(2)}, u32[]{:S(2)}) %collective-permute-start.39) | collective-permute-done | bytes 1081376 | tf_op jit(solution)/shard_map/ppermute | solution.py:18
  128.0 2.3 %collective-permute-start.40 = (bf16[1088,128]{1,0:T(8,128)(2,1)S(1)}, bf16[1088,128]{1,0:T(8,128)(2,1)S(1)}, u32[]{:S(2)}, u32[]{:S(2)}) collective-permute-start(bf16[1088,128]{1,0:T(8,128)(2,1)S(1)} %get-tuple-element.102), channel_id=1, source_target_pairs={{0,2},{1,3},{2,0},{3,1},{4,6},{5,7},{6,4},{7,5},{8,10},{9,11},{10,... | collective-permute-start | bytes 835592 | tf_op jit(solution)/shard_map/ppermute | solution.py:18
  130.4 2.1 %shard_map.92 = (bf16[128,512]{1,0:T(8,128)(2,1)S(1)}, bf16[128,512]{1,0:T(8,128)(2,1)S(1)}, bf16[128,512]{1,0:T(8,128)(2,1)S(1)}, bf16[128,512]{1,0:T(8,128)(2,...) custom-call(s32[1]{0:T(128)} %bitcast.2.refs_0_, ...), custom_call_target="tpu_custom_call" | custom-call | flops 2529999872 | bytes 1048576 | tf_op jit(solution)/shard_map/pallas_call | solution.py:352
  134.8 2.1 %collective-permute-start.34 = (bf16[128,512]{1,0:T(8,128)(2,1)}, bf16[128,512]{1,0:T(8,128)(2,1)}, u32[]{:S(2)}, u32[]{:S(2)}) collective-permute-start(bf16[128,512]{1,0:T(8,128)(2,1)} %get-tuple-element.93), channel_id=1, source_target_pairs={{0,20},{4,16},{8,28},{12,24},{16,4},{20,0},{24,12},{28,8},{1,21},{... | collective-permute-start | bytes 393224 | tf_op jit(solution)/shard_map/ppermute | solution.py:18
  140.7 2.0 %collective-permute-start.36 = (bf16[128,512]{1,0:T(8,128)(2,1)}, bf16[128,512]{1,0:T(8,128)(2,1)}, u32[]{:S(2)}, u32[]{:S(2)}) collective-permute-start(bf16[128,512]{1,0:T(8,128)(2,1)} %get-tuple-element.95), channel_id=1, source_target_pairs={{0,28},{4,24},{8,20},{12,16},{16,12},{20,8},{24,4},{28,0},{1,29},{... | collective-permute-start | bytes 393224 | tf_op jit(solution)/shard_map/ppermute | solution.py:18
  146.3 4.8 %collective-permute-done.33.refs_3_ = bf16[128,512]{1,0:T(8,128)(2,1)S(1)} collective-permute-done((bf16[128,512]{1,0:T(8,128)(2,1)S(1)}, bf16[128,512]{1,0:T(8,128)(2,1)S(1)}, u32[]{:S(2)}, u32[]{:S(2)}) %collective-permute-start.33) | collective-permute-done | bytes 131104 | tf_op jit(solution)/shard_map/ppermute | solution.py:18
  154.5 3.4 %collective-permute-start.38 = (bf16[128,512]{1,0:T(8,128)(2,1)S(1)}, bf16[128,512]{1,0:T(8,128)(2,1)S(1)}, u32[]{:S(2)}, u32[]{:S(2)}) collective-permute-start(bf16[128,512]{1,0:T(8,128)(2,1)S(1)} %get-tuple-element.97), channel_id=1, source_target_pairs={{0,12},{4,8},{8,4},{12,0},{16,28},{20,24},{24,20},{28,16},{1,13},{... | collective-permute-start | bytes 393224 | tf_op jit(solution)/shard_map/ppermute | solution.py:18
  161.0 2.1 %collective-permute-start.44 = (bf16[128,256]{1,0:T(8,128)(2,1)S(1)}, bf16[128,256]{1,0:T(8,128)(2,1)S(1)}, u32[]{:S(2)}, u32[]{:S(2)}) collective-permute-start(bf16[128,256]{1,0:T(8,128)(2,1)S(1)} %get-tuple-element.112), channel_id=1, source_target_pairs={{0,8},{4,12},{8,0},{12,4},{16,24},{20,28},{24,16},{28,20},{1,9},{5... | collective-permute-start | bytes 196616 | tf_op jit(solution)/shard_map/ppermute | solution.py:18
  167.8 2.5 %collective-permute-done.45 = bf16[128,256]{1,0:T(8,128)(2,1)S(1)} collective-permute-done((bf16[128,256]{1,0:T(8,128)(2,1)S(1)}, bf16[128,256]{1,0:T(8,128)(2,1)S(1)}, u32[]{:S(2)}, u32[]{:S(2)}) %collective-permute-start.45) | collective-permute-done | bytes 65568 | tf_op jit(solution)/shard_map/ppermute | solution.py:18
  (140 shorter events, 68.2 us)
Async XLA Ops:
  1.6 8.2 %collective-permute-start.2 = (bf16[128,256]{1,0:T(8,128)(2,1)S(1)}, bf16[128,256]{1,0:T(8,128)(2,1)S(1)}, u32[]{:S(2)}, u32[]{:S(2)}) collective-permute-start(bf16[128,256]{1,0:T(8,128)(2,1)S(1)} %constant_dynamic-slice_fusion.8.refs_0_), channel_id=1, source_target_pairs={{0,24},{4,28},{8,16},{12,20},{16,8},{20,12},{24,0},{28,4},{1,25},{... | collective-permute-start | bytes 196616 | tf_op jit(solution)/shard_map/ppermute | solution.py:18
  12.3 8.3 %collective-permute-start.4 = (bf16[4,128,256]{2,1,0:T(8,128)(2,1)S(1)}, bf16[4,128,256]{2,1,0:T(8,128)(2,1)S(1)}, u32[]{:S(2)}, u32[]{:S(2)}) collective-permute-start(bf16[4,128,256]{2,1,0:T(8,128)(2,1)S(1)} %shard_map.75.refs_0_), channel_id=1, source_target_pairs={{0,4},{4,0},{8,12},{12,8},{16,20},{20,16},{24,28},{28,24},{1,5},{5... | collective-permute-start | bytes 786440 | tf_op jit(solution)/shard_map/ppermute | solution.py:18
  13.9 12.3 %collective-permute-start.7 = (bf16[128,512]{1,0:T(8,128)(2,1)S(1)}, bf16[128,512]{1,0:T(8,128)(2,1)S(1)}, u32[]{:S(2)}, u32[]{:S(2)}) collective-permute-start(bf16[128,512]{1,0:T(8,128)(2,1)S(1)} %get-tuple-element.122.refs_5_), channel_id=1, source_target_pairs={{0,20},{4,16},{8,28},{12,24},{16,4},{20,0},{24,12},{28,8},{1,21},{... | collective-permute-start | bytes 393224 | tf_op jit(solution)/shard_map/ppermute | solution.py:18
  15.5 12.2 %collective-permute-start.6 = (bf16[128,512]{1,0:T(8,128)(2,1)S(1)}, bf16[128,512]{1,0:T(8,128)(2,1)S(1)}, u32[]{:S(2)}, u32[]{:S(2)}) collective-permute-start(bf16[128,512]{1,0:T(8,128)(2,1)S(1)} %get-tuple-element.123.refs_4_), channel_id=1, source_target_pairs={{0,16},{4,20},{8,24},{12,28},{16,0},{20,4},{24,8},{28,12},{1,17},{... | collective-permute-start | bytes 393224 | tf_op jit(solution)/shard_map/ppermute | solution.py:18
  16.8 17.9 %collective-permute-start.3 = (bf16[4,128,256]{2,1,0:T(8,128)(2,1)S(1)}, bf16[4,128,256]{2,1,0:T(8,128)(2,1)S(1)}, u32[]{:S(2)}, u32[]{:S(2)}) collective-permute-start(bf16[4,128,256]{2,1,0:T(8,128)(2,1)S(1)} %shard_map.75.refs_0_), channel_id=1, source_target_pairs={{0,2},{1,3},{2,0},{3,1},{4,6},{5,7},{6,4},{7,5},{8,10},{9,11},{10,... | collective-permute-start | bytes 786440 | tf_op jit(solution)/shard_map/ppermute | solution.py:18
  20.7 14.0 %collective-permute-start.5 = (bf16[4,128,256]{2,1,0:T(8,128)(2,1)S(1)}, bf16[4,128,256]{2,1,0:T(8,128)(2,1)S(1)}, u32[]{:S(2)}, u32[]{:S(2)}) collective-permute-start(bf16[4,128,256]{2,1,0:T(8,128)(2,1)S(1)} %collective-permute-done.4.refs_2_), channel_id=1, source_target_pairs={{0,2},{1,3},{2,0},{3,1},{4,6},{5,7},{6,4},{7,5},{8,10},{9,11},{10,... | collective-permute-start | bytes 786440 | tf_op jit(solution)/shard_map/ppermute | solution.py:18
  22.4 8.0 %collective-permute-start.10 = (bf16[128,512]{1,0:T(8,128)(2,1)}, bf16[128,512]{1,0:T(8,128)(2,1)S(1)}, u32[]{:S(2)}, u32[]{:S(2)}) collective-permute-start(bf16[128,512]{1,0:T(8,128)(2,1)} %get-tuple-element.117), channel_id=1, source_target_pairs={{0,8},{4,12},{8,0},{12,4},{16,24},{20,28},{24,16},{28,20},{1,9},{5... | collective-permute-start | bytes 393224 | tf_op jit(solution)/shard_map/ppermute | solution.py:18
  34.8 9.9 %collective-permute-start.11 = (bf16[2,1024,256]{2,1,0:T(8,128)(2,1)S(1)}, bf16[2,1024,256]{2,1,0:T(8,128)(2,1)S(1)}, u32[]{:S(2)}, u32[]{:S(2)}) collective-permute-start(bf16[2,1024,256]{2,1,0:T(8,128)(2,1)S(1)} %shard_map.78.refs_0_.refs_2_), channel_id=1, source_target_pairs={{0,1},{1,0},{2,3},{3,2},{4,5},{5,4},{6,7},{7,6},{8,9},{9,8},{10,11... | collective-permute-start | bytes 3145736 | tf_op jit(solution)/shard_map/ppermute | solution.py:18
  35.5 8.9 %collective-permute-start.12 = (bf16[128,512]{1,0:T(8,128)(2,1)S(1)}, bf16[128,512]{1,0:T(8,128)(2,1)S(1)}, u32[]{:S(2)}, u32[]{:S(2)}) collective-permute-start(bf16[128,512]{1,0:T(8,128)(2,1)S(1)} %get-tuple-element.120.refs_7_), channel_id=1, source_target_pairs={{0,28},{4,24},{8,20},{12,16},{16,12},{20,8},{24,4},{28,0},{1,29},{... | collective-permute-start | bytes 393224 | tf_op jit(solution)/shard_map/ppermute | solution.py:18
  48.9 8.1 %collective-permute-start.15 = (bf16[512,128]{1,0:T(8,128)(2,1)S(1)}, bf16[512,128]{1,0:T(8,128)(2,1)S(1)}, u32[]{:S(2)}, u32[]{:S(2)}) collective-permute-start(bf16[512,128]{1,0:T(8,128)(2,1)S(1)} %get-tuple-element.62), channel_id=1, source_target_pairs={{0,8},{4,12},{8,0},{12,4},{16,24},{20,28},{24,16},{28,20},{1,9},{5... | collective-permute-start | bytes 393224 | tf_op jit(solution)/shard_map/ppermute | solution.py:18
  50.6 11.0 %collective-permute-start.16 = (bf16[512,128]{1,0:T(8,128)(2,1)}, bf16[512,128]{1,0:T(8,128)(2,1)}, u32[]{:S(2)}, u32[]{:S(2)}) collective-permute-start(bf16[512,128]{1,0:T(8,128)(2,1)} %get-tuple-element.63), channel_id=1, source_target_pairs={{0,12},{4,8},{8,4},{12,0},{16,28},{20,24},{24,20},{28,16},{1,13},{... | collective-permute-start | bytes 393224 | tf_op jit(solution)/shard_map/ppermute | solution.py:18
  51.4 18.4 %collective-permute-start.17 = (bf16[512,128]{1,0:T(8,128)(2,1)}, bf16[512,128]{1,0:T(8,128)(2,1)}, u32[]{:S(2)}, u32[]{:S(2)}) collective-permute-start(bf16[512,128]{1,0:T(8,128)(2,1)} %get-tuple-element.64), channel_id=1, source_target_pairs={{0,16},{4,20},{8,24},{12,28},{16,0},{20,4},{24,8},{28,12},{1,17},{... | collective-permute-start | bytes 393224 | tf_op jit(solution)/shard_map/ppermute | solution.py:18
  53.7 19.5 %collective-permute-start.18 = (bf16[512,128]{1,0:T(8,128)(2,1)}, bf16[512,128]{1,0:T(8,128)(2,1)}, u32[]{:S(2)}, u32[]{:S(2)}) collective-permute-start(bf16[512,128]{1,0:T(8,128)(2,1)} %get-tuple-element.65), channel_id=1, source_target_pairs={{0,20},{4,16},{8,28},{12,24},{16,4},{20,0},{24,12},{28,8},{1,21},{... | collective-permute-start | bytes 393224 | tf_op jit(solution)/shard_map/ppermute | solution.py:18
  55.4 17.8 %collective-permute-start.19 = (bf16[512,128]{1,0:T(8,128)(2,1)}, bf16[512,128]{1,0:T(8,128)(2,1)}, u32[]{:S(2)}, u32[]{:S(2)}) collective-permute-start(bf16[512,128]{1,0:T(8,128)(2,1)} %get-tuple-element.66), channel_id=1, source_target_pairs={{0,24},{4,28},{8,16},{12,20},{16,8},{20,12},{24,0},{28,4},{1,25},{... | collective-permute-start | bytes 393224 | tf_op jit(solution)/shard_map/ppermute | solution.py:18
  57.0 16.2 %collective-permute-start.20 = (bf16[512,128]{1,0:T(8,128)(2,1)}, bf16[512,128]{1,0:T(8,128)(2,1)}, u32[]{:S(2)}, u32[]{:S(2)}) collective-permute-start(bf16[512,128]{1,0:T(8,128)(2,1)} %get-tuple-element.67), channel_id=1, source_target_pairs={{0,28},{4,24},{8,20},{12,16},{16,12},{20,8},{24,4},{28,0},{1,29},{... | collective-permute-start | bytes 393224 | tf_op jit(solution)/shard_map/ppermute | solution.py:18
  81.5 7.8 %collective-permute-start.23 = (bf16[1024,128]{1,0:T(8,128)(2,1)S(1)}, bf16[1024,128]{1,0:T(8,128)(2,1)S(1)}, u32[]{:S(2)}, u32[]{:S(2)}) collective-permute-start(bf16[1024,128]{1,0:T(8,128)(2,1)S(1)} %get-tuple-element.75), channel_id=1, source_target_pairs={{0,1},{1,0},{2,3},{3,2},{4,5},{5,4},{6,7},{7,6},{8,9},{9,8},{10,11... | collective-permute-start | bytes 786440 | tf_op jit(solution)/shard_map/ppermute | solution.py:181
  91.8 10.8 %collective-permute-start.25 = (bf16[512,128]{1,0:T(8,128)(2,1)S(1)}, bf16[512,128]{1,0:T(8,128)(2,1)S(1)}, u32[]{:S(2)}, u32[]{:S(2)}) collective-permute-start(bf16[512,128]{1,0:T(8,128)(2,1)S(1)} %get-tuple-element.78), channel_id=1, source_target_pairs={{0,4},{4,0},{8,12},{12,8},{16,20},{20,16},{24,28},{28,24},{1,5},{5... | collective-permute-start | bytes 393224 | tf_op jit(solution)/shard_map/ppermute | solution.py:18
  92.6 20.1 %collective-permute-start.26 = (bf16[512,128]{1,0:T(8,128)(2,1)S(1)}, bf16[512,128]{1,0:T(8,128)(2,1)S(1)}, u32[]{:S(2)}, u32[]{:S(2)}) collective-permute-start(bf16[512,128]{1,0:T(8,128)(2,1)S(1)} %get-tuple-element.82), channel_id=1, source_target_pairs={{0,16},{4,20},{8,24},{12,28},{16,0},{20,4},{24,8},{28,12},{1,17},{... | collective-permute-start | bytes 393224 | tf_op jit(solution)/shard_map/ppermute | solution.py:18
  97.8 18.1 %collective-permute-start.27 = (bf16[512,128]{1,0:T(8,128)(2,1)S(1)}, bf16[512,128]{1,0:T(8,128)(2,1)S(1)}, u32[]{:S(2)}, u32[]{:S(2)}) collective-permute-start(bf16[512,128]{1,0:T(8,128)(2,1)S(1)} %get-tuple-element.83), channel_id=1, source_target_pairs={{0,20},{4,16},{8,28},{12,24},{16,4},{20,0},{24,12},{28,8},{1,21},{... | collective-permute-start | bytes 393224 | tf_op jit(solution)/shard_map/ppermute | solution.py:18
  98.4 17.5 %collective-permute-start.28 = (bf16[512,128]{1,0:T(8,128)(2,1)S(1)}, bf16[512,128]{1,0:T(8,128)(2,1)S(1)}, u32[]{:S(2)}, u32[]{:S(2)}) collective-permute-start(bf16[512,128]{1,0:T(8,128)(2,1)S(1)} %get-tuple-element.84), channel_id=1, source_target_pairs={{0,24},{4,28},{8,16},{12,20},{16,8},{20,12},{24,0},{28,4},{1,25},{... | collective-permute-start | bytes 393224 | tf_op jit(solution)/shard_map/ppermute | solution.py:18
  100.4 15.6 %collective-permute-start.29 = (bf16[512,128]{1,0:T(8,128)(2,1)S(1)}, bf16[512,128]{1,0:T(8,128)(2,1)S(1)}, u32[]{:S(2)}, u32[]{:S(2)}) collective-permute-start(bf16[512,128]{1,0:T(8,128)(2,1)S(1)} %get-tuple-element.85), channel_id=1, source_target_pairs={{0,28},{4,24},{8,20},{12,16},{16,12},{20,8},{24,4},{28,0},{1,29},{... | collective-permute-start | bytes 393224 | tf_op jit(solution)/shard_map/ppermute | solution.py:18
  112.7 9.2 %collective-permute-start.31 = (bf16[512,128]{1,0:T(8,128)(2,1)S(1)}, bf16[512,128]{1,0:T(8,128)(2,1)S(1)}, u32[]{:S(2)}, u32[]{:S(2)}) collective-permute-start(bf16[512,128]{1,0:T(8,128)(2,1)S(1)} %get-tuple-element.88), channel_id=1, source_target_pairs={{0,12},{4,8},{8,4},{12,0},{16,28},{20,24},{24,20},{28,16},{1,13},{... | collective-permute-start | bytes 393224 | tf_op jit(solution)/shard_map/ppermute | solution.py:18
  127.3 13.4 %collective-permute-start.41 = (bf16[2,4,128,128]{3,2,1,0:T(8,128)(2,1)S(1)}, bf16[2,4,128,128]{3,2,1,0:T(8,128)(2,1)S(1)}, u32[]{:S(2)}, u32[]{:S(2)}) collective-permute-start(bf16[2,4,128,128]{3,2,1,0:T(8,128)(2,1)S(1)} %get-tuple-element.105), channel_id=1, source_target_pairs={{0,4},{4,0},{8,12},{12,8},{16,20},{20,16},{24,28},{28,24},{1,5},{5... | collective-permute-start | bytes 786440 | tf_op jit(solution)/shard_map/ppermute | solution.py:18
  128.0 14.7 %collective-permute-start.40 = (bf16[1088,128]{1,0:T(8,128)(2,1)S(1)}, bf16[1088,128]{1,0:T(8,128)(2,1)S(1)}, u32[]{:S(2)}, u32[]{:S(2)}) collective-permute-start(bf16[1088,128]{1,0:T(8,128)(2,1)S(1)} %get-tuple-element.102), channel_id=1, source_target_pairs={{0,2},{1,3},{2,0},{3,1},{4,6},{5,7},{6,4},{7,5},{8,10},{9,11},{10,... | collective-permute-start | bytes 835592 | tf_op jit(solution)/shard_map/ppermute | solution.py:18
  133.7 17.4 %collective-permute-start.33 = (bf16[128,512]{1,0:T(8,128)(2,1)S(1)}, bf16[128,512]{1,0:T(8,128)(2,1)S(1)}, u32[]{:S(2)}, u32[]{:S(2)}) collective-permute-start(bf16[128,512]{1,0:T(8,128)(2,1)S(1)} %get-tuple-element.92), channel_id=1, source_target_pairs={{0,16},{4,20},{8,24},{12,28},{16,0},{20,4},{24,8},{28,12},{1,17},{... | collective-permute-start | bytes 393224 | tf_op jit(solution)/shard_map/ppermute | solution.py:18
  134.8 19.7 %collective-permute-start.34 = (bf16[128,512]{1,0:T(8,128)(2,1)}, bf16[128,512]{1,0:T(8,128)(2,1)}, u32[]{:S(2)}, u32[]{:S(2)}) collective-permute-start(bf16[128,512]{1,0:T(8,128)(2,1)} %get-tuple-element.93), channel_id=1, source_target_pairs={{0,20},{4,16},{8,28},{12,24},{16,4},{20,0},{24,12},{28,8},{1,21},{... | collective-permute-start | bytes 393224 | tf_op jit(solution)/shard_map/ppermute | solution.py:18
  138.7 15.8 %collective-permute-start.35 = (bf16[128,512]{1,0:T(8,128)(2,1)}, bf16[128,512]{1,0:T(8,128)(2,1)}, u32[]{:S(2)}, u32[]{:S(2)}) collective-permute-start(bf16[128,512]{1,0:T(8,128)(2,1)} %get-tuple-element.94), channel_id=1, source_target_pairs={{0,24},{4,28},{8,16},{12,20},{16,8},{20,12},{24,0},{28,4},{1,25},{... | collective-permute-start | bytes 393224 | tf_op jit(solution)/shard_map/ppermute | solution.py:18
  140.7 17.2 %collective-permute-start.36 = (bf16[128,512]{1,0:T(8,128)(2,1)}, bf16[128,512]{1,0:T(8,128)(2,1)}, u32[]{:S(2)}, u32[]{:S(2)}) collective-permute-start(bf16[128,512]{1,0:T(8,128)(2,1)} %get-tuple-element.95), channel_id=1, source_target_pairs={{0,28},{4,24},{8,20},{12,16},{16,12},{20,8},{24,4},{28,0},{1,29},{... | collective-permute-start | bytes 393224 | tf_op jit(solution)/shard_map/ppermute | solution.py:18
  145.0 15.0 %collective-permute-start.42 = (bf16[4,128,128]{2,1,0:T(8,128)(2,1)}, bf16[4,128,128]{2,1,0:T(8,128)(2,1)}, u32[]{:S(2)}, u32[]{:S(2)}) collective-permute-start(bf16[4,128,128]{2,1,0:T(8,128)(2,1)} %get-tuple-element.108), channel_id=1, source_target_pairs={{0,4},{4,0},{8,12},{12,8},{16,20},{20,16},{24,28},{28,24},{1,5},{5... | collective-permute-start | bytes 393224 | tf_op jit(solution)/shard_map/ppermute | solution.py:18
  151.7 8.2 %collective-permute-start.43 = (bf16[4,128,128]{2,1,0:T(8,128)(2,1)}, bf16[4,128,128]{2,1,0:T(8,128)(2,1)}, u32[]{:S(2)}, u32[]{:S(2)}) collective-permute-start(bf16[4,128,128]{2,1,0:T(8,128)(2,1)} %get-tuple-element.110), channel_id=1, source_target_pairs={{0,2},{1,3},{2,0},{3,1},{4,6},{5,7},{6,4},{7,5},{8,10},{9,11},{10,... | collective-permute-start | bytes 393224 | tf_op jit(solution)/shard_map/ppermute | solution.py:18
  154.5 11.6 %collective-permute-start.37 = (bf16[128,512]{1,0:T(8,128)(2,1)}, bf16[128,512]{1,0:T(8,128)(2,1)S(1)}, u32[]{:S(2)}, u32[]{:S(2)}) collective-permute-start(bf16[128,512]{1,0:T(8,128)(2,1)} %copy-done.11), channel_id=1, source_target_pairs={{0,8},{4,12},{8,0},{12,4},{16,24},{20,28},{24,16},{28,20},{1,9},{5... | collective-permute-start | bytes 393224 | tf_op jit(solution)/shard_map/ppermute | solution.py:18
  154.5 11.6 %collective-permute-start.38 = (bf16[128,512]{1,0:T(8,128)(2,1)S(1)}, bf16[128,512]{1,0:T(8,128)(2,1)S(1)}, u32[]{:S(2)}, u32[]{:S(2)}) collective-permute-start(bf16[128,512]{1,0:T(8,128)(2,1)S(1)} %get-tuple-element.97), channel_id=1, source_target_pairs={{0,12},{4,8},{8,4},{12,0},{16,28},{20,24},{24,20},{28,16},{1,13},{... | collective-permute-start | bytes 393224 | tf_op jit(solution)/shard_map/ppermute | solution.py:18
  (38 other events, 152.8 us)

commit v10 on v9

--- a/solution.py
+++ b/solution.py
@@ -238,7 +238,7 @@
             silu[k, cells, :] = spatial * sig
             return carry
 
-        lax.fori_loop(0, flat // lanes, strip, 0)
+        lax.fori_loop(0, flat // lanes, strip, 0, unroll=2)
 
 
 def forward_middle(group, planes, m, taps, up, grad, silu, pad):
@@ -263,7 +263,7 @@
             put(k, p, pl.multiple_of(f * lanes, lanes), jnp.concatenate(lines, axis=0).astype(BF))
             return carry
 
-        lax.fori_loop(0, flat // lanes, strip, 0)
+        lax.fori_loop(0, flat // lanes, strip, 0, unroll=2)
 
 
 def backward_middle(group, where, planes, g0, g1, taps, out, pad):
@@ -314,7 +314,7 @@
             output[:, lane] = (vol[:, lane].astype(F32) + turned).astype(BF)
             return carry
 
-        lax.fori_loop(0, flat // lanes, strip, 0)
+        lax.fori_loop(0, flat // lanes, strip, 0, unroll=2)
     where = {p: (0, p) for p in range(planes)}
     load_planes(pad, (m,), where, (odd, near, far), range(-1, planes + 1), planes)
     load_planes(gpad, (g0, g1), where_grad, (), range(planes), planes)

time: 171 us -> 170 us (level)
  Pallas kernels: 33.9 us -> 31.8 us
  waiting for transfers between devices: 45.4 us -> 47.4 us
    pallas_call x24, Pallas kernels: 33.9 us -> 31.8 us  [call(): pl.pallas_call(wrapped, out_shape=out_shape, in_specs=specs + [pl.BlockSp...]
    ppermute x43, waiting for transfers between devices: 45.4 us -> 47.4 us  [swap(): return lax.ppermute(block, axis, [(i, i ^ step) for i in range(size)])]
  transfers between devices with their start and end apart: 47 -> 47, of which waited for: 19 -> 20; matrix products, arithmetic and copies ran while one was open for 4% -> 4% of each run, Pallas kernels for 13% -> 12%
where the time goes in v10:
time: 170 us
  starting transfers between devices  73.2 us (43%)
  waiting for transfers between devices  47.4 us (28%)
  Pallas kernels  31.8 us (19%)
  local copies, waits for them, and re-layouts  15.3 us (9%)
    ppermute x43, starting transfers between devices, swap(): return lax.ppermute(block, axis, [(i, i ^ step) for i in range(size)])  66.8 us
    ppermute x43, waiting for transfers between devices, swap(): return lax.ppermute(block, axis, [(i, i ^ step) for i in range(size)])  47.4 us
    pallas_call x24, Pallas kernels, call(): pl.pallas_call(wrapped, out_shape=out_shape, in_specs=specs + [pl.BlockSp...  31.8 us
    unnamed x48, local copies, waits for them, and re-layouts  10.7 us
    ppermute x2, starting transfers between devices, halo(): return (lax.ppermute(near, 'space', inner), far)  4.9 us
  transfers between devices with their start and end apart: 47, of which 20 were waited for; matrix products, arithmetic and copies ran while one was open for 4% of the time, Pallas kernels for 12%

profile of v10, /device:TPU:0, one launch (start us, length us, event | category | flops | bytes accessed | tf_op | source)
XLA Modules:
  0.0 169.5 jit_solution(12050201027496931575)
XLA Ops:
  1.6 5.1 %collective-permute-start.2 = (bf16[128,256]{1,0:T(8,128)(2,1)S(1)}, bf16[128,256]{1,0:T(8,128)(2,1)S(1)}, u32[]{:S(2)}, u32[]{:S(2)}) collective-permute-start(bf16[128,256]{1,0:T(8,128)(2,1)S(1)} %constant_dynamic-slice_fusion.8.refs_0_), channel_id=1, source_target_pairs={{0,24},{4,28},{8,16},{12,20},{16,8},{20,12},{24,0},{28,4},{1,25},{... | collective-permute-start | bytes 196616 | tf_op jit(solution)/shard_map/ppermute | solution.py:18
  9.8 2.5 %collective-permute-done.1.refs_2_ = bf16[128,256]{1,0:T(8,128)(2,1)S(1)} collective-permute-done((bf16[128,256]{1,0:T(8,128)(2,1)S(1)}, bf16[128,256]{1,0:T(8,128)(2,1)S(1)}, u32[]{:S(2)}, u32[]{:S(2)}) %collective-permute-start.1) | collective-permute-done | bytes 65568 | tf_op jit(solution)/shard_map/ppermute | solution.py:18
  18.3 2.3 %collective-permute-done.4.refs_2_ = bf16[4,128,256]{2,1,0:T(8,128)(2,1)S(1)} collective-permute-done((bf16[4,128,256]{2,1,0:T(8,128)(2,1)S(1)}, bf16[4,128,256]{2,1,0:T(8,128)(2,1)S(1)}, u32[]{:S(2)}, u32[]{:S(2)}) %collective-permute-start.4) | collective-permute-done | bytes 262176 | tf_op jit(solution)/shard_map/ppermute | solution.py:18
  22.4 2.4 %collective-permute-start.10 = (bf16[128,512]{1,0:T(8,128)(2,1)}, bf16[128,512]{1,0:T(8,128)(2,1)S(1)}, u32[]{:S(2)}, u32[]{:S(2)}) collective-permute-start(bf16[128,512]{1,0:T(8,128)(2,1)} %get-tuple-element.117), channel_id=1, source_target_pairs={{0,8},{4,12},{8,0},{12,4},{16,24},{20,28},{24,16},{28,20},{1,9},{5... | collective-permute-start | bytes 393224 | tf_op jit(solution)/shard_map/ppermute | solution.py:18
  31.2 3.3 %collective-permute-done.8.refs_2_ = bf16[128,512]{1,0:T(8,128)(2,1)S(1)} collective-permute-done((bf16[128,512]{1,0:T(8,128)(2,1)S(1)}, bf16[128,512]{1,0:T(8,128)(2,1)S(1)}, u32[]{:S(2)}, u32[]{:S(2)}) %collective-permute-start.8) | collective-permute-done | bytes 131104 | tf_op jit(solution)/shard_map/ppermute | solution.py:18
  35.5 2.6 %collective-permute-start.12 = (bf16[128,512]{1,0:T(8,128)(2,1)S(1)}, bf16[128,512]{1,0:T(8,128)(2,1)S(1)}, u32[]{:S(2)}, u32[]{:S(2)}) collective-permute-start(bf16[128,512]{1,0:T(8,128)(2,1)S(1)} %get-tuple-element.120.refs_7_), channel_id=1, source_target_pairs={{0,28},{4,24},{8,20},{12,16},{16,12},{20,8},{24,4},{28,0},{1,29},{... | collective-permute-start | bytes 393224 | tf_op jit(solution)/shard_map/ppermute | solution.py:18
  38.5 2.3 %shard_map.80.refs_3_.refs_2_.refs_5_ = bf16[4096,128]{1,0:T(8,128)(2,1)S(1)} custom-call(bf16[128,4096]{1,0:T(8,128)(2,1)S(1)} %bitcast.11), custom_call_target="tpu_custom_call" | custom-call | flops 1380000000 | bytes 1048576 | tf_op jit(solution)/shard_map/pallas_call | solution.py:352
  44.6 2.1 %shard_map.81 = (bf16[512,128]{1,0:T(8,128)(2,1)S(1)}, bf16[512,128]{1,0:T(8,128)(2,1)S(1)}, bf16[512,128]{1,0:T(8,128)(2,1)S(1)}, bf16[512,128]{1,0:T(8,128)(2,...) custom-call(bf16[2,1024,256]{2,1,0:T(8,128)(2,1)S(1)} %shard_map.78., ...), custom_call_target="tpu_custom_call" | custom-call | flops 2990000128 | bytes 1048576 | tf_op jit(solution)/shard_map/pallas_call | solution.py:352
  51.4 2.3 %collective-permute-start.17 = (bf16[512,128]{1,0:T(8,128)(2,1)}, bf16[512,128]{1,0:T(8,128)(2,1)}, u32[]{:S(2)}, u32[]{:S(2)}) collective-permute-start(bf16[512,128]{1,0:T(8,128)(2,1)} %get-tuple-element.64), channel_id=1, source_target_pairs={{0,16},{4,20},{8,24},{12,28},{16,0},{20,4},{24,8},{28,12},{1,17},{... | collective-permute-start | bytes 393224 | tf_op jit(solution)/shard_map/ppermute | solution.py:18
  57.0 2.8 %collective-permute-start.20 = (bf16[512,128]{1,0:T(8,128)(2,1)}, bf16[512,128]{1,0:T(8,128)(2,1)}, u32[]{:S(2)}, u32[]{:S(2)}) collective-permute-start(bf16[512,128]{1,0:T(8,128)(2,1)} %get-tuple-element.67), channel_id=1, source_target_pairs={{0,28},{4,24},{8,20},{12,16},{16,12},{20,8},{24,4},{28,0},{1,29},{... | collective-permute-start | bytes 393224 | tf_op jit(solution)/shard_map/ppermute | solution.py:18
  62.6 7.2 %collective-permute-done.17.refs_3_ = bf16[512,128]{1,0:T(8,128)(2,1)} collective-permute-done((bf16[512,128]{1,0:T(8,128)(2,1)}, bf16[512,128]{1,0:T(8,128)(2,1)}, u32[]{:S(2)}, u32[]{:S(2)}) %collective-permute-start.17) | collective-permute-done | bytes 131104 | tf_op jit(solution)/shard_map/ppermute | solution.py:18
  69.8 3.5 %collective-permute-done.18.refs_4_ = bf16[512,128]{1,0:T(8,128)(2,1)} collective-permute-done((bf16[512,128]{1,0:T(8,128)(2,1)}, bf16[512,128]{1,0:T(8,128)(2,1)}, u32[]{:S(2)}, u32[]{:S(2)}) %collective-permute-start.18) | collective-permute-done | bytes 131104 | tf_op jit(solution)/shard_map/ppermute | solution.py:18
  75.4 2.7 %shard_map.85 = (bf16[2,1024,128]{2,1,0:T(8,128)(2,1)S(1)}, f32[2,1024,128]{2,1,0:T(8,128)S(1)}) custom-call(bf16[4,1024,128]{2,1,0:T(8,128)(2,1)S(1)} %bitcast.17, f32[27,128]{1,0:T(8,128)S(1)} %bitcast.20, bf16[4096,128]{1,0:T(8,128)(2,1)S(1)} %copy-done.20), custom_call_target="tpu_custom_call" | custom-call | flops 3680000000 | bytes 1048576 | tf_op jit(solution)/shard_map/pallas_call | solution.py:352
  78.1 2.9 %shard_map.86 = (bf16[2,1024,128]{2,1,0:T(8,128)(2,1)S(1)}, f32[2,1024,128]{2,1,0:T(8,128)S(1)}, bf16[1024,128]{1,0:T(8,128)(2,1)S(1)}, bf16[1024,128]{1,0:T(8,128)(2,1)S(1)}) custom-call(s32[1]{0:T(128)} %bitcast.refs_1_.refs_0_, bf16[4,1024,128]{2,1,0:T(8,128)(2,1)S(1)} %bitcast.18, bf16[1024,128]{1,0:T(8,128)(2,1)S(1)} %collective-permute-done.21.refs_2_, ...), custom_call_target="tpu_custom_call" | custom-call | flops 3680000000 | bytes 1048576 | tf_op jit(solution)/shard_map/pallas_call | solution.py:352
  81.0 4.8 %collective-permute-start.23 = (bf16[1024,128]{1,0:T(8,128)(2,1)S(1)}, bf16[1024,128]{1,0:T(8,128)(2,1)S(1)}, u32[]{:S(2)}, u32[]{:S(2)}) collective-permute-start(bf16[1024,128]{1,0:T(8,128)(2,1)S(1)} %get-tuple-element.75), channel_id=1, source_target_pairs={{0,1},{1,0},{2,3},{3,2},{4,5},{5,4},{6,7},{7,6},{8,9},{9,8},{10,11... | collective-permute-start | bytes 786440 | tf_op jit(solution)/shard_map/ppermute | solution.py:181
  86.7 2.3 %shard_map.87.refs_7_ = bf16[2,1024,128]{2,1,0:T(8,128)(2,1)S(1)} custom-call(bf16[2,1024,128]{2,1,0:T(8,128)(2,1)S(1)} %get-tuple-element.72.refs_0_.refs_2_.refs_4_, bf16[2,1024,128]{2,1,0:T(8,128)(2,1)S(1)} %get-tuple-element.71.refs_6_.refs_1_.refs_3_.refs_5_, f32[27,128]{1,0:T(8,128)S(1)} %bitcast.22), custom_call_target="tpu_custom_call" | custom-call | flops 2644999936 | bytes 1048576 | tf_op jit(solution)/shard_map/pallas_call | solution.py:352
  89.0 2.5 %shard_map.88 = (bf16[4096,128]{1,0:T(8,128)(2,1)S(1)}, bf16[512,128]{1,0:T(8,128)(2,1)S(1)}, bf16[512,128]{1,0:T(8,128)(2,1)S(1)}, bf16[512,128]{1,0:T(8,128)(2...) custom-call(s32[1]{0:T(128)} %bitcast.1.refs_0_, ...), custom_call_target="tpu_custom_call" | custom-call | flops 3220000000 | bytes 1048576 | tf_op jit(solution)/shard_map/pallas_call | solution.py:352
  92.3 5.2 %collective-permute-start.26 = (bf16[512,128]{1,0:T(8,128)(2,1)S(1)}, bf16[512,128]{1,0:T(8,128)(2,1)S(1)}, u32[]{:S(2)}, u32[]{:S(2)}) collective-permute-start(bf16[512,128]{1,0:T(8,128)(2,1)S(1)} %get-tuple-element.82), channel_id=1, source_target_pairs={{0,16},{4,20},{8,24},{12,28},{16,0},{20,4},{24,8},{28,12},{1,17},{... | collective-permute-start | bytes 393224 | tf_op jit(solution)/shard_map/ppermute | solution.py:18
  98.1 1.9 %collective-permute-start.28 = (bf16[512,128]{1,0:T(8,128)(2,1)S(1)}, bf16[512,128]{1,0:T(8,128)(2,1)S(1)}, u32[]{:S(2)}, u32[]{:S(2)}) collective-permute-start(bf16[512,128]{1,0:T(8,128)(2,1)S(1)} %get-tuple-element.84), channel_id=1, source_target_pairs={{0,24},{4,28},{8,16},{12,20},{16,8},{20,12},{24,0},{28,4},{1,25},{... | collective-permute-start | bytes 393224 | tf_op jit(solution)/shard_map/ppermute | solution.py:18
  100.1 2.2 %collective-permute-start.29 = (bf16[512,128]{1,0:T(8,128)(2,1)S(1)}, bf16[512,128]{1,0:T(8,128)(2,1)S(1)}, u32[]{:S(2)}, u32[]{:S(2)}) collective-permute-start(bf16[512,128]{1,0:T(8,128)(2,1)S(1)} %get-tuple-element.85), channel_id=1, source_target_pairs={{0,28},{4,24},{8,20},{12,16},{16,12},{20,8},{24,4},{28,0},{1,29},{... | collective-permute-start | bytes 393224 | tf_op jit(solution)/shard_map/ppermute | solution.py:18
  102.2 7.2 %shard_map.89 = (f32[32,128]{1,0:T(8,128)S(1)}, bf16[128,4096]{1,0:T(8,128)(2,1)S(1)}, bf16[512,1024]{1,0:T(8,128)(2,1)S(1)}) custom-call(s32[1]{0:T(128)} %bitcast.refs_1_.refs_0_, bf16[4,1024,128]{2,1,0:T(8,128)(2,1)S(1)} %bitcast.19, bf16[1024,128]{1,0:T(8,128)(2,1)S(1)} %collective-permute-done.21.refs_2_, ...), custom_call_target="tpu_custom_call" | custom-call | flops 6670000128 | bytes 1048576 | tf_op jit(solution)/shard_map/pallas_call | solution.py:352
  110.9 2.2 %collective-permute-start.31 = (bf16[512,128]{1,0:T(8,128)(2,1)S(1)}, bf16[512,128]{1,0:T(8,128)(2,1)S(1)}, u32[]{:S(2)}, u32[]{:S(2)}) collective-permute-start(bf16[512,128]{1,0:T(8,128)(2,1)S(1)} %get-tuple-element.88), channel_id=1, source_target_pairs={{0,12},{4,8},{8,4},{12,0},{16,28},{20,24},{24,20},{28,16},{1,13},{... | collective-permute-start | bytes 393224 | tf_op jit(solution)/shard_map/ppermute | solution.py:18
  113.1 2.6 %collective-permute-done.27.refs_4_ = bf16[512,128]{1,0:T(8,128)(2,1)S(1)} collective-permute-done((bf16[512,128]{1,0:T(8,128)(2,1)S(1)}, bf16[512,128]{1,0:T(8,128)(2,1)S(1)}, u32[]{:S(2)}, u32[]{:S(2)}) %collective-permute-start.27) | collective-permute-done | bytes 131104 | tf_op jit(solution)/shard_map/ppermute | solution.py:18
  115.7 2.3 %collective-permute-done.30.refs_7_ = bf16[512,128]{1,0:T(8,128)(2,1)S(1)} collective-permute-done((bf16[512,128]{1,0:T(8,128)(2,1)S(1)}, bf16[512,128]{1,0:T(8,128)(2,1)S(1)}, u32[]{:S(2)}, u32[]{:S(2)}) %collective-permute-start.30) | collective-permute-done | bytes 131104 | tf_op jit(solution)/shard_map/ppermute | solution.py:18
  118.0 3.9 %collective-permute-done.31.refs_8_ = bf16[512,128]{1,0:T(8,128)(2,1)S(1)} collective-permute-done((bf16[512,128]{1,0:T(8,128)(2,1)S(1)}, bf16[512,128]{1,0:T(8,128)(2,1)S(1)}, u32[]{:S(2)}, u32[]{:S(2)}) %collective-permute-start.31) | collective-permute-done | bytes 131104 | tf_op jit(solution)/shard_map/ppermute | solution.py:18
  124.1 2.3 %collective-permute-done.39.refs_2_ = bf16[2,1056,256]{2,1,0:T(8,128)(2,1)S(1)} collective-permute-done((bf16[2,1056,256]{2,1,0:T(8,128)(2,1)S(1)}, bf16[2,1056,256]{2,1,0:T(8,128)(2,1)S(1)}, u32[]{:S(2)}, u32[]{:S(2)}) %collective-permute-start.39) | collective-permute-done | bytes 1081376 | tf_op jit(solution)/shard_map/ppermute | solution.py:18
  128.6 2.1 %shard_map.92 = (bf16[128,512]{1,0:T(8,128)(2,1)S(1)}, bf16[128,512]{1,0:T(8,128)(2,1)S(1)}, bf16[128,512]{1,0:T(8,128)(2,1)S(1)}, bf16[128,512]{1,0:T(8,128)(2,...) custom-call(s32[1]{0:T(128)} %bitcast.2.refs_0_, ...), custom_call_target="tpu_custom_call" | custom-call | flops 2529999872 | bytes 1048576 | tf_op jit(solution)/shard_map/pallas_call | solution.py:352
  131.9 2.3 %collective-permute-start.33 = (bf16[128,512]{1,0:T(8,128)(2,1)S(1)}, bf16[128,512]{1,0:T(8,128)(2,1)S(1)}, u32[]{:S(2)}, u32[]{:S(2)}) collective-permute-start(bf16[128,512]{1,0:T(8,128)(2,1)S(1)} %get-tuple-element.92), channel_id=1, source_target_pairs={{0,16},{4,20},{8,24},{12,28},{16,0},{20,4},{24,8},{28,12},{1,17},{... | collective-permute-start | bytes 393224 | tf_op jit(solution)/shard_map/ppermute | solution.py:18
  135.1 3.0 %collective-permute-done.32.refs_3_ = bf16[128,512]{1,0:T(8,128)(2,1)S(1)} collective-permute-done((bf16[128,512]{1,0:T(8,128)(2,1)S(1)}, bf16[128,512]{1,0:T(8,128)(2,1)S(1)}, u32[]{:S(2)}, u32[]{:S(2)}) %collective-permute-start.32) | collective-permute-done | bytes 131104 | tf_op jit(solution)/shard_map/ppermute | solution.py:18
  145.7 4.4 %collective-permute-done.33.refs_3_ = bf16[128,512]{1,0:T(8,128)(2,1)S(1)} collective-permute-done((bf16[128,512]{1,0:T(8,128)(2,1)S(1)}, bf16[128,512]{1,0:T(8,128)(2,1)S(1)}, u32[]{:S(2)}, u32[]{:S(2)}) %collective-permute-start.33) | collective-permute-done | bytes 131104 | tf_op jit(solution)/shard_map/ppermute | solution.py:18
  153.2 3.4 %collective-permute-start.38 = (bf16[128,512]{1,0:T(8,128)(2,1)S(1)}, bf16[128,512]{1,0:T(8,128)(2,1)S(1)}, u32[]{:S(2)}, u32[]{:S(2)}) collective-permute-start(bf16[128,512]{1,0:T(8,128)(2,1)S(1)} %get-tuple-element.97), channel_id=1, source_target_pairs={{0,12},{4,8},{8,4},{12,0},{16,28},{20,24},{24,20},{28,16},{1,13},{... | collective-permute-start | bytes 393224 | tf_op jit(solution)/shard_map/ppermute | solution.py:18
  159.7 2.2 %collective-permute-start.44 = (bf16[128,256]{1,0:T(8,128)(2,1)S(1)}, bf16[128,256]{1,0:T(8,128)(2,1)S(1)}, u32[]{:S(2)}, u32[]{:S(2)}) collective-permute-start(bf16[128,256]{1,0:T(8,128)(2,1)S(1)} %get-tuple-element.112), channel_id=1, source_target_pairs={{0,8},{4,12},{8,0},{12,4},{16,24},{20,28},{24,16},{28,20},{1,9},{5... | collective-permute-start | bytes 196616 | tf_op jit(solution)/shard_map/ppermute | solution.py:18
  (140 shorter events, 67.7 us)
Async XLA Ops:
  1.6 8.2 %collective-permute-start.2 = (bf16[128,256]{1,0:T(8,128)(2,1)S(1)}, bf16[128,256]{1,0:T(8,128)(2,1)S(1)}, u32[]{:S(2)}, u32[]{:S(2)}) collective-permute-start(bf16[128,256]{1,0:T(8,128)(2,1)S(1)} %constant_dynamic-slice_fusion.8.refs_0_), channel_id=1, source_target_pairs={{0,24},{4,28},{8,16},{12,20},{16,8},{20,12},{24,0},{28,4},{1,25},{... | collective-permute-start | bytes 196616 | tf_op jit(solution)/shard_map/ppermute | solution.py:18
  12.3 8.3 %collective-permute-start.4 = (bf16[4,128,256]{2,1,0:T(8,128)(2,1)S(1)}, bf16[4,128,256]{2,1,0:T(8,128)(2,1)S(1)}, u32[]{:S(2)}, u32[]{:S(2)}) collective-permute-start(bf16[4,128,256]{2,1,0:T(8,128)(2,1)S(1)} %shard_map.75.refs_0_), channel_id=1, source_target_pairs={{0,4},{4,0},{8,12},{12,8},{16,20},{20,16},{24,28},{28,24},{1,5},{5... | collective-permute-start | bytes 786440 | tf_op jit(solution)/shard_map/ppermute | solution.py:18
  13.9 12.3 %collective-permute-start.7 = (bf16[128,512]{1,0:T(8,128)(2,1)S(1)}, bf16[128,512]{1,0:T(8,128)(2,1)S(1)}, u32[]{:S(2)}, u32[]{:S(2)}) collective-permute-start(bf16[128,512]{1,0:T(8,128)(2,1)S(1)} %get-tuple-element.122.refs_5_), channel_id=1, source_target_pairs={{0,20},{4,16},{8,28},{12,24},{16,4},{20,0},{24,12},{28,8},{1,21},{... | collective-permute-start | bytes 393224 | tf_op jit(solution)/shard_map/ppermute | solution.py:18
  15.5 12.2 %collective-permute-start.6 = (bf16[128,512]{1,0:T(8,128)(2,1)S(1)}, bf16[128,512]{1,0:T(8,128)(2,1)S(1)}, u32[]{:S(2)}, u32[]{:S(2)}) collective-permute-start(bf16[128,512]{1,0:T(8,128)(2,1)S(1)} %get-tuple-element.123.refs_4_), channel_id=1, source_target_pairs={{0,16},{4,20},{8,24},{12,28},{16,0},{20,4},{24,8},{28,12},{1,17},{... | collective-permute-start | bytes 393224 | tf_op jit(solution)/shard_map/ppermute | solution.py:18
  16.8 17.9 %collective-permute-start.3 = (bf16[4,128,256]{2,1,0:T(8,128)(2,1)S(1)}, bf16[4,128,256]{2,1,0:T(8,128)(2,1)S(1)}, u32[]{:S(2)}, u32[]{:S(2)}) collective-permute-start(bf16[4,128,256]{2,1,0:T(8,128)(2,1)S(1)} %shard_map.75.refs_0_), channel_id=1, source_target_pairs={{0,2},{1,3},{2,0},{3,1},{4,6},{5,7},{6,4},{7,5},{8,10},{9,11},{10,... | collective-permute-start | bytes 786440 | tf_op jit(solution)/shard_map/ppermute | solution.py:18
  20.7 14.0 %collective-permute-start.5 = (bf16[4,128,256]{2,1,0:T(8,128)(2,1)S(1)}, bf16[4,128,256]{2,1,0:T(8,128)(2,1)S(1)}, u32[]{:S(2)}, u32[]{:S(2)}) collective-permute-start(bf16[4,128,256]{2,1,0:T(8,128)(2,1)S(1)} %collective-permute-done.4.refs_2_), channel_id=1, source_target_pairs={{0,2},{1,3},{2,0},{3,1},{4,6},{5,7},{6,4},{7,5},{8,10},{9,11},{10,... | collective-permute-start | bytes 786440 | tf_op jit(solution)/shard_map/ppermute | solution.py:18
  22.4 8.0 %collective-permute-start.10 = (bf16[128,512]{1,0:T(8,128)(2,1)}, bf16[128,512]{1,0:T(8,128)(2,1)S(1)}, u32[]{:S(2)}, u32[]{:S(2)}) collective-permute-start(bf16[128,512]{1,0:T(8,128)(2,1)} %get-tuple-element.117), channel_id=1, source_target_pairs={{0,8},{4,12},{8,0},{12,4},{16,24},{20,28},{24,16},{28,20},{1,9},{5... | collective-permute-start | bytes 393224 | tf_op jit(solution)/shard_map/ppermute | solution.py:18
  34.8 9.9 %collective-permute-start.11 = (bf16[2,1024,256]{2,1,0:T(8,128)(2,1)S(1)}, bf16[2,1024,256]{2,1,0:T(8,128)(2,1)S(1)}, u32[]{:S(2)}, u32[]{:S(2)}) collective-permute-start(bf16[2,1024,256]{2,1,0:T(8,128)(2,1)S(1)} %shard_map.78.refs_0_.refs_2_), channel_id=1, source_target_pairs={{0,1},{1,0},{2,3},{3,2},{4,5},{5,4},{6,7},{7,6},{8,9},{9,8},{10,11... | collective-permute-start | bytes 3145736 | tf_op jit(solution)/shard_map/ppermute | solution.py:18
  35.5 8.9 %collective-permute-start.12 = (bf16[128,512]{1,0:T(8,128)(2,1)S(1)}, bf16[128,512]{1,0:T(8,128)(2,1)S(1)}, u32[]{:S(2)}, u32[]{:S(2)}) collective-permute-start(bf16[128,512]{1,0:T(8,128)(2,1)S(1)} %get-tuple-element.120.refs_7_), channel_id=1, source_target_pairs={{0,28},{4,24},{8,20},{12,16},{16,12},{20,8},{24,4},{28,0},{1,29},{... | collective-permute-start | bytes 393224 | tf_op jit(solution)/shard_map/ppermute | solution.py:18
  48.9 8.1 %collective-permute-start.15 = (bf16[512,128]{1,0:T(8,128)(2,1)S(1)}, bf16[512,128]{1,0:T(8,128)(2,1)S(1)}, u32[]{:S(2)}, u32[]{:S(2)}) collective-permute-start(bf16[512,128]{1,0:T(8,128)(2,1)S(1)} %get-tuple-element.62), channel_id=1, source_target_pairs={{0,8},{4,12},{8,0},{12,4},{16,24},{20,28},{24,16},{28,20},{1,9},{5... | collective-permute-start | bytes 393224 | tf_op jit(solution)/shard_map/ppermute | solution.py:18
  50.6 11.0 %collective-permute-start.16 = (bf16[512,128]{1,0:T(8,128)(2,1)}, bf16[512,128]{1,0:T(8,128)(2,1)}, u32[]{:S(2)}, u32[]{:S(2)}) collective-permute-start(bf16[512,128]{1,0:T(8,128)(2,1)} %get-tuple-element.63), channel_id=1, source_target_pairs={{0,12},{4,8},{8,4},{12,0},{16,28},{20,24},{24,20},{28,16},{1,13},{... | collective-permute-start | bytes 393224 | tf_op jit(solution)/shard_map/ppermute | solution.py:18
  51.4 18.4 %collective-permute-start.17 = (bf16[512,128]{1,0:T(8,128)(2,1)}, bf16[512,128]{1,0:T(8,128)(2,1)}, u32[]{:S(2)}, u32[]{:S(2)}) collective-permute-start(bf16[512,128]{1,0:T(8,128)(2,1)} %get-tuple-element.64), channel_id=1, source_target_pairs={{0,16},{4,20},{8,24},{12,28},{16,0},{20,4},{24,8},{28,12},{1,17},{... | collective-permute-start | bytes 393224 | tf_op jit(solution)/shard_map/ppermute | solution.py:18
  53.7 19.5 %collective-permute-start.18 = (bf16[512,128]{1,0:T(8,128)(2,1)}, bf16[512,128]{1,0:T(8,128)(2,1)}, u32[]{:S(2)}, u32[]{:S(2)}) collective-permute-start(bf16[512,128]{1,0:T(8,128)(2,1)} %get-tuple-element.65), channel_id=1, source_target_pairs={{0,20},{4,16},{8,28},{12,24},{16,4},{20,0},{24,12},{28,8},{1,21},{... | collective-permute-start | bytes 393224 | tf_op jit(solution)/shard_map/ppermute | solution.py:18
  55.4 17.8 %collective-permute-start.19 = (bf16[512,128]{1,0:T(8,128)(2,1)}, bf16[512,128]{1,0:T(8,128)(2,1)}, u32[]{:S(2)}, u32[]{:S(2)}) collective-permute-start(bf16[512,128]{1,0:T(8,128)(2,1)} %get-tuple-element.66), channel_id=1, source_target_pairs={{0,24},{4,28},{8,16},{12,20},{16,8},{20,12},{24,0},{28,4},{1,25},{... | collective-permute-start | bytes 393224 | tf_op jit(solution)/shard_map/ppermute | solution.py:18
  57.0 16.2 %collective-permute-start.20 = (bf16[512,128]{1,0:T(8,128)(2,1)}, bf16[512,128]{1,0:T(8,128)(2,1)}, u32[]{:S(2)}, u32[]{:S(2)}) collective-permute-start(bf16[512,128]{1,0:T(8,128)(2,1)} %get-tuple-element.67), channel_id=1, source_target_pairs={{0,28},{4,24},{8,20},{12,16},{16,12},{20,8},{24,4},{28,0},{1,29},{... | collective-permute-start | bytes 393224 | tf_op jit(solution)/shard_map/ppermute | solution.py:18
  81.0 8.0 %collective-permute-start.23 = (bf16[1024,128]{1,0:T(8,128)(2,1)S(1)}, bf16[1024,128]{1,0:T(8,128)(2,1)S(1)}, u32[]{:S(2)}, u32[]{:S(2)}) collective-permute-start(bf16[1024,128]{1,0:T(8,128)(2,1)S(1)} %get-tuple-element.75), channel_id=1, source_target_pairs={{0,1},{1,0},{2,3},{3,2},{4,5},{5,4},{6,7},{7,6},{8,9},{9,8},{10,11... | collective-permute-start | bytes 786440 | tf_op jit(solution)/shard_map/ppermute | solution.py:181
  91.5 10.8 %collective-permute-start.25 = (bf16[512,128]{1,0:T(8,128)(2,1)S(1)}, bf16[512,128]{1,0:T(8,128)(2,1)S(1)}, u32[]{:S(2)}, u32[]{:S(2)}) collective-permute-start(bf16[512,128]{1,0:T(8,128)(2,1)S(1)} %get-tuple-element.78), channel_id=1, source_target_pairs={{0,4},{4,0},{8,12},{12,8},{16,20},{20,16},{24,28},{28,24},{1,5},{5... | collective-permute-start | bytes 393224 | tf_op jit(solution)/shard_map/ppermute | solution.py:18
  92.3 18.6 %collective-permute-start.26 = (bf16[512,128]{1,0:T(8,128)(2,1)S(1)}, bf16[512,128]{1,0:T(8,128)(2,1)S(1)}, u32[]{:S(2)}, u32[]{:S(2)}) collective-permute-start(bf16[512,128]{1,0:T(8,128)(2,1)S(1)} %get-tuple-element.82), channel_id=1, source_target_pairs={{0,16},{4,20},{8,24},{12,28},{16,0},{20,4},{24,8},{28,12},{1,17},{... | collective-permute-start | bytes 393224 | tf_op jit(solution)/shard_map/ppermute | solution.py:18
  97.5 18.2 %collective-permute-start.27 = (bf16[512,128]{1,0:T(8,128)(2,1)S(1)}, bf16[512,128]{1,0:T(8,128)(2,1)S(1)}, u32[]{:S(2)}, u32[]{:S(2)}) collective-permute-start(bf16[512,128]{1,0:T(8,128)(2,1)S(1)} %get-tuple-element.83), channel_id=1, source_target_pairs={{0,20},{4,16},{8,28},{12,24},{16,4},{20,0},{24,12},{28,8},{1,21},{... | collective-permute-start | bytes 393224 | tf_op jit(solution)/shard_map/ppermute | solution.py:18
  98.1 17.6 %collective-permute-start.28 = (bf16[512,128]{1,0:T(8,128)(2,1)S(1)}, bf16[512,128]{1,0:T(8,128)(2,1)S(1)}, u32[]{:S(2)}, u32[]{:S(2)}) collective-permute-start(bf16[512,128]{1,0:T(8,128)(2,1)S(1)} %get-tuple-element.84), channel_id=1, source_target_pairs={{0,24},{4,28},{8,16},{12,20},{16,8},{20,12},{24,0},{28,4},{1,25},{... | collective-permute-start | bytes 393224 | tf_op jit(solution)/shard_map/ppermute | solution.py:18
  100.1 15.7 %collective-permute-start.29 = (bf16[512,128]{1,0:T(8,128)(2,1)S(1)}, bf16[512,128]{1,0:T(8,128)(2,1)S(1)}, u32[]{:S(2)}, u32[]{:S(2)}) collective-permute-start(bf16[512,128]{1,0:T(8,128)(2,1)S(1)} %get-tuple-element.85), channel_id=1, source_target_pairs={{0,28},{4,24},{8,20},{12,16},{16,12},{20,8},{24,4},{28,0},{1,29},{... | collective-permute-start | bytes 393224 | tf_op jit(solution)/shard_map/ppermute | solution.py:18
  110.9 10.9 %collective-permute-start.31 = (bf16[512,128]{1,0:T(8,128)(2,1)S(1)}, bf16[512,128]{1,0:T(8,128)(2,1)S(1)}, u32[]{:S(2)}, u32[]{:S(2)}) collective-permute-start(bf16[512,128]{1,0:T(8,128)(2,1)S(1)} %get-tuple-element.88), channel_id=1, source_target_pairs={{0,12},{4,8},{8,4},{12,0},{16,28},{20,24},{24,20},{28,16},{1,13},{... | collective-permute-start | bytes 393224 | tf_op jit(solution)/shard_map/ppermute | solution.py:18
  126.7 13.3 %collective-permute-start.41 = (bf16[2,4,128,128]{3,2,1,0:T(8,128)(2,1)S(1)}, bf16[2,4,128,128]{3,2,1,0:T(8,128)(2,1)S(1)}, u32[]{:S(2)}, u32[]{:S(2)}) collective-permute-start(bf16[2,4,128,128]{3,2,1,0:T(8,128)(2,1)S(1)} %get-tuple-element.105), channel_id=1, source_target_pairs={{0,4},{4,0},{8,12},{12,8},{16,20},{20,16},{24,28},{28,24},{1,5},{5... | collective-permute-start | bytes 786440 | tf_op jit(solution)/shard_map/ppermute | solution.py:18
  127.3 14.7 %collective-permute-start.40 = (bf16[1088,128]{1,0:T(8,128)(2,1)S(1)}, bf16[1088,128]{1,0:T(8,128)(2,1)S(1)}, u32[]{:S(2)}, u32[]{:S(2)}) collective-permute-start(bf16[1088,128]{1,0:T(8,128)(2,1)S(1)} %get-tuple-element.102), channel_id=1, source_target_pairs={{0,2},{1,3},{2,0},{3,1},{4,6},{5,7},{6,4},{7,5},{8,10},{9,11},{10,... | collective-permute-start | bytes 835592 | tf_op jit(solution)/shard_map/ppermute | solution.py:18
  131.9 18.3 %collective-permute-start.33 = (bf16[128,512]{1,0:T(8,128)(2,1)S(1)}, bf16[128,512]{1,0:T(8,128)(2,1)S(1)}, u32[]{:S(2)}, u32[]{:S(2)}) collective-permute-start(bf16[128,512]{1,0:T(8,128)(2,1)S(1)} %get-tuple-element.92), channel_id=1, source_target_pairs={{0,16},{4,20},{8,24},{12,28},{16,0},{20,4},{24,8},{28,12},{1,17},{... | collective-permute-start | bytes 393224 | tf_op jit(solution)/shard_map/ppermute | solution.py:18
  134.2 19.0 %collective-permute-start.34 = (bf16[128,512]{1,0:T(8,128)(2,1)}, bf16[128,512]{1,0:T(8,128)(2,1)}, u32[]{:S(2)}, u32[]{:S(2)}) collective-permute-start(bf16[128,512]{1,0:T(8,128)(2,1)} %get-tuple-element.93), channel_id=1, source_target_pairs={{0,20},{4,16},{8,28},{12,24},{16,4},{20,0},{24,12},{28,8},{1,21},{... | collective-permute-start | bytes 393224 | tf_op jit(solution)/shard_map/ppermute | solution.py:18
  138.1 15.0 %collective-permute-start.35 = (bf16[128,512]{1,0:T(8,128)(2,1)}, bf16[128,512]{1,0:T(8,128)(2,1)}, u32[]{:S(2)}, u32[]{:S(2)}) collective-permute-start(bf16[128,512]{1,0:T(8,128)(2,1)} %get-tuple-element.94), channel_id=1, source_target_pairs={{0,24},{4,28},{8,16},{12,20},{16,8},{20,12},{24,0},{28,4},{1,25},{... | collective-permute-start | bytes 393224 | tf_op jit(solution)/shard_map/ppermute | solution.py:18
  140.0 16.5 %collective-permute-start.36 = (bf16[128,512]{1,0:T(8,128)(2,1)}, bf16[128,512]{1,0:T(8,128)(2,1)}, u32[]{:S(2)}, u32[]{:S(2)}) collective-permute-start(bf16[128,512]{1,0:T(8,128)(2,1)} %get-tuple-element.95), channel_id=1, source_target_pairs={{0,28},{4,24},{8,20},{12,16},{16,12},{20,8},{24,4},{28,0},{1,29},{... | collective-permute-start | bytes 393224 | tf_op jit(solution)/shard_map/ppermute | solution.py:18
  144.3 14.4 %collective-permute-start.42 = (bf16[4,128,128]{2,1,0:T(8,128)(2,1)}, bf16[4,128,128]{2,1,0:T(8,128)(2,1)}, u32[]{:S(2)}, u32[]{:S(2)}) collective-permute-start(bf16[4,128,128]{2,1,0:T(8,128)(2,1)} %get-tuple-element.108), channel_id=1, source_target_pairs={{0,4},{4,0},{8,12},{12,8},{16,20},{20,16},{24,28},{28,24},{1,5},{5... | collective-permute-start | bytes 393224 | tf_op jit(solution)/shard_map/ppermute | solution.py:18
  150.8 7.8 %collective-permute-start.43 = (bf16[4,128,128]{2,1,0:T(8,128)(2,1)}, bf16[4,128,128]{2,1,0:T(8,128)(2,1)}, u32[]{:S(2)}, u32[]{:S(2)}) collective-permute-start(bf16[4,128,128]{2,1,0:T(8,128)(2,1)} %get-tuple-element.110), channel_id=1, source_target_pairs={{0,2},{1,3},{2,0},{3,1},{4,6},{5,7},{6,4},{7,5},{8,10},{9,11},{10,... | collective-permute-start | bytes 393224 | tf_op jit(solution)/shard_map/ppermute | solution.py:18
  153.2 11.8 %collective-permute-start.37 = (bf16[128,512]{1,0:T(8,128)(2,1)}, bf16[128,512]{1,0:T(8,128)(2,1)S(1)}, u32[]{:S(2)}, u32[]{:S(2)}) collective-permute-start(bf16[128,512]{1,0:T(8,128)(2,1)} %copy-done.11), channel_id=1, source_target_pairs={{0,8},{4,12},{8,0},{12,4},{16,24},{20,28},{24,16},{28,20},{1,9},{5... | collective-permute-start | bytes 393224 | tf_op jit(solution)/shard_map/ppermute | solution.py:18
  153.2 11.8 %collective-permute-start.38 = (bf16[128,512]{1,0:T(8,128)(2,1)S(1)}, bf16[128,512]{1,0:T(8,128)(2,1)S(1)}, u32[]{:S(2)}, u32[]{:S(2)}) collective-permute-start(bf16[128,512]{1,0:T(8,128)(2,1)S(1)} %get-tuple-element.97), channel_id=1, source_target_pairs={{0,12},{4,8},{8,4},{12,0},{16,28},{20,24},{24,20},{28,16},{1,13},{... | collective-permute-start | bytes 393224 | tf_op jit(solution)/shard_map/ppermute | solution.py:18
  (38 other events, 153.9 us)

commit v11 on v10

--- a/solution.py
+++ b/solution.py
@@ -555,7 +555,7 @@
             refs[-1][:, lane] = (up[:, lane].astype(F32) + piece[...].astype(F32)).astype(BF)
 
     shape = jax.ShapeDtypeStruct(up.shape, BF)
-    return in_place(kernel, shape, (me, up), base, pieces, 0.25 * len(pieces))
+    return in_place(kernel, shape, (me, up), base, pieces, 0.1)
 
 
 def body(volume, mixing, kernel_taps, upstream):

time: 170 us -> 169 us (level)
    unnamed x48 -> x46, local copies, waits for them, and re-layouts: 10.7 us -> 9.18 us
  transfers between devices with their start and end apart: 47 -> 47, of which waited for: 20 -> 20; matrix products, arithmetic and copies ran while one was open for 4% -> 4% of each run, Pallas kernels for 12% -> 13%
where the time goes in v11:
time: 169 us; the launch traced here: 168 us
  starting transfers between devices  73.2 us (43%)
  waiting for transfers between devices  47.7 us (28%)
  Pallas kernels  31.8 us (19%)
  local copies, waits for them, and re-layouts  13.8 us (8%)
    ppermute x43, starting transfers between devices, swap(): return lax.ppermute(block, axis, [(i, i ^ step) for i in range(size)])  66.7 us
    ppermute x43, waiting for transfers between devices, swap(): return lax.ppermute(block, axis, [(i, i ^ step) for i in range(size)])  47.7 us
    pallas_call x24, Pallas kernels, call(): pl.pallas_call(wrapped, out_shape=out_shape, in_specs=specs + [pl.BlockSp...  31.8 us
    unnamed x46, local copies, waits for them, and re-layouts  9.18 us
    ppermute x2, starting transfers between devices, halo(): return (lax.ppermute(near, 'space', inner), far)  4.9 us
  transfers between devices with their start and end apart: 47, of which 20 were waited for; matrix products, arithmetic and copies ran while one was open for 4% of the time, Pallas kernels for 13%

profile of v11, /device:TPU:0, one launch (start us, length us, event | category | flops | bytes accessed | tf_op | source)
XLA Modules:
  0.0 168.2 jit_solution(17357396512824446931)
XLA Ops:
  1.6 5.1 %collective-permute-start.2 = (bf16[128,256]{1,0:T(8,128)(2,1)S(1)}, bf16[128,256]{1,0:T(8,128)(2,1)S(1)}, u32[]{:S(2)}, u32[]{:S(2)}) collective-permute-start(bf16[128,256]{1,0:T(8,128)(2,1)S(1)} %constant_dynamic-slice_fusion.8.refs_0_), channel_id=1, source_target_pairs={{0,24},{4,28},{8,16},{12,20},{16,8},{20,12},{24,0},{28,4},{1,25},{... | collective-permute-start | bytes 196616 | tf_op jit(solution)/shard_map/ppermute | solution.py:18
  9.8 2.5 %collective-permute-done.1.refs_2_ = bf16[128,256]{1,0:T(8,128)(2,1)S(1)} collective-permute-done((bf16[128,256]{1,0:T(8,128)(2,1)S(1)}, bf16[128,256]{1,0:T(8,128)(2,1)S(1)}, u32[]{:S(2)}, u32[]{:S(2)}) %collective-permute-start.1) | collective-permute-done | bytes 65568 | tf_op jit(solution)/shard_map/ppermute | solution.py:18
  18.3 2.3 %collective-permute-done.4.refs_2_ = bf16[4,128,256]{2,1,0:T(8,128)(2,1)S(1)} collective-permute-done((bf16[4,128,256]{2,1,0:T(8,128)(2,1)S(1)}, bf16[4,128,256]{2,1,0:T(8,128)(2,1)S(1)}, u32[]{:S(2)}, u32[]{:S(2)}) %collective-permute-start.4) | collective-permute-done | bytes 262176 | tf_op jit(solution)/shard_map/ppermute | solution.py:18
  22.4 2.4 %collective-permute-start.10 = (bf16[128,512]{1,0:T(8,128)(2,1)}, bf16[128,512]{1,0:T(8,128)(2,1)S(1)}, u32[]{:S(2)}, u32[]{:S(2)}) collective-permute-start(bf16[128,512]{1,0:T(8,128)(2,1)} %get-tuple-element.117), channel_id=1, source_target_pairs={{0,8},{4,12},{8,0},{12,4},{16,24},{20,28},{24,16},{28,20},{1,9},{5... | collective-permute-start | bytes 393224 | tf_op jit(solution)/shard_map/ppermute | solution.py:18
  31.2 3.3 %collective-permute-done.8.refs_2_ = bf16[128,512]{1,0:T(8,128)(2,1)S(1)} collective-permute-done((bf16[128,512]{1,0:T(8,128)(2,1)S(1)}, bf16[128,512]{1,0:T(8,128)(2,1)S(1)}, u32[]{:S(2)}, u32[]{:S(2)}) %collective-permute-start.8) | collective-permute-done | bytes 131104 | tf_op jit(solution)/shard_map/ppermute | solution.py:18
  35.5 2.6 %collective-permute-start.12 = (bf16[128,512]{1,0:T(8,128)(2,1)S(1)}, bf16[128,512]{1,0:T(8,128)(2,1)S(1)}, u32[]{:S(2)}, u32[]{:S(2)}) collective-permute-start(bf16[128,512]{1,0:T(8,128)(2,1)S(1)} %get-tuple-element.120.refs_7_), channel_id=1, source_target_pairs={{0,28},{4,24},{8,20},{12,16},{16,12},{20,8},{24,4},{28,0},{1,29},{... | collective-permute-start | bytes 393224 | tf_op jit(solution)/shard_map/ppermute | solution.py:18
  38.5 2.3 %shard_map.80.refs_3_.refs_2_.refs_5_ = bf16[4096,128]{1,0:T(8,128)(2,1)S(1)} custom-call(bf16[128,4096]{1,0:T(8,128)(2,1)S(1)} %bitcast.11), custom_call_target="tpu_custom_call" | custom-call | flops 1380000000 | bytes 1048576 | tf_op jit(solution)/shard_map/pallas_call | solution.py:352
  44.6 2.1 %shard_map.81 = (bf16[512,128]{1,0:T(8,128)(2,1)S(1)}, bf16[512,128]{1,0:T(8,128)(2,1)S(1)}, bf16[512,128]{1,0:T(8,128)(2,1)S(1)}, bf16[512,128]{1,0:T(8,128)(2,...) custom-call(bf16[2,1024,256]{2,1,0:T(8,128)(2,1)S(1)} %shard_map.78., ...), custom_call_target="tpu_custom_call" | custom-call | flops 2990000128 | bytes 1048576 | tf_op jit(solution)/shard_map/pallas_call | solution.py:352
  51.4 2.3 %collective-permute-start.17 = (bf16[512,128]{1,0:T(8,128)(2,1)}, bf16[512,128]{1,0:T(8,128)(2,1)}, u32[]{:S(2)}, u32[]{:S(2)}) collective-permute-start(bf16[512,128]{1,0:T(8,128)(2,1)} %get-tuple-element.64), channel_id=1, source_target_pairs={{0,16},{4,20},{8,24},{12,28},{16,0},{20,4},{24,8},{28,12},{1,17},{... | collective-permute-start | bytes 393224 | tf_op jit(solution)/shard_map/ppermute | solution.py:18
  57.0 2.8 %collective-permute-start.20 = (bf16[512,128]{1,0:T(8,128)(2,1)}, bf16[512,128]{1,0:T(8,128)(2,1)}, u32[]{:S(2)}, u32[]{:S(2)}) collective-permute-start(bf16[512,128]{1,0:T(8,128)(2,1)} %get-tuple-element.67), channel_id=1, source_target_pairs={{0,28},{4,24},{8,20},{12,16},{16,12},{20,8},{24,4},{28,0},{1,29},{... | collective-permute-start | bytes 393224 | tf_op jit(solution)/shard_map/ppermute | solution.py:18
  62.6 7.2 %collective-permute-done.17.refs_3_ = bf16[512,128]{1,0:T(8,128)(2,1)} collective-permute-done((bf16[512,128]{1,0:T(8,128)(2,1)}, bf16[512,128]{1,0:T(8,128)(2,1)}, u32[]{:S(2)}, u32[]{:S(2)}) %collective-permute-start.17) | collective-permute-done | bytes 131104 | tf_op jit(solution)/shard_map/ppermute | solution.py:18
  69.8 3.5 %collective-permute-done.18.refs_4_ = bf16[512,128]{1,0:T(8,128)(2,1)} collective-permute-done((bf16[512,128]{1,0:T(8,128)(2,1)}, bf16[512,128]{1,0:T(8,128)(2,1)}, u32[]{:S(2)}, u32[]{:S(2)}) %collective-permute-start.18) | collective-permute-done | bytes 131104 | tf_op jit(solution)/shard_map/ppermute | solution.py:18
  75.4 2.7 %shard_map.85 = (bf16[2,1024,128]{2,1,0:T(8,128)(2,1)S(1)}, f32[2,1024,128]{2,1,0:T(8,128)S(1)}) custom-call(bf16[4,1024,128]{2,1,0:T(8,128)(2,1)S(1)} %bitcast.17, f32[27,128]{1,0:T(8,128)S(1)} %bitcast.20, bf16[4096,128]{1,0:T(8,128)(2,1)S(1)} %copy-done.19), custom_call_target="tpu_custom_call" | custom-call | flops 3680000000 | bytes 1048576 | tf_op jit(solution)/shard_map/pallas_call | solution.py:352
  78.1 2.9 %shard_map.86 = (bf16[2,1024,128]{2,1,0:T(8,128)(2,1)S(1)}, f32[2,1024,128]{2,1,0:T(8,128)S(1)}, bf16[1024,128]{1,0:T(8,128)(2,1)S(1)}, bf16[1024,128]{1,0:T(8,128)(2,1)S(1)}) custom-call(s32[1]{0:T(128)} %bitcast.refs_1_.refs_0_, bf16[4,1024,128]{2,1,0:T(8,128)(2,1)S(1)} %bitcast.18, bf16[1024,128]{1,0:T(8,128)(2,1)S(1)} %collective-permute-done.21.refs_2_, ...), custom_call_target="tpu_custom_call" | custom-call | flops 3680000000 | bytes 1048576 | tf_op jit(solution)/shard_map/pallas_call | solution.py:352
  81.0 4.8 %collective-permute-start.23 = (bf16[1024,128]{1,0:T(8,128)(2,1)S(1)}, bf16[1024,128]{1,0:T(8,128)(2,1)S(1)}, u32[]{:S(2)}, u32[]{:S(2)}) collective-permute-start(bf16[1024,128]{1,0:T(8,128)(2,1)S(1)} %get-tuple-element.75), channel_id=1, source_target_pairs={{0,1},{1,0},{2,3},{3,2},{4,5},{5,4},{6,7},{7,6},{8,9},{9,8},{10,11... | collective-permute-start | bytes 786440 | tf_op jit(solution)/shard_map/ppermute | solution.py:181
  86.7 2.3 %shard_map.87.refs_7_ = bf16[2,1024,128]{2,1,0:T(8,128)(2,1)S(1)} custom-call(bf16[2,1024,128]{2,1,0:T(8,128)(2,1)S(1)} %get-tuple-element.72.refs_0_.refs_2_.refs_4_, bf16[2,1024,128]{2,1,0:T(8,128)(2,1)S(1)} %get-tuple-element.71.refs_6_.refs_1_.refs_3_.refs_5_, f32[27,128]{1,0:T(8,128)S(1)} %bitcast.22), custom_call_target="tpu_custom_call" | custom-call | flops 2644999936 | bytes 1048576 | tf_op jit(solution)/shard_map/pallas_call | solution.py:352
  89.0 2.5 %shard_map.88 = (bf16[4096,128]{1,0:T(8,128)(2,1)S(1)}, bf16[512,128]{1,0:T(8,128)(2,1)S(1)}, bf16[512,128]{1,0:T(8,128)(2,1)S(1)}, bf16[512,128]{1,0:T(8,128)(2...) custom-call(s32[1]{0:T(128)} %bitcast.1.refs_0_, ...), custom_call_target="tpu_custom_call" | custom-call | flops 3220000000 | bytes 1048576 | tf_op jit(solution)/shard_map/pallas_call | solution.py:352
  92.4 5.2 %collective-permute-start.26 = (bf16[512,128]{1,0:T(8,128)(2,1)S(1)}, bf16[512,128]{1,0:T(8,128)(2,1)S(1)}, u32[]{:S(2)}, u32[]{:S(2)}) collective-permute-start(bf16[512,128]{1,0:T(8,128)(2,1)S(1)} %get-tuple-element.82), channel_id=1, source_target_pairs={{0,16},{4,20},{8,24},{12,28},{16,0},{20,4},{24,8},{28,12},{1,17},{... | collective-permute-start | bytes 393224 | tf_op jit(solution)/shard_map/ppermute | solution.py:18
  100.1 2.2 %collective-permute-start.29 = (bf16[512,128]{1,0:T(8,128)(2,1)S(1)}, bf16[512,128]{1,0:T(8,128)(2,1)S(1)}, u32[]{:S(2)}, u32[]{:S(2)}) collective-permute-start(bf16[512,128]{1,0:T(8,128)(2,1)S(1)} %get-tuple-element.85), channel_id=1, source_target_pairs={{0,28},{4,24},{8,20},{12,16},{16,12},{20,8},{24,4},{28,0},{1,29},{... | collective-permute-start | bytes 393224 | tf_op jit(solution)/shard_map/ppermute | solution.py:18
  102.3 7.2 %shard_map.89 = (f32[32,128]{1,0:T(8,128)S(1)}, bf16[128,4096]{1,0:T(8,128)(2,1)S(1)}, bf16[512,1024]{1,0:T(8,128)(2,1)S(1)}) custom-call(s32[1]{0:T(128)} %bitcast.refs_1_.refs_0_, bf16[4,1024,128]{2,1,0:T(8,128)(2,1)S(1)} %bitcast.19, bf16[1024,128]{1,0:T(8,128)(2,1)S(1)} %collective-permute-done.21.refs_2_, ...), custom_call_target="tpu_custom_call" | custom-call | flops 6670000128 | bytes 1048576 | tf_op jit(solution)/shard_map/pallas_call | solution.py:352
  110.9 2.2 %collective-permute-start.31 = (bf16[512,128]{1,0:T(8,128)(2,1)S(1)}, bf16[512,128]{1,0:T(8,128)(2,1)S(1)}, u32[]{:S(2)}, u32[]{:S(2)}) collective-permute-start(bf16[512,128]{1,0:T(8,128)(2,1)S(1)} %get-tuple-element.88), channel_id=1, source_target_pairs={{0,12},{4,8},{8,4},{12,0},{16,28},{20,24},{24,20},{28,16},{1,13},{... | collective-permute-start | bytes 393224 | tf_op jit(solution)/shard_map/ppermute | solution.py:18
  113.1 2.6 %collective-permute-done.27.refs_4_ = bf16[512,128]{1,0:T(8,128)(2,1)S(1)} collective-permute-done((bf16[512,128]{1,0:T(8,128)(2,1)S(1)}, bf16[512,128]{1,0:T(8,128)(2,1)S(1)}, u32[]{:S(2)}, u32[]{:S(2)}) %collective-permute-start.27) | collective-permute-done | bytes 131104 | tf_op jit(solution)/shard_map/ppermute | solution.py:18
  115.7 2.3 %collective-permute-done.30.refs_7_ = bf16[512,128]{1,0:T(8,128)(2,1)S(1)} collective-permute-done((bf16[512,128]{1,0:T(8,128)(2,1)S(1)}, bf16[512,128]{1,0:T(8,128)(2,1)S(1)}, u32[]{:S(2)}, u32[]{:S(2)}) %collective-permute-start.30) | collective-permute-done | bytes 131104 | tf_op jit(solution)/shard_map/ppermute | solution.py:18
  118.0 3.9 %collective-permute-done.31.refs_8_ = bf16[512,128]{1,0:T(8,128)(2,1)S(1)} collective-permute-done((bf16[512,128]{1,0:T(8,128)(2,1)S(1)}, bf16[512,128]{1,0:T(8,128)(2,1)S(1)}, u32[]{:S(2)}, u32[]{:S(2)}) %collective-permute-start.31) | collective-permute-done | bytes 131104 | tf_op jit(solution)/shard_map/ppermute | solution.py:18
  124.1 2.3 %collective-permute-done.39.refs_2_ = bf16[2,1056,256]{2,1,0:T(8,128)(2,1)S(1)} collective-permute-done((bf16[2,1056,256]{2,1,0:T(8,128)(2,1)S(1)}, bf16[2,1056,256]{2,1,0:T(8,128)(2,1)S(1)}, u32[]{:S(2)}, u32[]{:S(2)}) %collective-permute-start.39) | collective-permute-done | bytes 1081376 | tf_op jit(solution)/shard_map/ppermute | solution.py:18
  128.6 2.1 %shard_map.92 = (bf16[128,512]{1,0:T(8,128)(2,1)S(1)}, bf16[128,512]{1,0:T(8,128)(2,1)S(1)}, bf16[128,512]{1,0:T(8,128)(2,1)S(1)}, bf16[128,512]{1,0:T(8,128)(2,...) custom-call(s32[1]{0:T(128)} %bitcast.2.refs_0_, ...), custom_call_target="tpu_custom_call" | custom-call | flops 2529999872 | bytes 1048576 | tf_op jit(solution)/shard_map/pallas_call | solution.py:352
  131.9 2.3 %collective-permute-start.33 = (bf16[128,512]{1,0:T(8,128)(2,1)S(1)}, bf16[128,512]{1,0:T(8,128)(2,1)S(1)}, u32[]{:S(2)}, u32[]{:S(2)}) collective-permute-start(bf16[128,512]{1,0:T(8,128)(2,1)S(1)} %get-tuple-element.92), channel_id=1, source_target_pairs={{0,16},{4,20},{8,24},{12,28},{16,0},{20,4},{24,8},{28,12},{1,17},{... | collective-permute-start | bytes 393224 | tf_op jit(solution)/shard_map/ppermute | solution.py:18
  135.1 3.0 %collective-permute-done.32.refs_3_ = bf16[128,512]{1,0:T(8,128)(2,1)S(1)} collective-permute-done((bf16[128,512]{1,0:T(8,128)(2,1)S(1)}, bf16[128,512]{1,0:T(8,128)(2,1)S(1)}, u32[]{:S(2)}, u32[]{:S(2)}) %collective-permute-start.32) | collective-permute-done | bytes 131104 | tf_op jit(solution)/shard_map/ppermute | solution.py:18
  140.1 2.0 %collective-permute-start.36 = (bf16[128,512]{1,0:T(8,128)(2,1)}, bf16[128,512]{1,0:T(8,128)(2,1)}, u32[]{:S(2)}, u32[]{:S(2)}) collective-permute-start(bf16[128,512]{1,0:T(8,128)(2,1)} %get-tuple-element.95), channel_id=1, source_target_pairs={{0,28},{4,24},{8,20},{12,16},{16,12},{20,8},{24,4},{28,0},{1,29},{... | collective-permute-start | bytes 393224 | tf_op jit(solution)/shard_map/ppermute | solution.py:18
  145.8 4.3 %collective-permute-done.33.refs_3_ = bf16[128,512]{1,0:T(8,128)(2,1)S(1)} collective-permute-done((bf16[128,512]{1,0:T(8,128)(2,1)S(1)}, bf16[128,512]{1,0:T(8,128)(2,1)S(1)}, u32[]{:S(2)}, u32[]{:S(2)}) %collective-permute-start.33) | collective-permute-done | bytes 131104 | tf_op jit(solution)/shard_map/ppermute | solution.py:18
  153.2 3.4 %collective-permute-start.38 = (bf16[128,512]{1,0:T(8,128)(2,1)}, bf16[128,512]{1,0:T(8,128)(2,1)S(1)}, u32[]{:S(2)}, u32[]{:S(2)}) collective-permute-start(bf16[128,512]{1,0:T(8,128)(2,1)} %copy-done.11), channel_id=1, source_target_pairs={{0,12},{4,8},{8,4},{12,0},{16,28},{20,24},{24,20},{28,16},{1,13},{... | collective-permute-start | bytes 393224 | tf_op jit(solution)/shard_map/ppermute | solution.py:18
  158.8 2.1 %collective-permute-start.44 = (bf16[128,256]{1,0:T(8,128)(2,1)S(1)}, bf16[128,256]{1,0:T(8,128)(2,1)S(1)}, u32[]{:S(2)}, u32[]{:S(2)}) collective-permute-start(bf16[128,256]{1,0:T(8,128)(2,1)S(1)} %get-tuple-element.112), channel_id=1, source_target_pairs={{0,8},{4,12},{8,0},{12,4},{16,24},{20,28},{24,16},{28,20},{1,9},{5... | collective-permute-start | bytes 196616 | tf_op jit(solution)/shard_map/ppermute | solution.py:18
  (138 shorter events, 66.5 us)
Async XLA Ops:
  1.6 8.2 %collective-permute-start.2 = (bf16[128,256]{1,0:T(8,128)(2,1)S(1)}, bf16[128,256]{1,0:T(8,128)(2,1)S(1)}, u32[]{:S(2)}, u32[]{:S(2)}) collective-permute-start(bf16[128,256]{1,0:T(8,128)(2,1)S(1)} %constant_dynamic-slice_fusion.8.refs_0_), channel_id=1, source_target_pairs={{0,24},{4,28},{8,16},{12,20},{16,8},{20,12},{24,0},{28,4},{1,25},{... | collective-permute-start | bytes 196616 | tf_op jit(solution)/shard_map/ppermute | solution.py:18
  12.3 8.3 %collective-permute-start.4 = (bf16[4,128,256]{2,1,0:T(8,128)(2,1)S(1)}, bf16[4,128,256]{2,1,0:T(8,128)(2,1)S(1)}, u32[]{:S(2)}, u32[]{:S(2)}) collective-permute-start(bf16[4,128,256]{2,1,0:T(8,128)(2,1)S(1)} %shard_map.75.refs_0_), channel_id=1, source_target_pairs={{0,4},{4,0},{8,12},{12,8},{16,20},{20,16},{24,28},{28,24},{1,5},{5... | collective-permute-start | bytes 786440 | tf_op jit(solution)/shard_map/ppermute | solution.py:18
  13.9 12.3 %collective-permute-start.7 = (bf16[128,512]{1,0:T(8,128)(2,1)S(1)}, bf16[128,512]{1,0:T(8,128)(2,1)S(1)}, u32[]{:S(2)}, u32[]{:S(2)}) collective-permute-start(bf16[128,512]{1,0:T(8,128)(2,1)S(1)} %get-tuple-element.122.refs_5_), channel_id=1, source_target_pairs={{0,20},{4,16},{8,28},{12,24},{16,4},{20,0},{24,12},{28,8},{1,21},{... | collective-permute-start | bytes 393224 | tf_op jit(solution)/shard_map/ppermute | solution.py:18
  15.5 12.2 %collective-permute-start.6 = (bf16[128,512]{1,0:T(8,128)(2,1)S(1)}, bf16[128,512]{1,0:T(8,128)(2,1)S(1)}, u32[]{:S(2)}, u32[]{:S(2)}) collective-permute-start(bf16[128,512]{1,0:T(8,128)(2,1)S(1)} %get-tuple-element.123.refs_4_), channel_id=1, source_target_pairs={{0,16},{4,20},{8,24},{12,28},{16,0},{20,4},{24,8},{28,12},{1,17},{... | collective-permute-start | bytes 393224 | tf_op jit(solution)/shard_map/ppermute | solution.py:18
  16.8 17.9 %collective-permute-start.3 = (bf16[4,128,256]{2,1,0:T(8,128)(2,1)S(1)}, bf16[4,128,256]{2,1,0:T(8,128)(2,1)S(1)}, u32[]{:S(2)}, u32[]{:S(2)}) collective-permute-start(bf16[4,128,256]{2,1,0:T(8,128)(2,1)S(1)} %shard_map.75.refs_0_), channel_id=1, source_target_pairs={{0,2},{1,3},{2,0},{3,1},{4,6},{5,7},{6,4},{7,5},{8,10},{9,11},{10,... | collective-permute-start | bytes 786440 | tf_op jit(solution)/shard_map/ppermute | solution.py:18
  20.7 14.0 %collective-permute-start.5 = (bf16[4,128,256]{2,1,0:T(8,128)(2,1)S(1)}, bf16[4,128,256]{2,1,0:T(8,128)(2,1)S(1)}, u32[]{:S(2)}, u32[]{:S(2)}) collective-permute-start(bf16[4,128,256]{2,1,0:T(8,128)(2,1)S(1)} %collective-permute-done.4.refs_2_), channel_id=1, source_target_pairs={{0,2},{1,3},{2,0},{3,1},{4,6},{5,7},{6,4},{7,5},{8,10},{9,11},{10,... | collective-permute-start | bytes 786440 | tf_op jit(solution)/shard_map/ppermute | solution.py:18
  22.4 8.0 %collective-permute-start.10 = (bf16[128,512]{1,0:T(8,128)(2,1)}, bf16[128,512]{1,0:T(8,128)(2,1)S(1)}, u32[]{:S(2)}, u32[]{:S(2)}) collective-permute-start(bf16[128,512]{1,0:T(8,128)(2,1)} %get-tuple-element.117), channel_id=1, source_target_pairs={{0,8},{4,12},{8,0},{12,4},{16,24},{20,28},{24,16},{28,20},{1,9},{5... | collective-permute-start | bytes 393224 | tf_op jit(solution)/shard_map/ppermute | solution.py:18
  34.8 9.9 %collective-permute-start.11 = (bf16[2,1024,256]{2,1,0:T(8,128)(2,1)S(1)}, bf16[2,1024,256]{2,1,0:T(8,128)(2,1)S(1)}, u32[]{:S(2)}, u32[]{:S(2)}) collective-permute-start(bf16[2,1024,256]{2,1,0:T(8,128)(2,1)S(1)} %shard_map.78.refs_0_.refs_2_), channel_id=1, source_target_pairs={{0,1},{1,0},{2,3},{3,2},{4,5},{5,4},{6,7},{7,6},{8,9},{9,8},{10,11... | collective-permute-start | bytes 3145736 | tf_op jit(solution)/shard_map/ppermute | solution.py:18
  35.5 8.9 %collective-permute-start.12 = (bf16[128,512]{1,0:T(8,128)(2,1)S(1)}, bf16[128,512]{1,0:T(8,128)(2,1)S(1)}, u32[]{:S(2)}, u32[]{:S(2)}) collective-permute-start(bf16[128,512]{1,0:T(8,128)(2,1)S(1)} %get-tuple-element.120.refs_7_), channel_id=1, source_target_pairs={{0,28},{4,24},{8,20},{12,16},{16,12},{20,8},{24,4},{28,0},{1,29},{... | collective-permute-start | bytes 393224 | tf_op jit(solution)/shard_map/ppermute | solution.py:18
  48.9 8.1 %collective-permute-start.15 = (bf16[512,128]{1,0:T(8,128)(2,1)S(1)}, bf16[512,128]{1,0:T(8,128)(2,1)S(1)}, u32[]{:S(2)}, u32[]{:S(2)}) collective-permute-start(bf16[512,128]{1,0:T(8,128)(2,1)S(1)} %get-tuple-element.62), channel_id=1, source_target_pairs={{0,8},{4,12},{8,0},{12,4},{16,24},{20,28},{24,16},{28,20},{1,9},{5... | collective-permute-start | bytes 393224 | tf_op jit(solution)/shard_map/ppermute | solution.py:18
  50.6 11.0 %collective-permute-start.16 = (bf16[512,128]{1,0:T(8,128)(2,1)}, bf16[512,128]{1,0:T(8,128)(2,1)}, u32[]{:S(2)}, u32[]{:S(2)}) collective-permute-start(bf16[512,128]{1,0:T(8,128)(2,1)} %get-tuple-element.63), channel_id=1, source_target_pairs={{0,12},{4,8},{8,4},{12,0},{16,28},{20,24},{24,20},{28,16},{1,13},{... | collective-permute-start | bytes 393224 | tf_op jit(solution)/shard_map/ppermute | solution.py:18
  51.4 18.4 %collective-permute-start.17 = (bf16[512,128]{1,0:T(8,128)(2,1)}, bf16[512,128]{1,0:T(8,128)(2,1)}, u32[]{:S(2)}, u32[]{:S(2)}) collective-permute-start(bf16[512,128]{1,0:T(8,128)(2,1)} %get-tuple-element.64), channel_id=1, source_target_pairs={{0,16},{4,20},{8,24},{12,28},{16,0},{20,4},{24,8},{28,12},{1,17},{... | collective-permute-start | bytes 393224 | tf_op jit(solution)/shard_map/ppermute | solution.py:18
  53.7 19.5 %collective-permute-start.18 = (bf16[512,128]{1,0:T(8,128)(2,1)}, bf16[512,128]{1,0:T(8,128)(2,1)}, u32[]{:S(2)}, u32[]{:S(2)}) collective-permute-start(bf16[512,128]{1,0:T(8,128)(2,1)} %get-tuple-element.65), channel_id=1, source_target_pairs={{0,20},{4,16},{8,28},{12,24},{16,4},{20,0},{24,12},{28,8},{1,21},{... | collective-permute-start | bytes 393224 | tf_op jit(solution)/shard_map/ppermute | solution.py:18
  55.4 17.9 %collective-permute-start.19 = (bf16[512,128]{1,0:T(8,128)(2,1)}, bf16[512,128]{1,0:T(8,128)(2,1)}, u32[]{:S(2)}, u32[]{:S(2)}) collective-permute-start(bf16[512,128]{1,0:T(8,128)(2,1)} %get-tuple-element.66), channel_id=1, source_target_pairs={{0,24},{4,28},{8,16},{12,20},{16,8},{20,12},{24,0},{28,4},{1,25},{... | collective-permute-start | bytes 393224 | tf_op jit(solution)/shard_map/ppermute | solution.py:18
  57.0 16.2 %collective-permute-start.20 = (bf16[512,128]{1,0:T(8,128)(2,1)}, bf16[512,128]{1,0:T(8,128)(2,1)}, u32[]{:S(2)}, u32[]{:S(2)}) collective-permute-start(bf16[512,128]{1,0:T(8,128)(2,1)} %get-tuple-element.67), channel_id=1, source_target_pairs={{0,28},{4,24},{8,20},{12,16},{16,12},{20,8},{24,4},{28,0},{1,29},{... | collective-permute-start | bytes 393224 | tf_op jit(solution)/shard_map/ppermute | solution.py:18
  81.0 8.0 %collective-permute-start.23 = (bf16[1024,128]{1,0:T(8,128)(2,1)S(1)}, bf16[1024,128]{1,0:T(8,128)(2,1)S(1)}, u32[]{:S(2)}, u32[]{:S(2)}) collective-permute-start(bf16[1024,128]{1,0:T(8,128)(2,1)S(1)} %get-tuple-element.75), channel_id=1, source_target_pairs={{0,1},{1,0},{2,3},{3,2},{4,5},{5,4},{6,7},{7,6},{8,9},{9,8},{10,11... | collective-permute-start | bytes 786440 | tf_op jit(solution)/shard_map/ppermute | solution.py:181
  91.5 10.8 %collective-permute-start.25 = (bf16[512,128]{1,0:T(8,128)(2,1)S(1)}, bf16[512,128]{1,0:T(8,128)(2,1)S(1)}, u32[]{:S(2)}, u32[]{:S(2)}) collective-permute-start(bf16[512,128]{1,0:T(8,128)(2,1)S(1)} %get-tuple-element.78), channel_id=1, source_target_pairs={{0,4},{4,0},{8,12},{12,8},{16,20},{20,16},{24,28},{28,24},{1,5},{5... | collective-permute-start | bytes 393224 | tf_op jit(solution)/shard_map/ppermute | solution.py:18
  92.4 18.6 %collective-permute-start.26 = (bf16[512,128]{1,0:T(8,128)(2,1)S(1)}, bf16[512,128]{1,0:T(8,128)(2,1)S(1)}, u32[]{:S(2)}, u32[]{:S(2)}) collective-permute-start(bf16[512,128]{1,0:T(8,128)(2,1)S(1)} %get-tuple-element.82), channel_id=1, source_target_pairs={{0,16},{4,20},{8,24},{12,28},{16,0},{20,4},{24,8},{28,12},{1,17},{... | collective-permute-start | bytes 393224 | tf_op jit(solution)/shard_map/ppermute | solution.py:18
  97.5 18.2 %collective-permute-start.27 = (bf16[512,128]{1,0:T(8,128)(2,1)S(1)}, bf16[512,128]{1,0:T(8,128)(2,1)S(1)}, u32[]{:S(2)}, u32[]{:S(2)}) collective-permute-start(bf16[512,128]{1,0:T(8,128)(2,1)S(1)} %get-tuple-element.83), channel_id=1, source_target_pairs={{0,20},{4,16},{8,28},{12,24},{16,4},{20,0},{24,12},{28,8},{1,21},{... | collective-permute-start | bytes 393224 | tf_op jit(solution)/shard_map/ppermute | solution.py:18
  98.1 17.6 %collective-permute-start.28 = (bf16[512,128]{1,0:T(8,128)(2,1)S(1)}, bf16[512,128]{1,0:T(8,128)(2,1)S(1)}, u32[]{:S(2)}, u32[]{:S(2)}) collective-permute-start(bf16[512,128]{1,0:T(8,128)(2,1)S(1)} %get-tuple-element.84), channel_id=1, source_target_pairs={{0,24},{4,28},{8,16},{12,20},{16,8},{20,12},{24,0},{28,4},{1,25},{... | collective-permute-start | bytes 393224 | tf_op jit(solution)/shard_map/ppermute | solution.py:18
  100.1 15.7 %collective-permute-start.29 = (bf16[512,128]{1,0:T(8,128)(2,1)S(1)}, bf16[512,128]{1,0:T(8,128)(2,1)S(1)}, u32[]{:S(2)}, u32[]{:S(2)}) collective-permute-start(bf16[512,128]{1,0:T(8,128)(2,1)S(1)} %get-tuple-element.85), channel_id=1, source_target_pairs={{0,28},{4,24},{8,20},{12,16},{16,12},{20,8},{24,4},{28,0},{1,29},{... | collective-permute-start | bytes 393224 | tf_op jit(solution)/shard_map/ppermute | solution.py:18
  110.9 10.9 %collective-permute-start.31 = (bf16[512,128]{1,0:T(8,128)(2,1)S(1)}, bf16[512,128]{1,0:T(8,128)(2,1)S(1)}, u32[]{:S(2)}, u32[]{:S(2)}) collective-permute-start(bf16[512,128]{1,0:T(8,128)(2,1)S(1)} %get-tuple-element.88), channel_id=1, source_target_pairs={{0,12},{4,8},{8,4},{12,0},{16,28},{20,24},{24,20},{28,16},{1,13},{... | collective-permute-start | bytes 393224 | tf_op jit(solution)/shard_map/ppermute | solution.py:18
  126.7 13.4 %collective-permute-start.41 = (bf16[2,4,128,128]{3,2,1,0:T(8,128)(2,1)S(1)}, bf16[2,4,128,128]{3,2,1,0:T(8,128)(2,1)S(1)}, u32[]{:S(2)}, u32[]{:S(2)}) collective-permute-start(bf16[2,4,128,128]{3,2,1,0:T(8,128)(2,1)S(1)} %get-tuple-element.105), channel_id=1, source_target_pairs={{0,4},{4,0},{8,12},{12,8},{16,20},{20,16},{24,28},{28,24},{1,5},{5... | collective-permute-start | bytes 786440 | tf_op jit(solution)/shard_map/ppermute | solution.py:18
  127.3 14.8 %collective-permute-start.40 = (bf16[1088,128]{1,0:T(8,128)(2,1)S(1)}, bf16[1088,128]{1,0:T(8,128)(2,1)S(1)}, u32[]{:S(2)}, u32[]{:S(2)}) collective-permute-start(bf16[1088,128]{1,0:T(8,128)(2,1)S(1)} %get-tuple-element.102), channel_id=1, source_target_pairs={{0,2},{1,3},{2,0},{3,1},{4,6},{5,7},{6,4},{7,5},{8,10},{9,11},{10,... | collective-permute-start | bytes 835592 | tf_op jit(solution)/shard_map/ppermute | solution.py:18
  131.9 18.3 %collective-permute-start.33 = (bf16[128,512]{1,0:T(8,128)(2,1)S(1)}, bf16[128,512]{1,0:T(8,128)(2,1)S(1)}, u32[]{:S(2)}, u32[]{:S(2)}) collective-permute-start(bf16[128,512]{1,0:T(8,128)(2,1)S(1)} %get-tuple-element.92), channel_id=1, source_target_pairs={{0,16},{4,20},{8,24},{12,28},{16,0},{20,4},{24,8},{28,12},{1,17},{... | collective-permute-start | bytes 393224 | tf_op jit(solution)/shard_map/ppermute | solution.py:18
  134.2 19.0 %collective-permute-start.34 = (bf16[128,512]{1,0:T(8,128)(2,1)}, bf16[128,512]{1,0:T(8,128)(2,1)}, u32[]{:S(2)}, u32[]{:S(2)}) collective-permute-start(bf16[128,512]{1,0:T(8,128)(2,1)} %get-tuple-element.93), channel_id=1, source_target_pairs={{0,20},{4,16},{8,28},{12,24},{16,4},{20,0},{24,12},{28,8},{1,21},{... | collective-permute-start | bytes 393224 | tf_op jit(solution)/shard_map/ppermute | solution.py:18
  138.2 15.0 %collective-permute-start.35 = (bf16[128,512]{1,0:T(8,128)(2,1)}, bf16[128,512]{1,0:T(8,128)(2,1)}, u32[]{:S(2)}, u32[]{:S(2)}) collective-permute-start(bf16[128,512]{1,0:T(8,128)(2,1)} %get-tuple-element.94), channel_id=1, source_target_pairs={{0,24},{4,28},{8,16},{12,20},{16,8},{20,12},{24,0},{28,4},{1,25},{... | collective-permute-start | bytes 393224 | tf_op jit(solution)/shard_map/ppermute | solution.py:18
  140.1 16.4 %collective-permute-start.36 = (bf16[128,512]{1,0:T(8,128)(2,1)}, bf16[128,512]{1,0:T(8,128)(2,1)}, u32[]{:S(2)}, u32[]{:S(2)}) collective-permute-start(bf16[128,512]{1,0:T(8,128)(2,1)} %get-tuple-element.95), channel_id=1, source_target_pairs={{0,28},{4,24},{8,20},{12,16},{16,12},{20,8},{24,4},{28,0},{1,29},{... | collective-permute-start | bytes 393224 | tf_op jit(solution)/shard_map/ppermute | solution.py:18
  144.3 13.4 %collective-permute-start.42 = (bf16[4,128,128]{2,1,0:T(8,128)(2,1)}, bf16[4,128,128]{2,1,0:T(8,128)(2,1)}, u32[]{:S(2)}, u32[]{:S(2)}) collective-permute-start(bf16[4,128,128]{2,1,0:T(8,128)(2,1)} %get-tuple-element.108), channel_id=1, source_target_pairs={{0,4},{4,0},{8,12},{12,8},{16,20},{20,16},{24,28},{28,24},{1,5},{5... | collective-permute-start | bytes 393224 | tf_op jit(solution)/shard_map/ppermute | solution.py:18
  150.1 7.6 %collective-permute-start.43 = (bf16[4,128,128]{2,1,0:T(8,128)(2,1)}, bf16[4,128,128]{2,1,0:T(8,128)(2,1)}, u32[]{:S(2)}, u32[]{:S(2)}) collective-permute-start(bf16[4,128,128]{2,1,0:T(8,128)(2,1)} %get-tuple-element.110), channel_id=1, source_target_pairs={{0,2},{1,3},{2,0},{3,1},{4,6},{5,7},{6,4},{7,5},{8,10},{9,11},{10,... | collective-permute-start | bytes 393224 | tf_op jit(solution)/shard_map/ppermute | solution.py:18
  153.2 10.8 %collective-permute-start.37 = (bf16[128,512]{1,0:T(8,128)(2,1)}, bf16[128,512]{1,0:T(8,128)(2,1)S(1)}, u32[]{:S(2)}, u32[]{:S(2)}) collective-permute-start(bf16[128,512]{1,0:T(8,128)(2,1)} %copy-done.12), channel_id=1, source_target_pairs={{0,8},{4,12},{8,0},{12,4},{16,24},{20,28},{24,16},{28,20},{1,9},{5... | collective-permute-start | bytes 393224 | tf_op jit(solution)/shard_map/ppermute | solution.py:18
  153.2 10.7 %collective-permute-start.38 = (bf16[128,512]{1,0:T(8,128)(2,1)}, bf16[128,512]{1,0:T(8,128)(2,1)S(1)}, u32[]{:S(2)}, u32[]{:S(2)}) collective-permute-start(bf16[128,512]{1,0:T(8,128)(2,1)} %copy-done.11), channel_id=1, source_target_pairs={{0,12},{4,8},{8,4},{12,0},{16,28},{20,24},{24,20},{28,16},{1,13},{... | collective-permute-start | bytes 393224 | tf_op jit(solution)/shard_map/ppermute | solution.py:18
  (37 other events, 161.1 us)

commit v12 on v11

--- a/solution.py
+++ b/solution.py
@@ -135,7 +135,7 @@
         )
         kernel = functools.partial(halves_first, rows, nf)
         a_keep, a_send, b_keep, b_next, b_send, sums = call(
-            kernel, shapes, [], *mine, theirs, taps, us=0.8
+            kernel, shapes, [], *mine, theirs, taps, us=0.1
         )
         a_got = swap(a_send, "space", 2)
         b_got = swap(b_send, "filter", 1)
@@ -147,14 +147,14 @@
         kernel = functools.partial(halves_second, rows, nf)
         near, a_send, far, b_send, taps = call(
             kernel, shapes, [], a_keep, a_got, b_keep, b_next, b_got, sums,
-            us=0.6, after=(first_in,),
+            us=0.1, after=(first_in,),
         )
         a_got = swap(a_send, "filter", 1)
         b_got = swap(b_send, "space", 2)
         shapes = [jax.ShapeDtypeStruct((rows, share), F32)]
         shapes += [jax.ShapeDtypeStruct((rows, share), BF)] * (n - 1)
         keep, *rest = call(
-            halves_third, shapes, [], near, a_got, far, b_got, us=0.5, after=(second_in,)
+            halves_third, shapes, [], near, a_got, far, b_got, us=0.1, after=(second_in,)
         )
     else:
         step = 1

time: 169 us -> 170 us (level)
    unnamed x46 -> x50, local copies, waits for them, and re-layouts: 9.18 us -> 10.7 us
  transfers between devices with their start and end apart: 47 -> 47, of which waited for: 20 -> 20; matrix products, arithmetic and copies ran while one was open for 4% -> 4% of each run, Pallas kernels for 13% -> 12%
where the time goes in v12:
time: 170 us; the launch traced here: 169 us
  starting transfers between devices  73.3 us (43%)
  waiting for transfers between devices  47.1 us (28%)
  Pallas kernels  31.7 us (19%)
  local copies, waits for them, and re-layouts  15.3 us (9%)
    ppermute x43, starting transfers between devices, swap(): return lax.ppermute(block, axis, [(i, i ^ step) for i in range(size)])  66.8 us
    ppermute x43, waiting for transfers between devices, swap(): return lax.ppermute(block, axis, [(i, i ^ step) for i in range(size)])  47.1 us
    pallas_call x24, Pallas kernels, call(): pl.pallas_call(wrapped, out_shape=out_shape, in_specs=specs + [pl.BlockSp...  31.7 us
    unnamed x50, local copies, waits for them, and re-layouts  10.7 us
    ppermute x2, starting transfers between devices, halo(): return (lax.ppermute(near, 'space', inner), far)  4.9 us
  transfers between devices with their start and end apart: 47, of which 20 were waited for; matrix products, arithmetic and copies ran while one was open for 4% of the time, Pallas kernels for 12%

profile of v12, /device:TPU:0, one launch (start us, length us, event | category | flops | bytes accessed | tf_op | source)
XLA Modules:
  0.0 169.2 jit_solution(12586371813386144154)
XLA Ops:
  1.6 5.1 %collective-permute-start.2 = (bf16[128,256]{1,0:T(8,128)(2,1)S(1)}, bf16[128,256]{1,0:T(8,128)(2,1)S(1)}, u32[]{:S(2)}, u32[]{:S(2)}) collective-permute-start(bf16[128,256]{1,0:T(8,128)(2,1)S(1)} %constant_dynamic-slice_fusion.8.refs_0_), channel_id=1, source_target_pairs={{0,24},{4,28},{8,16},{12,20},{16,8},{20,12},{24,0},{28,4},{1,25},{... | collective-permute-start | bytes 196616 | tf_op jit(solution)/shard_map/ppermute | solution.py:18
  9.8 2.5 %collective-permute-done.1.refs_2_ = bf16[128,256]{1,0:T(8,128)(2,1)S(1)} collective-permute-done((bf16[128,256]{1,0:T(8,128)(2,1)S(1)}, bf16[128,256]{1,0:T(8,128)(2,1)S(1)}, u32[]{:S(2)}, u32[]{:S(2)}) %collective-permute-start.1) | collective-permute-done | bytes 65568 | tf_op jit(solution)/shard_map/ppermute | solution.py:18
  18.3 2.3 %collective-permute-done.4.refs_2_ = bf16[4,128,256]{2,1,0:T(8,128)(2,1)S(1)} collective-permute-done((bf16[4,128,256]{2,1,0:T(8,128)(2,1)S(1)}, bf16[4,128,256]{2,1,0:T(8,128)(2,1)S(1)}, u32[]{:S(2)}, u32[]{:S(2)}) %collective-permute-start.4) | collective-permute-done | bytes 262176 | tf_op jit(solution)/shard_map/ppermute | solution.py:18
  22.4 2.4 %collective-permute-start.10 = (bf16[128,512]{1,0:T(8,128)(2,1)}, bf16[128,512]{1,0:T(8,128)(2,1)S(1)}, u32[]{:S(2)}, u32[]{:S(2)}) collective-permute-start(bf16[128,512]{1,0:T(8,128)(2,1)} %get-tuple-element.117), channel_id=1, source_target_pairs={{0,8},{4,12},{8,0},{12,4},{16,24},{20,28},{24,16},{28,20},{1,9},{5... | collective-permute-start | bytes 393224 | tf_op jit(solution)/shard_map/ppermute | solution.py:18
  31.2 3.3 %collective-permute-done.8.refs_2_ = bf16[128,512]{1,0:T(8,128)(2,1)S(1)} collective-permute-done((bf16[128,512]{1,0:T(8,128)(2,1)S(1)}, bf16[128,512]{1,0:T(8,128)(2,1)S(1)}, u32[]{:S(2)}, u32[]{:S(2)}) %collective-permute-start.8) | collective-permute-done | bytes 131104 | tf_op jit(solution)/shard_map/ppermute | solution.py:18
  35.5 2.6 %collective-permute-start.12 = (bf16[128,512]{1,0:T(8,128)(2,1)S(1)}, bf16[128,512]{1,0:T(8,128)(2,1)S(1)}, u32[]{:S(2)}, u32[]{:S(2)}) collective-permute-start(bf16[128,512]{1,0:T(8,128)(2,1)S(1)} %get-tuple-element.120.refs_7_), channel_id=1, source_target_pairs={{0,28},{4,24},{8,20},{12,16},{16,12},{20,8},{24,4},{28,0},{1,29},{... | collective-permute-start | bytes 393224 | tf_op jit(solution)/shard_map/ppermute | solution.py:18
  38.5 2.3 %shard_map.80.refs_3_.refs_2_.refs_5_ = bf16[4096,128]{1,0:T(8,128)(2,1)S(1)} custom-call(bf16[128,4096]{1,0:T(8,128)(2,1)S(1)} %bitcast.11), custom_call_target="tpu_custom_call" | custom-call | flops 1380000000 | bytes 1048576 | tf_op jit(solution)/shard_map/pallas_call | solution.py:352
  44.6 2.1 %shard_map.81 = (bf16[512,128]{1,0:T(8,128)(2,1)S(1)}, bf16[512,128]{1,0:T(8,128)(2,1)S(1)}, bf16[512,128]{1,0:T(8,128)(2,1)S(1)}, bf16[512,128]{1,0:T(8,128)(2,...) custom-call(bf16[2,1024,256]{2,1,0:T(8,128)(2,1)S(1)} %shard_map.78., ...), custom_call_target="tpu_custom_call" | custom-call | flops 2990000128 | bytes 1048576 | tf_op jit(solution)/shard_map/pallas_call | solution.py:352
  51.4 2.3 %collective-permute-start.17 = (bf16[512,128]{1,0:T(8,128)(2,1)}, bf16[512,128]{1,0:T(8,128)(2,1)}, u32[]{:S(2)}, u32[]{:S(2)}) collective-permute-start(bf16[512,128]{1,0:T(8,128)(2,1)} %get-tuple-element.64), channel_id=1, source_target_pairs={{0,16},{4,20},{8,24},{12,28},{16,0},{20,4},{24,8},{28,12},{1,17},{... | collective-permute-start | bytes 393224 | tf_op jit(solution)/shard_map/ppermute | solution.py:18
  57.0 2.8 %collective-permute-start.20 = (bf16[512,128]{1,0:T(8,128)(2,1)}, bf16[512,128]{1,0:T(8,128)(2,1)}, u32[]{:S(2)}, u32[]{:S(2)}) collective-permute-start(bf16[512,128]{1,0:T(8,128)(2,1)} %get-tuple-element.67), channel_id=1, source_target_pairs={{0,28},{4,24},{8,20},{12,16},{16,12},{20,8},{24,4},{28,0},{1,29},{... | collective-permute-start | bytes 393224 | tf_op jit(solution)/shard_map/ppermute | solution.py:18
  62.6 7.2 %collective-permute-done.17.refs_3_ = bf16[512,128]{1,0:T(8,128)(2,1)} collective-permute-done((bf16[512,128]{1,0:T(8,128)(2,1)}, bf16[512,128]{1,0:T(8,128)(2,1)}, u32[]{:S(2)}, u32[]{:S(2)}) %collective-permute-start.17) | collective-permute-done | bytes 131104 | tf_op jit(solution)/shard_map/ppermute | solution.py:18
  69.8 3.4 %collective-permute-done.18.refs_4_ = bf16[512,128]{1,0:T(8,128)(2,1)} collective-permute-done((bf16[512,128]{1,0:T(8,128)(2,1)}, bf16[512,128]{1,0:T(8,128)(2,1)}, u32[]{:S(2)}, u32[]{:S(2)}) %collective-permute-start.18) | collective-permute-done | bytes 131104 | tf_op jit(solution)/shard_map/ppermute | solution.py:18
  75.3 2.7 %shard_map.85 = (bf16[2,1024,128]{2,1,0:T(8,128)(2,1)S(1)}, f32[2,1024,128]{2,1,0:T(8,128)S(1)}) custom-call(bf16[4,1024,128]{2,1,0:T(8,128)(2,1)S(1)} %bitcast.17, f32[27,128]{1,0:T(8,128)S(1)} %bitcast.20, bf16[4096,128]{1,0:T(8,128)(2,1)S(1)} %copy-done.21), custom_call_target="tpu_custom_call" | custom-call | flops 3680000000 | bytes 1048576 | tf_op jit(solution)/shard_map/pallas_call | solution.py:352
  78.0 3.0 %shard_map.86 = (bf16[2,1024,128]{2,1,0:T(8,128)(2,1)S(1)}, f32[2,1024,128]{2,1,0:T(8,128)S(1)}, bf16[1024,128]{1,0:T(8,128)(2,1)S(1)}, bf16[1024,128]{1,0:T(8,128)(2,1)S(1)}) custom-call(s32[1]{0:T(128)} %bitcast.refs_1_.refs_0_, bf16[4,1024,128]{2,1,0:T(8,128)(2,1)S(1)} %bitcast.18, bf16[1024,128]{1,0:T(8,128)(2,1)S(1)} %collective-permute-done.21.refs_2_, ...), custom_call_target="tpu_custom_call" | custom-call | flops 3680000000 | bytes 1048576 | tf_op jit(solution)/shard_map/pallas_call | solution.py:352
  81.0 4.8 %collective-permute-start.23 = (bf16[1024,128]{1,0:T(8,128)(2,1)S(1)}, bf16[1024,128]{1,0:T(8,128)(2,1)S(1)}, u32[]{:S(2)}, u32[]{:S(2)}) collective-permute-start(bf16[1024,128]{1,0:T(8,128)(2,1)S(1)} %get-tuple-element.75), channel_id=1, source_target_pairs={{0,1},{1,0},{2,3},{3,2},{4,5},{5,4},{6,7},{7,6},{8,9},{9,8},{10,11... | collective-permute-start | bytes 786440 | tf_op jit(solution)/shard_map/ppermute | solution.py:181
  86.7 2.3 %shard_map.87.refs_7_ = bf16[2,1024,128]{2,1,0:T(8,128)(2,1)S(1)} custom-call(bf16[2,1024,128]{2,1,0:T(8,128)(2,1)S(1)} %get-tuple-element.72.refs_0_.refs_2_.refs_4_, bf16[2,1024,128]{2,1,0:T(8,128)(2,1)S(1)} %get-tuple-element.71.refs_6_.refs_1_.refs_3_.refs_5_, f32[27,128]{1,0:T(8,128)S(1)} %bitcast.22), custom_call_target="tpu_custom_call" | custom-call | flops 2644999936 | bytes 1048576 | tf_op jit(solution)/shard_map/pallas_call | solution.py:352
  89.0 2.5 %shard_map.88 = (bf16[4096,128]{1,0:T(8,128)(2,1)S(1)}, bf16[512,128]{1,0:T(8,128)(2,1)S(1)}, bf16[512,128]{1,0:T(8,128)(2,1)S(1)}, bf16[512,128]{1,0:T(8,128)(2...) custom-call(s32[1]{0:T(128)} %bitcast.1.refs_0_, ...), custom_call_target="tpu_custom_call" | custom-call | flops 3220000000 | bytes 1048576 | tf_op jit(solution)/shard_map/pallas_call | solution.py:352
  92.3 5.2 %collective-permute-start.26 = (bf16[512,128]{1,0:T(8,128)(2,1)S(1)}, bf16[512,128]{1,0:T(8,128)(2,1)S(1)}, u32[]{:S(2)}, u32[]{:S(2)}) collective-permute-start(bf16[512,128]{1,0:T(8,128)(2,1)S(1)} %get-tuple-element.82), channel_id=1, source_target_pairs={{0,16},{4,20},{8,24},{12,28},{16,0},{20,4},{24,8},{28,12},{1,17},{... | collective-permute-start | bytes 393224 | tf_op jit(solution)/shard_map/ppermute | solution.py:18
  100.0 2.2 %collective-permute-start.29 = (bf16[512,128]{1,0:T(8,128)(2,1)S(1)}, bf16[512,128]{1,0:T(8,128)(2,1)S(1)}, u32[]{:S(2)}, u32[]{:S(2)}) collective-permute-start(bf16[512,128]{1,0:T(8,128)(2,1)S(1)} %get-tuple-element.85), channel_id=1, source_target_pairs={{0,28},{4,24},{8,20},{12,16},{16,12},{20,8},{24,4},{28,0},{1,29},{... | collective-permute-start | bytes 393224 | tf_op jit(solution)/shard_map/ppermute | solution.py:18
  102.2 7.2 %shard_map.89 = (f32[32,128]{1,0:T(8,128)S(1)}, bf16[128,4096]{1,0:T(8,128)(2,1)S(1)}, bf16[512,1024]{1,0:T(8,128)(2,1)S(1)}) custom-call(s32[1]{0:T(128)} %bitcast.refs_1_.refs_0_, bf16[4,1024,128]{2,1,0:T(8,128)(2,1)S(1)} %bitcast.19, bf16[1024,128]{1,0:T(8,128)(2,1)S(1)} %collective-permute-done.21.refs_2_, ...), custom_call_target="tpu_custom_call" | custom-call | flops 6670000128 | bytes 1048576 | tf_op jit(solution)/shard_map/pallas_call | solution.py:352
  110.9 2.2 %collective-permute-start.31 = (bf16[512,128]{1,0:T(8,128)(2,1)S(1)}, bf16[512,128]{1,0:T(8,128)(2,1)S(1)}, u32[]{:S(2)}, u32[]{:S(2)}) collective-permute-start(bf16[512,128]{1,0:T(8,128)(2,1)S(1)} %get-tuple-element.88), channel_id=1, source_target_pairs={{0,12},{4,8},{8,4},{12,0},{16,28},{20,24},{24,20},{28,16},{1,13},{... | collective-permute-start | bytes 393224 | tf_op jit(solution)/shard_map/ppermute | solution.py:18
  113.1 2.6 %collective-permute-done.27.refs_4_ = bf16[512,128]{1,0:T(8,128)(2,1)S(1)} collective-permute-done((bf16[512,128]{1,0:T(8,128)(2,1)S(1)}, bf16[512,128]{1,0:T(8,128)(2,1)S(1)}, u32[]{:S(2)}, u32[]{:S(2)}) %collective-permute-start.27) | collective-permute-done | bytes 131104 | tf_op jit(solution)/shard_map/ppermute | solution.py:18
  115.7 2.3 %collective-permute-done.30.refs_7_ = bf16[512,128]{1,0:T(8,128)(2,1)S(1)} collective-permute-done((bf16[512,128]{1,0:T(8,128)(2,1)S(1)}, bf16[512,128]{1,0:T(8,128)(2,1)S(1)}, u32[]{:S(2)}, u32[]{:S(2)}) %collective-permute-start.30) | collective-permute-done | bytes 131104 | tf_op jit(solution)/shard_map/ppermute | solution.py:18
  117.9 3.8 %collective-permute-done.31.refs_8_ = bf16[512,128]{1,0:T(8,128)(2,1)S(1)} collective-permute-done((bf16[512,128]{1,0:T(8,128)(2,1)S(1)}, bf16[512,128]{1,0:T(8,128)(2,1)S(1)}, u32[]{:S(2)}, u32[]{:S(2)}) %collective-permute-start.31) | collective-permute-done | bytes 131104 | tf_op jit(solution)/shard_map/ppermute | solution.py:18
  124.1 2.3 %collective-permute-done.39.refs_2_ = bf16[2,1056,256]{2,1,0:T(8,128)(2,1)S(1)} collective-permute-done((bf16[2,1056,256]{2,1,0:T(8,128)(2,1)S(1)}, bf16[2,1056,256]{2,1,0:T(8,128)(2,1)S(1)}, u32[]{:S(2)}, u32[]{:S(2)}) %collective-permute-start.39) | collective-permute-done | bytes 1081376 | tf_op jit(solution)/shard_map/ppermute | solution.py:18
  128.5 2.1 %shard_map.92 = (bf16[128,512]{1,0:T(8,128)(2,1)S(1)}, bf16[128,512]{1,0:T(8,128)(2,1)S(1)}, bf16[128,512]{1,0:T(8,128)(2,1)S(1)}, bf16[128,512]{1,0:T(8,128)(2,...) custom-call(s32[1]{0:T(128)} %bitcast.2.refs_0_, ...), custom_call_target="tpu_custom_call" | custom-call | flops 2529999872 | bytes 1048576 | tf_op jit(solution)/shard_map/pallas_call | solution.py:352
  131.8 2.3 %collective-permute-start.33 = (bf16[128,512]{1,0:T(8,128)(2,1)S(1)}, bf16[128,512]{1,0:T(8,128)(2,1)S(1)}, u32[]{:S(2)}, u32[]{:S(2)}) collective-permute-start(bf16[128,512]{1,0:T(8,128)(2,1)S(1)} %get-tuple-element.92), channel_id=1, source_target_pairs={{0,16},{4,20},{8,24},{12,28},{16,0},{20,4},{24,8},{28,12},{1,17},{... | collective-permute-start | bytes 393224 | tf_op jit(solution)/shard_map/ppermute | solution.py:18
  135.1 3.0 %collective-permute-done.32.refs_3_ = bf16[128,512]{1,0:T(8,128)(2,1)S(1)} collective-permute-done((bf16[128,512]{1,0:T(8,128)(2,1)S(1)}, bf16[128,512]{1,0:T(8,128)(2,1)S(1)}, u32[]{:S(2)}, u32[]{:S(2)}) %collective-permute-start.32) | collective-permute-done | bytes 131104 | tf_op jit(solution)/shard_map/ppermute | solution.py:18
  140.0 2.0 %collective-permute-start.36 = (bf16[128,512]{1,0:T(8,128)(2,1)}, bf16[128,512]{1,0:T(8,128)(2,1)}, u32[]{:S(2)}, u32[]{:S(2)}) collective-permute-start(bf16[128,512]{1,0:T(8,128)(2,1)} %get-tuple-element.95), channel_id=1, source_target_pairs={{0,28},{4,24},{8,20},{12,16},{16,12},{20,8},{24,4},{28,0},{1,29},{... | collective-permute-start | bytes 393224 | tf_op jit(solution)/shard_map/ppermute | solution.py:18
  145.7 4.3 %collective-permute-done.33.refs_3_ = bf16[128,512]{1,0:T(8,128)(2,1)S(1)} collective-permute-done((bf16[128,512]{1,0:T(8,128)(2,1)S(1)}, bf16[128,512]{1,0:T(8,128)(2,1)S(1)}, u32[]{:S(2)}, u32[]{:S(2)}) %collective-permute-start.33) | collective-permute-done | bytes 131104 | tf_op jit(solution)/shard_map/ppermute | solution.py:18
  153.1 3.4 %collective-permute-start.38 = (bf16[128,512]{1,0:T(8,128)(2,1)}, bf16[128,512]{1,0:T(8,128)(2,1)S(1)}, u32[]{:S(2)}, u32[]{:S(2)}) collective-permute-start(bf16[128,512]{1,0:T(8,128)(2,1)} %copy-done.13), channel_id=1, source_target_pairs={{0,12},{4,8},{8,4},{12,0},{16,28},{20,24},{24,20},{28,16},{1,13},{... | collective-permute-start | bytes 393224 | tf_op jit(solution)/shard_map/ppermute | solution.py:18
  159.5 2.1 %collective-permute-start.44 = (bf16[128,256]{1,0:T(8,128)(2,1)S(1)}, bf16[128,256]{1,0:T(8,128)(2,1)S(1)}, u32[]{:S(2)}, u32[]{:S(2)}) collective-permute-start(bf16[128,256]{1,0:T(8,128)(2,1)S(1)} %get-tuple-element.112), channel_id=1, source_target_pairs={{0,8},{4,12},{8,0},{12,4},{16,24},{20,28},{24,16},{28,20},{1,9},{5... | collective-permute-start | bytes 196616 | tf_op jit(solution)/shard_map/ppermute | solution.py:18
  (142 shorter events, 67.6 us)
Async XLA Ops:
  1.6 8.2 %collective-permute-start.2 = (bf16[128,256]{1,0:T(8,128)(2,1)S(1)}, bf16[128,256]{1,0:T(8,128)(2,1)S(1)}, u32[]{:S(2)}, u32[]{:S(2)}) collective-permute-start(bf16[128,256]{1,0:T(8,128)(2,1)S(1)} %constant_dynamic-slice_fusion.8.refs_0_), channel_id=1, source_target_pairs={{0,24},{4,28},{8,16},{12,20},{16,8},{20,12},{24,0},{28,4},{1,25},{... | collective-permute-start | bytes 196616 | tf_op jit(solution)/shard_map/ppermute | solution.py:18
  12.3 8.3 %collective-permute-start.4 = (bf16[4,128,256]{2,1,0:T(8,128)(2,1)S(1)}, bf16[4,128,256]{2,1,0:T(8,128)(2,1)S(1)}, u32[]{:S(2)}, u32[]{:S(2)}) collective-permute-start(bf16[4,128,256]{2,1,0:T(8,128)(2,1)S(1)} %shard_map.75.refs_0_), channel_id=1, source_target_pairs={{0,4},{4,0},{8,12},{12,8},{16,20},{20,16},{24,28},{28,24},{1,5},{5... | collective-permute-start | bytes 786440 | tf_op jit(solution)/shard_map/ppermute | solution.py:18
  13.9 12.3 %collective-permute-start.7 = (bf16[128,512]{1,0:T(8,128)(2,1)S(1)}, bf16[128,512]{1,0:T(8,128)(2,1)S(1)}, u32[]{:S(2)}, u32[]{:S(2)}) collective-permute-start(bf16[128,512]{1,0:T(8,128)(2,1)S(1)} %get-tuple-element.122.refs_5_), channel_id=1, source_target_pairs={{0,20},{4,16},{8,28},{12,24},{16,4},{20,0},{24,12},{28,8},{1,21},{... | collective-permute-start | bytes 393224 | tf_op jit(solution)/shard_map/ppermute | solution.py:18
  15.5 12.2 %collective-permute-start.6 = (bf16[128,512]{1,0:T(8,128)(2,1)S(1)}, bf16[128,512]{1,0:T(8,128)(2,1)S(1)}, u32[]{:S(2)}, u32[]{:S(2)}) collective-permute-start(bf16[128,512]{1,0:T(8,128)(2,1)S(1)} %get-tuple-element.123.refs_4_), channel_id=1, source_target_pairs={{0,16},{4,20},{8,24},{12,28},{16,0},{20,4},{24,8},{28,12},{1,17},{... | collective-permute-start | bytes 393224 | tf_op jit(solution)/shard_map/ppermute | solution.py:18
  16.8 17.9 %collective-permute-start.3 = (bf16[4,128,256]{2,1,0:T(8,128)(2,1)S(1)}, bf16[4,128,256]{2,1,0:T(8,128)(2,1)S(1)}, u32[]{:S(2)}, u32[]{:S(2)}) collective-permute-start(bf16[4,128,256]{2,1,0:T(8,128)(2,1)S(1)} %shard_map.75.refs_0_), channel_id=1, source_target_pairs={{0,2},{1,3},{2,0},{3,1},{4,6},{5,7},{6,4},{7,5},{8,10},{9,11},{10,... | collective-permute-start | bytes 786440 | tf_op jit(solution)/shard_map/ppermute | solution.py:18
  20.7 14.0 %collective-permute-start.5 = (bf16[4,128,256]{2,1,0:T(8,128)(2,1)S(1)}, bf16[4,128,256]{2,1,0:T(8,128)(2,1)S(1)}, u32[]{:S(2)}, u32[]{:S(2)}) collective-permute-start(bf16[4,128,256]{2,1,0:T(8,128)(2,1)S(1)} %collective-permute-done.4.refs_2_), channel_id=1, source_target_pairs={{0,2},{1,3},{2,0},{3,1},{4,6},{5,7},{6,4},{7,5},{8,10},{9,11},{10,... | collective-permute-start | bytes 786440 | tf_op jit(solution)/shard_map/ppermute | solution.py:18
  22.4 8.0 %collective-permute-start.10 = (bf16[128,512]{1,0:T(8,128)(2,1)}, bf16[128,512]{1,0:T(8,128)(2,1)S(1)}, u32[]{:S(2)}, u32[]{:S(2)}) collective-permute-start(bf16[128,512]{1,0:T(8,128)(2,1)} %get-tuple-element.117), channel_id=1, source_target_pairs={{0,8},{4,12},{8,0},{12,4},{16,24},{20,28},{24,16},{28,20},{1,9},{5... | collective-permute-start | bytes 393224 | tf_op jit(solution)/shard_map/ppermute | solution.py:18
  34.8 9.9 %collective-permute-start.11 = (bf16[2,1024,256]{2,1,0:T(8,128)(2,1)S(1)}, bf16[2,1024,256]{2,1,0:T(8,128)(2,1)S(1)}, u32[]{:S(2)}, u32[]{:S(2)}) collective-permute-start(bf16[2,1024,256]{2,1,0:T(8,128)(2,1)S(1)} %shard_map.78.refs_0_.refs_2_), channel_id=1, source_target_pairs={{0,1},{1,0},{2,3},{3,2},{4,5},{5,4},{6,7},{7,6},{8,9},{9,8},{10,11... | collective-permute-start | bytes 3145736 | tf_op jit(solution)/shard_map/ppermute | solution.py:18
  35.5 8.9 %collective-permute-start.12 = (bf16[128,512]{1,0:T(8,128)(2,1)S(1)}, bf16[128,512]{1,0:T(8,128)(2,1)S(1)}, u32[]{:S(2)}, u32[]{:S(2)}) collective-permute-start(bf16[128,512]{1,0:T(8,128)(2,1)S(1)} %get-tuple-element.120.refs_7_), channel_id=1, source_target_pairs={{0,28},{4,24},{8,20},{12,16},{16,12},{20,8},{24,4},{28,0},{1,29},{... | collective-permute-start | bytes 393224 | tf_op jit(solution)/shard_map/ppermute | solution.py:18
  48.9 8.2 %collective-permute-start.15 = (bf16[512,128]{1,0:T(8,128)(2,1)S(1)}, bf16[512,128]{1,0:T(8,128)(2,1)S(1)}, u32[]{:S(2)}, u32[]{:S(2)}) collective-permute-start(bf16[512,128]{1,0:T(8,128)(2,1)S(1)} %get-tuple-element.62), channel_id=1, source_target_pairs={{0,8},{4,12},{8,0},{12,4},{16,24},{20,28},{24,16},{28,20},{1,9},{5... | collective-permute-start | bytes 393224 | tf_op jit(solution)/shard_map/ppermute | solution.py:18
  50.6 11.1 %collective-permute-start.16 = (bf16[512,128]{1,0:T(8,128)(2,1)}, bf16[512,128]{1,0:T(8,128)(2,1)}, u32[]{:S(2)}, u32[]{:S(2)}) collective-permute-start(bf16[512,128]{1,0:T(8,128)(2,1)} %get-tuple-element.63), channel_id=1, source_target_pairs={{0,12},{4,8},{8,4},{12,0},{16,28},{20,24},{24,20},{28,16},{1,13},{... | collective-permute-start | bytes 393224 | tf_op jit(solution)/shard_map/ppermute | solution.py:18
  51.4 18.4 %collective-permute-start.17 = (bf16[512,128]{1,0:T(8,128)(2,1)}, bf16[512,128]{1,0:T(8,128)(2,1)}, u32[]{:S(2)}, u32[]{:S(2)}) collective-permute-start(bf16[512,128]{1,0:T(8,128)(2,1)} %get-tuple-element.64), channel_id=1, source_target_pairs={{0,16},{4,20},{8,24},{12,28},{16,0},{20,4},{24,8},{28,12},{1,17},{... | collective-permute-start | bytes 393224 | tf_op jit(solution)/shard_map/ppermute | solution.py:18
  53.7 19.5 %collective-permute-start.18 = (bf16[512,128]{1,0:T(8,128)(2,1)}, bf16[512,128]{1,0:T(8,128)(2,1)}, u32[]{:S(2)}, u32[]{:S(2)}) collective-permute-start(bf16[512,128]{1,0:T(8,128)(2,1)} %get-tuple-element.65), channel_id=1, source_target_pairs={{0,20},{4,16},{8,28},{12,24},{16,4},{20,0},{24,12},{28,8},{1,21},{... | collective-permute-start | bytes 393224 | tf_op jit(solution)/shard_map/ppermute | solution.py:18
  55.4 17.8 %collective-permute-start.19 = (bf16[512,128]{1,0:T(8,128)(2,1)}, bf16[512,128]{1,0:T(8,128)(2,1)}, u32[]{:S(2)}, u32[]{:S(2)}) collective-permute-start(bf16[512,128]{1,0:T(8,128)(2,1)} %get-tuple-element.66), channel_id=1, source_target_pairs={{0,24},{4,28},{8,16},{12,20},{16,8},{20,12},{24,0},{28,4},{1,25},{... | collective-permute-start | bytes 393224 | tf_op jit(solution)/shard_map/ppermute | solution.py:18
  57.0 16.2 %collective-permute-start.20 = (bf16[512,128]{1,0:T(8,128)(2,1)}, bf16[512,128]{1,0:T(8,128)(2,1)}, u32[]{:S(2)}, u32[]{:S(2)}) collective-permute-start(bf16[512,128]{1,0:T(8,128)(2,1)} %get-tuple-element.67), channel_id=1, source_target_pairs={{0,28},{4,24},{8,20},{12,16},{16,12},{20,8},{24,4},{28,0},{1,29},{... | collective-permute-start | bytes 393224 | tf_op jit(solution)/shard_map/ppermute | solution.py:18
  81.0 7.9 %collective-permute-start.23 = (bf16[1024,128]{1,0:T(8,128)(2,1)S(1)}, bf16[1024,128]{1,0:T(8,128)(2,1)S(1)}, u32[]{:S(2)}, u32[]{:S(2)}) collective-permute-start(bf16[1024,128]{1,0:T(8,128)(2,1)S(1)} %get-tuple-element.75), channel_id=1, source_target_pairs={{0,1},{1,0},{2,3},{3,2},{4,5},{5,4},{6,7},{7,6},{8,9},{9,8},{10,11... | collective-permute-start | bytes 786440 | tf_op jit(solution)/shard_map/ppermute | solution.py:181
  91.4 10.8 %collective-permute-start.25 = (bf16[512,128]{1,0:T(8,128)(2,1)S(1)}, bf16[512,128]{1,0:T(8,128)(2,1)S(1)}, u32[]{:S(2)}, u32[]{:S(2)}) collective-permute-start(bf16[512,128]{1,0:T(8,128)(2,1)S(1)} %get-tuple-element.78), channel_id=1, source_target_pairs={{0,4},{4,0},{8,12},{12,8},{16,20},{20,16},{24,28},{28,24},{1,5},{5... | collective-permute-start | bytes 393224 | tf_op jit(solution)/shard_map/ppermute | solution.py:18
  92.3 18.6 %collective-permute-start.26 = (bf16[512,128]{1,0:T(8,128)(2,1)S(1)}, bf16[512,128]{1,0:T(8,128)(2,1)S(1)}, u32[]{:S(2)}, u32[]{:S(2)}) collective-permute-start(bf16[512,128]{1,0:T(8,128)(2,1)S(1)} %get-tuple-element.82), channel_id=1, source_target_pairs={{0,16},{4,20},{8,24},{12,28},{16,0},{20,4},{24,8},{28,12},{1,17},{... | collective-permute-start | bytes 393224 | tf_op jit(solution)/shard_map/ppermute | solution.py:18
  97.5 18.2 %collective-permute-start.27 = (bf16[512,128]{1,0:T(8,128)(2,1)S(1)}, bf16[512,128]{1,0:T(8,128)(2,1)S(1)}, u32[]{:S(2)}, u32[]{:S(2)}) collective-permute-start(bf16[512,128]{1,0:T(8,128)(2,1)S(1)} %get-tuple-element.83), channel_id=1, source_target_pairs={{0,20},{4,16},{8,28},{12,24},{16,4},{20,0},{24,12},{28,8},{1,21},{... | collective-permute-start | bytes 393224 | tf_op jit(solution)/shard_map/ppermute | solution.py:18
  98.1 17.6 %collective-permute-start.28 = (bf16[512,128]{1,0:T(8,128)(2,1)S(1)}, bf16[512,128]{1,0:T(8,128)(2,1)S(1)}, u32[]{:S(2)}, u32[]{:S(2)}) collective-permute-start(bf16[512,128]{1,0:T(8,128)(2,1)S(1)} %get-tuple-element.84), channel_id=1, source_target_pairs={{0,24},{4,28},{8,16},{12,20},{16,8},{20,12},{24,0},{28,4},{1,25},{... | collective-permute-start | bytes 393224 | tf_op jit(solution)/shard_map/ppermute | solution.py:18
  100.0 15.6 %collective-permute-start.29 = (bf16[512,128]{1,0:T(8,128)(2,1)S(1)}, bf16[512,128]{1,0:T(8,128)(2,1)S(1)}, u32[]{:S(2)}, u32[]{:S(2)}) collective-permute-start(bf16[512,128]{1,0:T(8,128)(2,1)S(1)} %get-tuple-element.85), channel_id=1, source_target_pairs={{0,28},{4,24},{8,20},{12,16},{16,12},{20,8},{24,4},{28,0},{1,29},{... | collective-permute-start | bytes 393224 | tf_op jit(solution)/shard_map/ppermute | solution.py:18
  110.9 10.9 %collective-permute-start.31 = (bf16[512,128]{1,0:T(8,128)(2,1)S(1)}, bf16[512,128]{1,0:T(8,128)(2,1)S(1)}, u32[]{:S(2)}, u32[]{:S(2)}) collective-permute-start(bf16[512,128]{1,0:T(8,128)(2,1)S(1)} %get-tuple-element.88), channel_id=1, source_target_pairs={{0,12},{4,8},{8,4},{12,0},{16,28},{20,24},{24,20},{28,16},{1,13},{... | collective-permute-start | bytes 393224 | tf_op jit(solution)/shard_map/ppermute | solution.py:18
  126.6 13.4 %collective-permute-start.41 = (bf16[2,4,128,128]{3,2,1,0:T(8,128)(2,1)S(1)}, bf16[2,4,128,128]{3,2,1,0:T(8,128)(2,1)S(1)}, u32[]{:S(2)}, u32[]{:S(2)}) collective-permute-start(bf16[2,4,128,128]{3,2,1,0:T(8,128)(2,1)S(1)} %get-tuple-element.105), channel_id=1, source_target_pairs={{0,4},{4,0},{8,12},{12,8},{16,20},{20,16},{24,28},{28,24},{1,5},{5... | collective-permute-start | bytes 786440 | tf_op jit(solution)/shard_map/ppermute | solution.py:18
  127.2 14.8 %collective-permute-start.40 = (bf16[1088,128]{1,0:T(8,128)(2,1)S(1)}, bf16[1088,128]{1,0:T(8,128)(2,1)S(1)}, u32[]{:S(2)}, u32[]{:S(2)}) collective-permute-start(bf16[1088,128]{1,0:T(8,128)(2,1)S(1)} %get-tuple-element.102), channel_id=1, source_target_pairs={{0,2},{1,3},{2,0},{3,1},{4,6},{5,7},{6,4},{7,5},{8,10},{9,11},{10,... | collective-permute-start | bytes 835592 | tf_op jit(solution)/shard_map/ppermute | solution.py:18
  131.8 18.3 %collective-permute-start.33 = (bf16[128,512]{1,0:T(8,128)(2,1)S(1)}, bf16[128,512]{1,0:T(8,128)(2,1)S(1)}, u32[]{:S(2)}, u32[]{:S(2)}) collective-permute-start(bf16[128,512]{1,0:T(8,128)(2,1)S(1)} %get-tuple-element.92), channel_id=1, source_target_pairs={{0,16},{4,20},{8,24},{12,28},{16,0},{20,4},{24,8},{28,12},{1,17},{... | collective-permute-start | bytes 393224 | tf_op jit(solution)/shard_map/ppermute | solution.py:18
  134.1 19.0 %collective-permute-start.34 = (bf16[128,512]{1,0:T(8,128)(2,1)}, bf16[128,512]{1,0:T(8,128)(2,1)}, u32[]{:S(2)}, u32[]{:S(2)}) collective-permute-start(bf16[128,512]{1,0:T(8,128)(2,1)} %get-tuple-element.93), channel_id=1, source_target_pairs={{0,20},{4,16},{8,28},{12,24},{16,4},{20,0},{24,12},{28,8},{1,21},{... | collective-permute-start | bytes 393224 | tf_op jit(solution)/shard_map/ppermute | solution.py:18
  138.1 15.0 %collective-permute-start.35 = (bf16[128,512]{1,0:T(8,128)(2,1)}, bf16[128,512]{1,0:T(8,128)(2,1)}, u32[]{:S(2)}, u32[]{:S(2)}) collective-permute-start(bf16[128,512]{1,0:T(8,128)(2,1)} %get-tuple-element.94), channel_id=1, source_target_pairs={{0,24},{4,28},{8,16},{12,20},{16,8},{20,12},{24,0},{28,4},{1,25},{... | collective-permute-start | bytes 393224 | tf_op jit(solution)/shard_map/ppermute | solution.py:18
  140.0 16.4 %collective-permute-start.36 = (bf16[128,512]{1,0:T(8,128)(2,1)}, bf16[128,512]{1,0:T(8,128)(2,1)}, u32[]{:S(2)}, u32[]{:S(2)}) collective-permute-start(bf16[128,512]{1,0:T(8,128)(2,1)} %get-tuple-element.95), channel_id=1, source_target_pairs={{0,28},{4,24},{8,20},{12,16},{16,12},{20,8},{24,4},{28,0},{1,29},{... | collective-permute-start | bytes 393224 | tf_op jit(solution)/shard_map/ppermute | solution.py:18
  144.3 14.3 %collective-permute-start.42 = (bf16[4,128,128]{2,1,0:T(8,128)(2,1)}, bf16[4,128,128]{2,1,0:T(8,128)(2,1)S(1)}, u32[]{:S(2)}, u32[]{:S(2)}) collective-permute-start(bf16[4,128,128]{2,1,0:T(8,128)(2,1)} %get-tuple-element.108), channel_id=1, source_target_pairs={{0,4},{4,0},{8,12},{12,8},{16,20},{20,16},{24,28},{28,24},{1,5},{5... | collective-permute-start | bytes 393224 | tf_op jit(solution)/shard_map/ppermute | solution.py:18
  150.7 7.8 %collective-permute-start.43 = (bf16[4,128,128]{2,1,0:T(8,128)(2,1)}, bf16[4,128,128]{2,1,0:T(8,128)(2,1)}, u32[]{:S(2)}, u32[]{:S(2)}) collective-permute-start(bf16[4,128,128]{2,1,0:T(8,128)(2,1)} %get-tuple-element.110), channel_id=1, source_target_pairs={{0,2},{1,3},{2,0},{3,1},{4,6},{5,7},{6,4},{7,5},{8,10},{9,11},{10,... | collective-permute-start | bytes 393224 | tf_op jit(solution)/shard_map/ppermute | solution.py:18
  153.1 11.6 %collective-permute-start.37 = (bf16[128,512]{1,0:T(8,128)(2,1)}, bf16[128,512]{1,0:T(8,128)(2,1)S(1)}, u32[]{:S(2)}, u32[]{:S(2)}) collective-permute-start(bf16[128,512]{1,0:T(8,128)(2,1)} %copy-done.14), channel_id=1, source_target_pairs={{0,8},{4,12},{8,0},{12,4},{16,24},{20,28},{24,16},{28,20},{1,9},{5... | collective-permute-start | bytes 393224 | tf_op jit(solution)/shard_map/ppermute | solution.py:18
  153.1 11.6 %collective-permute-start.38 = (bf16[128,512]{1,0:T(8,128)(2,1)}, bf16[128,512]{1,0:T(8,128)(2,1)S(1)}, u32[]{:S(2)}, u32[]{:S(2)}) collective-permute-start(bf16[128,512]{1,0:T(8,128)(2,1)} %copy-done.13), channel_id=1, source_target_pairs={{0,12},{4,8},{8,4},{12,0},{16,28},{20,24},{24,20},{28,16},{1,13},{... | collective-permute-start | bytes 393224 | tf_op jit(solution)/shard_map/ppermute | solution.py:18
  (39 other events, 173.0 us)
